TPU v7x, 32 devices: a whole 2x2x4 slice. The times are simulated.
32 devices in a mesh: img: 8 (over z, core), row: 4 (over y, x).
Axes of the slice: x: 2, y: 2, z: 4, core: 2. Of those that a mesh axis runs over, the one named last changes fastest.
Arguments:
- patches: bfloat16 [16, 32, 32, 192], P('img', 'row'), may hold values from -6 to 6
- valid_mask: int32 [16, 32, 32], P('img'), may hold values from 0 to 1, as said below
- norm_gains: float32 [2, 192], replicated, may hold values from 0.5 to 1.5
- w_u: bfloat16 [192, 192], P('row', 'img'), may hold values from -0.4375 to 0.4375
- decay_rate: bfloat16 [192, 64], P('row', 'img'), may hold values from 0.019897461 to 1
- out_coef: bfloat16 [192, 64], P('row', 'img'), may hold values from -0.8984375 to 0.8984375
- w_qkv: bfloat16 [192, 576], P('row', 'img'), may hold values from -0.4375 to 0.4375
- w_o: bfloat16 [192, 192], P('row', 'img'), may hold values from -1.75 to 1.75
- w_fc1: bfloat16 [192, 768], P('row', 'img'), may hold values from -0.4375 to 0.4375
- w_fc2: bfloat16 [768, 192], P('row', 'img'), may hold values from -0.21875 to 0.21875
- cotangent: bfloat16 [16, 32, 32, 192], P('img', 'row'), may hold values from -6 to 6
Outputs:
- block_out: bfloat16 [16, 32, 32, 192], P('img', 'row')
- grad_patches: bfloat16 [16, 32, 32, 192], P('img', 'row')
- grad_gain_one: float32 [192], replicated
- grad_gain_two: float32 [192], replicated
- grad_w_u: float32 [192, 192], P('row', 'img')
- grad_decay: float32 [192, 64], P('row', 'img')
- grad_coef: float32 [192, 64], P('row', 'img')
- grad_w_qkv: float32 [192, 576], P('row', 'img')
- grad_w_o: float32 [192, 192], P('row', 'img')
- grad_w_fc1: float32 [192, 768], P('row', 'img')
- grad_w_fc2: float32 [768, 192], P('row', 'img')
Inputs may be any that keep to these rules, and one draw needn't show every extreme that they name: `valid_mask`: the valid slots of an image are those in its first h rows or in its first w columns (or both), with 16 <= h, w <= 31 drawn for each image.
All inputs are finite; a program needn't handle non-finite values.
Results may differ from a plain program's by a relative error of at most 0.025.
The roundings to bfloat16 on the way count: a program that leaves them out, or rounds other values in their place, can miss the bound.
Values may be sent and summed in bfloat16 or wider, within the bound.
No kernel may reach another device: no remote copies, remote signals or barrier semaphores. Data moves between devices by JAX's collectives and lax.ppermute only.
A program may use at most 128 MiB of HBM per device.

v0:
```python
from functools import partial

import jax
import jax.numpy as jnp
import numpy as np
from jax import lax
from jax.sharding import PartitionSpec as P

HEADS = 3
HEAD_DIM = 64
STATE = 16
GRID = 32


def layer_norm(values, gain):
    center = values - jnp.mean(values, -1, keepdims=True)
    spread = jnp.mean(center * center, -1, keepdims=True)
    return center * lax.rsqrt(spread + 1e-05) * gain


def kernels(rate_values, coef_values):
    lag_steps = jnp.arange(GRID, dtype=jnp.float32)
    powers = jnp.exp(-rate_values[None, :, :] * lag_steps[:, None, None])
    kernel_table = jnp.sum(
        (coef_values[None, :, :] * powers).reshape(GRID, rate_values.shape[0], 4, STATE), -1
    )
    offset = np.abs(np.arange(GRID)[:, None] - np.arange(GRID)[None, :])
    lower_part = (np.arange(GRID)[:, None] >= np.arange(GRID)[None, :])[:, :, None]
    upper_part = (np.arange(GRID)[:, None] <= np.arange(GRID)[None, :])[:, :, None]
    picked = kernel_table[offset]
    across = jnp.where(lower_part, picked[:, :, :, 0], 0.0) + jnp.where(
        upper_part, picked[:, :, :, 1], 0.0
    )
    downward = jnp.where(lower_part, picked[:, :, :, 2], 0.0) + jnp.where(
        upper_part, picked[:, :, :, 3], 0.0
    )
    return (across, downward)


def outer_sum(left, right):
    return jnp.einsum("bijd,bije->de", left, right, preferred_element_type=jnp.float32)


def back_product(grad_rows, weight):
    return jnp.einsum("bije,de->bijd", grad_rows, weight, preferred_element_type=jnp.float32)


def per_device(
    patches, valid_mask, norm_gains, w_u, decay_rate, out_coef, w_qkv, w_o, w_fc1, w_fc2, cotangent
):
    image_count, rows_here, grid_width, model_width = patches.shape
    row_index = lax.axis_index("row")
    head_scale = HEAD_DIM ** (-0.5)
    valid_full = valid_mask.astype(jnp.float32)
    valid_rows = lax.dynamic_slice_in_dim(valid_full, row_index * rows_here, rows_here, 1)
    row_masks = valid_rows[..., None]
    mask_low = row_masks.astype(jnp.bfloat16)
    key_valid = valid_full.reshape(image_count, -1)
    wu_part, rate_part, coef_part, qkv_part, wo_part, fc1_part, fc2_part = (
        lax.all_gather(w_u, "img", axis=1, tiled=True),
        lax.all_gather(decay_rate, "img", axis=1, tiled=True),
        lax.all_gather(out_coef, "img", axis=1, tiled=True),
        lax.all_gather(w_qkv, "img", axis=1, tiled=True),
        lax.all_gather(w_o, "img", axis=1, tiled=True),
        lax.all_gather(w_fc1, "img", axis=1, tiled=True),
        lax.all_gather(w_fc2, "img", axis=1, tiled=True),
    )
    wu_full, rate_full, coef_full, qkv_full, wo_full, fc1_full, fc2_full = (
        lax.all_gather(wu_part, "row", axis=0, tiled=True),
        lax.all_gather(rate_part, "row", axis=0, tiled=True),
        lax.all_gather(coef_part, "row", axis=0, tiled=True),
        lax.all_gather(qkv_part, "row", axis=0, tiled=True),
        lax.all_gather(wo_part, "row", axis=0, tiled=True),
        lax.all_gather(fc1_part, "row", axis=0, tiled=True),
        lax.all_gather(fc2_part, "row", axis=0, tiled=True),
    )
    source = patches.astype(jnp.float32)
    first_low = layer_norm(source, norm_gains[0]).astype(jnp.bfloat16)
    mixed_low = (
        jnp.einsum("bijd,de->bije", first_low, wu_full, preferred_element_type=jnp.float32)
        * row_masks
    ).astype(jnp.bfloat16)
    (across, downward), kernel_back = jax.vjp(
        kernels, rate_full.astype(jnp.float32), coef_full.astype(jnp.float32)
    )
    across_low = across.astype(jnp.bfloat16)
    down_low = downward.astype(jnp.bfloat16)
    along_rows = jnp.einsum(
        "tsc,bisc->bitc", across_low, mixed_low, preferred_element_type=jnp.float32
    )
    column_in = lax.all_to_all(mixed_low, "row", split_axis=2, concat_axis=1, tiled=True)
    along_cols = jnp.einsum(
        "tsc,bsjc->btjc", down_low, column_in, preferred_element_type=jnp.float32
    ).astype(jnp.bfloat16)
    cols_back = lax.all_to_all(along_cols, "row", split_axis=1, concat_axis=2, tiled=True)
    scanned = ((along_rows + cols_back.astype(jnp.float32)) * row_masks).astype(jnp.bfloat16)
    triple = jnp.einsum("bijd,de->bije", scanned, qkv_full, preferred_element_type=jnp.float32)
    head_shape = (image_count, rows_here * grid_width, HEADS, HEAD_DIM)
    queries = (triple[..., :model_width] * head_scale).astype(jnp.bfloat16).reshape(head_shape)
    key_rows = (
        triple[..., model_width : 2 * model_width]
        .astype(jnp.bfloat16)
        .reshape(image_count, -1, model_width)
    )
    value_rows = (
        triple[..., 2 * model_width :].astype(jnp.bfloat16).reshape(image_count, -1, model_width)
    )
    all_keys, all_values = (
        lax.all_gather(key_rows, "row", axis=1, tiled=True),
        lax.all_gather(value_rows, "row", axis=1, tiled=True),
    )
    key_heads = all_keys.reshape(image_count, -1, HEADS, HEAD_DIM)
    value_heads = all_values.reshape(image_count, -1, HEADS, HEAD_DIM)
    scores = jnp.einsum("bqhe,bkhe->bhqk", queries, key_heads, preferred_element_type=jnp.float32)
    scores = jnp.where(key_valid[:, None, None, :] > 0, scores, -1e30)
    soft_weights = jax.nn.softmax(scores, axis=-1)
    soft_low = soft_weights.astype(jnp.bfloat16)
    attended = jnp.einsum(
        "bhqk,bkhe->bqhe", soft_low, value_heads, preferred_element_type=jnp.float32
    ).astype(jnp.bfloat16)
    attended_rows = attended.reshape(patches.shape)
    branch = jnp.einsum("bijd,de->bije", attended_rows, wo_full, preferred_element_type=jnp.float32)
    middle = source + branch * row_masks
    second_low = layer_norm(middle, norm_gains[1]).astype(jnp.bfloat16)
    pre_act = jnp.einsum("bijd,df->bijf", second_low, fc1_full, preferred_element_type=jnp.float32)
    hidden = jax.nn.gelu(pre_act, approximate=False).astype(jnp.bfloat16)
    block_out = (
        middle + jnp.einsum("bijf,fd->bijd", hidden, fc2_full, preferred_element_type=jnp.float32)
    ).astype(jnp.bfloat16)
    grad_fc2 = jnp.einsum("bijf,bijd->fd", hidden, cotangent, preferred_element_type=jnp.float32)
    grad_hidden = jnp.einsum(
        "bijd,fd->bijf", cotangent, fc2_full, preferred_element_type=jnp.float32
    )
    gelu_back = jax.vjp(partial(jax.nn.gelu, approximate=False), pre_act)[1]
    grad_pre = gelu_back(grad_hidden)[0].astype(jnp.bfloat16)
    grad_fc1 = jnp.einsum("bijd,bijf->df", second_low, grad_pre, preferred_element_type=jnp.float32)
    grad_second = jnp.einsum(
        "bijf,df->bijd", grad_pre, fc1_full, preferred_element_type=jnp.float32
    )
    norm_back_two = jax.vjp(layer_norm, middle, norm_gains[1])[1]
    grad_norm_mid, gain_two = norm_back_two(grad_second)
    grad_middle = cotangent.astype(jnp.float32) + grad_norm_mid
    grad_branch = (grad_middle * row_masks).astype(jnp.bfloat16)
    grad_wo = outer_sum(attended_rows, grad_branch)
    grad_attended = back_product(grad_branch, wo_full).astype(jnp.bfloat16).reshape(head_shape)
    grad_soft = jnp.einsum(
        "bqhe,bkhe->bhqk", grad_attended, value_heads, preferred_element_type=jnp.float32
    )
    row_total = jnp.sum(soft_weights * grad_soft, -1, keepdims=True)
    grad_scores = (soft_weights * (grad_soft - row_total)).astype(jnp.bfloat16)
    grad_queries = (
        jnp.einsum(
            "bhqk,bkhe->bqhe", grad_scores, key_heads, preferred_element_type=jnp.float32
        ).astype(jnp.bfloat16)
        * head_scale
    )
    key_terms = jnp.einsum(
        "bhqk,bqhe->bkhe", grad_scores, queries, preferred_element_type=jnp.float32
    ).reshape(image_count, -1, model_width)
    value_terms = jnp.einsum(
        "bhqk,bqhe->bkhe", soft_low, grad_attended, preferred_element_type=jnp.float32
    ).reshape(image_count, -1, model_width)
    key_sums, value_sums = (
        lax.psum_scatter(
            key_terms.astype(jnp.bfloat16), "row", scatter_dimension=1, tiled=True
        ).astype(jnp.float32),
        lax.psum_scatter(
            value_terms.astype(jnp.bfloat16), "row", scatter_dimension=1, tiled=True
        ).astype(jnp.float32),
    )
    grad_keys = key_sums.astype(jnp.bfloat16)
    grad_values = value_sums.astype(jnp.bfloat16)
    grad_triple = jnp.concatenate(
        [
            grad_queries.reshape(patches.shape),
            grad_keys.reshape(patches.shape),
            grad_values.reshape(patches.shape),
        ],
        -1,
    )
    grad_wqkv = outer_sum(scanned, grad_triple)
    grad_scanned = back_product(grad_triple, qkv_full).astype(jnp.bfloat16) * mask_low
    grad_cols = lax.all_to_all(grad_scanned, "row", split_axis=2, concat_axis=1, tiled=True)
    grad_down = jnp.einsum(
        "btjc,bsjc->tsc", grad_cols, column_in, preferred_element_type=jnp.float32
    )
    grad_col_in = jnp.einsum(
        "tsc,btjc->bsjc", down_low, grad_cols, preferred_element_type=jnp.float32
    ).astype(jnp.bfloat16)
    grad_row_in = lax.all_to_all(grad_col_in, "row", split_axis=1, concat_axis=2, tiled=True)
    grad_across = jnp.einsum(
        "bitc,bisc->tsc", grad_scanned, mixed_low, preferred_element_type=jnp.float32
    )
    grad_mixed = jnp.einsum(
        "tsc,bitc->bisc", across_low, grad_scanned, preferred_element_type=jnp.float32
    ) + grad_row_in.astype(jnp.float32)
    grad_mixed = grad_mixed.astype(jnp.bfloat16) * mask_low
    grad_rate, grad_coef = kernel_back((grad_across, grad_down))
    grad_wu = outer_sum(first_low, grad_mixed)
    grad_first = back_product(grad_mixed, wu_full)
    norm_back_one = jax.vjp(layer_norm, source, norm_gains[0])[1]
    grad_norm_src, gain_one = norm_back_one(grad_first)
    grad_patches = (grad_middle + grad_norm_src).astype(jnp.bfloat16)
    gain_sums = lax.psum(jnp.stack([gain_one, gain_two]), ("img", "row"))
    sum_wu, sum_rate, sum_coef, sum_qkv, sum_wo, sum_fc1, sum_fc2 = (
        lax.psum_scatter(
            grad_wu.astype(jnp.bfloat16), "row", scatter_dimension=0, tiled=True
        ).astype(jnp.float32),
        lax.psum_scatter(
            grad_rate.astype(jnp.bfloat16), "row", scatter_dimension=0, tiled=True
        ).astype(jnp.float32),
        lax.psum_scatter(
            grad_coef.astype(jnp.bfloat16), "row", scatter_dimension=0, tiled=True
        ).astype(jnp.float32),
        lax.psum_scatter(
            grad_wqkv.astype(jnp.bfloat16), "row", scatter_dimension=0, tiled=True
        ).astype(jnp.float32),
        lax.psum_scatter(
            grad_wo.astype(jnp.bfloat16), "row", scatter_dimension=0, tiled=True
        ).astype(jnp.float32),
        lax.psum_scatter(
            grad_fc1.astype(jnp.bfloat16), "row", scatter_dimension=0, tiled=True
        ).astype(jnp.float32),
        lax.psum_scatter(
            grad_fc2.astype(jnp.bfloat16), "row", scatter_dimension=0, tiled=True
        ).astype(jnp.float32),
    )
    final_wu, final_rate, final_coef, final_qkv, final_wo, final_fc1, final_fc2 = (
        lax.psum_scatter(
            sum_wu.astype(jnp.bfloat16), "img", scatter_dimension=1, tiled=True
        ).astype(jnp.float32),
        lax.psum_scatter(
            sum_rate.astype(jnp.bfloat16), "img", scatter_dimension=1, tiled=True
        ).astype(jnp.float32),
        lax.psum_scatter(
            sum_coef.astype(jnp.bfloat16), "img", scatter_dimension=1, tiled=True
        ).astype(jnp.float32),
        lax.psum_scatter(
            sum_qkv.astype(jnp.bfloat16), "img", scatter_dimension=1, tiled=True
        ).astype(jnp.float32),
        lax.psum_scatter(
            sum_wo.astype(jnp.bfloat16), "img", scatter_dimension=1, tiled=True
        ).astype(jnp.float32),
        lax.psum_scatter(
            sum_fc1.astype(jnp.bfloat16), "img", scatter_dimension=1, tiled=True
        ).astype(jnp.float32),
        lax.psum_scatter(
            sum_fc2.astype(jnp.bfloat16), "img", scatter_dimension=1, tiled=True
        ).astype(jnp.float32),
    )
    return (
        block_out,
        grad_patches,
        gain_sums[0],
        gain_sums[1],
        final_wu,
        final_rate,
        final_coef,
        final_qkv,
        final_wo,
        final_fc1,
        final_fc2,
    )


def solution(mesh):
    in_specs = (
        P("img", "row", None, None),
        P("img", None, None),
        P(),
        P("row", "img"),
        P("row", "img"),
        P("row", "img"),
        P("row", "img"),
        P("row", "img"),
        P("row", "img"),
        P("row", "img"),
        P("img", "row", None, None),
    )
    out_specs = (
        P("img", "row", None, None),
        P("img", "row", None, None),
        P(),
        P(),
        P("row", "img"),
        P("row", "img"),
        P("row", "img"),
        P("row", "img"),
        P("row", "img"),
        P("row", "img"),
        P("row", "img"),
    )
    return jax.shard_map(
        per_device, mesh=mesh, in_specs=in_specs, out_specs=out_specs, check_vma=False
    )
```

profile of v0, /device:TPU:0, one launch (start us, length us, event | category | flops | bytes accessed | tf_op | source)
XLA Modules:
  0.0 696.4 jit_solution(987558202515493780)
XLA Ops:
  11.1 15.9 %all_gather.48 = bf16[48,192]{0,1:T(8,128)(2,1)S(1)} all-gather(bf16[48,24]{0,1:T(8,128)(2,1)} %param.18), channel_id=1, replica_groups=mesh['img'=8,'row'=4] {'img'}, dimensions={1}, use_global_device_ids=true | all-gather | bytes 20736 | tf_op jit(solution)/shard_map/all_gather | solution.py:60
  27.0 8.4 %all_gather.49 = bf16[192,192]{1,0:T(8,128)(2,1)S(1)} all-gather(bf16[48,192]{1,0:T(8,128)(2,1)S(1)} %copy.378), channel_id=1, replica_groups=mesh['img'=8,'row'=4] {'row'}, dimensions={0}, use_global_device_ids=true | all-gather | bytes 92160 | tf_op jit(solution)/shard_map/all_gather | solution.py:69
  42.4 12.7 %all_gather.52 = bf16[48,64]{0,1:T(8,128)(2,1)S(1)} all-gather(bf16[48,8]{0,1:T(8,128)(2,1)S(1)} %copy-done.62), channel_id=1, replica_groups=mesh['img'=8,'row'=4] {'img'}, dimensions={1}, use_global_device_ids=true | all-gather | bytes 6912 | tf_op jit(solution)/shard_map/all_gather | solution.py:61
  55.2 12.7 %all_gather.50 = bf16[48,64]{0,1:T(8,128)(2,1)S(1)} all-gather(bf16[48,8]{0,1:T(8,128)(2,1)S(1)} %copy-done.63), channel_id=1, replica_groups=mesh['img'=8,'row'=4] {'img'}, dimensions={1}, use_global_device_ids=true | all-gather | bytes 6912 | tf_op jit(solution)/shard_map/all_gather | solution.py:62
  68.0 8.7 %all_gather.51 = bf16[192,64]{1,0:T(8,128)(2,1)S(1)} all-gather(bf16[48,64]{1,0:T(8,128)(2,1)S(1)} %copy.379), channel_id=1, replica_groups=mesh['img'=8,'row'=4] {'row'}, dimensions={0}, use_global_device_ids=true | all-gather | bytes 30720 | tf_op jit(solution)/shard_map/all_gather | solution.py:71
  76.8 8.2 %all_gather.53 = bf16[192,64]{1,0:T(8,128)(2,1)S(1)} all-gather(bf16[48,64]{1,0:T(8,128)(2,1)S(1)} %copy.381), channel_id=1, replica_groups=mesh['img'=8,'row'=4] {'row'}, dimensions={0}, use_global_device_ids=true | all-gather | bytes 30720 | tf_op jit(solution)/shard_map/all_gather | solution.py:70
  85.8 9.5 %gather_fusion = f32[1024,192,4]{1,2,0:T(4,128)} fusion(f32[32,192,4]{1,2,0:T(4,128)S(1)} %multiply_reduce_fusion.3, s32[1024]{0:T(1024)S(1)} %broadcast_clamp_fusion), kind=kCustom, calls=%fused_computation | custom fusion | bytes 6295552 | tf_op jit(solution)/shard_map/jvp()/gather | solution.py:30
  103.3 14.0 %all_gather.58 = bf16[48,192]{0,1:T(8,128)(2,1)S(1)} all-gather(bf16[48,24]{0,1:T(8,128)(2,1)S(1)} %copy-done.61), channel_id=1, replica_groups=mesh['img'=8,'row'=4] {'img'}, dimensions={1}, use_global_device_ids=true | all-gather | bytes 20736 | tf_op jit(solution)/shard_map/all_gather | solution.py:64
  117.4 13.9 %all-gather = bf16[8,72,48]{1,2,0:T(8,128)(2,1)S(1)} all-gather(bf16[1,72,48]{1,2,0:T(8,128)(2,1)S(1)} %bitcast.325), channel_id=1, replica_groups=mesh['img'=8,'row'=4] {'img'}, dimensions={0}, use_global_device_ids=true | all-gather | bytes 62208 | tf_op jit(solution)/shard_map/all_gather | solution.py:63
  132.1 13.9 %all-gather.1 = bf16[8,96,48]{1,2,0:T(8,128)(2,1)S(1)} all-gather(bf16[1,96,48]{1,2,0:T(8,128)(2,1)S(1)} %bitcast.326), channel_id=1, replica_groups=mesh['img'=8,'row'=4] {'img'}, dimensions={0}, use_global_device_ids=true | all-gather | bytes 82944 | tf_op jit(solution)/shard_map/all_gather | solution.py:65
  146.8 13.9 %all_gather.62 = bf16[192,192]{0,1:T(8,128)(2,1)S(1)} all-gather(bf16[192,24]{0,1:T(8,128)(2,1)S(1)} %copy-done.60), channel_id=1, replica_groups=mesh['img'=8,'row'=4] {'img'}, dimensions={1}, use_global_device_ids=true | all-gather | bytes 82944 | tf_op jit(solution)/shard_map/all_gather | solution.py:66
  165.3 7.6 %all_gather.59 = bf16[192,192]{1,0:T(8,128)(2,1)S(1)} all-gather(bf16[48,192]{1,0:T(8,128)(2,1)S(1)} %copy.400), channel_id=1, replica_groups=mesh['img'=8,'row'=4] {'row'}, dimensions={0}, use_global_device_ids=true | all-gather | bytes 92160 | tf_op jit(solution)/shard_map/all_gather | solution.py:73
  180.8 9.7 %all_gather.55 = bf16[192,576]{1,0:T(8,128)(2,1)S(1)} all-gather(bf16[48,576]{1,0:T(8,128)(2,1)S(1)} %bitcast.310), channel_id=1, replica_groups=mesh['img'=8,'row'=4] {'row'}, dimensions={0}, use_global_device_ids=true | all-gather | bytes 276480 | tf_op jit(solution)/shard_map/all_gather | solution.py:72
  190.5 8.7 %all_gather.61 = bf16[192,768]{1,0:T(8,128)(2,1)S(1)} all-gather(bf16[48,768]{1,0:T(8,128)(2,1)S(1)} %bitcast.305), channel_id=1, replica_groups=mesh['img'=8,'row'=4] {'row'}, dimensions={0}, use_global_device_ids=true | all-gather | bytes 368640 | tf_op jit(solution)/shard_map/all_gather | solution.py:74
  199.3 8.9 %all_gather.63 = bf16[768,192]{1,0:T(8,128)(2,1)S(1)} all-gather(bf16[192,192]{1,0:T(8,128)(2,1)S(1)} %copy-done.34), channel_id=1, replica_groups=mesh['img'=8,'row'=4] {'row'}, dimensions={0}, use_global_device_ids=true | all-gather | bytes 368640 | tf_op jit(solution)/shard_map/all_gather | solution.py:75
  209.5 13.9 %all_gather.56 = bf16[2,1024,192]{2,1,0:T(8,128)(2,1)S(1)} all-gather(bf16[2,256,192]{2,1,0:T(8,128)(2,1)S(1)} %bitcast.295), channel_id=1, replica_groups=mesh['img'=8,'row'=4] {'row'}, dimensions={1}, use_global_device_ids=true | all-gather | bytes 983040 | tf_op jit(solution)/shard_map/all_gather | solution.py:110
  224.7 10.6 %all_gather.57 = bf16[2,1024,192]{2,1,0:T(8,128)(2,1)S(1)} all-gather(bf16[2,256,192]{2,1,0:T(8,128)(2,1)S(1)} %bitcast.294), channel_id=1, replica_groups=mesh['img'=8,'row'=4] {'row'}, dimensions={1}, use_global_device_ids=true | all-gather | bytes 983040 | tf_op jit(solution)/shard_map/all_gather | solution.py:109
  235.8 4.6 fusion.100
  246.8 4.4 multiply_convert_fusion.1
  259.3 16.6 %reduce-scatter.31.cloned.1.call-done = bf16[192,192]{1,0:T(8,128)(2,1)} async-done(((bf16[768,192]{1,0:T(8,128)(2,1)}), bf16[192,192]{1,0:T(8,128)(2,1)}) %reduce-scatter.31.cloned.1.call-update) | async-done | bytes 73744 | tf_op jit(solution)/shard_map/reduce_scatter | solution.py:224
  278.3 24.6 %reduce-scatter.29.cloned.1.call-done = bf16[48,768]{1,0:T(8,128)(2,1)} async-done(((bf16[192,768]{1,0:T(8,128)(2,1)}), bf16[48,768]{1,0:T(8,128)(2,1)}) %reduce-scatter.29.cloned.1.call-update) | async-done | bytes 73744 | tf_op jit(solution)/shard_map/reduce_scatter | solution.py:221
  304.7 4.6 fusion.16
  329.6 5.8 reduce-scatter.35.cloned.1.call-done
  336.9 29.1 %reduce-scatter.33.cloned.1.call-done = bf16[96,48]{1,0:T(8,128)(2,1)} async-done(((bf16[768,48]{1,0:T(8,128)(2,1)}), bf16[96,48]{1,0:T(8,128)(2,1)}) %reduce-scatter.33.cloned.1.call-update) | async-done | bytes 9232
  367.5 25.6 %reduce-scatter.23.cloned.1.call-done = bf16[2,256,192]{1,2,0:T(8,128)(2,1)} async-done(((bf16[2,1024,192]{1,2,0:T(8,128)(2,1)}), bf16[2,256,192]{1,2,0:T(8,128)(2,1)}) %reduce-scatter.23.cloned.1.call-update) | async-done | bytes 196624 | tf_op jit(solution)/shard_map/reduce_scatter | solution.py:167
  394.2 27.8 %reduce-scatter.21.cloned.1.call-done = bf16[2,256,192]{1,2,0:T(8,128)(2,1)} async-done(((bf16[2,1024,192]{1,2,0:T(8,128)(2,1)}), bf16[2,256,192]{1,2,0:T(8,128)(2,1)}) %reduce-scatter.21.cloned.1.call-update) | async-done | bytes 196624 | tf_op jit(solution)/shard_map/reduce_scatter | solution.py:164
  460.2 4.7 copy.426
  464.9 76.0 %scatter_fusion = f32[32,192,4]{1,2,0:T(4,128)S(1)} fusion(f32[32,192,4]{1,2,0:T(4,128)S(1)} %broadcast_in_dim.107, s32[1024]{0:T(1024)S(1)} %copy-done.45, f32[1024,192,4]{1,2,0:T(4,128)} %copy.426), kind=kCustom, calls=%fused_computation.1 | custom fusion | flops 786432 | bytes 9441280 | tf_op jit(solution)/shard_map/transpose(jvp())/scatter-add | solution.py:30
  541.8 17.9 %all-reduce.13 = (bf16[192,64]{0,1:T(8,128)(2,1)S(1)}, bf16[192,64]{0,1:T(8,128)(2,1)S(1)}) all-reduce(bf16[192,64]{0,1:T(8,128)(2,1)S(1)} %bitcast.311, bf16[192,64]{0,1:T(8,128)(2,1)S(1)} %bitcast.314), channel_id=6, replica_groups=mesh['img'=8,'row'=4] {'row'}, use_global_device_ids=true, to_apply=%region_21.22.clone | all-reduce | flops 24576 | bytes 98304
  562.3 39.3 %psum.7 = f32[2,192]{1,0:T(2,128)S(1)} all-reduce(f32[2,192]{1,0:T(2,128)S(1)} %pad_maximum_fusion.3), channel_id=1, replica_groups=mesh['img'=8,'row'=4] {'img','row'}, use_global_device_ids=true, to_apply=%region_16.17 | all-reduce | flops 384 | bytes 3072 | tf_op jit(solution)/shard_map/psum | solution.py:204
  604.0 22.6 %reduce-scatter.25.cloned.1.call-done = bf16[48,192]{1,0:T(8,128)(2,1)} async-done(((bf16[192,192]{1,0:T(8,128)(2,1)}), bf16[48,192]{1,0:T(8,128)(2,1)}) %reduce-scatter.25.cloned.1.call-update) | async-done | bytes 18448 | tf_op jit(solution)/shard_map/reduce_scatter | solution.py:206
  627.1 55.3 %all-reduce.16.cloned.1.call-done = (bf16[48,192]{1,0:T(8,128)(2,1)}, bf16[48,64]{0,1:T(8,128)(2,1)}, bf16[48,64]{0,1:T(8,128)(2,1)}, bf16[48,576]{1,0:T(8,128)(2,1)}, bf16[48,192]{1,0:T(8,128)(2,1)}) async-done(((bf16[48,192]{1,0:T(8,128)(2,1)}, bf16[48,64]{0,1:T(8,128)(2,1)}, bf16[48,64]{0,1:T(8,128)(2,1)}, bf16[48,576]{1,0:T(8,128)(2,1)}, bf16[48,192]{1,0:T(8,128)(2,1)}), (bf16[48,192]{1,0:T(8,128)(2,1)}, ...) | async-done | bytes 104464
  (282 shorter events, 127.8 us)
Async XLA Ops:
  7.9 34.4 %copy-start.56 = (f32[1,192]{1,0:T(1,128)}, f32[1,192]{1,0:T(1,128)S(1)}, u32[]{:S(2)}) copy-start(f32[1,192]{1,0:T(1,128)S(1)} %get-tuple-element.133) | copy-start | bytes 2308
  9.1 28.6 %copy-start.42 = (f32[2,8,32]{2,1,0:T(8,128)}, f32[2,8,32]{2,1,0:T(8,128)S(1)}, u32[]{:S(2)}) copy-start(f32[2,8,32]{2,1,0:T(8,128)S(1)} %broadcast_multiply_fusion.1) | copy-start | bytes 6148
  10.3 27.3 %copy-start.46 = (f32[2,8,32]{2,1,0:T(8,128)}, f32[2,8,32]{2,1,0:T(8,128)S(1)}, u32[]{:S(2)}) copy-start(f32[2,8,32]{2,1,0:T(8,128)S(1)} %fusion.88) | copy-start | bytes 6148
  37.6 135.3 %all-to-all-start = ((bf16[2,8,32,192]{3,1,0,2:T(8,128)(2,1)}), bf16[2,8,32,192]{3,1,0,2:T(8,128)(2,1)}, u32[]{:S(2)}, u32[]{:S(2)}) async-start(bf16[2,8,32,192]{3,1,0,2:T(8,128)(2,1)} %copy.387), calls=%async_computation | async-start | bytes 524288 | tf_op jit(solution)/shard_map/all_to_all | solution.py:91
  42.4 58.6 %copy-start.10 = (bf16[2,8,32,192]{2,1,0,3:T(8,128)(2,1)}, bf16[2,8,32,192]{2,1,0,3:T(8,128)(2,1)S(1)}, u32[]{:S(2)}) copy-start(bf16[2,8,32,192]{2,1,0,3:T(8,128)(2,1)S(1)} %copy.384) | copy-start | bytes 589828
  101.1 31.1 %copy-start.59 = (bf16[48,96]{1,0:T(8,128)(2,1)S(1)}, bf16[48,96]{1,0:T(8,128)(2,1)}, u32[]{:S(2)}) copy-start(bf16[48,96]{1,0:T(8,128)(2,1)} %param.23) | copy-start | bytes 27652
  101.1 45.7 %copy-start.60 = (bf16[192,24]{0,1:T(8,128)(2,1)S(1)}, bf16[192,24]{0,1:T(8,128)(2,1)}, u32[]{:S(2)}) copy-start(bf16[192,24]{0,1:T(8,128)(2,1)} %param.24) | copy-start | bytes 27652
  131.3 32.5 %copy-start.13 = (f32[192,2,8,32]{3,2,1,0:T(8,128)S(1)}, f32[192,2,8,32]{3,2,1,0:T(8,128)}, u32[]{:S(2)}) copy-start(f32[192,2,8,32]{3,2,1,0:T(8,128)} %fusion.102) | copy-start | bytes 1179652
  175.7 23.6 %copy-start.34 = (bf16[192,192]{1,0:T(8,128)(2,1)S(1)}, bf16[192,192]{1,0:T(8,128)(2,1)}, u32[]{:S(2)}) copy-start(bf16[192,192]{1,0:T(8,128)(2,1)} %copy.402) | copy-start | bytes 221188
  175.7 32.5 %copy-start.20 = (f32[192,2,8,32]{0,3,2,1:T(8,128)S(1)}, f32[192,2,8,32]{0,3,2,1:T(8,128)}, u32[]{:S(2)}) copy-start(f32[192,2,8,32]{0,3,2,1:T(8,128)} %copy.386) | copy-start | bytes 1179652
  177.3 30.9 %all-to-all-start.1 = ((bf16[2,32,8,192]{3,2,0,1:T(8,128)(2,1)}), bf16[2,32,8,192]{3,2,0,1:T(8,128)(2,1)S(1)}, u32[]{:S(2)}, u32[]{:S(2)}) async-start(bf16[2,32,8,192]{3,2,0,1:T(8,128)(2,1)} %copy.392), calls=%async_computation.1 | async-start | bytes 524288 | tf_op jit(solution)/shard_map/all_to_all | solution.py:95
  180.7 95.2 %reduce-scatter.31.cloned.1.call-start = ((), (), s32[]{:S(2)}) async-start(), calls=%async_computation.18 | async-start | bytes 491520 | tf_op jit(solution)/shard_map/reduce_scatter | solution.py:224
  208.2 45.5 %copy-start.21 = (bf16[768,192]{1,0:T(8,128)(2,1)}, bf16[768,192]{1,0:T(8,128)(2,1)S(1)}, u32[]{:S(2)}) copy-start(bf16[768,192]{1,0:T(8,128)(2,1)S(1)} %all_gather.63) | copy-start | bytes 884740
  209.5 26.3 %copy-start.30 = (bf16[2,256,3,64]{1,3,2,0:T(8,128)(2,1)}, bf16[2,256,3,64]{1,3,2,0:T(8,128)(2,1)S(1)}, u32[]{:S(2)}) copy-start(bf16[2,256,3,64]{1,3,2,0:T(8,128)(2,1)S(1)} %copy.398) | copy-start | bytes 589828
  253.3 49.7 %reduce-scatter.29.cloned.1.call-start = ((), (), s32[]{:S(2)}) async-start(), calls=%async_computation.17 | async-start | bytes 368640 | tf_op jit(solution)/shard_map/reduce_scatter | solution.py:221
  257.9 77.5 %reduce-scatter.35.cloned.1.call-start = ((), (), s32[]{:S(2)}) async-start(), calls=%async_computation.20 | async-start | bytes 110592
  277.6 88.4 %reduce-scatter.33.cloned.1.call-start = ((), (), s32[]{:S(2)}) async-start(), calls=%async_computation.19 | async-start | bytes 221184
  304.7 88.4 %reduce-scatter.23.cloned.1.call-start = ((), (), s32[]{:S(2)}) async-start(), calls=%async_computation.14 | async-start | bytes 983040 | tf_op jit(solution)/shard_map/reduce_scatter | solution.py:167
  309.4 112.6 %reduce-scatter.21.cloned.1.call-start = ((), (), s32[]{:S(2)}) async-start(), calls=%async_computation.13 | async-start | bytes 983040 | tf_op jit(solution)/shard_map/reduce_scatter | solution.py:164
  318.1 285.8 %reduce-scatter.27.cloned.1.call-start = ((), (), s32[]{:S(2)}) async-start(), calls=%async_computation.16 | async-start | bytes 122880 | tf_op jit(solution)/shard_map/reduce_scatter | solution.py:218
  326.5 96.6 %copy-start.38 = (bf16[2,8,32,192]{3,2,1,0:T(8,128)(2,1)}, bf16[2,8,32,192]{3,2,1,0:T(8,128)(2,1)S(1)}, u32[]{:S(2)}) copy-start(bf16[2,8,32,192]{3,2,1,0:T(8,128)(2,1)S(1)} %reshape.170) | copy-start | bytes 589828
  328.5 94.6 %copy-start.29 = (bf16[192,576]{1,0:T(8,128)(2,1)S(1)}, bf16[192,576]{1,0:T(8,128)(2,1)}, u32[]{:S(2)}) copy-start(bf16[192,576]{1,0:T(8,128)(2,1)} %copy-done.28) | copy-start | bytes 663556
  394.2 29.3 %copy-start.39 = (bf16[2,256,192]{2,1,0:T(8,128)(2,1)}, bf16[2,256,192]{2,1,0:T(8,128)(2,1)S(1)}, u32[]{:S(2)}) copy-start(bf16[2,256,192]{2,1,0:T(8,128)(2,1)S(1)} %copy.408) | copy-start | bytes 589828
  429.7 12.4 %all-to-all-start.2 = ((bf16[2,8,32,192]{3,1,0,2:T(8,128)(2,1)}), bf16[2,8,32,192]{3,1,0,2:T(8,128)(2,1)}, u32[]{:S(2)}, u32[]{:S(2)}) async-start(bf16[2,8,32,192]{3,1,0,2:T(8,128)(2,1)} %copy.412), calls=%async_computation.4 | async-start | bytes 524288 | tf_op jit(solution)/shard_map/all_to_all | solution.py:183
  433.8 170.2 %reduce-scatter.37.cloned.1.call-start = ((), (), s32[]{:S(2)}) async-start(), calls=%async_computation.21 | async-start | bytes 307200
  451.0 109.3 %all-to-all-start.3 = ((bf16[2,32,8,192]{3,2,0,1:T(8,128)(2,1)}), bf16[2,32,8,192]{3,2,0,1:T(8,128)(2,1)}, u32[]{:S(2)}, u32[]{:S(2)}) async-start(bf16[2,32,8,192]{3,2,0,1:T(8,128)(2,1)} %copy.417), calls=%async_computation.5 | async-start | bytes 524288 | tf_op jit(solution)/shard_map/all_to_all | solution.py:190
  455.1 171.4 %reduce-scatter.25.cloned.1.call-start = ((), (), s32[]{:S(2)}) async-start(), calls=%async_computation.15 | async-start | bytes 122880 | tf_op jit(solution)/shard_map/reduce_scatter | solution.py:206
  464.9 76.1 %copy-start.51 = (f32[192,4,16]{0,2,1:T(8,128)S(1)}, f32[192,4,16]{0,2,1:T(8,128)}, u32[]{:S(2)}) copy-start(f32[192,4,16]{0,2,1:T(8,128)} %copy-done.50) | copy-start | bytes 147460
  464.9 76.1 %copy-start.53 = (f32[192,64]{0,1:T(8,128)S(1)}, f32[192,64]{0,1:T(8,128)}, u32[]{:S(2)}) copy-start(f32[192,64]{0,1:T(8,128)} %copy-done.52) | copy-start | bytes 147460
  561.8 41.0 %copy-start.15 = (f32[2,8,32,192]{3,2,1,0:T(8,128)S(1)}, f32[2,8,32,192]{3,2,1,0:T(8,128)}, u32[]{:S(2)}) copy-start(f32[2,8,32,192]{3,2,1,0:T(8,128)} %copy-done.14) | copy-start | bytes 1179652
  561.9 41.0 %copy-start.24 = (bf16[2,8,32,192]{3,2,1,0:T(8,128)(2,1)S(1)}, bf16[2,8,32,192]{3,2,1,0:T(8,128)(2,1)}, u32[]{:S(2)}) copy-start(bf16[2,8,32,192]{3,2,1,0:T(8,128)(2,1)} %param.25) | copy-start | bytes 589828
  602.8 79.7 %all-reduce.16.cloned.1.call-start = ((), (), s32[]{:S(2)}) async-start(), calls=%async_computation.22 | async-start | bytes 286720
  (48 other events, 350.6 us)
Sparse Core Ops, SparseCore 0:
  253.4 22.5 reduce-scatter.30
  278.7 24.1 reduce-scatter.28
  305.2 30.1 reduce-scatter.34
  337.6 28.4 reduce-scatter.32
  368.8 24.2 reduce-scatter.22
  395.9 26.0 reduce-scatter.20
  424.7 23.8 reduce-scatter.26
  451.6 23.6 reduce-scatter.36
  602.9 23.6 reduce-scatter.24
  629.7 52.7 all-reduce.15
where the time goes:
time: 709 us; the launch traced here: 696 us
  blocking collectives  239 us (34%)
  waiting for transfers between devices  208 us (29%)
  other arithmetic  101 us (14%)
  local copies, waits for them, and re-layouts  67.8 us (10%)
  matrix products  46.5 us (7%)
  between operations  18.2 us (3%)
  starting transfers between devices  16.6 us (2%)
    unnamed x14, waiting for transfers between devices  90.4 us
    scatter-add x1, other arithmetic, kernels(): picked = kernel_table[offset]  76 us
    psum x1, blocking collectives, per_device(): gain_sums = lax.psum(jnp.stack([gain_one, gain_two]), ('img', 'row'))  39.3 us
    reduce_scatter x1, waiting for transfers between devices, per_device(): lax.psum_scatter(key_terms.astype(jnp.bfloat16), 'row', scatter_dimension...  27.8 us
    reduce_scatter x1, waiting for transfers between devices, per_device(): lax.psum_scatter(value_terms.astype(jnp.bfloat16), 'row', scatter_dimensi...  25.6 us
    reduce_scatter x1, waiting for transfers between devices, per_device(): lax.psum_scatter(grad_fc1.astype(jnp.bfloat16), 'row', scatter_dimension=...  24.6 us
    reduce_scatter x1, waiting for transfers between devices, per_device(): lax.psum_scatter(grad_wu.astype(jnp.bfloat16), 'row', scatter_dimension=0...  22.6 us
    unnamed x1, blocking collectives  17.9 us
  transfers between devices with their start and end apart: 14, of which 8 were waited for; matrix products, arithmetic and copies ran while one was open for 25% of the time, Pallas kernels for 0%

commit v1 on v0

v1 whole, which is shorter than its diff:
```python
import jax
import jax.numpy as jnp
import numpy as np
from jax import lax
from jax.experimental import pallas as pl
from jax.experimental.pallas import tpu as pltpu
from jax.sharding import Mesh
from jax.sharding import PartitionSpec as P

HEADS = 3
HEAD_DIM = 64
STATE = 16
GRID = 32
SLOTS = GRID * GRID
OWN = SLOTS // 2
D = HEADS * HEAD_DIM
FF = 4 * D
LANES = 128
TILE = HEADS * LANES
LAGS = 2 * GRID
CENTER = GRID - 1
EPS = 1e-05
BF16 = jnp.bfloat16
F32 = jnp.float32


def late_layout(parts):
    a_u, a_r, a_q = D // parts, 4 * STATE // parts, 3 * D // parts
    return a_u, a_r, a_q, (0, a_u, a_u + a_r, a_u + 2 * a_r)


def late_selections(parts):
    a_u, a_r, a_q, (o_u, o_r, o_c, o_q) = late_layout(parts)
    sel_u = np.zeros((parts, LANES, D), np.float32)
    sel_rc = np.zeros((parts, LANES, LANES), np.float32)
    full = np.zeros((parts, LANES, 3, TILE), np.float32)
    for m in range(parts):
        for col in range(a_u):
            sel_u[m, o_u + col, m * a_u + col] = 1
        for col in range(a_r):
            sel_rc[m, o_r + col, m * a_r + col] = 1
            sel_rc[m, o_c + col, 4 * STATE + m * a_r + col] = 1
        for col in range(a_q):
            whole = m * a_q + col
            third, rest = divmod(whole, D)
            head, lane = divmod(rest, HEAD_DIM)
            full[m, o_q + col, third, head * LANES + lane] = 1
    spans = []
    for third in range(3):
        used = [m for m in range(parts) if full[m, :, third].any()]
        spans.append((min(used), max(used) + 1))
    width = max(stop - start for start, stop in spans)
    starts = [min(start, parts - width) for start, _ in spans]
    sel_q = np.stack(
        [full[s : s + width, :, third].reshape(width * LANES, TILE) for third, s in enumerate(starts)]
    )
    return (
        sel_u.reshape(parts * LANES, D).astype(BF16),
        sel_rc.reshape(parts * LANES, LANES).astype(BF16),
        sel_q.astype(BF16),
        starts,
        width,
    )


def early_selections(parts):
    a_1, a_o = FF // parts, D // parts
    half = parts // 2
    sel_1 = np.zeros((half, LANES, FF // 2), np.float32)
    sel_o = np.zeros((parts, LANES, D), np.float32)
    sel_2 = np.zeros((4, parts, LANES, D), np.float32)
    for m in range(half):
        for col in range(a_1):
            sel_1[m, col, m * a_1 + col] = 1
    for m in range(parts):
        for col in range(a_o):
            sel_o[m, a_1 + col, m * a_o + col] = 1
            for g in range(4):
                sel_2[g, m, g * a_o + col, m * a_o + col] = 1
    return (
        sel_1.reshape(half * LANES, FF // 2).astype(BF16),
        sel_o.reshape(parts * LANES, D).astype(BF16),
        sel_2.reshape(4, parts * LANES, D).astype(BF16),
    )


def dot(a, b):
    return lax.dot_general(a, b, (((1,), (0,)), ((), ())), preferred_element_type=F32)


def dot_nt(a, b):
    return lax.dot_general(a, b, (((1,), (1,)), ((), ())), preferred_element_type=F32)


def dot_tn(a, b):
    return lax.dot_general(a, b, (((0,), (0,)), ((), ())), preferred_element_type=F32)


def normalise(values):
    center = values - jnp.mean(values, -1, keepdims=True)
    spread = jnp.mean(center * center, -1, keepdims=True)
    inverse = lax.rsqrt(spread + EPS)
    return center * inverse, inverse


def norm_back(grad, gain, unit, inverse):
    scaled = grad * gain
    first = jnp.mean(scaled, -1, keepdims=True)
    second = jnp.mean(scaled * unit, -1, keepdims=True)
    return inverse * (scaled - first - unit * second)


def widen(mask):
    return jnp.concatenate([mask, mask[:, : D - LANES]], axis=1)


def put_lanes(ref, rows, values):
    ref[0, rows, :] = values[:, :LANES]
    ref[1, rows, : D - LANES] = values[:, LANES:]


def block_sum(src, table, way, lane, first, count, step, offset, sublane, sign):
    total = [None] * count
    for base in range(0, GRID, 8):
        low, high = -(base + 7), count - 1 - base
        coef = {
            lag: table[way, lane, first * sign + (lag * sign + CENTER)]
            for lag in range(low, high + 1)
        }
        for s in range(base, base + 8):
            x = src[lane, pl.ds(pl.multiple_of(s * step + sublane, 8), 8), :]
            for t in range(count):
                term = coef[t - s] * x
                total[t] = term if total[t] is None else total[t] + term
    return total


def compiler(limit=60 << 20):
    return pltpu.CompilerParams(vmem_limit_bytes=limit)


VMEM = pl.BlockSpec(memory_space=pltpu.VMEM)
SMEM = pl.BlockSpec(memory_space=pltpu.SMEM)


def scan_kernel(
    starts,
    width,
    core_ref,
    own_ref,
    other_ref,
    mask_ref,
    gains_ref,
    late_ref,
    sel_u_ref,
    sel_rc_ref,
    sel_q_ref,
    q_ref,
    k_ref,
    v_ref,
    scanned_ref,
    mixed_ref,
    table_ref,
    rates_ref,
    wu_ref,
    wqkv_ref,
    first_ref,
    xs,
    xt,
    cols,
    rows,
    scanned_own,
):
    core = core_ref[0]
    blocks, _, rows_slots, _ = own_ref.shape
    half_rows = rows_slots // GRID
    parts = late_ref.shape[0]
    gain = gains_ref[0:1, :]

    late = jnp.concatenate([late_ref[m] for m in range(parts)], axis=1)
    wu = dot(late, sel_u_ref[...]).astype(BF16)
    wu_ref[...] = wu
    rates = dot(late, sel_rc_ref[...])
    rates = jnp.concatenate([rates.T, jnp.zeros((LANES, 2 * LANES - D), F32)], axis=1)
    rates_ref[...] = rates
    for third in range(3):
        window = late[:, starts[third] * LANES : (starts[third] + width) * LANES]
        wqkv_ref[third] = dot(window, sel_q_ref[third]).astype(BF16)

    decay, coef = rates[: 4 * STATE], rates[4 * STATE :]

    def lag_row(k):
        powers = jnp.exp(-decay * k) * coef
        return [jnp.sum(powers[d * STATE : (d + 1) * STATE], 0, keepdims=True) for d in range(4)]

    def store_lag(way, lag, row):
        row = row.astype(BF16).astype(F32)
        for lane in range(2):
            table_ref[way, lane, lag + CENTER] = jnp.broadcast_to(
                row[:, lane * LANES : (lane + 1) * LANES], (8, LANES)
            )

    def lag_step(k, _):
        found = lag_row(k.astype(F32))
        for way in range(2):
            store_lag(way, k, found[2 * way])
            store_lag(way, -k, found[2 * way + 1])
        return 0

    lax.fori_loop(1, GRID, lag_step, 0)
    found = lag_row(0.0)
    for way in range(2):
        store_lag(way, 0, found[2 * way] + found[2 * way + 1])

    xs[1, :, D - LANES :] = jnp.zeros((SLOTS, 2 * LANES - D), F32)

    def norm_step(block, _):
        for which in range(2):
            ref = own_ref.at[block, 0] if which == 0 else other_ref.at[block]
            place = core if which == 0 else 1 - core
            unit, _ = normalise(ref[...].astype(F32))
            start = pl.multiple_of((block * 2 + place) * rows_slots, rows_slots)
            first_ref[pl.ds(start, rows_slots), :] = (unit * gain).astype(BF16)
        return 0

    lax.fori_loop(0, blocks, norm_step, 0)
    mixed = dot(first_ref[...], wu) * widen(mask_ref[...])
    mixed = mixed.astype(BF16)
    mixed_ref[...] = mixed
    mixed = mixed.astype(F32)
    put_lanes(xs, slice(None), mixed)
    for lane in range(2):
        for j in range(GRID):
            xt[lane, j * GRID : (j + 1) * GRID, :] = xs[lane, pl.ds(j, GRID, stride=GRID), :]

    def scan_step(index, _):
        sublane = pl.multiple_of((index % 4) * 8, 8)
        first = (index // 4) * 8
        for way, src, dst in ((0, xt, rows), (1, xs, cols)):
            for lane in range(2):
                total = block_sum(src, table_ref, way, lane, first, 8, GRID, 0, sublane, 1)
                for t in range(8):
                    place = pl.multiple_of((first + t) * GRID + sublane, 8)
                    dst[lane, pl.ds(place, 8), :] = total[t]
        return 0

    lax.fori_loop(0, 16, scan_step, 0)

    def join_step(i, _):
        place = pl.ds(pl.multiple_of(i * GRID, GRID), GRID)
        mask = mask_ref[place, :]
        both = []
        for lane in range(2):
            down = cols[lane, place, :].astype(BF16).astype(F32)
            both.append((rows[lane, pl.ds(i, GRID, stride=GRID), :] + down) * mask)
        both = jnp.concatenate([both[0], both[1][:, : D - LANES]], axis=1)
        scanned_ref[place, :] = both.astype(BF16)
        return 0

    lax.fori_loop(0, GRID, join_step, 0)

    for block in range(blocks):
        start = pl.multiple_of((block * 2 + core) * rows_slots, rows_slots)
        scanned_own[block * rows_slots : (block + 1) * rows_slots, :] = scanned_ref[
            pl.ds(start, rows_slots), :
        ]

    lane_own = lax.broadcasted_iota(jnp.int32, (OWN, LANES), 1)
    lane_all = lax.broadcasted_iota(jnp.int32, (SLOTS, LANES), 1)
    bias = jnp.where(lane_all == HEAD_DIM, (mask_ref[...] - 1.0) * 1e30, 0.0)
    ones = jnp.where((lane_all == HEAD_DIM) | (lane_all == HEAD_DIM + 1), 1.0, 0.0)
    one_own = jnp.where(lane_own == HEAD_DIM, 1.0, 0.0)
    for h in range(HEADS):
        tile = slice(h * LANES, (h + 1) * LANES)
        q_ref[h] = (
            dot(scanned_own[...], wqkv_ref[0, :, tile]) * HEAD_DIM ** (-0.5) + one_own
        ).astype(BF16)
        k_ref[h] = (dot(scanned_ref[...], wqkv_ref[1, :, tile]) + bias).astype(BF16)
        v_ref[h] = (dot(scanned_ref[...], wqkv_ref[2, :, tile]) + ones).astype(BF16)


def middle_kernel(
    core_ref,
    own_ref,
    mask_ref,
    gains_ref,
    early_ref,
    sel_1_ref,
    sel_o_ref,
    sel_2_ref,
    q_ref,
    k_ref,
    v_ref,
    soft_ref,
    lifted_ref,
    out_ref,
    grad_middle_ref,
    gain_ref,
    keep_ref,
    send_ref,
    scores,
    wo,
    w1,
    w2,
    att,
    outs,
    sums,
    middle,
    second,
    pre,
    hidden,
    grad_pre,
    wire,
):
    core = core_ref[0]
    blocks, _, rows_slots, _ = own_ref.shape
    parts = early_ref.shape[0]
    per_block = D // blocks
    gain = gains_ref[1:2, :]

    left = jnp.concatenate([early_ref[m, :, :LANES] for m in range(parts)], axis=1)
    right = jnp.concatenate([early_ref[m, :, LANES:] for m in range(parts)], axis=1)
    span = parts // 2 * LANES
    for half in range(2):
        w1[:, half * FF // 2 : (half + 1) * FF // 2] = dot(
            left[:, half * span : (half + 1) * span], sel_1_ref[...]
        ).astype(BF16)
    out_weight = dot(left, sel_o_ref[...]).astype(BF16)
    for h in range(HEADS):
        wo[h, :HEAD_DIM] = out_weight[h * HEAD_DIM : (h + 1) * HEAD_DIM]
        wo[h, HEAD_DIM:] = jnp.zeros((LANES - HEAD_DIM, D), BF16)
    for g in range(4):
        part = dot(right, sel_2_ref[g])
        for r in range(blocks):
            start = r * 4 * per_block + g * per_block
            w2[start : start + per_block] = part[r * per_block : (r + 1) * per_block].astype(BF16)

    for h in range(HEADS):
        scores[...] = dot_nt(q_ref[h], k_ref[h])

        def soft_step(i, _, h=h):
            place = pl.ds(pl.multiple_of(i * 32, 32), 32)
            values = scores[place, :]
            top = jnp.max(values, -1, keepdims=True)
            soft_ref[h, place, :] = jnp.exp(values - top).astype(BF16)
            return 0

        lax.fori_loop(0, OWN // 32, soft_step, 0)
        raw = dot(soft_ref[h], v_ref[h])
        total = raw[:, HEAD_DIM : HEAD_DIM + 1]
        sums[h] = jnp.broadcast_to(1.0 / total, (OWN, LANES))
        result = raw * sums[h]
        outs[h] = result
        att[h] = result.astype(BF16)

    branch = dot(att[0], wo[0]) + dot(att[1], wo[1]) + dot(att[2], wo[2])
    middle[...] = branch

    def own_mask(block):
        start = pl.multiple_of((block * 2 + core) * rows_slots, rows_slots)
        return widen(mask_ref[pl.ds(start, rows_slots), :])

    def norm_step(block, _):
        place = pl.ds(pl.multiple_of(block * rows_slots, rows_slots), rows_slots)
        mid = own_ref[block, 0].astype(F32) + middle[place, :] * own_mask(block)
        middle[place, :] = mid
        unit, _ = normalise(mid)
        second[place, :] = (unit * gain).astype(BF16)
        return 0

    lax.fori_loop(0, blocks, norm_step, 0)

    pre[...] = dot(second[...], w1[...])
    cot = jnp.concatenate([own_ref[b, 1] for b in range(blocks)], axis=0)
    grad_hidden = scores.at[:, :FF]
    grad_hidden[...] = dot_nt(cot, w2[...])

    def gelu_step(i, _):
        place = pl.ds(pl.multiple_of(i * 16, 16), 16)
        x = pre[place, :]
        phi = 0.5 * (1.0 + lax.erf(x * np.float32(0.5**0.5)))
        hidden[place, :] = (x * phi).astype(BF16)
        slope = phi + x * jnp.exp(x * x * -0.5) * np.float32((2 * np.pi) ** -0.5)
        grad_pre[place, :] = (scores[place, :FF] * slope).astype(BF16)
        return 0

    lax.fori_loop(0, OWN // 16, gelu_step, 0)

    out_ref[...] = (middle[...] + dot(hidden[...], w2[...])).astype(BF16)
    grad_2 = dot_tn(hidden[...], cot).astype(BF16)
    grad_1 = dot_tn(second[...], grad_pre[...]).astype(BF16)
    grad_middle_ref[...] = dot_nt(grad_pre[...], w1[...])

    def back_step(block, total):
        place = pl.ds(pl.multiple_of(block * rows_slots, rows_slots), rows_slots)
        unit, inverse = normalise(middle[place, :])
        grad = grad_middle_ref[place, :]
        total = total + jnp.sum(grad * unit, 0, keepdims=True)
        grad = own_ref[block, 1].astype(F32) + norm_back(grad, gain, unit, inverse)
        grad_middle_ref[place, :] = grad
        second[place, :] = (grad * own_mask(block)).astype(BF16)
        return total

    gain_ref[...] = lax.fori_loop(0, blocks, back_step, jnp.zeros((1, D), F32))

    grad_o = []
    lane_own = lax.broadcasted_iota(jnp.int32, (OWN, LANES), 1)
    for h in range(HEADS):
        grad_o.append(dot_tn(att[h], second[...])[:HEAD_DIM])
        grad_att = dot_nt(second[...], wo[h]).astype(BF16).astype(F32)
        scaled = (grad_att * sums[h]).astype(BF16).astype(F32)
        shift = -jnp.sum(scaled * outs[h], -1, keepdims=True)
        high = shift.astype(BF16).astype(F32)
        lifted = jnp.where(
            lane_own == HEAD_DIM, high, jnp.where(lane_own == HEAD_DIM + 1, shift - high, scaled)
        )
        lifted_ref[h] = lifted.astype(BF16)

    for half in range(2):
        wire[:, half * span : (half + 1) * span] = dot_nt(
            grad_1[:, half * FF // 2 : (half + 1) * FF // 2], sel_1_ref[...]
        )
    grad_o = jnp.concatenate(grad_o, axis=0).astype(BF16)
    wire[...] += dot_nt(grad_o, sel_o_ref[...])

    def deliver(lanes):
        for m in range(parts):
            value = wire[:, m * LANES : (m + 1) * LANES].astype(BF16)

            @pl.when(core == m % 2)
            def _(value=value, m=m):
                keep_ref[m // 2, :, lanes] = value

            @pl.when(core != m % 2)
            def _(value=value, m=m):
                send_ref[m // 2, :, lanes] = value

    deliver(slice(0, LANES))
    total = None
    for g in range(4):
        rows = [
            grad_2[r * 4 * per_block + g * per_block : r * 4 * per_block + (g + 1) * per_block]
            for r in range(blocks)
        ]
        part = dot_nt(jnp.concatenate(rows, axis=0), sel_2_ref[g])
        total = part if total is None else total + part
    wire[...] = total
    deliver(slice(LANES, 2 * LANES))


def attention_back_kernel(
    core_ref,
    soft_ref,
    lifted_ref,
    q_ref,
    k_ref,
    v_ref,
    scanned_ref,
    wqkv_ref,
    part_ref,
    grad_w_ref,
    scores,
    grad_scores,
    triple,
    grad_q,
    scanned_own,
    part,
    *,
    blocks,
):
    core = core_ref[0]
    rows_slots = OWN // blocks
    for h in range(HEADS):
        tile = slice(h * LANES, (h + 1) * LANES)
        scores[...] = dot_nt(lifted_ref[h], v_ref[h])

        def back_step(i, _, h=h):
            place = pl.ds(pl.multiple_of(i * 32, 32), 32)
            grad_scores[place, :] = (soft_ref[h, place, :].astype(F32) * scores[place, :]).astype(
                BF16
            )
            return 0

        lax.fori_loop(0, OWN // 32, back_step, 0)
        grad_q[:, tile] = (dot(grad_scores[...], k_ref[h]).astype(BF16) * HEAD_DIM ** (-0.5)).astype(
            BF16
        )
        triple[0, :, tile] = dot_tn(grad_scores[...], q_ref[h]).astype(BF16)
        triple[1, :, tile] = dot_tn(soft_ref[h], lifted_ref[h]).astype(BF16)

    part[...] = dot_nt(triple[0], wqkv_ref[1]) + dot_nt(triple[1], wqkv_ref[2])
    from_q = dot_nt(grad_q[...], wqkv_ref[0])
    for block in range(blocks):
        here = slice(block * rows_slots, (block + 1) * rows_slots)
        place = pl.ds(pl.multiple_of((block * 2 + core) * rows_slots, rows_slots), rows_slots)
        part[place, :] += from_q[here]
        scanned_own[here, :] = scanned_ref[place, :]
    part_ref[...] = part[...].astype(BF16)
    grad_w_ref[0] = dot_tn(scanned_own[...], grad_q[...]).astype(BF16)
    grad_w_ref[1] = dot_tn(scanned_ref[...], triple[0]).astype(BF16)
    grad_w_ref[2] = dot_tn(scanned_ref[...], triple[1]).astype(BF16)


def scan_back_kernel(
    starts,
    width,
    core_ref,
    own_ref,
    mask_ref,
    gains_ref,
    part_ref,
    got_ref,
    mixed_ref,
    first_ref,
    table_ref,
    rates_ref,
    wu_ref,
    grad_middle_ref,
    grad_w_ref,
    gain_two_ref,
    sel_u_ref,
    sel_rc_ref,
    sel_q_ref,
    grad_ref,
    keep_ref,
    send_ref,
    gains_out_ref,
    gs,
    gt,
    xs,
    xt,
    own,
    rows,
    cols,
    lag_sums,
    lag_rows,
    mixed_back,
    first_own,
    wire,
):
    core = core_ref[0]
    blocks, _, rows_slots, _ = own_ref.shape
    half_rows = rows_slots // GRID
    own_rows = GRID // 2
    parts = sel_rc_ref.shape[0] // LANES
    gain = gains_ref[0:1, :]
    pad = jnp.zeros((SLOTS, 2 * LANES - D), F32)

    xs[1, :, D - LANES :] = pad
    gs[1, :, D - LANES :] = pad
    put_lanes(xs, slice(None), mixed_ref[...].astype(F32))
    grads = (part_ref[...].astype(F32) + got_ref[...].astype(F32)) * widen(mask_ref[...])
    put_lanes(gs, slice(None), grads.astype(BF16).astype(F32))

    def place_of(block):
        return pl.ds(pl.multiple_of((block * 2 + core) * rows_slots, rows_slots), rows_slots)

    for block in range(blocks):
        here = slice(block * rows_slots, (block + 1) * rows_slots)
        first_own[here, :] = first_ref[place_of(block), :]
    for src, dst in ((gs, gt), (xs, xt)):
        for lane in range(2):
            for block in range(blocks):
                here = slice(block * rows_slots, (block + 1) * rows_slots)
                own[lane, here, :] = src[lane, place_of(block), :]
            for j in range(GRID):
                dst[lane, j * own_rows : (j + 1) * own_rows, :] = own[
                    lane, pl.ds(j, own_rows, stride=GRID), :
                ]

    def row_step(index, _):
        sublane = pl.multiple_of((index % 2) * 8, 8)
        first = (index // 2) * 8
        for lane in range(2):
            total = block_sum(gt, table_ref, 0, lane, first, 8, own_rows, 0, sublane, -1)
            for t in range(8):
                rows[lane, pl.ds(pl.multiple_of((first + t) * own_rows + sublane, 8), 8), :] = total[
                    t
                ]
        return 0

    lax.fori_loop(0, 8, row_step, 0)

    def col_step(index, _):
        sublane = pl.multiple_of((index % 4) * 8, 8)
        block = index // 4
        first = (block * 2 + core) * half_rows
        for lane in range(2):
            total = block_sum(gs, table_ref, 1, lane, first, half_rows, GRID, 0, sublane, -1)
            for t in range(half_rows):
                at = pl.multiple_of((block * half_rows + t) * GRID + sublane, 8)
                cols[lane, pl.ds(at, 8), :] = total[t]
        return 0

    lax.fori_loop(0, blocks * 4, col_step, 0)

    lag_sums[...] = jnp.zeros_like(lag_sums)

    def add_lags(way, lane, first, count, base, gref, xref, step, groups):
        total = {}
        for u in range(groups):
            g = [
                gref[lane, pl.ds(pl.multiple_of((first + t) * step + u * 8, 8), 8), :]
                for t in range(count)
            ]
            for s in range(8):
                x = xref[lane, pl.ds(pl.multiple_of((base + s) * step + u * 8, 8), 8), :]
                for t in range(count):
                    term = g[t] * x
                    total[t - s] = term if t - s not in total else total[t - s] + term
        for lag, value in total.items():
            at = first - base + (lag + CENTER)
            lag_sums[way, lane, at] += value

    def lag_row_step(index, _):
        first, base = (index // 4) * 8, (index % 4) * 8
        for lane in range(2):
            add_lags(0, lane, first, 8, base, gt, xt, own_rows, own_rows // 8)
        return 0

    lax.fori_loop(0, 16, lag_row_step, 0)

    def lag_col_step(index, _):
        first, base = ((index // 4) * 2 + core) * half_rows, (index % 4) * 8
        for lane in range(2):
            add_lags(1, lane, first, half_rows, base, gs, xs, GRID, GRID // 8)
        return 0

    lax.fori_loop(0, blocks * 4, lag_col_step, 0)

    for way in range(2):
        for lane in range(2):
            lag_rows[way, :, lane * LANES : (lane + 1) * LANES] = jnp.sum(lag_sums[way, lane], 1)

    decay, coef = rates_ref[: 4 * STATE], rates_ref[4 * STATE :]

    def table_step(k, carry):
        to_rate, to_coef = carry
        lag = k.astype(F32)
        powers = jnp.exp(-decay * lag)
        grads = []
        for way in range(2):
            for at in (CENTER + k, CENTER - k):
                grads.append(
                    jnp.broadcast_to(lag_rows[way, pl.ds(at, 1), :], (STATE, 2 * LANES))
                )
        scaled = jnp.concatenate(grads, axis=0) * powers
        return to_rate - lag * scaled, to_coef + scaled

    zero = jnp.zeros((4 * STATE, 2 * LANES), F32)
    to_rate, to_coef = lax.fori_loop(0, GRID, table_step, (zero, zero))
    grad_rc = jnp.concatenate([to_rate * coef, to_coef], axis=0).T[:D].astype(BF16)

    def join_step(i, _):
        place = pl.ds(pl.multiple_of(i * GRID, GRID), GRID)
        block = i // half_rows
        at = ((block * 2 + core) * half_rows + i % half_rows) * GRID
        mask = mask_ref[pl.ds(pl.multiple_of(at, GRID), GRID), :]
        both = []
        for lane in range(2):
            down = cols[lane, place, :].astype(BF16).astype(F32)
            both.append((rows[lane, pl.ds(i, GRID, stride=own_rows), :] + down) * mask)
        both = jnp.concatenate([both[0], both[1][:, : D - LANES]], axis=1)
        mixed_back[place, :] = both.astype(BF16)
        return 0

    lax.fori_loop(0, own_rows, join_step, 0)
    grad_u = dot_tn(first_own[...], mixed_back[...]).astype(BF16)
    grad_first = dot_nt(mixed_back[...], wu_ref[...])
    gain_one = jnp.zeros((1, D), F32)
    for block in range(blocks):
        here = slice(block * rows_slots, (block + 1) * rows_slots)
        unit, inverse = normalise(own_ref[block, 0].astype(F32))
        grad = grad_first[here]
        gain_one = gain_one + jnp.sum(grad * unit, 0, keepdims=True)
        grad = grad_middle_ref[here, :] + norm_back(grad, gain, unit, inverse)
        grad_ref[here, :] = grad.astype(BF16)

    wire[...] = dot_nt(grad_u, sel_u_ref[...]) + dot_nt(grad_rc, sel_rc_ref[...])
    for third in range(3):
        span = slice(starts[third] * LANES, (starts[third] + width) * LANES)
        wire[:, span] += dot_nt(grad_w_ref[third], sel_q_ref[third])
    for m in range(parts):
        value = wire[:, m * LANES : (m + 1) * LANES].astype(BF16)

        @pl.when(core == m % 2)
        def _(value=value, m=m):
            keep_ref[m // 2] = value

        @pl.when(core != m % 2)
        def _(value=value, m=m):
            send_ref[m // 2] = value

    lines = []
    for value in (gain_one, gain_two_ref[...]):
        high = value.astype(BF16).astype(F32)
        for piece in (high, value - high):
            lines.append(piece[:, :LANES])
            lines.append(
                jnp.concatenate([piece[:, LANES:], jnp.zeros((1, 2 * LANES - D), F32)], axis=1)
            )
    lines.append(jnp.zeros((8, LANES), F32))
    gains_out_ref[...] = jnp.concatenate(lines, axis=0).astype(BF16)


def pair_sum_kernel(keep_ref, got_ref, gains_ref, gains_got_ref, out_ref):
    depth, blocks, rows, _ = out_ref.shape
    rows -= 16
    gains = gains_ref[...].astype(F32) + gains_got_ref[...].astype(F32)
    lines = []
    for g in range(2):
        for lane in range(2):
            at = 4 * g + lane
            lines.append(gains[at : at + 1] + gains[at + 2 : at + 3])
    value = jnp.concatenate(lines, axis=0)
    high = value.astype(BF16).astype(F32)
    gains = jnp.concatenate([high, value - high, jnp.zeros((8, LANES), F32)], axis=0).astype(BF16)
    for z in range(depth):
        total = keep_ref[z].astype(F32) + got_ref[z].astype(F32)
        for r in range(blocks):
            out_ref[z, r, :rows] = total[r * rows : (r + 1) * rows].astype(BF16)
            out_ref[z, r, rows:] = gains


def final_kernel(
    parts,
    late_ref,
    early_ref,
    g1_ref,
    g2_ref,
    wu_ref,
    rate_ref,
    coef_ref,
    qkv_ref,
    wo_ref,
    fc1_ref,
    fc2_ref,
):
    a_u, a_r, a_q, (o_u, o_r, o_c, o_q) = late_layout(parts)
    count = late_ref.shape[0]
    total = late_ref[0].astype(F32)
    early = early_ref[0].astype(F32)
    for i in range(1, count):
        total = total + late_ref[i].astype(F32)
        early = early + early_ref[i].astype(F32)
    rows = wu_ref.shape[0]
    weights, gains = total[:rows], total[rows:]
    wu_ref[...] = weights[:, o_u : o_u + a_u]
    rate_ref[...] = weights[:, o_r : o_r + a_r]
    coef_ref[...] = weights[:, o_c : o_c + a_r]
    qkv_ref[...] = weights[:, o_q : o_q + a_q]
    gains = gains[0:4] + gains[4:8]
    for g, ref in ((0, g1_ref), (1, g2_ref)):
        ref[...] = jnp.concatenate(
            [gains[2 * g : 2 * g + 1], gains[2 * g + 1 : 2 * g + 2, : D - LANES]], axis=1
        )
    a_1, a_o = FF // parts, D // parts
    fc1_ref[...] = early[:, :a_1]
    wo_ref[...] = early[:, a_1 : a_1 + a_o]
    for g in range(4):
        fc2_ref[g * rows : (g + 1) * rows] = early[
            :, LANES + g * a_o : LANES + (g + 1) * a_o
        ]


def per_device(
    patches, valid_mask, norm_gains, w_u, decay_rate, out_coef, w_qkv, w_o, w_fc1, w_fc2, cotangent
):
    images, rows_here, _, _ = patches.shape
    depth, blocks = lax.axis_size("z"), lax.axis_size("row")
    parts = 2 * depth
    half_rows = rows_here // 2
    rows_slots = half_rows * GRID
    core = lax.axis_index("core")
    row = lax.axis_index("row")
    first_core = core == 0
    swap = [(0, 1), (1, 0)]
    core_index = core.astype(jnp.int32).reshape(1)
    shape = jax.ShapeDtypeStruct

    sel_u, sel_rc, sel_q, starts, width = late_selections(parts)
    sel_1, sel_o, sel_2 = early_selections(parts)

    late = jnp.concatenate([w_u, decay_rate, out_coef, w_qkv], axis=1)
    late = jnp.pad(late, ((0, 0), (0, LANES - late.shape[1])))
    late_all = lax.all_to_all(
        jnp.broadcast_to(late[None], (parts * blocks,) + late.shape),
        ("z", "core", "row"),
        0,
        0,
        tiled=True,
    ).reshape(parts, D, LANES)
    rows_weight = w_u.shape[0]
    left = jnp.concatenate([w_fc1, w_o], axis=1)
    right = jnp.concatenate(
        [w_fc2[g * rows_weight : (g + 1) * rows_weight] for g in range(4)], axis=1
    )
    early = jnp.concatenate(
        [
            jnp.pad(left, ((0, 0), (0, LANES - left.shape[1]))),
            jnp.pad(right, ((0, 0), (0, LANES - right.shape[1]))),
        ],
        axis=1,
    )
    early_all = lax.all_gather(lax.all_gather(early, "row"), ("z", "core")).reshape(
        parts, D, 2 * LANES
    )

    both = jnp.stack([patches, cotangent], axis=1)
    both = both.reshape(images, 2, 2, rows_slots, D)
    mine = lax.dynamic_index_in_dim(both, core, 2, keepdims=False)
    theirs = lax.dynamic_index_in_dim(both, 1 - core, 2, keepdims=False)
    got = lax.ppermute(theirs, "core", swap)
    plane = jnp.where(
        first_core, jnp.concatenate([mine, got], axis=0), jnp.concatenate([got, mine], axis=0)
    )
    own = lax.all_to_all(plane, "row", 0, 0, tiled=True)
    other = lax.ppermute(own[:, 0], "core", swap)

    mask_got = lax.ppermute(valid_mask, "core", swap)
    mask_plane = jnp.where(
        first_core,
        jnp.concatenate([valid_mask, mask_got], axis=0),
        jnp.concatenate([mask_got, valid_mask], axis=0),
    )
    mask = lax.dynamic_index_in_dim(mask_plane, row, 0, keepdims=False)
    mask = jnp.broadcast_to(mask.reshape(SLOTS, 1).astype(F32), (SLOTS, LANES))

    head_own = shape((HEADS, OWN, LANES), BF16)
    head_all = shape((HEADS, SLOTS, LANES), BF16)
    q, k, v, scanned, mixed, table, rates, wu, wqkv, first = pl.pallas_call(
        lambda *refs: scan_kernel(starts, width, *refs),
        name="scan_forward",
        out_shape=(
            head_own,
            head_all,
            head_all,
            shape((SLOTS, D), BF16),
            shape((SLOTS, D), BF16),
            shape((2, 2, LAGS, 8, LANES), F32),
            shape((LANES, 2 * LANES), F32),
            shape((D, D), BF16),
            shape((3, D, TILE), BF16),
            shape((SLOTS, D), BF16),
        ),
        in_specs=[SMEM] + [VMEM] * 8,
        out_specs=[VMEM] * 10,
        scratch_shapes=[pltpu.VMEM((2, SLOTS, LANES), F32)] * 4 + [pltpu.VMEM((OWN, D), BF16)],
        compiler_params=compiler(),
    )(core_index, own, other, mask, norm_gains, late_all, sel_u, sel_rc, sel_q)

    wire_early = shape((depth, D, 2 * LANES), BF16)
    soft, lifted, out_own, grad_middle, gain_two, early_keep, early_send = pl.pallas_call(
        middle_kernel,
        name="attention_and_feed_forward",
        out_shape=(
            shape((HEADS, OWN, SLOTS), BF16),
            head_own,
            shape((OWN, D), BF16),
            shape((OWN, D), F32),
            shape((1, D), F32),
            wire_early,
            wire_early,
        ),
        in_specs=[SMEM] + [VMEM] * 10,
        out_specs=[VMEM] * 7,
        scratch_shapes=[
            pltpu.VMEM((OWN, SLOTS), F32),
            pltpu.VMEM((HEADS, LANES, D), BF16),
            pltpu.VMEM((D, FF), BF16),
            pltpu.VMEM((FF, D), BF16),
            pltpu.VMEM((HEADS, OWN, LANES), BF16),
            pltpu.VMEM((HEADS, OWN, LANES), F32),
            pltpu.VMEM((HEADS, OWN, LANES), F32),
            pltpu.VMEM((OWN, D), F32),
            pltpu.VMEM((OWN, D), BF16),
            pltpu.VMEM((OWN, FF), F32),
            pltpu.VMEM((OWN, FF), BF16),
            pltpu.VMEM((OWN, FF), BF16),
            pltpu.VMEM((D, parts * LANES), F32),
        ],
        compiler_params=compiler(),
    )(core_index, own, mask, norm_gains, early_all, sel_1, sel_o, sel_2, q, k, v)

    early_sum = (
        early_keep.astype(F32) + lax.ppermute(early_send, "core", swap).astype(F32)
    ).astype(BF16)
    early_sum = early_sum.reshape(depth * blocks, D // blocks, 2 * LANES)
    early_got = lax.all_to_all(early_sum, ("z", "row"), 0, 0, tiled=True)

    part, grad_w = pl.pallas_call(
        lambda *refs: attention_back_kernel(*refs, blocks=blocks),
        name="attention_backward",
        out_shape=(shape((SLOTS, D), BF16), shape((3, D, TILE), BF16)),
        in_specs=[SMEM] + [VMEM] * 7,
        out_specs=[VMEM] * 2,
        scratch_shapes=[
            pltpu.VMEM((OWN, SLOTS), F32),
            pltpu.VMEM((OWN, SLOTS), BF16),
            pltpu.VMEM((2, SLOTS, TILE), BF16),
            pltpu.VMEM((OWN, TILE), BF16),
            pltpu.VMEM((OWN, D), BF16),
            pltpu.VMEM((SLOTS, D), F32),
        ],
        compiler_params=compiler(),
    )(core_index, soft, lifted, q, k, v, scanned, wqkv)

    part_got = lax.ppermute(part, "core", swap)
    wire_late = shape((depth, D, LANES), BF16)
    grad_own, late_keep, late_send, gains_keep = pl.pallas_call(
        lambda *refs: scan_back_kernel(starts, width, *refs),
        name="scan_backward",
        out_shape=(shape((OWN, D), BF16), wire_late, wire_late, shape((16, LANES), BF16)),
        in_specs=[SMEM] + [VMEM] * 16,
        out_specs=[VMEM] * 4,
        scratch_shapes=[
            pltpu.VMEM((2, SLOTS, LANES), F32),
            pltpu.VMEM((2, OWN, LANES), F32),
            pltpu.VMEM((2, SLOTS, LANES), F32),
            pltpu.VMEM((2, OWN, LANES), F32),
            pltpu.VMEM((2, OWN, LANES), F32),
            pltpu.VMEM((2, OWN, LANES), F32),
            pltpu.VMEM((2, OWN, LANES), F32),
            pltpu.VMEM((2, 2, LAGS, 8, LANES), F32),
            pltpu.VMEM((2, LAGS, 2 * LANES), F32),
            pltpu.VMEM((OWN, D), BF16),
            pltpu.VMEM((OWN, D), BF16),
            pltpu.VMEM((D, parts * LANES), F32),
        ],
        compiler_params=compiler(),
    )(
        core_index,
        own,
        mask,
        norm_gains,
        part,
        part_got,
        mixed,
        first,
        table,
        rates,
        wu,
        grad_middle,
        grad_w,
        gain_two,
        sel_u,
        sel_rc,
        sel_q,
    )

    late_recv = lax.ppermute(late_send, "core", swap)
    gains_recv = lax.ppermute(gains_keep, "core", swap)
    rows_weight = D // blocks
    late_sum = pl.pallas_call(
        pair_sum_kernel,
        name="pair_sum",
        out_shape=shape((depth, blocks, rows_weight + 16, LANES), BF16),
        in_specs=[VMEM] * 4,
        out_specs=VMEM,
        compiler_params=compiler(),
    )(late_keep, late_recv, gains_keep, gains_recv)
    late_got = lax.all_to_all(
        late_sum.reshape(depth * blocks, rows_weight + 16, LANES), ("z", "row"), 0, 0, tiled=True
    )

    results = jnp.stack(
        [out_own.reshape(blocks, rows_slots, D), grad_own.reshape(blocks, rows_slots, D)], axis=1
    )
    results = lax.all_to_all(results, "row", 0, 0, tiled=True)
    mine = jnp.where(first_core, results[:images], results[images:])
    theirs = jnp.where(first_core, results[images:], results[:images])
    got = lax.ppermute(theirs, "core", swap)
    whole = jnp.where(
        first_core, jnp.stack([mine, got], axis=2), jnp.stack([got, mine], axis=2)
    )
    block_out = whole[:, 0].reshape(patches.shape)
    grad_patches = whole[:, 1].reshape(patches.shape)

    weight = (rows_weight,)
    g1, g2, f_u, f_rate, f_coef, f_qkv, f_o, f_1, f_2 = pl.pallas_call(
        lambda *refs: final_kernel(parts, *refs),
        name="final_sum",
        out_shape=(
            shape((1, D), F32),
            shape((1, D), F32),
            shape(weight + (D // parts,), F32),
            shape(weight + (4 * STATE // parts,), F32),
            shape(weight + (4 * STATE // parts,), F32),
            shape(weight + (3 * D // parts,), F32),
            shape(weight + (D // parts,), F32),
            shape(weight + (FF // parts,), F32),
            shape((4 * rows_weight, D // parts), F32),
        ),
        in_specs=[VMEM] * 2,
        out_specs=[VMEM] * 9,
        compiler_params=compiler(),
    )(late_got, early_got)
    return (
        block_out,
        grad_patches,
        g1.reshape(D),
        g2.reshape(D),
        f_u,
        f_rate,
        f_coef,
        f_qkv,
        f_o,
        f_1,
        f_2,
    )


def solution(mesh):
    images, rows = mesh.devices.shape
    fine = Mesh(mesh.devices.reshape(images // 2, 2, rows), ("z", "core", "row"))
    img = ("z", "core")
    grid = P(img, "row", None, None)
    weight = P("row", img)
    in_specs = (grid, P(img, None, None), P()) + (weight,) * 7 + (grid,)
    out_specs = (grid, grid, P(), P()) + (weight,) * 7
    return jax.shard_map(
        per_device, mesh=fine, in_specs=in_specs, out_specs=out_specs, check_vma=False
    )
```

time: 709 us -> 170 us (0.24); the launches traced: 696 us -> 169 us
  blocking collectives: 239 us -> 25.9 us
  waiting for transfers between devices: 208 us -> 32.6 us
  other arithmetic: 101 us -> 2.87 us
  Pallas kernels: 0 us -> 63.9 us
  local copies, waits for them, and re-layouts: 67.8 us -> 18.1 us
  matrix products: 46.5 us -> 0 us
  between operations: 18.2 us -> 0.95 us
  starting transfers between devices: 16.6 us -> 24.5 us
    all_gather x16 -> x2, blocking collectives: 182 us -> 25.9 us  [the longest x1 16.8 us: per_device(): lax.all_gather(lax.all_gather(early, 'row'), ('z', 'core'))]
    reduce_scatter x6 -> x0, waiting for transfers between devices: 117 us -> none  [the longest x1 27.8 us: per_device(): lax.psum_scatter(key_terms.astype(jnp.bfloat16), 'row', scatter_dimension...]
    unnamed x14 -> x0, waiting for transfers between devices: 90.4 us -> none
    scatter-add x1 -> x0, other arithmetic: 76 us -> none  [kernels(): picked = kernel_table[offset]]
    pallas_call x0 -> x6, Pallas kernels: none -> 63.9 us  [the longest x1 21 us: per_device(): pl.pallas_call(middle_kernel, name='attention_and_feed_forward', out_shap...]
    dot_general x26 -> x0, matrix products: 41.9 us -> none  [the longest x3 5.46 us: outer_sum(): jnp.einsum('bijd,bije->de', left, right, preferred_element_type=jnp.float32)]
    psum x1 -> x0, blocking collectives: 39.3 us -> none  [per_device(): gain_sums = lax.psum(jnp.stack([gain_one, gain_two]), ('img', 'row'))]
    all_to_all x4 -> x5, waiting for transfers between devices: 0.01 us -> 27.3 us  [the longest x1 9.28 us: per_device(): early_got = lax.all_to_all(early_sum, ('z', 'row'), 0, 0, tiled=True)]
  transfers between devices with their start and end apart: 14 -> 13, of which waited for: 8 -> 8; matrix products, arithmetic and copies ran while one was open for 25% -> 4% of each run, Pallas kernels for 0% -> 10%
where the time goes in v1:
time: 170 us; the launch traced here: 169 us
  Pallas kernels  63.9 us (38%)
  waiting for transfers between devices  32.6 us (19%)
  blocking collectives  25.9 us (15%)
  starting transfers between devices  24.5 us (14%)
  local copies, waits for them, and re-layouts  18.1 us (11%)
  other arithmetic  2.87 us (2%)
    pallas_call x1, Pallas kernels, per_device(): pl.pallas_call(middle_kernel, name='attention_and_feed_forward', out_shap...  21 us
    all_gather x1, blocking collectives, per_device(): lax.all_gather(lax.all_gather(early, 'row'), ('z', 'core'))  16.8 us
    pallas_call x1, Pallas kernels, per_device(): pl.pallas_call(lambda *refs: scan_kernel(starts, width, *refs), name='sca...  14.9 us
    pallas_call x1, Pallas kernels, per_device(): pl.pallas_call(lambda *refs: scan_back_kernel(starts, width, *refs), name...  14.6 us
    unnamed x52, local copies, waits for them, and re-layouts  10.7 us
    pallas_call x1, Pallas kernels, per_device(): pl.pallas_call(lambda *refs: attention_back_kernel(*refs, blocks=blocks),...  9.8 us
    all_to_all x1, waiting for transfers between devices, per_device(): early_got = lax.all_to_all(early_sum, ('z', 'row'), 0, 0, tiled=True)  9.28 us
    all_gather x1, blocking collectives, per_device(): lax.all_gather(early, 'row')  9.15 us
  transfers between devices with their start and end apart: 13, of which 8 were waited for; matrix products, arithmetic and copies ran while one was open for 4% of the time, Pallas kernels for 10%

profile of v1, /device:TPU:0, one launch (start us, length us, event | category | flops | bytes accessed | tf_op | source)
XLA Modules:
  0.0 168.8 jit_solution(13123346045705139084)
XLA Ops:
  0.7 1.1 copy.80
  1.9 1.1 copy.81
  3.6 1.1 collective-permute-done
  5.4 5.1 %all-to-all-start = ((bf16[4,2,128,192]{2,3,1,0:T(8,128)(2,1)}), bf16[4,2,128,192]{2,3,1,0:T(8,128)(2,1)S(1)}, u32[]{:S(2)}, u32[]{:S(2)}) async-start(bf16[4,2,128,192]{2,3,1,0:T(8,128)(2,1)} %maximum_select_fusion.1), calls=%async_computation | async-start | bytes 786432 | tf_op jit(solution)/shard_map/all_to_all | solution.py:817
  10.9 6.5 %all-to-all-done = bf16[4,2,128,192]{2,3,1,0:T(8,128)(2,1)S(1)} async-done(((bf16[4,2,128,192]{2,3,1,0:T(8,128)(2,1)}), bf16[4,2,128,192]{2,3,1,0:T(8,128)(2,1)S(1)}, u32[]{:S(2)}, u32[]{:S(2)}) %all-to-all-start) | async-done | bytes 393248 | tf_op jit(solution)/shard_map/all_to_all | solution.py:817
  18.2 4.9 %all-to-all-start.1 = ((bf16[32,48,128]{2,1,0:T(8,128)(2,1)}), bf16[32,48,128]{2,1,0:T(8,128)(2,1)S(1)}, u32[]{:S(2)}, u32[]{:S(2)}) async-start(bf16[32,48,128]{2,1,0:T(8,128)(2,1)} %broadcast_in_dim.5), calls=%async_computation.1 | async-start | bytes 786432 | tf_op jit(solution)/shard_map/all_to_all | solution.py:786
  23.8 9.2 %all-gather = bf16[192,256]{1,0:T(8,128)(2,1)S(1)} all-gather(bf16[48,256]{1,0:T(8,128)(2,1)S(1)} %pad_maximum_fusion.1), channel_id=2, replica_groups=mesh['z'=4,'core'=2,'row'=4] {'row'}, dimensions={0}, use_global_device_ids=true | all-gather | bytes 122880 | tf_op jit(solution)/shard_map/all_gather | solution.py:805
  33.2 16.8 %all-gather.1 = bf16[32,48,256]{2,1,0:T(8,128)(2,1)} all-gather(bf16[4,48,256]{2,1,0:T(8,128)(2,1)S(1)} %bitcast.25), channel_id=3, replica_groups=mesh['z'=4,'core'=2,'row'=4] {'z','core'}, dimensions={0}, use_global_device_ids=true | all-gather | bytes 884736 | tf_op jit(solution)/shard_map/all_gather | solution.py:805
  50.1 1.0 copy.92.refs_1_.own_ref
  51.1 1.1 broadcast_in_dim.4.refs_3_.mask_ref.refs_2_
  52.2 14.9 %scan_forward.1 = (bf16[3,512,128]{2,1,0:T(8,128)(2,1)}, bf16[3,1024,128]{2,1,0:T(8,128)(2,1)}, bf16[3,1024,128]{2,1,0:T(8,128)(2,1)}, bf16[1024,192]{1,0:T(8,12...) custom-call(s32[1]{0:T(128)} %bitcast.refs_0_.core_ref, ...), custom_call_target="tpu_custom_call" | custom-call | tf_op jit(solution)/shard_map/scan_forward/pallas_call | solution.py:831
  67.0 21.0 %attention_and_feed_forward.1 = (bf16[3,512,1024]{2,1,0:T(8,128)(2,1)}, bf16[3,512,128]{2,1,0:T(8,128)(2,1)}, bf16[512,192]{1,0:T(8,128)(2,1)}, f32[512,192]{1,0...) custom-call(s32[1]{0:T(128)} %bitcast.refs_0_.core_ref, ...), custom_call_target="tpu_custom_call" | custom-call | tf_op jit(solution)/shard_map/attention_and_feed_forward/pallas_call | solution.py:853
  88.0 9.8 %attention_backward.1 = (bf16[1024,192]{1,0:T(8,128)(2,1)}, bf16[3,192,384]{2,1,0:T(8,128)(2,1)}) custom-call(s32[1]{0:T(128)} %bitcast.refs_0_.core_ref, bf16[3,512,1024]{2,1,0:T(8,128)(2,1)} %get-tuple-element.47.refs_1_, bf16[3,512,128]{2,1,0:T(8,128)(2,1)} %get-tuple-element.48.refs_2_, bf16[3,512,128]{2,1,0:T(8,128)(2,1)} %get-tuple-element.43.q_ref.refs_3_, ...), custom_call_target="tpu_custom_call" | custom-call | tf_op jit(solution)/shard_map/attention_backward/pallas_call | solution.py:891
  98.5 1.4 collective-permute-done.3.refs_5_
  100.7 14.6 %scan_backward.1 = (bf16[512,192]{1,0:T(8,128)(2,1)}, bf16[4,192,128]{2,1,0:T(8,128)(2,1)}, bf16[4,192,128]{2,1,0:T(8,128)(2,1)}, bf16[16,128]{1,0:T(8,128)(2,1)}) custom-call(s32[1]{0:T(128)} %bitcast.refs_0_.core_ref, bf16[4,2,128,192]{3,2,1,0:T(8,128)(2,1)} %copy.92.refs_1_.own_ref, f32[1024,128]{1,0:T(8,128)} %broadcast_in_dim.4.refs_3_.mask_ref.refs_2_, ...), custom_call_target="tpu_custom_call" | custom-call | tf_op jit(solution)/shard_map/scan_backward/pallas_call | solution.py:910
  115.3 1.2 copy.95
  117.3 3.5 %all-to-all-start.2 = ((bf16[4,2,128,192]{2,3,1,0:T(8,128)(2,1)}), bf16[4,2,128,192]{2,3,1,0:T(8,128)(2,1)S(1)}, u32[]{:S(2)}, u32[]{:S(2)}) async-start(bf16[4,2,128,192]{2,3,1,0:T(8,128)(2,1)} %pad_maximum_fusion), calls=%async_computation.2 | async-start | bytes 786432 | tf_op jit(solution)/shard_map/all_to_all | solution.py:969
  121.3 1.2 collective-permute-done.6.gains_got_ref
  123.2 1.8 %pair_sum.1 = bf16[4,4,64,128]{3,2,1,0:T(8,128)(2,1)} custom-call(bf16[4,192,128]{2,1,0:T(8,128)(2,1)} %get-tuple-element.61.keep_ref, bf16[4,192,128]{2,1,0:T(8,128)(2,1)} %copy-done.7, bf16[16,128]{1,0:T(8,128)(2,1)} %get-tuple-element.63.gains_ref, bf16[16,128]{1,0:T(8,128)(2,1)} %copy-done.14), custom_call_target="tpu_custom_call" | custom-call | tf_op jit(solution)/shard_map/pair_sum/pallas_call | solution.py:954
  125.0 3.1 %all-to-all-done.2 = bf16[4,2,128,192]{2,3,1,0:T(8,128)(2,1)S(1)} async-done(((bf16[4,2,128,192]{2,3,1,0:T(8,128)(2,1)}), bf16[4,2,128,192]{2,3,1,0:T(8,128)(2,1)S(1)}, u32[]{:S(2)}, u32[]{:S(2)}) %all-to-all-start.2) | async-done | bytes 393248 | tf_op jit(solution)/shard_map/all_to_all | solution.py:969
  128.1 5.8 %all-to-all-start.3 = ((bf16[16,64,128]{2,1,0:T(8,128)(2,1)}), bf16[16,64,128]{2,1,0:T(8,128)(2,1)S(1)}, u32[]{:S(2)}, u32[]{:S(2)}) async-start(bf16[16,64,128]{2,1,0:T(8,128)(2,1)} %bitcast.24), calls=%async_computation.3 | async-start | bytes 524288 | tf_op jit(solution)/shard_map/all_to_all | solution.py:962
  133.9 0.8 add_convert_fusion
  135.1 8.4 %all-to-all-done.3.refs_0_ = bf16[16,64,128]{2,1,0:T(8,128)(2,1)S(1)} async-done(((bf16[16,64,128]{2,1,0:T(8,128)(2,1)}), bf16[16,64,128]{2,1,0:T(8,128)(2,1)S(1)}, u32[]{:S(2)}, u32[]{:S(2)}) %all-to-all-start.3) | async-done | bytes 262176 | tf_op jit(solution)/shard_map/all_to_all | solution.py:962
  143.5 3.6 %all-to-all-start.4 = ((bf16[16,48,256]{2,1,0:T(8,128)(2,1)}), bf16[16,48,256]{2,1,0:T(8,128)(2,1)S(1)}, u32[]{:S(2)}, u32[]{:S(2)}) async-start(bf16[16,48,256]{2,1,0:T(8,128)(2,1)} %bitcast.16), calls=%async_computation.4 | async-start | bytes 786432 | tf_op jit(solution)/shard_map/all_to_all | solution.py:889
  147.2 1.5 collective-permute-done.4
  149.7 9.3 %all-to-all-done.4.refs_1_ = bf16[16,48,256]{2,1,0:T(8,128)(2,1)S(1)} async-done(((bf16[16,48,256]{2,1,0:T(8,128)(2,1)}), bf16[16,48,256]{2,1,0:T(8,128)(2,1)S(1)}, u32[]{:S(2)}, u32[]{:S(2)}) %all-to-all-start.4) | async-done | bytes 393248 | tf_op jit(solution)/shard_map/all_to_all | solution.py:889
  159.7 1.9 %final_sum.1 = (f32[1,192]{1,0:T(1,128)}, f32[1,192]{1,0:T(1,128)}, f32[48,24]{1,0:T(8,128)}, f32[48,8]{1,0:T(8,128)}, f32[48,8]{1,0:T(8,128)}, /*index=5*/f32[4...) custom-call(bf16[16,64,128]{2,1,0:T(8,128)(2,1)} %copy-done.2, bf16[16,48,256]{2,1,0:T(8,128)(2,1)} %copy-done.1), custom_call_target="tpu_custom_call" | custom-call | tf_op jit(solution)/shard_map/final_sum/pallas_call | solution.py:980
  161.6 1.6 copy.102
  163.2 1.4 copy.101
  164.6 1.4 copy.98
  166.0 1.4 copy.100
  167.4 1.4 copy.99
  (76 shorter events, 9.2 us)
Async XLA Ops:
  0.6 9.9 %copy-start.9 = (s32[2,32,32]{2,1,0:T(8,128)S(1)}, s32[2,32,32]{2,1,0:T(8,128)}, u32[]{:S(2)}) copy-start(s32[2,32,32]{2,1,0:T(8,128)} %param.18) | copy-start | bytes 24580
  0.7 9.9 %copy-start.12 = (bf16[48,24]{0,1:T(8,128)(2,1)S(1)}, bf16[48,24]{0,1:T(8,128)(2,1)}, u32[]{:S(2)}) copy-start(bf16[48,24]{0,1:T(8,128)(2,1)} %param.20) | copy-start | bytes 6916
  0.7 10.0 %copy-start.15 = (bf16[48,8]{0,1:T(8,128)(2,1)S(1)}, bf16[48,8]{0,1:T(8,128)(2,1)}, u32[]{:S(2)}) copy-start(bf16[48,8]{0,1:T(8,128)(2,1)} %param.21) | copy-start | bytes 2308
  0.7 10.1 %copy-start.16 = (bf16[48,8]{0,1:T(8,128)(2,1)S(1)}, bf16[48,8]{0,1:T(8,128)(2,1)}, u32[]{:S(2)}) copy-start(bf16[48,8]{0,1:T(8,128)(2,1)} %param.22) | copy-start | bytes 2308
  0.7 10.1 %copy-start.11 = (bf16[48,72]{1,0:T(8,128)(2,1)S(1)}, bf16[48,72]{1,0:T(8,128)(2,1)}, u32[]{:S(2)}) copy-start(bf16[48,72]{1,0:T(8,128)(2,1)} %param.23) | copy-start | bytes 20740
  1.8 21.3 %copy-start.8 = (bf16[192,24]{0,1:T(8,128)(2,1)S(1)}, bf16[192,24]{0,1:T(8,128)(2,1)}, u32[]{:S(2)}) copy-start(bf16[192,24]{0,1:T(8,128)(2,1)} %param.26) | copy-start | bytes 27652
  1.8 21.7 %copy-start.13 = (bf16[48,24]{0,1:T(8,128)(2,1)S(1)}, bf16[48,24]{0,1:T(8,128)(2,1)}, u32[]{:S(2)}) copy-start(bf16[48,24]{0,1:T(8,128)(2,1)} %param.24) | copy-start | bytes 6916
  1.9 21.8 %copy-start.10 = (bf16[48,96]{1,0:T(8,128)(2,1)S(1)}, bf16[48,96]{1,0:T(8,128)(2,1)}, u32[]{:S(2)}) copy-start(bf16[48,96]{1,0:T(8,128)(2,1)} %param.25) | copy-start | bytes 27652
  3.1 1.6 collective-permute-start
  5.4 12.0 %all-to-all-start = ((bf16[4,2,128,192]{2,3,1,0:T(8,128)(2,1)}), bf16[4,2,128,192]{2,3,1,0:T(8,128)(2,1)S(1)}, u32[]{:S(2)}, u32[]{:S(2)}) async-start(bf16[4,2,128,192]{2,3,1,0:T(8,128)(2,1)} %maximum_select_fusion.1), calls=%async_computation | async-start | bytes 786432 | tf_op jit(solution)/shard_map/all_to_all | solution.py:817
  10.5 39.4 %collective-permute-start.1 = (s32[2,32,32]{2,1,0:T(8,128)S(1)}, s32[2,32,32]{2,1,0:T(8,128)S(1)}, u32[]{:S(2)}, u32[]{:S(2)}) collective-permute-start(s32[2,32,32]{2,1,0:T(8,128)S(1)} %copy-done.9), channel_id=1, source_target_pairs={{0,4},{4,0},{1,5},{5,1},{2,6},{6,2},{3,7},{7,3},{8,12},{12,8},{9,1... | collective-permute-start | bytes 24584 | tf_op jit(solution)/shard_map/ppermute | solution.py:820
  18.2 32.8 %all-to-all-start.1 = ((bf16[32,48,128]{2,1,0:T(8,128)(2,1)}), bf16[32,48,128]{2,1,0:T(8,128)(2,1)S(1)}, u32[]{:S(2)}, u32[]{:S(2)}) async-start(bf16[32,48,128]{2,1,0:T(8,128)(2,1)} %broadcast_in_dim.5), calls=%async_computation.1 | async-start | bytes 786432 | tf_op jit(solution)/shard_map/all_to_all | solution.py:786
  33.1 17.9 %collective-permute-start.2 = (bf16[4,128,192]{2,1,0:T(8,128)(2,1)S(1)}, bf16[4,128,192]{2,1,0:T(8,128)(2,1)S(1)}, u32[]{:S(2)}, u32[]{:S(2)}) collective-permute-start(bf16[4,128,192]{2,1,0:T(8,128)(2,1)S(1)} %bitcast.28), channel_id=1, source_target_pairs={{0,4},{4,0},{1,5},{5,1},{2,6},{6,2},{3,7},{7,3},{8,12},{12,8},{9,1... | collective-permute-start | bytes 589832 | tf_op jit(solution)/shard_map/ppermute | solution.py:818
  51.1 1.1 copy-start.5
  51.1 1.1 copy-start
  88.0 10.2 %copy-start.17 = (bf16[4,192,256]{2,1,0:T(8,128)(2,1)S(1)}, bf16[4,192,256]{2,1,0:T(8,128)(2,1)}, u32[]{:S(2)}) copy-start(bf16[4,192,256]{2,1,0:T(8,128)(2,1)} %get-tuple-element.65) | copy-start | bytes 1179652
  88.0 10.3 %copy-start.6 = (bf16[512,192]{1,0:T(8,128)(2,1)S(1)}, bf16[512,192]{1,0:T(8,128)(2,1)}, u32[]{:S(2)}) copy-start(bf16[512,192]{1,0:T(8,128)(2,1)} %get-tuple-element.46) | copy-start | bytes 589828
  97.8 2.1 %collective-permute-start.3 = (bf16[1024,192]{1,0:T(8,128)(2,1)}, bf16[1024,192]{1,0:T(8,128)(2,1)S(1)}, u32[]{:S(2)}, u32[]{:S(2)}) collective-permute-start(bf16[1024,192]{1,0:T(8,128)(2,1)} %get-tuple-element.51.refs_4_), channel_id=1, source_target_pairs={{0,4},{4,0},{1,5},{5,1},{2,6},{6,2},{3,7},{7,3},{8,12},{12,8},{9,1... | collective-permute-start | bytes 1179656 | tf_op jit(solution)/shard_map/ppermute | solution.py:908
  98.2 35.7 %collective-permute-start.7 = (bf16[4,192,256]{2,1,0:T(8,128)(2,1)S(1)}, bf16[4,192,256]{2,1,0:T(8,128)(2,1)S(1)}, u32[]{:S(2)}, u32[]{:S(2)}) collective-permute-start(bf16[4,192,256]{2,1,0:T(8,128)(2,1)S(1)} %copy-done.17), channel_id=1, source_target_pairs={{0,4},{4,0},{1,5},{5,1},{2,6},{6,2},{3,7},{7,3},{8,12},{12,8},{9,1... | collective-permute-start | bytes 1179656 | tf_op jit(solution)/shard_map/ppermute | solution.py:886
  99.9 0.8 copy-start.3
  115.3 18.6 %copy-start.4 = (bf16[4,192,256]{2,1,0:T(8,128)(2,1)S(1)}, bf16[4,192,256]{2,1,0:T(8,128)(2,1)}, u32[]{:S(2)}) copy-start(bf16[4,192,256]{2,1,0:T(8,128)(2,1)} %get-tuple-element.64) | copy-start | bytes 1179652
  117.3 10.9 %all-to-all-start.2 = ((bf16[4,2,128,192]{2,3,1,0:T(8,128)(2,1)}), bf16[4,2,128,192]{2,3,1,0:T(8,128)(2,1)S(1)}, u32[]{:S(2)}, u32[]{:S(2)}) async-start(bf16[4,2,128,192]{2,3,1,0:T(8,128)(2,1)} %pad_maximum_fusion), calls=%async_computation.2 | async-start | bytes 786432 | tf_op jit(solution)/shard_map/all_to_all | solution.py:969
  120.7 1.8 %collective-permute-start.5 = (bf16[4,192,128]{2,1,0:T(8,128)(2,1)}, bf16[4,192,128]{2,1,0:T(8,128)(2,1)S(1)}, u32[]{:S(2)}, u32[]{:S(2)}) collective-permute-start(bf16[4,192,128]{2,1,0:T(8,128)(2,1)} %get-tuple-element.62), channel_id=1, source_target_pairs={{0,4},{4,0},{1,5},{5,1},{2,6},{6,2},{3,7},{7,3},{8,12},{12,8},{9,1... | collective-permute-start | bytes 589832 | tf_op jit(solution)/shard_map/ppermute | solution.py:951
  121.1 1.4 collective-permute-start.6
  122.5 0.6 copy-start.14
  122.5 0.7 copy-start.7
  128.1 15.4 %all-to-all-start.3 = ((bf16[16,64,128]{2,1,0:T(8,128)(2,1)}), bf16[16,64,128]{2,1,0:T(8,128)(2,1)S(1)}, u32[]{:S(2)}, u32[]{:S(2)}) async-start(bf16[16,64,128]{2,1,0:T(8,128)(2,1)} %bitcast.24), calls=%async_computation.3 | async-start | bytes 524288 | tf_op jit(solution)/shard_map/all_to_all | solution.py:962
  143.5 15.5 %copy-start.2 = (bf16[16,64,128]{2,1,0:T(8,128)(2,1)}, bf16[16,64,128]{2,1,0:T(8,128)(2,1)S(1)}, u32[]{:S(2)}) copy-start(bf16[16,64,128]{2,1,0:T(8,128)(2,1)S(1)} %all-to-all-done.3.refs_0_) | copy-start | bytes 786436
  143.5 15.5 %all-to-all-start.4 = ((bf16[16,48,256]{2,1,0:T(8,128)(2,1)}), bf16[16,48,256]{2,1,0:T(8,128)(2,1)S(1)}, u32[]{:S(2)}, u32[]{:S(2)}) async-start(bf16[16,48,256]{2,1,0:T(8,128)(2,1)} %bitcast.16), calls=%async_computation.4 | async-start | bytes 786432 | tf_op jit(solution)/shard_map/all_to_all | solution.py:889
  147.1 1.6 collective-permute-start.4
  158.9 0.8 copy-start.1

commit v2 on v1

--- a/solution.py
+++ b/solution.py
@@ -114,6 +114,12 @@
     return jnp.concatenate([mask, mask[:, : D - LANES]], axis=1)
 
 
+def put_blocks(ref, z, lanes, value):
+    rows = ref.shape[2]
+    for r in range(ref.shape[0]):
+        ref[r, z, :, lanes] = value[r * rows : (r + 1) * rows]
+
+
 def put_lanes(ref, rows, values):
     ref[0, rows, :] = values[:, :LANES]
     ref[1, rows, : D - LANES] = values[:, LANES:]
@@ -135,26 +141,172 @@
     return total
 
 
-def compiler(limit=60 << 20):
+def gather_parts(place_ref, mine_refs, got_refs, block, out_ref):
+    core, row, depth = place_ref[0], place_ref[1], place_ref[2]
+    lanes = slice(block * LANES, (block + 1) * LANES)
+    count = out_ref.shape[0] // 2
+    rows = out_ref.shape[2]
+    for refs, which in ((mine_refs, core), (got_refs, 1 - core)):
+        for k, ref in enumerate(refs):
+            for j in range(count):
+                value = ref[j * rows : (j + 1) * rows, lanes]
+                out_ref[2 * (depth ^ j) + which, row ^ k] = value
+    wide = []
+    for m in range(2 * count):
+        wide.append(jnp.concatenate([out_ref[m, r] for r in range(out_ref.shape[1])], axis=0))
+    return jnp.concatenate(wide, axis=1)
+
+
+LARGE = 60 << 20
+
+
+def compiler(limit=24 << 20):
     return pltpu.CompilerParams(vmem_limit_bytes=limit)
 
 
 VMEM = pl.BlockSpec(memory_space=pltpu.VMEM)
 SMEM = pl.BlockSpec(memory_space=pltpu.SMEM)
+
+
+def pack(values):
+    half = values.shape[0] // 2
+    tail = jnp.concatenate([values[:half, LANES:], values[half:, LANES:]], axis=1)
+    return jnp.concatenate([values[:, :LANES], tail], axis=0)
+
+
+def unpack(packed):
+    count = packed.shape[0] * 2 // 3
+    tail = packed[count:]
+    tail = jnp.concatenate([tail[:, : D - LANES], tail[:, D - LANES :]], axis=0)
+    return jnp.concatenate([packed[:count], tail], axis=1)
+
+
+def pack_weights_kernel(turned_refs, qkv_ref, fc1_ref, out_ref):
+    wu, rate, coef, wo, fc2 = [ref[...].astype(F32) for ref in turned_refs]
+    rows = qkv_ref.shape[0]
+    a_o, a_r = wo.shape[0], rate.shape[0]
+    pieces = [wu, rate, coef, wo] + [fc2[:, g * rows : (g + 1) * rows] for g in range(4)]
+    joined = jnp.concatenate(pieces, axis=0)
+    joined = jnp.concatenate([joined, jnp.zeros((joined.shape[0], LANES - rows), F32)], axis=1)
+    joined = joined.T[:rows]
+    first, second = a_o + 2 * a_r, 2 * a_o + 2 * a_r
+
+    def fill(parts):
+        used = sum(part.shape[1] for part in parts)
+        return parts + [jnp.zeros((rows, LANES - used), F32)]
+
+    packed = jnp.concatenate(
+        fill([joined[:, :first], qkv_ref[...].astype(F32)])
+        + fill([fc1_ref[...].astype(F32), joined[:, first:second]])
+        + fill([joined[:, second:]]),
+        axis=1,
+    ).astype(BF16)
+    out_ref[...] = packed
+
+
+def route_kernel(place_ref, patch_ref, cot_ref, valid_ref, *out_refs):
+    row = place_ref[1]
+    images, slots, _ = patch_ref.shape
+    half = slots // 2
+    packed = half * 3 // 2
+    for j, out_ref in enumerate(out_refs):
+        target = row ^ j
+        core, image = target // images, target % images
+        out_ref[:packed] = pack(patch_ref[image, :half])
+        out_ref[packed : 2 * packed] = pack(patch_ref[image, half:])
+        start = pl.multiple_of(core * half, half)
+        out_ref[2 * packed : 3 * packed] = pack(cot_ref[image, pl.ds(start, half), :])
+        valid = valid_ref[image].astype(F32).astype(BF16)
+        out_ref[3 * packed :] = jnp.concatenate(
+            [valid, jnp.zeros((GRID, LANES - GRID), BF16)], axis=1
+        )
+
+
+def depart_kernel(place_ref, *refs):
+    turned, (qkv_ref, fc1_ref, patch_ref, cot_ref, valid_ref, out_ref) = refs[:5], refs[5:11]
+    pack_weights_kernel(turned, qkv_ref, fc1_ref, out_ref)
+    route_kernel(place_ref, patch_ref, cot_ref, valid_ref, *refs[11:])
+
+
+def norm_kernel(place_ref, gains_ref, *refs):
+    core, row = place_ref[0], place_ref[1]
+    got_refs, (own_ref, first_ref, mask_ref) = refs[:-3], refs[-3:]
+    images = len(got_refs) // 2
+    gain = gains_ref[0:1, :]
+    slots = own_ref.shape[2]
+    packed = slots * 3 // 2
+    valid = got_refs[0][3 * packed :].astype(F32).T
+    for i in range(GRID):
+        mask_ref[i * GRID : (i + 1) * GRID, :] = jnp.broadcast_to(
+            valid[:GRID, i : i + 1], (GRID, LANES)
+        )
+    for j, got in enumerate(got_refs):
+        block = (core * images + row % images) ^ j
+        own_ref[block, 1] = unpack(got[2 * packed : 3 * packed])
+        for half in range(2):
+            patch = unpack(got[half * packed : (half + 1) * packed])
+
+            @pl.when(core == half)
+            def _(patch=patch, block=block):
+                own_ref[block, 0] = patch
+
+            unit, _ = normalise(patch.astype(F32))
+            start = pl.multiple_of((block * 2 + half) * slots, slots)
+            first_ref[pl.ds(start, slots), :] = (unit * gain).astype(BF16)
+
+
+def home_kernel(place_ref, *refs):
+    row = place_ref[1]
+    got_refs, out_refs = refs[:-2], refs[-2:]
+    images, slots, _ = out_refs[0].shape
+    half = slots // 2
+    for j, got in enumerate(got_refs):
+        source = row ^ j
+        core, image = source // images, source % images
+        place = pl.ds(pl.multiple_of(core * half, half), half)
+        for which, out_ref in enumerate(out_refs):
+            out_ref[image, place, :] = unpack(got[which])
 
 
 def scan_kernel(
     starts,
     width,
     core_ref,
-    own_ref,
-    other_ref,
+    first_ref,
     mask_ref,
-    gains_ref,
-    late_ref,
     sel_u_ref,
     sel_rc_ref,
     sel_q_ref,
+    *refs,
+    blocks,
+):
+    mine_refs, got_refs, refs = refs[:blocks], refs[blocks : 2 * blocks], refs[2 * blocks :]
+    scan_body(
+        starts,
+        width,
+        core_ref,
+        first_ref,
+        mask_ref,
+        sel_u_ref,
+        sel_rc_ref,
+        sel_q_ref,
+        mine_refs,
+        got_refs,
+        *refs,
+    )
+
+
+def scan_body(
+    starts,
+    width,
+    core_ref,
+    first_ref,
+    mask_ref,
+    sel_u_ref,
+    sel_rc_ref,
+    sel_q_ref,
+    mine_refs,
+    got_refs,
     q_ref,
     k_ref,
     v_ref,
@@ -164,7 +316,7 @@
     rates_ref,
     wu_ref,
     wqkv_ref,
-    first_ref,
+    late_ref,
     xs,
     xt,
     cols,
@@ -172,12 +324,10 @@
     scanned_own,
 ):
     core = core_ref[0]
-    blocks, _, rows_slots, _ = own_ref.shape
-    half_rows = rows_slots // GRID
-    parts = late_ref.shape[0]
-    gain = gains_ref[0:1, :]
-
-    late = jnp.concatenate([late_ref[m] for m in range(parts)], axis=1)
+    blocks = len(mine_refs)
+    rows_slots = OWN // blocks
+
+    late = gather_parts(core_ref, mine_refs, got_refs, 0, late_ref)
     wu = dot(late, sel_u_ref[...]).astype(BF16)
     wu_ref[...] = wu
     rates = dot(late, sel_rc_ref[...])
@@ -214,16 +364,6 @@
 
     xs[1, :, D - LANES :] = jnp.zeros((SLOTS, 2 * LANES - D), F32)
 
-    def norm_step(block, _):
-        for which in range(2):
-            ref = own_ref.at[block, 0] if which == 0 else other_ref.at[block]
-            place = core if which == 0 else 1 - core
-            unit, _ = normalise(ref[...].astype(F32))
-            start = pl.multiple_of((block * 2 + place) * rows_slots, rows_slots)
-            first_ref[pl.ds(start, rows_slots), :] = (unit * gain).astype(BF16)
-        return 0
-
-    lax.fori_loop(0, blocks, norm_step, 0)
     mixed = dot(first_ref[...], wu) * widen(mask_ref[...])
     mixed = mixed.astype(BF16)
     mixed_ref[...] = mixed
@@ -284,13 +424,45 @@
     own_ref,
     mask_ref,
     gains_ref,
-    early_ref,
     sel_1_ref,
     sel_o_ref,
     sel_2_ref,
     q_ref,
     k_ref,
     v_ref,
+    *refs,
+):
+    blocks = own_ref.shape[0]
+    middle_body(
+        core_ref,
+        own_ref,
+        mask_ref,
+        gains_ref,
+        sel_1_ref,
+        sel_o_ref,
+        sel_2_ref,
+        q_ref,
+        k_ref,
+        v_ref,
+        refs[:blocks],
+        refs[blocks : 2 * blocks],
+        *refs[2 * blocks :],
+    )
+
+
+def middle_body(
+    core_ref,
+    own_ref,
+    mask_ref,
+    gains_ref,
+    sel_1_ref,
+    sel_o_ref,
+    sel_2_ref,
+    q_ref,
+    k_ref,
+    v_ref,
+    mine_refs,
+    got_refs,
     soft_ref,
     lifted_ref,
     out_ref,
@@ -298,6 +470,7 @@
     gain_ref,
     keep_ref,
     send_ref,
+    early_ref,
     scores,
     wo,
     w1,
@@ -318,8 +491,8 @@
     per_block = D // blocks
     gain = gains_ref[1:2, :]
 
-    left = jnp.concatenate([early_ref[m, :, :LANES] for m in range(parts)], axis=1)
-    right = jnp.concatenate([early_ref[m, :, LANES:] for m in range(parts)], axis=1)
+    left = gather_parts(core_ref, mine_refs, got_refs, 1, early_ref)
+    right = gather_parts(core_ref, mine_refs, got_refs, 2, early_ref)
     span = parts // 2 * LANES
     for half in range(2):
         w1[:, half * FF // 2 : (half + 1) * FF // 2] = dot(
@@ -429,11 +602,11 @@
 
             @pl.when(core == m % 2)
             def _(value=value, m=m):
-                keep_ref[m // 2, :, lanes] = value
+                put_blocks(keep_ref, m // 2, lanes, value)
 
             @pl.when(core != m % 2)
             def _(value=value, m=m):
-                send_ref[m // 2, :, lanes] = value
+                put_blocks(send_ref, m // 2, lanes, value)
 
     deliver(slice(0, LANES))
     total = None
@@ -518,13 +691,75 @@
     grad_middle_ref,
     grad_w_ref,
     gain_two_ref,
+    out_own_ref,
     sel_u_ref,
     sel_rc_ref,
     sel_q_ref,
-    grad_ref,
     keep_ref,
     send_ref,
     gains_out_ref,
+    *refs,
+):
+    routed_refs, scratch = refs[:-13], refs[-13:]
+    scan_back_body(
+        starts,
+        width,
+        core_ref,
+        own_ref,
+        mask_ref,
+        gains_ref,
+        part_ref,
+        got_ref,
+        mixed_ref,
+        first_ref,
+        table_ref,
+        rates_ref,
+        wu_ref,
+        grad_middle_ref,
+        grad_w_ref,
+        gain_two_ref,
+        sel_u_ref,
+        sel_rc_ref,
+        sel_q_ref,
+        keep_ref,
+        send_ref,
+        gains_out_ref,
+        *scratch,
+    )
+    images = len(routed_refs) // 2
+    mine = core_ref[0] * images + core_ref[1] % images
+    slots = own_ref.shape[2]
+    grad = scratch[0]
+    for j, routed in enumerate(routed_refs):
+        place = pl.ds(pl.multiple_of((mine ^ j) * slots, slots), slots)
+        routed[0] = pack(out_own_ref[place, :])
+        routed[1] = pack(grad[place, :])
+
+
+def scan_back_body(
+    starts,
+    width,
+    core_ref,
+    own_ref,
+    mask_ref,
+    gains_ref,
+    part_ref,
+    got_ref,
+    mixed_ref,
+    first_ref,
+    table_ref,
+    rates_ref,
+    wu_ref,
+    grad_middle_ref,
+    grad_w_ref,
+    gain_two_ref,
+    sel_u_ref,
+    sel_rc_ref,
+    sel_q_ref,
+    keep_ref,
+    send_ref,
+    gains_out_ref,
+    grad_ref,
     gs,
     gt,
     xs,
@@ -685,11 +920,11 @@
 
         @pl.when(core == m % 2)
         def _(value=value, m=m):
-            keep_ref[m // 2] = value
+            put_blocks(keep_ref, m // 2, slice(None), value)
 
         @pl.when(core != m % 2)
         def _(value=value, m=m):
-            send_ref[m // 2] = value
+            put_blocks(send_ref, m // 2, slice(None), value)
 
     lines = []
     for value in (gain_one, gain_two_ref[...]):
@@ -703,29 +938,63 @@
     gains_out_ref[...] = jnp.concatenate(lines, axis=0).astype(BF16)
 
 
-def pair_sum_kernel(keep_ref, got_ref, gains_ref, gains_got_ref, out_ref):
-    depth, blocks, rows, _ = out_ref.shape
-    rows -= 16
+def split(value):
+    high = value.astype(BF16).astype(F32)
+    return jnp.concatenate([high, value - high], axis=0)
+
+
+def early_sum_kernel(place_ref, keep_ref, got_ref, *out_refs):
+    for k, out_ref in enumerate(out_refs):
+        block = place_ref[1] ^ k
+        for z in range(keep_ref.shape[1]):
+            total = keep_ref[block, z].astype(F32) + got_ref[block, z].astype(F32)
+            out_ref[z] = total.astype(BF16)
+
+
+def late_sum_kernel(place_ref, keep_ref, got_ref, gains_ref, gains_got_ref, *out_refs):
+    depth = keep_ref.shape[1]
     gains = gains_ref[...].astype(F32) + gains_got_ref[...].astype(F32)
     lines = []
     for g in range(2):
         for lane in range(2):
             at = 4 * g + lane
             lines.append(gains[at : at + 1] + gains[at + 2 : at + 3])
-    value = jnp.concatenate(lines, axis=0)
-    high = value.astype(BF16).astype(F32)
-    gains = jnp.concatenate([high, value - high, jnp.zeros((8, LANES), F32)], axis=0).astype(BF16)
-    for z in range(depth):
-        total = keep_ref[z].astype(F32) + got_ref[z].astype(F32)
-        for r in range(blocks):
-            out_ref[z, r, :rows] = total[r * rows : (r + 1) * rows].astype(BF16)
-            out_ref[z, r, rows:] = gains
-
-
-def final_kernel(
+    gains = jnp.concatenate([split(jnp.concatenate(lines, axis=0)), jnp.zeros((8, LANES), F32)], axis=0)
+    gains = gains.astype(BF16)
+    for k, out_ref in enumerate(out_refs):
+        block = place_ref[1] ^ k
+        rows = keep_ref.shape[2]
+        for z in range(depth):
+            total = keep_ref[block, z].astype(F32) + got_ref[block, z].astype(F32)
+            out_ref[z, :rows] = total.astype(BF16)
+            out_ref[z, rows:] = gains
+
+
+def row_sum_kernel(blocks, place_ref, *refs):
+    early_refs, late_refs, out_refs = refs[:blocks], refs[blocks : 2 * blocks], refs[2 * blocks :]
+    rows = early_refs[0].shape[1]
+    for j, out_ref in enumerate(out_refs):
+        z = place_ref[2] ^ j
+        early = early_refs[0][z].astype(F32)
+        late = late_refs[0][z].astype(F32)
+        for k in range(1, blocks):
+            early = early + early_refs[k][z].astype(F32)
+            late = late + late_refs[k][z].astype(F32)
+        out_ref[:rows, LANES:] = early.astype(BF16)
+        out_ref[:rows, :LANES] = late[:rows].astype(BF16)
+        gains = split(late[rows : rows + 4] + late[rows + 4 : rows + 8])
+        gains = jnp.concatenate([gains, jnp.zeros((8, LANES), F32)], axis=0).astype(BF16)
+        out_ref[rows:, :LANES] = gains
+        out_ref[rows:, LANES:] = jnp.zeros((16, 2 * LANES), BF16)
+
+
+def final_kernel(parts, *refs):
+    final_body(parts, refs[: parts // 2], *refs[parts // 2 :])
+
+
+def final_body(
     parts,
-    late_ref,
-    early_ref,
+    got_refs,
     g1_ref,
     g2_ref,
     wu_ref,
@@ -737,17 +1006,17 @@
     fc2_ref,
 ):
     a_u, a_r, a_q, (o_u, o_r, o_c, o_q) = late_layout(parts)
-    count = late_ref.shape[0]
-    total = late_ref[0].astype(F32)
-    early = early_ref[0].astype(F32)
-    for i in range(1, count):
-        total = total + late_ref[i].astype(F32)
-        early = early + early_ref[i].astype(F32)
-    rows = wu_ref.shape[0]
+    total = got_refs[0][...].astype(F32)
+    for ref in got_refs[1:]:
+        total = total + ref[...].astype(F32)
+    early = total[: fc1_ref.shape[0], LANES:]
+    total = total[:, :LANES]
+    rows = fc1_ref.shape[0]
     weights, gains = total[:rows], total[rows:]
-    wu_ref[...] = weights[:, o_u : o_u + a_u]
-    rate_ref[...] = weights[:, o_r : o_r + a_r]
-    coef_ref[...] = weights[:, o_c : o_c + a_r]
+    turned = weights.T
+    wu_ref[...] = turned[o_u : o_u + a_u]
+    rate_ref[...] = turned[o_r : o_r + a_r]
+    coef_ref[...] = turned[o_c : o_c + a_r]
     qkv_ref[...] = weights[:, o_q : o_q + a_q]
     gains = gains[0:4] + gains[4:8]
     for g, ref in ((0, g1_ref), (1, g2_ref)):
@@ -756,11 +1025,9 @@
         )
     a_1, a_o = FF // parts, D // parts
     fc1_ref[...] = early[:, :a_1]
-    wo_ref[...] = early[:, a_1 : a_1 + a_o]
-    for g in range(4):
-        fc2_ref[g * rows : (g + 1) * rows] = early[
-            :, LANES + g * a_o : LANES + (g + 1) * a_o
-        ]
+    wo_ref[...] = early[:, :LANES].T[a_1 : a_1 + a_o]
+    turned = early[:, LANES:].T
+    fc2_ref[...] = jnp.concatenate([turned[g * a_o : (g + 1) * a_o] for g in range(4)], axis=1)
 
 
 def per_device(
@@ -769,67 +1036,112 @@
     images, rows_here, _, _ = patches.shape
     depth, blocks = lax.axis_size("z"), lax.axis_size("row")
     parts = 2 * depth
-    half_rows = rows_here // 2
-    rows_slots = half_rows * GRID
+    rows_slots = rows_here // 2 * GRID
+    packed_rows = rows_slots * 3 // 2
     core = lax.axis_index("core")
     row = lax.axis_index("row")
-    first_core = core == 0
     swap = [(0, 1), (1, 0)]
-    core_index = core.astype(jnp.int32).reshape(1)
+    place = jnp.stack([core, row, lax.axis_index("z")]).astype(jnp.int32)
     shape = jax.ShapeDtypeStruct
+
+    def swapped(value):
+        return lax.ppermute(value, "core", swap)
+
+    def exchanged(values, axis):
+        size = len(values)
+        return [values[0]] + [
+            lax.ppermute(values[k], axis, [(i, i ^ k) for i in range(size)]) for k in range(1, size)
+        ]
+
+    def to_chips(value, j):
+        pairs = []
+        for home in range(2):
+            for source in range(blocks):
+                target, image = divmod(source ^ j, images)
+                pairs.append((home * blocks + source, target * blocks + home * images + image))
+        return lax.ppermute(value, ("core", "row"), pairs)
+
+    def to_homes(value, j):
+        pairs = []
+        for source in range(2):
+            for chip in range(blocks):
+                home, image = divmod(chip, images)
+                target = (source * images + image) ^ j
+                pairs.append((source * blocks + chip, home * blocks + target))
+        return lax.ppermute(value, ("core", "row"), pairs)
 
     sel_u, sel_rc, sel_q, starts, width = late_selections(parts)
     sel_1, sel_o, sel_2 = early_selections(parts)
 
-    late = jnp.concatenate([w_u, decay_rate, out_coef, w_qkv], axis=1)
-    late = jnp.pad(late, ((0, 0), (0, LANES - late.shape[1])))
-    late_all = lax.all_to_all(
-        jnp.broadcast_to(late[None], (parts * blocks,) + late.shape),
-        ("z", "core", "row"),
-        0,
-        0,
-        tiled=True,
-    ).reshape(parts, D, LANES)
     rows_weight = w_u.shape[0]
-    left = jnp.concatenate([w_fc1, w_o], axis=1)
-    right = jnp.concatenate(
-        [w_fc2[g * rows_weight : (g + 1) * rows_weight] for g in range(4)], axis=1
-    )
-    early = jnp.concatenate(
-        [
-            jnp.pad(left, ((0, 0), (0, LANES - left.shape[1]))),
-            jnp.pad(right, ((0, 0), (0, LANES - right.shape[1]))),
-        ],
-        axis=1,
-    )
-    early_all = lax.all_gather(lax.all_gather(early, "row"), ("z", "core")).reshape(
-        parts, D, 2 * LANES
-    )
-
-    both = jnp.stack([patches, cotangent], axis=1)
-    both = both.reshape(images, 2, 2, rows_slots, D)
-    mine = lax.dynamic_index_in_dim(both, core, 2, keepdims=False)
-    theirs = lax.dynamic_index_in_dim(both, 1 - core, 2, keepdims=False)
-    got = lax.ppermute(theirs, "core", swap)
-    plane = jnp.where(
-        first_core, jnp.concatenate([mine, got], axis=0), jnp.concatenate([got, mine], axis=0)
-    )
-    own = lax.all_to_all(plane, "row", 0, 0, tiled=True)
-    other = lax.ppermute(own[:, 0], "core", swap)
-
-    mask_got = lax.ppermute(valid_mask, "core", swap)
-    mask_plane = jnp.where(
-        first_core,
-        jnp.concatenate([valid_mask, mask_got], axis=0),
-        jnp.concatenate([mask_got, valid_mask], axis=0),
-    )
-    mask = lax.dynamic_index_in_dim(mask_plane, row, 0, keepdims=False)
-    mask = jnp.broadcast_to(mask.reshape(SLOTS, 1).astype(F32), (SLOTS, LANES))
+    payload = shape((3 * packed_rows + GRID, LANES), BF16)
+    shard = shape((rows_weight, 3 * LANES), BF16)
+    sources = [value.reshape(images, rows_here * GRID, D) for value in (patches, cotangent)]
+    if rows_weight % 16 == 0:
+        weights, *routed = pl.pallas_call(
+            depart_kernel,
+            name="depart",
+            out_shape=(shard,) + (payload,) * blocks,
+            in_specs=[SMEM] + [VMEM] * 10,
+            out_specs=[VMEM] * (1 + blocks),
+            compiler_params=compiler(LARGE),
+        )(
+            place,
+            w_u.T,
+            decay_rate.T,
+            out_coef.T,
+            w_o.T,
+            w_fc2.T,
+            w_qkv,
+            w_fc1,
+            *sources,
+            valid_mask,
+        )
+    else:
+
+        def fill(pieces):
+            joined = jnp.concatenate(pieces, axis=1)
+            return jnp.pad(joined, ((0, 0), (0, LANES - joined.shape[1])))
+
+        weights = jnp.concatenate(
+            [
+                fill([w_u, decay_rate, out_coef, w_qkv]),
+                fill([w_fc1, w_o]),
+                fill([w_fc2[g * rows_weight : (g + 1) * rows_weight] for g in range(4)]),
+            ],
+            axis=1,
+        )
+        routed = pl.pallas_call(
+            route_kernel,
+            name="route",
+            out_shape=(payload,) * blocks,
+            in_specs=[SMEM] + [VMEM] * 3,
+            out_specs=[VMEM] * blocks,
+            compiler_params=compiler(LARGE),
+        )(place, *sources, valid_mask)
+
+    weights = jnp.concatenate(exchanged([weights] * depth, "z"), axis=0)
+    weights = exchanged([weights] * blocks, "row")
+    weights = weights + [swapped(value) for value in weights]
+    routed = [to_chips(value, j) for j, value in enumerate(routed)]
+    own, first, mask = pl.pallas_call(
+        norm_kernel,
+        name="first_norm",
+        out_shape=(
+            shape((blocks, 2, rows_slots, D), BF16),
+            shape((SLOTS, D), BF16),
+            shape((SLOTS, LANES), F32),
+        ),
+        in_specs=[SMEM] + [VMEM] * (1 + blocks),
+        out_specs=[VMEM] * 3,
+        compiler_params=compiler(8 << 20),
+    )(place, norm_gains, *routed)
 
     head_own = shape((HEADS, OWN, LANES), BF16)
     head_all = shape((HEADS, SLOTS, LANES), BF16)
-    q, k, v, scanned, mixed, table, rates, wu, wqkv, first = pl.pallas_call(
-        lambda *refs: scan_kernel(starts, width, *refs),
+    part_scratch = pltpu.VMEM((parts, blocks, rows_weight, LANES), BF16)
+    q, k, v, scanned, mixed, table, rates, wu, wqkv = pl.pallas_call(
+        lambda *refs: scan_kernel(starts, width, *refs, blocks=blocks),
         name="scan_forward",
         out_shape=(
             head_own,
@@ -841,15 +1153,16 @@
             shape((LANES, 2 * LANES), F32),
             shape((D, D), BF16),
             shape((3, D, TILE), BF16),
-            shape((SLOTS, D), BF16),
         ),
-        in_specs=[SMEM] + [VMEM] * 8,
-        out_specs=[VMEM] * 10,
-        scratch_shapes=[pltpu.VMEM((2, SLOTS, LANES), F32)] * 4 + [pltpu.VMEM((OWN, D), BF16)],
+        in_specs=[SMEM] + [VMEM] * (5 + 2 * blocks),
+        out_specs=[VMEM] * 9,
+        scratch_shapes=[part_scratch]
+        + [pltpu.VMEM((2, SLOTS, LANES), F32)] * 4
+        + [pltpu.VMEM((OWN, D), BF16)],
         compiler_params=compiler(),
-    )(core_index, own, other, mask, norm_gains, late_all, sel_u, sel_rc, sel_q)
-
-    wire_early = shape((depth, D, 2 * LANES), BF16)
+    )(place, first, mask, sel_u, sel_rc, sel_q, *weights)
+
+    wire_early = shape((blocks, depth, rows_weight, 2 * LANES), BF16)
     soft, lifted, out_own, grad_middle, gain_two, early_keep, early_send = pl.pallas_call(
         middle_kernel,
         name="attention_and_feed_forward",
@@ -862,9 +1175,10 @@
             wire_early,
             wire_early,
         ),
-        in_specs=[SMEM] + [VMEM] * 10,
+        in_specs=[SMEM] + [VMEM] * (9 + 2 * blocks),
         out_specs=[VMEM] * 7,
         scratch_shapes=[
+            part_scratch,
             pltpu.VMEM((OWN, SLOTS), F32),
             pltpu.VMEM((HEADS, LANES, D), BF16),
             pltpu.VMEM((D, FF), BF16),
@@ -880,13 +1194,9 @@
             pltpu.VMEM((D, parts * LANES), F32),
         ],
         compiler_params=compiler(),
-    )(core_index, own, mask, norm_gains, early_all, sel_1, sel_o, sel_2, q, k, v)
-
-    early_sum = (
-        early_keep.astype(F32) + lax.ppermute(early_send, "core", swap).astype(F32)
-    ).astype(BF16)
-    early_sum = early_sum.reshape(depth * blocks, D // blocks, 2 * LANES)
-    early_got = lax.all_to_all(early_sum, ("z", "row"), 0, 0, tiled=True)
+    )(place, own, mask, norm_gains, sel_1, sel_o, sel_2, q, k, v, *weights)
+
+    early_recv = swapped(early_send)
 
     part, grad_w = pl.pallas_call(
         lambda *refs: attention_back_kernel(*refs, blocks=blocks),
@@ -903,17 +1213,30 @@
             pltpu.VMEM((SLOTS, D), F32),
         ],
         compiler_params=compiler(),
-    )(core_index, soft, lifted, q, k, v, scanned, wqkv)
-
-    part_got = lax.ppermute(part, "core", swap)
-    wire_late = shape((depth, D, LANES), BF16)
-    grad_own, late_keep, late_send, gains_keep = pl.pallas_call(
+    )(place, soft, lifted, q, k, v, scanned, wqkv)
+
+    part_got = swapped(part)
+    early_keep, early_recv, part = lax.optimization_barrier((early_keep, early_recv, part))
+    early = pl.pallas_call(
+        early_sum_kernel,
+        name="early_sum",
+        out_shape=(shape((depth, rows_weight, 2 * LANES), BF16),) * blocks,
+        in_specs=[SMEM] + [VMEM] * 2,
+        out_specs=[VMEM] * blocks,
+        compiler_params=compiler(8 << 20),
+    )(place, early_keep, early_recv)
+    early, part_got = lax.optimization_barrier((early, part_got))
+    early = exchanged(early, "row")
+    wire_late = shape((blocks, depth, rows_weight, LANES), BF16)
+    payload = shape((2, packed_rows, LANES), BF16)
+    late_keep, late_send, gains, *routed = pl.pallas_call(
         lambda *refs: scan_back_kernel(starts, width, *refs),
         name="scan_backward",
-        out_shape=(shape((OWN, D), BF16), wire_late, wire_late, shape((16, LANES), BF16)),
-        in_specs=[SMEM] + [VMEM] * 16,
-        out_specs=[VMEM] * 4,
+        out_shape=(wire_late, wire_late, shape((16, LANES), BF16)) + (payload,) * blocks,
+        in_specs=[SMEM] + [VMEM] * 17,
+        out_specs=[VMEM] * (3 + blocks),
         scratch_shapes=[
+            pltpu.VMEM((OWN, D), BF16),
             pltpu.VMEM((2, SLOTS, LANES), F32),
             pltpu.VMEM((2, OWN, LANES), F32),
             pltpu.VMEM((2, SLOTS, LANES), F32),
@@ -929,7 +1252,7 @@
         ],
         compiler_params=compiler(),
     )(
-        core_index,
+        place,
         own,
         mask,
         norm_gains,
@@ -943,70 +1266,73 @@
         grad_middle,
         grad_w,
         gain_two,
+        out_own,
         sel_u,
         sel_rc,
         sel_q,
     )
 
-    late_recv = lax.ppermute(late_send, "core", swap)
-    gains_recv = lax.ppermute(gains_keep, "core", swap)
-    rows_weight = D // blocks
-    late_sum = pl.pallas_call(
-        pair_sum_kernel,
-        name="pair_sum",
-        out_shape=shape((depth, blocks, rows_weight + 16, LANES), BF16),
-        in_specs=[VMEM] * 4,
-        out_specs=VMEM,
-        compiler_params=compiler(),
-    )(late_keep, late_recv, gains_keep, gains_recv)
-    late_got = lax.all_to_all(
-        late_sum.reshape(depth * blocks, rows_weight + 16, LANES), ("z", "row"), 0, 0, tiled=True
-    )
-
-    results = jnp.stack(
-        [out_own.reshape(blocks, rows_slots, D), grad_own.reshape(blocks, rows_slots, D)], axis=1
-    )
-    results = lax.all_to_all(results, "row", 0, 0, tiled=True)
-    mine = jnp.where(first_core, results[:images], results[images:])
-    theirs = jnp.where(first_core, results[images:], results[:images])
-    got = lax.ppermute(theirs, "core", swap)
-    whole = jnp.where(
-        first_core, jnp.stack([mine, got], axis=2), jnp.stack([got, mine], axis=2)
-    )
-    block_out = whole[:, 0].reshape(patches.shape)
-    grad_patches = whole[:, 1].reshape(patches.shape)
-
-    weight = (rows_weight,)
+    late = pl.pallas_call(
+        late_sum_kernel,
+        name="late_sum",
+        out_shape=(shape((depth, rows_weight + 16, LANES), BF16),) * blocks,
+        in_specs=[SMEM] + [VMEM] * 4,
+        out_specs=[VMEM] * blocks,
+        compiler_params=compiler(8 << 20),
+    )(place, late_keep, swapped(late_send), gains, swapped(gains))
+    late = exchanged(late, "row")
+    summed = pl.pallas_call(
+        lambda *refs: row_sum_kernel(blocks, *refs),
+        name="row_sum",
+        out_shape=(shape((rows_weight + 16, 3 * LANES), BF16),) * depth,
+        in_specs=[SMEM] + [VMEM] * (2 * blocks),
+        out_specs=[VMEM] * depth,
+        compiler_params=compiler(8 << 20),
+    )(place, *early, *late)
+    summed = exchanged(summed, "z")
+
+    routed = [to_homes(value, j) for j, value in enumerate(routed)]
+    whole = shape((images, rows_here * GRID, D), BF16)
+    block_out, grad_patches = pl.pallas_call(
+        home_kernel,
+        name="home",
+        out_shape=(whole, whole),
+        in_specs=[SMEM] + [VMEM] * blocks,
+        out_specs=[VMEM] * 2,
+        compiler_params=compiler(8 << 20),
+    )(place, *routed)
+
+    turned = (4 * STATE // parts, rows_weight)
     g1, g2, f_u, f_rate, f_coef, f_qkv, f_o, f_1, f_2 = pl.pallas_call(
         lambda *refs: final_kernel(parts, *refs),
         name="final_sum",
         out_shape=(
             shape((1, D), F32),
             shape((1, D), F32),
-            shape(weight + (D // parts,), F32),
-            shape(weight + (4 * STATE // parts,), F32),
-            shape(weight + (4 * STATE // parts,), F32),
-            shape(weight + (3 * D // parts,), F32),
-            shape(weight + (D // parts,), F32),
-            shape(weight + (FF // parts,), F32),
-            shape((4 * rows_weight, D // parts), F32),
+            shape((D // parts, rows_weight), F32),
+            shape(turned, F32),
+            shape(turned, F32),
+            shape((rows_weight, 3 * D // parts), F32),
+            shape((D // parts, rows_weight), F32),
+            shape((rows_weight, FF // parts), F32),
+            shape((D // parts, 4 * rows_weight), F32),
         ),
-        in_specs=[VMEM] * 2,
+        in_specs=[VMEM] * depth,
         out_specs=[VMEM] * 9,
-        compiler_params=compiler(),
-    )(late_got, early_got)
+        compiler_params=compiler(8 << 20),
+    )(*summed)
     return (
-        block_out,
-        grad_patches,
+        block_out.reshape(patches.shape),
+        grad_patches.reshape(patches.shape),
         g1.reshape(D),
         g2.reshape(D),
-        f_u,
-        f_rate,
-        f_coef,
+        f_u.T,
+        f_rate.T,
+        f_coef.T,
         f_qkv,
-        f_o,
+        f_o.T,
         f_1,
-        f_2,
+        f_2.T,
     )
 
 

time: 170 us -> 113 us (0.66)
  blocking collectives: 25.9 us -> 0 us
  waiting for transfers between devices: 32.6 us -> 16.6 us
  local copies, waits for them, and re-layouts: 18.1 us -> 4.81 us
  starting transfers between devices: 24.5 us -> 34.8 us
  Pallas kernels: 63.9 us -> 54.6 us
  other arithmetic: 2.87 us -> 0.59 us
    ppermute x8 -> x31, starting transfers between devices: 1.75 us -> 34.8 us  [the longest x15 23.8 us: exchanged(): lax.ppermute(values[k], axis, [(i, i ^ k) for i in range(size)])]
    all_to_all x5 -> x0, waiting for transfers between devices: 27.3 us -> none  [the longest x1 9.28 us: per_device(): early_got = lax.all_to_all(early_sum, ('z', 'row'), 0, 0, tiled=True)]
    all_gather x2 -> x0, blocking collectives: 25.9 us -> none  [the longest x1 16.8 us: per_device(): lax.all_gather(lax.all_gather(early, 'row'), ('z', 'core'))]
    all_to_all x5 -> x0, starting transfers between devices: 22.7 us -> none  [the longest x1 5.77 us: per_device(): lax.all_to_all(late_sum.reshape(depth * blocks, rows_weight + 16, LANES),...]
    ppermute x8 -> x31, waiting for transfers between devices: 5.27 us -> 16.6 us  [the longest x15 10.2 us: exchanged(): lax.ppermute(values[k], axis, [(i, i ^ k) for i in range(size)])]
    unnamed x52 -> x25, local copies, waits for them, and re-layouts: 10.7 us -> 4.8 us
    pallas_call x1, Pallas kernels: 21 us -> 16.4 us  [per_device(): pl.pallas_call(middle_kernel, name='attention_and_feed_forward', out_shap...]
    another operation x4 -> x0, local copies, waits for them, and re-layouts: 3.59 us -> none  [the longest x2 2.26 us: per_device(): both = jnp.stack([patches, cotangent], axis=1)]
  transfers between devices with their start and end apart: 13 -> 31, of which waited for: 8 -> 9; matrix products, arithmetic and copies ran while one was open for 4% -> 1% of each run, Pallas kernels for 10% -> 11%
where the time goes in v2:
time: 113 us; the launch traced here: 112 us
  Pallas kernels  54.6 us (48%)
  starting transfers between devices  34.8 us (31%)
  waiting for transfers between devices  16.6 us (15%)
  local copies, waits for them, and re-layouts  4.81 us (4%)
    ppermute x15, starting transfers between devices, exchanged(): lax.ppermute(values[k], axis, [(i, i ^ k) for i in range(size)])  23.8 us
    pallas_call x1, Pallas kernels, per_device(): pl.pallas_call(middle_kernel, name='attention_and_feed_forward', out_shap...  16.4 us
    pallas_call x1, Pallas kernels, per_device(): pl.pallas_call(lambda *refs: scan_kernel(starts, width, *refs, blocks=blo...  11.3 us
    pallas_call x1, Pallas kernels, per_device(): pl.pallas_call(lambda *refs: scan_back_kernel(starts, width, *refs), name...  11.3 us
    ppermute x15, waiting for transfers between devices, exchanged(): lax.ppermute(values[k], axis, [(i, i ^ k) for i in range(size)])  10.2 us
    ppermute x4, starting transfers between devices, to_chips(): return lax.ppermute(value, ('core', 'row'), pairs)  7.55 us
    pallas_call x1, Pallas kernels, per_device(): pl.pallas_call(lambda *refs: attention_back_kernel(*refs, blocks=blocks),...  6.81 us
    unnamed x25, local copies, waits for them, and re-layouts  4.8 us
  transfers between devices with their start and end apart: 31, of which 9 were waited for; matrix products, arithmetic and copies ran while one was open for 1% of the time, Pallas kernels for 11%

profile of v2, /device:TPU:0, one launch (start us, length us, event | category | flops | bytes accessed | tf_op | source)
XLA Modules:
  0.0 112.2 jit_solution(7897023895452818123)
XLA Ops:
  1.2 2.1 %depart.1 = (bf16[48,384]{1,0:T(8,128)(2,1)}, bf16[608,128]{1,0:T(8,128)(2,1)}, bf16[608,128]{1,0:T(8,128)(2,1)}, bf16[608,128]{1,0:T(8,128)(2,1)}, bf16[608,128]{1,0:T(8,128)(2,1)}) custom-call(s32[3]{0:T(128)} %pad_add_fusion.place_ref.refs_0_.core_ref, bf16[24,48]{1,0:T(8,128)(2,1)} %bitcast.22, bf16[8,48]{1,0:T(8,128)(2,1)} %bitcast.24, ...), custom_call_target="tpu_custom_call" | custom-call | tf_op jit(solution)/shard_map/depart/pallas_call | solution.py:1081
  3.4 5.0 %collective-permute-start.6 = (bf16[48,384]{1,0:T(8,128)(2,1)}, bf16[48,384]{1,0:T(8,128)(2,1)S(1)}, u32[]{:S(2)}, u32[]{:S(2)}) collective-permute-start(bf16[48,384]{1,0:T(8,128)(2,1)} %get-tuple-element.82), channel_id=1, source_target_pairs={{0,24},{8,16},{16,8},{24,0},{1,25},{9,17},{17,9},{25,1},{2,26},{10... | collective-permute-start | bytes 110600 | tf_op jit(solution)/shard_map/ppermute | solution.py:1053
  9.1 1.6 %collective-permute-start = (bf16[608,128]{1,0:T(8,128)(2,1)}, bf16[608,128]{1,0:T(8,128)(2,1)S(1)}, u32[]{:S(2)}, u32[]{:S(2)}) collective-permute-start(bf16[608,128]{1,0:T(8,128)(2,1)} %get-tuple-element.75), channel_id=1, source_target_pairs={{0,0},{1,1},{2,4},{3,5},{4,2},{5,3},{6,6},{7,7},{8,8},{9,9},{10,12... | collective-permute-start | bytes 466952 | tf_op jit(solution)/shard_map/ppermute | solution.py:1062
  10.6 1.6 %collective-permute-start.1 = (bf16[608,128]{1,0:T(8,128)(2,1)}, bf16[608,128]{1,0:T(8,128)(2,1)S(1)}, u32[]{:S(2)}, u32[]{:S(2)}) collective-permute-start(bf16[608,128]{1,0:T(8,128)(2,1)} %get-tuple-element.76), channel_id=1, source_target_pairs={{0,1},{1,0},{2,5},{3,4},{4,3},{5,2},{6,7},{7,6},{8,9},{9,8},{10,13... | collective-permute-start | bytes 466952 | tf_op jit(solution)/shard_map/ppermute | solution.py:1062
  12.3 0.8 constant_dynamic-update-slice_fusion.3
  13.0 1.5 %collective-permute-start.2 = (bf16[608,128]{1,0:T(8,128)(2,1)}, bf16[608,128]{1,0:T(8,128)(2,1)S(1)}, u32[]{:S(2)}, u32[]{:S(2)}) collective-permute-start(bf16[608,128]{1,0:T(8,128)(2,1)} %get-tuple-element.77), channel_id=1, source_target_pairs={{0,4},{1,5},{2,0},{3,1},{4,6},{5,7},{6,2},{7,3},{8,12},{9,13},{10,... | collective-permute-start | bytes 466952 | tf_op jit(solution)/shard_map/ppermute | solution.py:1062
  14.6 1.7 %collective-permute-start.9 = (bf16[192,384]{1,0:T(8,128)(2,1)S(1)}, bf16[192,384]{1,0:T(8,128)(2,1)S(1)}, u32[]{:S(2)}, u32[]{:S(2)}) collective-permute-start(bf16[192,384]{1,0:T(8,128)(2,1)S(1)} %constant_dynamic-update-slice_fusion.refs_6_.refs_0_), channel_id=1, source_target_pairs={{0,3},{1,2},{2,1},{3,0},{4,7},{5,6},{6,5},{7,4},{8,11},{9,10},{10,... | collective-permute-start | bytes 442376 | tf_op jit(solution)/shard_map/ppermute | solution.py:1053
  16.7 1.5 %collective-permute-start.7 = (bf16[192,384]{1,0:T(8,128)(2,1)S(1)}, bf16[192,384]{1,0:T(8,128)(2,1)S(1)}, u32[]{:S(2)}, u32[]{:S(2)}) collective-permute-start(bf16[192,384]{1,0:T(8,128)(2,1)S(1)} %constant_dynamic-update-slice_fusion.refs_6_.refs_0_), channel_id=1, source_target_pairs={{0,1},{1,0},{2,3},{3,2},{4,5},{5,4},{6,7},{7,6},{8,9},{9,8},{10,11... | collective-permute-start | bytes 442376 | tf_op jit(solution)/shard_map/ppermute | solution.py:1053
  18.1 2.8 %collective-permute-start.3 = (bf16[608,128]{1,0:T(8,128)(2,1)}, bf16[608,128]{1,0:T(8,128)(2,1)S(1)}, u32[]{:S(2)}, u32[]{:S(2)}) collective-permute-start(bf16[608,128]{1,0:T(8,128)(2,1)} %get-tuple-element.78), channel_id=1, source_target_pairs={{0,5},{1,4},{2,1},{3,0},{4,7},{5,6},{6,3},{7,2},{8,13},{9,12},{10,... | collective-permute-start | bytes 466952 | tf_op jit(solution)/shard_map/ppermute | solution.py:1062
  21.0 4.2 %collective-permute-done.2.refs_2_ = bf16[608,128]{1,0:T(8,128)(2,1)S(1)} collective-permute-done((bf16[608,128]{1,0:T(8,128)(2,1)}, bf16[608,128]{1,0:T(8,128)(2,1)S(1)}, u32[]{:S(2)}, u32[]{:S(2)}) %collective-permute-start.2) | collective-permute-done | bytes 155680 | tf_op jit(solution)/shard_map/ppermute | solution.py:1062
  25.7 2.1 %collective-permute-done.8.refs_8_.refs_2_ = bf16[192,384]{1,0:T(8,128)(2,1)S(1)} collective-permute-done((bf16[192,384]{1,0:T(8,128)(2,1)S(1)}, bf16[192,384]{1,0:T(8,128)(2,1)S(1)}, u32[]{:S(2)}, u32[]{:S(2)}) %collective-permute-start.8) | collective-permute-done | bytes 147488 | tf_op jit(solution)/shard_map/ppermute | solution.py:1053
  29.1 0.7 copy-done.10
  29.8 2.4 %first_norm.1 = (bf16[4,2,128,192]{3,2,1,0:T(8,128)(2,1)S(1)}, bf16[1024,192]{1,0:T(8,128)(2,1)S(1)}, f32[1024,128]{1,0:T(8,128)S(1)}) custom-call(s32[3]{0:T(128)S(1)} %copy-done.8, f32[2,192]{1,0:T(2,128)S(1)} %copy-done.10, bf16[608,128]{1,0:T(8,128)(2,1)S(1)} %collective-permute-done.refs_0_, bf16[608,128]{1,0:T(8,128)(2,1)S(1)} %collective-permute-done.1.refs_1_, ...), custom_call_target="tpu_custom_call" | custom-call | tf_op jit(solution)/shard_map/first_norm/pallas_call | solution.py:1127
  32.3 1.0 copy-done.1
  33.3 0.9 copy-done.4
  34.9 11.3 %scan_forward.1 = (bf16[3,512,128]{2,1,0:T(8,128)(2,1)S(1)}, bf16[3,1024,128]{2,1,0:T(8,128)(2,1)S(1)}, bf16[3,1024,128]{2,1,0:T(8,128)(2,1)S(1)}, bf16[1024,192...) custom-call(s32[3]{0:T(128)S(1)} %copy-done.9, ...), custom_call_target="tpu_custom_call" | custom-call | tf_op jit(solution)/shard_map/scan_forward/pallas_call | solution.py:1143
  46.3 16.4 %attention_and_feed_forward.1 = (bf16[3,512,1024]{2,1,0:T(8,128)(2,1)S(1)}, bf16[3,512,128]{2,1,0:T(8,128)(2,1)S(1)}, bf16[512,192]{1,0:T(8,128)(2,1)S(1)}, f32[...) custom-call(s32[3]{0:T(128)S(1)} %copy-done.9, ...), custom_call_target="tpu_custom_call" | custom-call | tf_op jit(solution)/shard_map/attention_and_feed_forward/pallas_call | solution.py:1166
  62.9 6.8 %attention_backward.1 = (bf16[1024,192]{1,0:T(8,128)(2,1)S(1)}, bf16[3,192,384]{2,1,0:T(8,128)(2,1)S(1)}) custom-call(s32[3]{0:T(128)S(1)} %copy-done.9, bf16[3,512,1024]{2,1,0:T(8,128)(2,1)S(1)} %get-tuple-element.88.refs_1_, bf16[3,512,128]{2,1,0:T(8,128)(2,1)S(1)} %get-tuple-element.89.refs_2_, bf16[3,512,128]{2,1,0:T(8,128)(2,1)S(1)} %get-tuple-element.83.q_ref.refs_3_, ...), custom_call_target="tpu_custom_call" | custom-call | tf_op jit(solution)/shard_map/attention_backward/pallas_call | solution.py:1201
  70.9 0.9 collective-permute-done.15.refs_5_
  71.8 11.3 %scan_backward.1 = (bf16[4,4,48,128]{3,2,1,0:T(8,128)(2,1)S(1)}, bf16[4,4,48,128]{3,2,1,0:T(8,128)(2,1)S(1)}, bf16[16,128]{1,0:T(8,128)(2,1)S(1)}, bf16[2,192,12...) custom-call(s32[3]{0:T(128)S(1)} %copy-done.9, ...), custom_call_target="tpu_custom_call" | custom-call | tf_op jit(solution)/shard_map/scan_backward/pallas_call | solution.py:1232
  83.5 1.5 %collective-permute-start.20 = (bf16[4,48,256]{2,1,0:T(8,128)(2,1)S(1)}, bf16[4,48,256]{2,1,0:T(8,128)(2,1)S(1)}, u32[]{:S(2)}, u32[]{:S(2)}) collective-permute-start(bf16[4,48,256]{2,1,0:T(8,128)(2,1)S(1)} %get-tuple-element.116), channel_id=1, source_target_pairs={{0,1},{1,0},{2,3},{3,2},{4,5},{5,4},{6,7},{7,6},{8,9},{9,8},{10,11... | collective-permute-start | bytes 294920 | tf_op jit(solution)/shard_map/ppermute | solution.py:1053
  85.4 1.7 %collective-permute-start.22 = (bf16[4,48,256]{2,1,0:T(8,128)(2,1)S(1)}, bf16[4,48,256]{2,1,0:T(8,128)(2,1)S(1)}, u32[]{:S(2)}, u32[]{:S(2)}) collective-permute-start(bf16[4,48,256]{2,1,0:T(8,128)(2,1)S(1)} %get-tuple-element.118), channel_id=1, source_target_pairs={{0,3},{1,2},{2,1},{3,0},{4,7},{5,6},{6,5},{7,4},{8,11},{9,10},{10,... | collective-permute-start | bytes 294920 | tf_op jit(solution)/shard_map/ppermute | solution.py:1053
  87.0 1.2 %collective-permute-done.24.gains_got_ref = bf16[16,128]{1,0:T(8,128)(2,1)S(1)} collective-permute-done((bf16[16,128]{1,0:T(8,128)(2,1)S(1)}, bf16[16,128]{1,0:T(8,128)(2,1)S(1)}, u32[]{:S(2)}, u32[]{:S(2)}) %collective-permute-start.24) | collective-permute-done | bytes 4128 | tf_op jit(solution)/shard_map/ppermute | solution.py:1048
  88.8 1.6 %collective-permute-start.25 = (bf16[4,64,128]{2,1,0:T(8,128)(2,1)S(1)}, bf16[4,64,128]{2,1,0:T(8,128)(2,1)S(1)}, u32[]{:S(2)}, u32[]{:S(2)}) collective-permute-start(bf16[4,64,128]{2,1,0:T(8,128)(2,1)S(1)} %get-tuple-element.123), channel_id=1, source_target_pairs={{0,1},{1,0},{2,3},{3,2},{4,5},{5,4},{6,7},{7,6},{8,9},{9,8},{10,11... | collective-permute-start | bytes 196616 | tf_op jit(solution)/shard_map/ppermute | solution.py:1053
  92.3 4.7 %collective-permute-start.27 = (bf16[4,64,128]{2,1,0:T(8,128)(2,1)S(1)}, bf16[4,64,128]{2,1,0:T(8,128)(2,1)S(1)}, u32[]{:S(2)}, u32[]{:S(2)}) collective-permute-start(bf16[4,64,128]{2,1,0:T(8,128)(2,1)S(1)} %get-tuple-element.125), channel_id=1, source_target_pairs={{0,3},{1,2},{2,1},{3,0},{4,7},{5,6},{6,5},{7,4},{8,11},{9,10},{10,... | collective-permute-start | bytes 196616 | tf_op jit(solution)/shard_map/ppermute | solution.py:1053
  97.2 3.4 %collective-permute-done.27.refs_8_ = bf16[4,64,128]{2,1,0:T(8,128)(2,1)S(1)} collective-permute-done((bf16[4,64,128]{2,1,0:T(8,128)(2,1)S(1)}, bf16[4,64,128]{2,1,0:T(8,128)(2,1)S(1)}, u32[]{:S(2)}, u32[]{:S(2)}) %collective-permute-start.27) | collective-permute-done | bytes 65568 | tf_op jit(solution)/shard_map/ppermute | solution.py:1053
  101.3 1.3 %collective-permute-start.28 = (bf16[64,384]{1,0:T(8,128)(2,1)S(1)}, bf16[64,384]{1,0:T(8,128)(2,1)S(1)}, u32[]{:S(2)}, u32[]{:S(2)}) collective-permute-start(bf16[64,384]{1,0:T(8,128)(2,1)S(1)} %get-tuple-element.127), channel_id=1, source_target_pairs={{0,8},{8,0},{16,24},{24,16},{1,9},{9,1},{17,25},{25,17},{2,10},{10... | collective-permute-start | bytes 147464 | tf_op jit(solution)/shard_map/ppermute | solution.py:1053
  102.6 2.9 %collective-permute-start.29 = (bf16[64,384]{1,0:T(8,128)(2,1)S(1)}, bf16[64,384]{1,0:T(8,128)(2,1)S(1)}, u32[]{:S(2)}, u32[]{:S(2)}) collective-permute-start(bf16[64,384]{1,0:T(8,128)(2,1)S(1)} %get-tuple-element.128), channel_id=1, source_target_pairs={{0,16},{8,24},{16,0},{24,8},{1,17},{9,25},{17,1},{25,9},{2,18},{10... | collective-permute-start | bytes 147464 | tf_op jit(solution)/shard_map/ppermute | solution.py:1053
  105.7 1.4 %home.1 = (bf16[2,256,192]{2,1,0:T(8,128)(2,1)}, bf16[2,256,192]{2,1,0:T(8,128)(2,1)}) custom-call(s32[3]{0:T(128)S(1)} %copy-done.9, bf16[2,192,128]{2,1,0:T(8,128)(2,1)S(1)} %collective-permute-done.16.refs_0_, bf16[2,192,128]{2,1,0:T(8,128)(2,1)S(1)} %collective-permute-done.17.refs_1_, bf16[2,192,128]{2,1,0:T(8,128)(2,1)S(1)} %collective-permute-done.18.refs_2_, ...), custom_call_target="tpu_custom_call" | custom-call | tf_op jit(solution)/shard_map/home/pallas_call | solution.py:1296
  107.2 1.5 %collective-permute-done.29.refs_2_ = bf16[64,384]{1,0:T(8,128)(2,1)S(1)} collective-permute-done((bf16[64,384]{1,0:T(8,128)(2,1)S(1)}, bf16[64,384]{1,0:T(8,128)(2,1)S(1)}, u32[]{:S(2)}, u32[]{:S(2)}) %collective-permute-start.29) | collective-permute-done | bytes 49184 | tf_op jit(solution)/shard_map/ppermute | solution.py:1053
  108.6 2.8 %collective-permute-done.30.refs_3_ = bf16[64,384]{1,0:T(8,128)(2,1)S(1)} collective-permute-done((bf16[64,384]{1,0:T(8,128)(2,1)S(1)}, bf16[64,384]{1,0:T(8,128)(2,1)S(1)}, u32[]{:S(2)}, u32[]{:S(2)}) %collective-permute-start.30) | collective-permute-done | bytes 49184 | tf_op jit(solution)/shard_map/ppermute | solution.py:1053
  111.4 0.8 final_sum.1
  (68 shorter events, 9.9 us)
Async XLA Ops:
  0.6 31.6 %copy-start = (bf16[3,512,384]{2,1,0:T(8,128)(2,1)S(1)}, bf16[3,512,384]{2,1,0:T(8,128)(2,1)}, u32[]{:S(2)}) copy-start(bf16[3,512,384]{2,1,0:T(8,128)(2,1)} %constant.26.clone.refs_5_.refs_17_) | copy-start | bytes 3538948
  3.4 11.2 %collective-permute-start.6 = (bf16[48,384]{1,0:T(8,128)(2,1)}, bf16[48,384]{1,0:T(8,128)(2,1)S(1)}, u32[]{:S(2)}, u32[]{:S(2)}) collective-permute-start(bf16[48,384]{1,0:T(8,128)(2,1)} %get-tuple-element.82), channel_id=1, source_target_pairs={{0,24},{8,16},{16,8},{24,0},{1,25},{9,17},{17,9},{25,1},{2,26},{10... | collective-permute-start | bytes 110600 | tf_op jit(solution)/shard_map/ppermute | solution.py:1053
  8.4 6.1 %collective-permute-start.5 = (bf16[48,384]{1,0:T(8,128)(2,1)}, bf16[48,384]{1,0:T(8,128)(2,1)S(1)}, u32[]{:S(2)}, u32[]{:S(2)}) collective-permute-start(bf16[48,384]{1,0:T(8,128)(2,1)} %get-tuple-element.82), channel_id=1, source_target_pairs={{0,16},{8,24},{16,0},{24,8},{1,17},{9,25},{17,1},{25,9},{2,18},{10... | collective-permute-start | bytes 110600 | tf_op jit(solution)/shard_map/ppermute | solution.py:1053
  8.4 4.6 %collective-permute-start.4 = (bf16[48,384]{1,0:T(8,128)(2,1)}, bf16[48,384]{1,0:T(8,128)(2,1)S(1)}, u32[]{:S(2)}, u32[]{:S(2)}) collective-permute-start(bf16[48,384]{1,0:T(8,128)(2,1)} %get-tuple-element.82), channel_id=1, source_target_pairs={{0,8},{8,0},{16,24},{24,16},{1,9},{9,1},{17,25},{25,17},{2,10},{10... | collective-permute-start | bytes 110600 | tf_op jit(solution)/shard_map/ppermute | solution.py:1053
  9.1 7.6 %collective-permute-start = (bf16[608,128]{1,0:T(8,128)(2,1)}, bf16[608,128]{1,0:T(8,128)(2,1)S(1)}, u32[]{:S(2)}, u32[]{:S(2)}) collective-permute-start(bf16[608,128]{1,0:T(8,128)(2,1)} %get-tuple-element.75), channel_id=1, source_target_pairs={{0,0},{1,1},{2,4},{3,5},{4,2},{5,3},{6,6},{7,7},{8,8},{9,9},{10,12... | collective-permute-start | bytes 466952 | tf_op jit(solution)/shard_map/ppermute | solution.py:1062
  10.6 7.5 %collective-permute-start.1 = (bf16[608,128]{1,0:T(8,128)(2,1)}, bf16[608,128]{1,0:T(8,128)(2,1)S(1)}, u32[]{:S(2)}, u32[]{:S(2)}) collective-permute-start(bf16[608,128]{1,0:T(8,128)(2,1)} %get-tuple-element.76), channel_id=1, source_target_pairs={{0,1},{1,0},{2,5},{3,4},{4,3},{5,2},{6,7},{7,6},{8,9},{9,8},{10,13... | collective-permute-start | bytes 466952 | tf_op jit(solution)/shard_map/ppermute | solution.py:1062
  13.0 12.1 %collective-permute-start.2 = (bf16[608,128]{1,0:T(8,128)(2,1)}, bf16[608,128]{1,0:T(8,128)(2,1)S(1)}, u32[]{:S(2)}, u32[]{:S(2)}) collective-permute-start(bf16[608,128]{1,0:T(8,128)(2,1)} %get-tuple-element.77), channel_id=1, source_target_pairs={{0,4},{1,5},{2,0},{3,1},{4,6},{5,7},{6,2},{7,3},{8,12},{9,13},{10,... | collective-permute-start | bytes 466952 | tf_op jit(solution)/shard_map/ppermute | solution.py:1062
  14.6 10.6 %collective-permute-start.9 = (bf16[192,384]{1,0:T(8,128)(2,1)S(1)}, bf16[192,384]{1,0:T(8,128)(2,1)S(1)}, u32[]{:S(2)}, u32[]{:S(2)}) collective-permute-start(bf16[192,384]{1,0:T(8,128)(2,1)S(1)} %constant_dynamic-update-slice_fusion.refs_6_.refs_0_), channel_id=1, source_target_pairs={{0,3},{1,2},{2,1},{3,0},{4,7},{5,6},{6,5},{7,4},{8,11},{9,10},{10,... | collective-permute-start | bytes 442376 | tf_op jit(solution)/shard_map/ppermute | solution.py:1053
  16.3 11.5 %collective-permute-start.8 = (bf16[192,384]{1,0:T(8,128)(2,1)S(1)}, bf16[192,384]{1,0:T(8,128)(2,1)S(1)}, u32[]{:S(2)}, u32[]{:S(2)}) collective-permute-start(bf16[192,384]{1,0:T(8,128)(2,1)S(1)} %constant_dynamic-update-slice_fusion.refs_6_.refs_0_), channel_id=1, source_target_pairs={{0,2},{1,3},{2,0},{3,1},{4,6},{5,7},{6,4},{7,5},{8,10},{9,11},{10,... | collective-permute-start | bytes 442376 | tf_op jit(solution)/shard_map/ppermute | solution.py:1053
  16.7 11.1 %collective-permute-start.7 = (bf16[192,384]{1,0:T(8,128)(2,1)S(1)}, bf16[192,384]{1,0:T(8,128)(2,1)S(1)}, u32[]{:S(2)}, u32[]{:S(2)}) collective-permute-start(bf16[192,384]{1,0:T(8,128)(2,1)S(1)} %constant_dynamic-update-slice_fusion.refs_6_.refs_0_), channel_id=1, source_target_pairs={{0,1},{1,0},{2,3},{3,2},{4,5},{5,4},{6,7},{7,6},{8,9},{9,8},{10,11... | collective-permute-start | bytes 442376 | tf_op jit(solution)/shard_map/ppermute | solution.py:1053
  18.1 10.3 %collective-permute-start.3 = (bf16[608,128]{1,0:T(8,128)(2,1)}, bf16[608,128]{1,0:T(8,128)(2,1)S(1)}, u32[]{:S(2)}, u32[]{:S(2)}) collective-permute-start(bf16[608,128]{1,0:T(8,128)(2,1)} %get-tuple-element.78), channel_id=1, source_target_pairs={{0,5},{1,4},{2,1},{3,0},{4,7},{5,6},{6,3},{7,2},{8,13},{9,12},{10,... | collective-permute-start | bytes 466952 | tf_op jit(solution)/shard_map/ppermute | solution.py:1062
  25.2 7.1 %collective-permute-start.10 = (bf16[192,384]{1,0:T(8,128)(2,1)S(1)}, bf16[192,384]{1,0:T(8,128)(2,1)S(1)}, u32[]{:S(2)}, u32[]{:S(2)}) collective-permute-start(bf16[192,384]{1,0:T(8,128)(2,1)S(1)} %constant_dynamic-update-slice_fusion.refs_6_.refs_0_), channel_id=1, source_target_pairs={{0,4},{4,0},{1,5},{5,1},{2,6},{6,2},{3,7},{7,3},{8,12},{12,8},{9,1... | collective-permute-start | bytes 442376 | tf_op jit(solution)/shard_map/ppermute | solution.py:1048
  25.2 7.1 %collective-permute-start.13 = (bf16[192,384]{1,0:T(8,128)(2,1)S(1)}, bf16[192,384]{1,0:T(8,128)(2,1)S(1)}, u32[]{:S(2)}, u32[]{:S(2)}) collective-permute-start(bf16[192,384]{1,0:T(8,128)(2,1)S(1)} %collective-permute-done.9.refs_9_.refs_3_), channel_id=1, source_target_pairs={{0,4},{4,0},{1,5},{5,1},{2,6},{6,2},{3,7},{7,3},{8,12},{12,8},{9,1... | collective-permute-start | bytes 442376 | tf_op jit(solution)/shard_map/ppermute | solution.py:1048
  27.8 4.4 %collective-permute-start.12 = (bf16[192,384]{1,0:T(8,128)(2,1)S(1)}, bf16[192,384]{1,0:T(8,128)(2,1)S(1)}, u32[]{:S(2)}, u32[]{:S(2)}) collective-permute-start(bf16[192,384]{1,0:T(8,128)(2,1)S(1)} %collective-permute-done.8.refs_8_.refs_2_), channel_id=1, source_target_pairs={{0,4},{4,0},{1,5},{5,1},{2,6},{6,2},{3,7},{7,3},{8,12},{12,8},{9,1... | collective-permute-start | bytes 442376 | tf_op jit(solution)/shard_map/ppermute | solution.py:1048
  27.8 4.5 %collective-permute-start.11 = (bf16[192,384]{1,0:T(8,128)(2,1)S(1)}, bf16[192,384]{1,0:T(8,128)(2,1)S(1)}, u32[]{:S(2)}, u32[]{:S(2)}) collective-permute-start(bf16[192,384]{1,0:T(8,128)(2,1)S(1)} %collective-permute-done.7.refs_7_.refs_1_), channel_id=1, source_target_pairs={{0,4},{4,0},{1,5},{5,1},{2,6},{6,2},{3,7},{7,3},{8,12},{12,8},{9,1... | collective-permute-start | bytes 442376 | tf_op jit(solution)/shard_map/ppermute | solution.py:1048
  62.8 7.5 %collective-permute-start.14 = (bf16[4,4,48,256]{3,2,1,0:T(8,128)(2,1)S(1)}, bf16[4,4,48,256]{3,2,1,0:T(8,128)(2,1)S(1)}, u32[]{:S(2)}, u32[]{:S(2)}) collective-permute-start(bf16[4,4,48,256]{3,2,1,0:T(8,128)(2,1)S(1)} %get-tuple-element.87), channel_id=1, source_target_pairs={{0,4},{4,0},{1,5},{5,1},{2,6},{6,2},{3,7},{7,3},{8,12},{12,8},{9,1... | collective-permute-start | bytes 1179656 | tf_op jit(solution)/shard_map/ppermute | solution.py:1048
  69.8 2.0 %collective-permute-start.15 = (bf16[1024,192]{1,0:T(8,128)(2,1)S(1)}, bf16[1024,192]{1,0:T(8,128)(2,1)S(1)}, u32[]{:S(2)}, u32[]{:S(2)}) collective-permute-start(bf16[1024,192]{1,0:T(8,128)(2,1)S(1)} %get-tuple-element.93.refs_4_), channel_id=1, source_target_pairs={{0,4},{4,0},{1,5},{5,1},{2,6},{6,2},{3,7},{7,3},{8,12},{12,8},{9,1... | collective-permute-start | bytes 1179656 | tf_op jit(solution)/shard_map/ppermute | solution.py:1048
  83.1 5.1 %collective-permute-start.23 = (bf16[4,4,48,128]{3,2,1,0:T(8,128)(2,1)S(1)}, bf16[4,4,48,128]{3,2,1,0:T(8,128)(2,1)S(1)}, u32[]{:S(2)}, u32[]{:S(2)}) collective-permute-start(bf16[4,4,48,128]{3,2,1,0:T(8,128)(2,1)S(1)} %get-tuple-element.120), channel_id=1, source_target_pairs={{0,4},{4,0},{1,5},{5,1},{2,6},{6,2},{3,7},{7,3},{8,12},{12,8},{9,1... | collective-permute-start | bytes 589832 | tf_op jit(solution)/shard_map/ppermute | solution.py:1048
  83.5 7.1 %collective-permute-start.20 = (bf16[4,48,256]{2,1,0:T(8,128)(2,1)S(1)}, bf16[4,48,256]{2,1,0:T(8,128)(2,1)S(1)}, u32[]{:S(2)}, u32[]{:S(2)}) collective-permute-start(bf16[4,48,256]{2,1,0:T(8,128)(2,1)S(1)} %get-tuple-element.116), channel_id=1, source_target_pairs={{0,1},{1,0},{2,3},{3,2},{4,5},{5,4},{6,7},{7,6},{8,9},{9,8},{10,11... | collective-permute-start | bytes 294920 | tf_op jit(solution)/shard_map/ppermute | solution.py:1053
  85.0 6.7 %collective-permute-start.21 = (bf16[4,48,256]{2,1,0:T(8,128)(2,1)S(1)}, bf16[4,48,256]{2,1,0:T(8,128)(2,1)S(1)}, u32[]{:S(2)}, u32[]{:S(2)}) collective-permute-start(bf16[4,48,256]{2,1,0:T(8,128)(2,1)S(1)} %get-tuple-element.117), channel_id=1, source_target_pairs={{0,2},{1,3},{2,0},{3,1},{4,6},{5,7},{6,4},{7,5},{8,10},{9,11},{10,... | collective-permute-start | bytes 294920 | tf_op jit(solution)/shard_map/ppermute | solution.py:1053
  85.4 6.9 %collective-permute-start.22 = (bf16[4,48,256]{2,1,0:T(8,128)(2,1)S(1)}, bf16[4,48,256]{2,1,0:T(8,128)(2,1)S(1)}, u32[]{:S(2)}, u32[]{:S(2)}) collective-permute-start(bf16[4,48,256]{2,1,0:T(8,128)(2,1)S(1)} %get-tuple-element.118), channel_id=1, source_target_pairs={{0,3},{1,2},{2,1},{3,0},{4,7},{5,6},{6,5},{7,4},{8,11},{9,10},{10,... | collective-permute-start | bytes 294920 | tf_op jit(solution)/shard_map/ppermute | solution.py:1053
  87.0 1.2 %collective-permute-start.24 = (bf16[16,128]{1,0:T(8,128)(2,1)S(1)}, bf16[16,128]{1,0:T(8,128)(2,1)S(1)}, u32[]{:S(2)}, u32[]{:S(2)}) collective-permute-start(bf16[16,128]{1,0:T(8,128)(2,1)S(1)} %get-tuple-element.121.gains_ref), channel_id=1, source_target_pairs={{0,4},{4,0},{1,5},{5,1},{2,6},{6,2},{3,7},{7,3},{8,12},{12,8},{9,1... | collective-permute-start | bytes 12296 | tf_op jit(solution)/shard_map/ppermute | solution.py:1048
  88.8 8.2 %collective-permute-start.25 = (bf16[4,64,128]{2,1,0:T(8,128)(2,1)S(1)}, bf16[4,64,128]{2,1,0:T(8,128)(2,1)S(1)}, u32[]{:S(2)}, u32[]{:S(2)}) collective-permute-start(bf16[4,64,128]{2,1,0:T(8,128)(2,1)S(1)} %get-tuple-element.123), channel_id=1, source_target_pairs={{0,1},{1,0},{2,3},{3,2},{4,5},{5,4},{6,7},{7,6},{8,9},{9,8},{10,11... | collective-permute-start | bytes 196616 | tf_op jit(solution)/shard_map/ppermute | solution.py:1053
  90.4 6.7 %collective-permute-start.26 = (bf16[4,64,128]{2,1,0:T(8,128)(2,1)S(1)}, bf16[4,64,128]{2,1,0:T(8,128)(2,1)S(1)}, u32[]{:S(2)}, u32[]{:S(2)}) collective-permute-start(bf16[4,64,128]{2,1,0:T(8,128)(2,1)S(1)} %get-tuple-element.124), channel_id=1, source_target_pairs={{0,2},{1,3},{2,0},{3,1},{4,6},{5,7},{6,4},{7,5},{8,10},{9,11},{10,... | collective-permute-start | bytes 196616 | tf_op jit(solution)/shard_map/ppermute | solution.py:1053
  90.7 11.9 %collective-permute-start.16 = (bf16[2,192,128]{2,1,0:T(8,128)(2,1)S(1)}, bf16[2,192,128]{2,1,0:T(8,128)(2,1)S(1)}, u32[]{:S(2)}, u32[]{:S(2)}) collective-permute-start(bf16[2,192,128]{2,1,0:T(8,128)(2,1)S(1)} %get-tuple-element.109), channel_id=1, source_target_pairs={{0,0},{1,1},{2,4},{3,5},{4,2},{5,3},{6,6},{7,7},{8,8},{9,9},{10,12... | collective-permute-start | bytes 294920 | tf_op jit(solution)/shard_map/ppermute | solution.py:1071
  91.8 13.8 %collective-permute-start.17 = (bf16[2,192,128]{2,1,0:T(8,128)(2,1)S(1)}, bf16[2,192,128]{2,1,0:T(8,128)(2,1)S(1)}, u32[]{:S(2)}, u32[]{:S(2)}) collective-permute-start(bf16[2,192,128]{2,1,0:T(8,128)(2,1)S(1)} %get-tuple-element.110), channel_id=1, source_target_pairs={{0,1},{1,0},{2,5},{3,4},{4,3},{5,2},{6,7},{7,6},{8,9},{9,8},{10,13... | collective-permute-start | bytes 294920 | tf_op jit(solution)/shard_map/ppermute | solution.py:1071
  92.3 8.3 %collective-permute-start.27 = (bf16[4,64,128]{2,1,0:T(8,128)(2,1)S(1)}, bf16[4,64,128]{2,1,0:T(8,128)(2,1)S(1)}, u32[]{:S(2)}, u32[]{:S(2)}) collective-permute-start(bf16[4,64,128]{2,1,0:T(8,128)(2,1)S(1)} %get-tuple-element.125), channel_id=1, source_target_pairs={{0,3},{1,2},{2,1},{3,0},{4,7},{5,6},{6,5},{7,4},{8,11},{9,10},{10,... | collective-permute-start | bytes 196616 | tf_op jit(solution)/shard_map/ppermute | solution.py:1053
  97.0 8.7 %collective-permute-start.18 = (bf16[2,192,128]{2,1,0:T(8,128)(2,1)S(1)}, bf16[2,192,128]{2,1,0:T(8,128)(2,1)S(1)}, u32[]{:S(2)}, u32[]{:S(2)}) collective-permute-start(bf16[2,192,128]{2,1,0:T(8,128)(2,1)S(1)} %get-tuple-element.111), channel_id=1, source_target_pairs={{0,2},{1,3},{2,6},{3,7},{4,0},{5,1},{6,4},{7,5},{8,10},{9,11},{10,... | collective-permute-start | bytes 294920 | tf_op jit(solution)/shard_map/ppermute | solution.py:1071
  97.0 8.7 %collective-permute-start.19 = (bf16[2,192,128]{2,1,0:T(8,128)(2,1)S(1)}, bf16[2,192,128]{2,1,0:T(8,128)(2,1)S(1)}, u32[]{:S(2)}, u32[]{:S(2)}) collective-permute-start(bf16[2,192,128]{2,1,0:T(8,128)(2,1)S(1)} %get-tuple-element.112), channel_id=1, source_target_pairs={{0,3},{1,2},{2,7},{3,6},{4,1},{5,0},{6,5},{7,4},{8,11},{9,10},{10,... | collective-permute-start | bytes 294920 | tf_op jit(solution)/shard_map/ppermute | solution.py:1071
  101.3 5.9 %collective-permute-start.28 = (bf16[64,384]{1,0:T(8,128)(2,1)S(1)}, bf16[64,384]{1,0:T(8,128)(2,1)S(1)}, u32[]{:S(2)}, u32[]{:S(2)}) collective-permute-start(bf16[64,384]{1,0:T(8,128)(2,1)S(1)} %get-tuple-element.127), channel_id=1, source_target_pairs={{0,8},{8,0},{16,24},{24,16},{1,9},{9,1},{17,25},{25,17},{2,10},{10... | collective-permute-start | bytes 147464 | tf_op jit(solution)/shard_map/ppermute | solution.py:1053
  102.6 6.0 %collective-permute-start.29 = (bf16[64,384]{1,0:T(8,128)(2,1)S(1)}, bf16[64,384]{1,0:T(8,128)(2,1)S(1)}, u32[]{:S(2)}, u32[]{:S(2)}) collective-permute-start(bf16[64,384]{1,0:T(8,128)(2,1)S(1)} %get-tuple-element.128), channel_id=1, source_target_pairs={{0,16},{8,24},{16,0},{24,8},{1,17},{9,25},{17,1},{25,9},{2,18},{10... | collective-permute-start | bytes 147464 | tf_op jit(solution)/shard_map/ppermute | solution.py:1053
  105.5 5.9 %collective-permute-start.30 = (bf16[64,384]{1,0:T(8,128)(2,1)S(1)}, bf16[64,384]{1,0:T(8,128)(2,1)S(1)}, u32[]{:S(2)}, u32[]{:S(2)}) collective-permute-start(bf16[64,384]{1,0:T(8,128)(2,1)S(1)} %get-tuple-element.129), channel_id=1, source_target_pairs={{0,24},{8,16},{16,8},{24,0},{1,25},{9,17},{17,9},{25,1},{2,26},{10... | collective-permute-start | bytes 147464 | tf_op jit(solution)/shard_map/ppermute | solution.py:1053
  (10 other events, 55.7 us)

commit v3 on v2

--- a/solution.py
+++ b/solution.py
@@ -29,38 +29,12 @@
     return a_u, a_r, a_q, (0, a_u, a_u + a_r, a_u + 2 * a_r)
 
 
-def late_selections(parts):
-    a_u, a_r, a_q, (o_u, o_r, o_c, o_q) = late_layout(parts)
-    sel_u = np.zeros((parts, LANES, D), np.float32)
-    sel_rc = np.zeros((parts, LANES, LANES), np.float32)
-    full = np.zeros((parts, LANES, 3, TILE), np.float32)
-    for m in range(parts):
-        for col in range(a_u):
-            sel_u[m, o_u + col, m * a_u + col] = 1
-        for col in range(a_r):
-            sel_rc[m, o_r + col, m * a_r + col] = 1
-            sel_rc[m, o_c + col, 4 * STATE + m * a_r + col] = 1
-        for col in range(a_q):
-            whole = m * a_q + col
-            third, rest = divmod(whole, D)
-            head, lane = divmod(rest, HEAD_DIM)
-            full[m, o_q + col, third, head * LANES + lane] = 1
-    spans = []
-    for third in range(3):
-        used = [m for m in range(parts) if full[m, :, third].any()]
-        spans.append((min(used), max(used) + 1))
-    width = max(stop - start for start, stop in spans)
-    starts = [min(start, parts - width) for start, _ in spans]
-    sel_q = np.stack(
-        [full[s : s + width, :, third].reshape(width * LANES, TILE) for third, s in enumerate(starts)]
-    )
-    return (
-        sel_u.reshape(parts * LANES, D).astype(BF16),
-        sel_rc.reshape(parts * LANES, LANES).astype(BF16),
-        sel_q.astype(BF16),
-        starts,
-        width,
-    )
+def late_spans(parts):
+    a_q = 3 * D // parts
+    first = [third * D // a_q for third in range(3)]
+    last = [((third + 1) * D - 1) // a_q for third in range(3)]
+    width = max(stop - start + 1 for start, stop in zip(first, last))
+    return [min(start, parts - width) for start in first], width
 
 
 def early_selections(parts):
@@ -84,6 +58,32 @@
     )
 
 
+def lane_and_part(shape):
+    place = lax.broadcasted_iota(jnp.int32, shape, 0)
+    return place % LANES, place // LANES, lax.broadcasted_iota(jnp.int32, shape, 1)
+
+
+def put_late_selections(starts, parts, sel_u_ref, sel_rc_ref, sel_q_ref):
+    a_u, a_r, a_q, (o_u, o_r, o_c, o_q) = late_layout(parts)
+
+    def put(hit):
+        return jnp.where(hit, 1.0, 0.0).astype(BF16)
+
+    lane, part, col = lane_and_part(sel_u_ref.shape)
+    sel_u_ref[...] = put((lane < a_u) & (part * a_u + lane == col))
+    lane, part, col = lane_and_part(sel_rc_ref.shape)
+    rate = (lane >= o_r) & (lane < o_c) & (part * a_r + lane - o_r == col)
+    coef = (lane >= o_c) & (lane < o_q) & (part * a_r + lane - o_c + 4 * STATE == col)
+    sel_rc_ref[...] = put(rate | coef)
+    lane, part, col = lane_and_part(sel_q_ref.shape[1:])
+    whole = jnp.where(
+        col % LANES < HEAD_DIM, col // LANES * HEAD_DIM + col % LANES, -4 * D
+    )
+    for third in range(3):
+        here = (part + starts[third]) * a_q + lane - o_q - third * D
+        sel_q_ref[third] = put((lane >= o_q) & (lane < o_q + a_q) & (here == whole))
+
+
 def dot(a, b):
     return lax.dot_general(a, b, (((1,), (0,)), ((), ())), preferred_element_type=F32)
 
@@ -118,6 +118,13 @@
     rows = ref.shape[2]
     for r in range(ref.shape[0]):
         ref[r, z, :, lanes] = value[r * rows : (r + 1) * rows]
+
+
+def put_late(ref, z, value):
+    rows = ref.shape[1]
+    depth = ref.shape[0] * rows // D
+    for r in range(D // rows):
+        ref[r * depth + z] = value[r * rows : (r + 1) * rows]
 
 
 def put_lanes(ref, rows, values):
@@ -141,16 +148,15 @@
     return total
 
 
-def gather_parts(place_ref, mine_refs, got_refs, block, out_ref):
-    core, row, depth = place_ref[0], place_ref[1], place_ref[2]
+def gather_parts(mine_refs, got_refs, block, out_ref):
+    core, row, depth = lax.axis_index("core"), lax.axis_index("row"), lax.axis_index("z")
     lanes = slice(block * LANES, (block + 1) * LANES)
     count = out_ref.shape[0] // 2
     rows = out_ref.shape[2]
     for refs, which in ((mine_refs, core), (got_refs, 1 - core)):
         for k, ref in enumerate(refs):
             for j in range(count):
-                value = ref[j * rows : (j + 1) * rows, lanes]
-                out_ref[2 * (depth ^ j) + which, row ^ k] = value
+                out_ref[2 * (depth ^ j) + which, row ^ k] = ref[j, :, lanes]
     wide = []
     for m in range(2 * count):
         wide.append(jnp.concatenate([out_ref[m, r] for r in range(out_ref.shape[1])], axis=0))
@@ -165,7 +171,6 @@
 
 
 VMEM = pl.BlockSpec(memory_space=pltpu.VMEM)
-SMEM = pl.BlockSpec(memory_space=pltpu.SMEM)
 
 
 def pack(values):
@@ -204,59 +209,56 @@
     out_ref[...] = packed
 
 
-def route_kernel(place_ref, patch_ref, cot_ref, valid_ref, *out_refs):
-    row = place_ref[1]
+def route_kernel(patch_ref, cot_ref, valid_ref, *out_refs):
+    row = lax.axis_index("row")
     images, slots, _ = patch_ref.shape
     half = slots // 2
     packed = half * 3 // 2
     for j, out_ref in enumerate(out_refs):
         target = row ^ j
         core, image = target // images, target % images
-        out_ref[:packed] = pack(patch_ref[image, :half])
-        out_ref[packed : 2 * packed] = pack(patch_ref[image, half:])
-        start = pl.multiple_of(core * half, half)
-        out_ref[2 * packed : 3 * packed] = pack(cot_ref[image, pl.ds(start, half), :])
+        place = pl.ds(pl.multiple_of(core * half, half), half)
+        out_ref[:packed] = pack(patch_ref[image, place, :])
+        out_ref[packed : 2 * packed] = pack(cot_ref[image, place, :])
         valid = valid_ref[image].astype(F32).astype(BF16)
-        out_ref[3 * packed :] = jnp.concatenate(
+        out_ref[2 * packed :] = jnp.concatenate(
             [valid, jnp.zeros((GRID, LANES - GRID), BF16)], axis=1
         )
 
 
-def depart_kernel(place_ref, *refs):
+def depart_kernel(*refs):
     turned, (qkv_ref, fc1_ref, patch_ref, cot_ref, valid_ref, out_ref) = refs[:5], refs[5:11]
     pack_weights_kernel(turned, qkv_ref, fc1_ref, out_ref)
-    route_kernel(place_ref, patch_ref, cot_ref, valid_ref, *refs[11:])
-
-
-def norm_kernel(place_ref, gains_ref, *refs):
-    core, row = place_ref[0], place_ref[1]
-    got_refs, (own_ref, first_ref, mask_ref) = refs[:-3], refs[-3:]
+    route_kernel(patch_ref, cot_ref, valid_ref, *refs[11:])
+
+
+def norm_kernel(starts, parts, gains_ref, *refs):
+    got_refs, refs = refs[:-6], refs[-6:]
+    own_ref, first_ref, mask_ref, *selections = refs
+    core, row = lax.axis_index("core"), lax.axis_index("row")
     images = len(got_refs) // 2
     gain = gains_ref[0:1, :]
     slots = own_ref.shape[2]
     packed = slots * 3 // 2
-    valid = got_refs[0][3 * packed :].astype(F32).T
+    for j, got in enumerate(got_refs):
+        block = (core * images + row % images) ^ j
+        patch = unpack(got[:packed])
+        own_ref[block, 0] = patch
+        own_ref[block, 1] = unpack(got[packed : 2 * packed])
+        unit, _ = normalise(patch.astype(F32))
+        first_ref[pl.ds(pl.multiple_of(block * slots, slots), slots), :] = (unit * gain).astype(
+            BF16
+        )
+    valid = got_refs[0][2 * packed :].astype(F32).T
     for i in range(GRID):
         mask_ref[i * GRID : (i + 1) * GRID, :] = jnp.broadcast_to(
             valid[:GRID, i : i + 1], (GRID, LANES)
         )
-    for j, got in enumerate(got_refs):
-        block = (core * images + row % images) ^ j
-        own_ref[block, 1] = unpack(got[2 * packed : 3 * packed])
-        for half in range(2):
-            patch = unpack(got[half * packed : (half + 1) * packed])
-
-            @pl.when(core == half)
-            def _(patch=patch, block=block):
-                own_ref[block, 0] = patch
-
-            unit, _ = normalise(patch.astype(F32))
-            start = pl.multiple_of((block * 2 + half) * slots, slots)
-            first_ref[pl.ds(start, slots), :] = (unit * gain).astype(BF16)
-
-
-def home_kernel(place_ref, *refs):
-    row = place_ref[1]
+    put_late_selections(starts, parts, *selections)
+
+
+def home_kernel(*refs):
+    row = lax.axis_index("row")
     got_refs, out_refs = refs[:-2], refs[-2:]
     images, slots, _ = out_refs[0].shape
     half = slots // 2
@@ -271,8 +273,8 @@
 def scan_kernel(
     starts,
     width,
-    core_ref,
-    first_ref,
+    first_own_ref,
+    first_other_ref,
     mask_ref,
     sel_u_ref,
     sel_rc_ref,
@@ -284,8 +286,8 @@
     scan_body(
         starts,
         width,
-        core_ref,
-        first_ref,
+        first_own_ref,
+        first_other_ref,
         mask_ref,
         sel_u_ref,
         sel_rc_ref,
@@ -299,8 +301,8 @@
 def scan_body(
     starts,
     width,
-    core_ref,
-    first_ref,
+    first_own_ref,
+    first_other_ref,
     mask_ref,
     sel_u_ref,
     sel_rc_ref,
@@ -322,12 +324,13 @@
     cols,
     rows,
     scanned_own,
+    first_ref,
 ):
-    core = core_ref[0]
+    core = lax.axis_index("core")
     blocks = len(mine_refs)
     rows_slots = OWN // blocks
 
-    late = gather_parts(core_ref, mine_refs, got_refs, 0, late_ref)
+    late = gather_parts(mine_refs, got_refs, 0, late_ref)
     wu = dot(late, sel_u_ref[...]).astype(BF16)
     wu_ref[...] = wu
     rates = dot(late, sel_rc_ref[...])
@@ -364,6 +367,11 @@
 
     xs[1, :, D - LANES :] = jnp.zeros((SLOTS, 2 * LANES - D), F32)
 
+    for block in range(blocks):
+        here = slice(block * rows_slots, (block + 1) * rows_slots)
+        for ref, which in ((first_own_ref, core), (first_other_ref, 1 - core)):
+            start = pl.multiple_of((block * 2 + which) * rows_slots, rows_slots)
+            first_ref[pl.ds(start, rows_slots), :] = ref[here, :]
     mixed = dot(first_ref[...], wu) * widen(mask_ref[...])
     mixed = mixed.astype(BF16)
     mixed_ref[...] = mixed
@@ -420,7 +428,6 @@
 
 
 def middle_kernel(
-    core_ref,
     own_ref,
     mask_ref,
     gains_ref,
@@ -434,7 +441,6 @@
 ):
     blocks = own_ref.shape[0]
     middle_body(
-        core_ref,
         own_ref,
         mask_ref,
         gains_ref,
@@ -451,7 +457,6 @@
 
 
 def middle_body(
-    core_ref,
     own_ref,
     mask_ref,
     gains_ref,
@@ -485,14 +490,14 @@
     grad_pre,
     wire,
 ):
-    core = core_ref[0]
+    core = lax.axis_index("core")
     blocks, _, rows_slots, _ = own_ref.shape
     parts = early_ref.shape[0]
     per_block = D // blocks
     gain = gains_ref[1:2, :]
 
-    left = gather_parts(core_ref, mine_refs, got_refs, 1, early_ref)
-    right = gather_parts(core_ref, mine_refs, got_refs, 2, early_ref)
+    left = gather_parts(mine_refs, got_refs, 1, early_ref)
+    right = gather_parts(mine_refs, got_refs, 2, early_ref)
     span = parts // 2 * LANES
     for half in range(2):
         w1[:, half * FF // 2 : (half + 1) * FF // 2] = dot(
@@ -622,7 +627,6 @@
 
 
 def attention_back_kernel(
-    core_ref,
     soft_ref,
     lifted_ref,
     q_ref,
@@ -641,7 +645,7 @@
     *,
     blocks,
 ):
-    core = core_ref[0]
+    core = lax.axis_index("core")
     rows_slots = OWN // blocks
     for h in range(HEADS):
         tile = slice(h * LANES, (h + 1) * LANES)
@@ -677,10 +681,8 @@
 def scan_back_kernel(
     starts,
     width,
-    core_ref,
     own_ref,
     mask_ref,
-    gains_ref,
     part_ref,
     got_ref,
     mixed_ref,
@@ -688,69 +690,6 @@
     table_ref,
     rates_ref,
     wu_ref,
-    grad_middle_ref,
-    grad_w_ref,
-    gain_two_ref,
-    out_own_ref,
-    sel_u_ref,
-    sel_rc_ref,
-    sel_q_ref,
-    keep_ref,
-    send_ref,
-    gains_out_ref,
-    *refs,
-):
-    routed_refs, scratch = refs[:-13], refs[-13:]
-    scan_back_body(
-        starts,
-        width,
-        core_ref,
-        own_ref,
-        mask_ref,
-        gains_ref,
-        part_ref,
-        got_ref,
-        mixed_ref,
-        first_ref,
-        table_ref,
-        rates_ref,
-        wu_ref,
-        grad_middle_ref,
-        grad_w_ref,
-        gain_two_ref,
-        sel_u_ref,
-        sel_rc_ref,
-        sel_q_ref,
-        keep_ref,
-        send_ref,
-        gains_out_ref,
-        *scratch,
-    )
-    images = len(routed_refs) // 2
-    mine = core_ref[0] * images + core_ref[1] % images
-    slots = own_ref.shape[2]
-    grad = scratch[0]
-    for j, routed in enumerate(routed_refs):
-        place = pl.ds(pl.multiple_of((mine ^ j) * slots, slots), slots)
-        routed[0] = pack(out_own_ref[place, :])
-        routed[1] = pack(grad[place, :])
-
-
-def scan_back_body(
-    starts,
-    width,
-    core_ref,
-    own_ref,
-    mask_ref,
-    gains_ref,
-    part_ref,
-    got_ref,
-    mixed_ref,
-    first_ref,
-    table_ref,
-    rates_ref,
-    wu_ref,
-    grad_middle_ref,
     grad_w_ref,
     gain_two_ref,
     sel_u_ref,
@@ -758,8 +697,7 @@
     sel_q_ref,
     keep_ref,
     send_ref,
-    gains_out_ref,
-    grad_ref,
+    back_ref,
     gs,
     gt,
     xs,
@@ -770,15 +708,13 @@
     lag_sums,
     lag_rows,
     mixed_back,
-    first_own,
     wire,
 ):
-    core = core_ref[0]
+    core = lax.axis_index("core")
     blocks, _, rows_slots, _ = own_ref.shape
     half_rows = rows_slots // GRID
     own_rows = GRID // 2
     parts = sel_rc_ref.shape[0] // LANES
-    gain = gains_ref[0:1, :]
     pad = jnp.zeros((SLOTS, 2 * LANES - D), F32)
 
     xs[1, :, D - LANES :] = pad
@@ -790,9 +726,6 @@
     def place_of(block):
         return pl.ds(pl.multiple_of((block * 2 + core) * rows_slots, rows_slots), rows_slots)
 
-    for block in range(blocks):
-        here = slice(block * rows_slots, (block + 1) * rows_slots)
-        first_own[here, :] = first_ref[place_of(block), :]
     for src, dst in ((gs, gt), (xs, xt)):
         for lane in range(2):
             for block in range(blocks):
@@ -900,16 +833,14 @@
         return 0
 
     lax.fori_loop(0, own_rows, join_step, 0)
-    grad_u = dot_tn(first_own[...], mixed_back[...]).astype(BF16)
+    grad_u = dot_tn(first_ref[...], mixed_back[...]).astype(BF16)
     grad_first = dot_nt(mixed_back[...], wu_ref[...])
+    back_ref[...] = grad_first
     gain_one = jnp.zeros((1, D), F32)
     for block in range(blocks):
         here = slice(block * rows_slots, (block + 1) * rows_slots)
-        unit, inverse = normalise(own_ref[block, 0].astype(F32))
-        grad = grad_first[here]
-        gain_one = gain_one + jnp.sum(grad * unit, 0, keepdims=True)
-        grad = grad_middle_ref[here, :] + norm_back(grad, gain, unit, inverse)
-        grad_ref[here, :] = grad.astype(BF16)
+        unit, _ = normalise(own_ref[block, 0].astype(F32))
+        gain_one = gain_one + jnp.sum(grad_first[here] * unit, 0, keepdims=True)
 
     wire[...] = dot_nt(grad_u, sel_u_ref[...]) + dot_nt(grad_rc, sel_rc_ref[...])
     for third in range(3):
@@ -920,11 +851,11 @@
 
         @pl.when(core == m % 2)
         def _(value=value, m=m):
-            put_blocks(keep_ref, m // 2, slice(None), value)
+            put_late(keep_ref, m // 2, value)
 
         @pl.when(core != m % 2)
         def _(value=value, m=m):
-            put_blocks(send_ref, m // 2, slice(None), value)
+            put_late(send_ref, m // 2, value)
 
     lines = []
     for value in (gain_one, gain_two_ref[...]):
@@ -934,8 +865,26 @@
             lines.append(
                 jnp.concatenate([piece[:, LANES:], jnp.zeros((1, 2 * LANES - D), F32)], axis=1)
             )
-    lines.append(jnp.zeros((8, LANES), F32))
-    gains_out_ref[...] = jnp.concatenate(lines, axis=0).astype(BF16)
+    lines = jnp.concatenate(lines, axis=0).astype(BF16)
+    for ref in (keep_ref, send_ref):
+        ref[ref.shape[0] - 1, :8] = lines
+        ref[ref.shape[0] - 1, 8:] = jnp.zeros((ref.shape[1] - 8, LANES), BF16)
+
+
+def last_norm_kernel(
+    own_ref, gains_ref, back_ref, grad_middle_ref, out_own_ref, *routed_refs
+):
+    blocks, _, slots, _ = own_ref.shape
+    images = blocks // 2
+    mine = lax.axis_index("core") * images + lax.axis_index("row") % images
+    gain = gains_ref[0:1, :]
+    for j, routed in enumerate(routed_refs):
+        block = mine ^ j
+        place = pl.ds(pl.multiple_of(block * slots, slots), slots)
+        unit, inverse = normalise(own_ref[block, 0].astype(F32))
+        grad = grad_middle_ref[place, :] + norm_back(back_ref[place, :], gain, unit, inverse)
+        routed[0] = pack(out_own_ref[place, :])
+        routed[1] = pack(grad.astype(BF16))
 
 
 def split(value):
@@ -943,38 +892,40 @@
     return jnp.concatenate([high, value - high], axis=0)
 
 
-def early_sum_kernel(place_ref, keep_ref, got_ref, *out_refs):
+def early_sum_kernel(keep_ref, got_ref, *out_refs):
     for k, out_ref in enumerate(out_refs):
-        block = place_ref[1] ^ k
+        block = lax.axis_index("row") ^ k
         for z in range(keep_ref.shape[1]):
             total = keep_ref[block, z].astype(F32) + got_ref[block, z].astype(F32)
             out_ref[z] = total.astype(BF16)
 
 
-def late_sum_kernel(place_ref, keep_ref, got_ref, gains_ref, gains_got_ref, *out_refs):
-    depth = keep_ref.shape[1]
-    gains = gains_ref[...].astype(F32) + gains_got_ref[...].astype(F32)
+def late_sum_kernel(keep_ref, got_ref, *out_refs):
+    depth, rows, _ = out_refs[0].shape
+    rows -= 16
+    last = keep_ref.shape[0] - 1
+    gains = keep_ref[last, :8].astype(F32) + got_ref[last, :8].astype(F32)
     lines = []
     for g in range(2):
         for lane in range(2):
             at = 4 * g + lane
             lines.append(gains[at : at + 1] + gains[at + 2 : at + 3])
-    gains = jnp.concatenate([split(jnp.concatenate(lines, axis=0)), jnp.zeros((8, LANES), F32)], axis=0)
-    gains = gains.astype(BF16)
+    gains = split(jnp.concatenate(lines, axis=0))
+    gains = jnp.concatenate([gains, jnp.zeros((8, LANES), F32)], axis=0).astype(BF16)
     for k, out_ref in enumerate(out_refs):
-        block = place_ref[1] ^ k
-        rows = keep_ref.shape[2]
+        block = lax.axis_index("row") ^ k
         for z in range(depth):
-            total = keep_ref[block, z].astype(F32) + got_ref[block, z].astype(F32)
+            at = block * depth + z
+            total = keep_ref[at].astype(F32) + got_ref[at].astype(F32)
             out_ref[z, :rows] = total.astype(BF16)
             out_ref[z, rows:] = gains
 
 
-def row_sum_kernel(blocks, place_ref, *refs):
+def row_sum_kernel(blocks, *refs):
     early_refs, late_refs, out_refs = refs[:blocks], refs[blocks : 2 * blocks], refs[2 * blocks :]
     rows = early_refs[0].shape[1]
     for j, out_ref in enumerate(out_refs):
-        z = place_ref[2] ^ j
+        z = lax.axis_index("z") ^ j
         early = early_refs[0][z].astype(F32)
         late = late_refs[0][z].astype(F32)
         for k in range(1, blocks):
@@ -1038,10 +989,7 @@
     parts = 2 * depth
     rows_slots = rows_here // 2 * GRID
     packed_rows = rows_slots * 3 // 2
-    core = lax.axis_index("core")
-    row = lax.axis_index("row")
     swap = [(0, 1), (1, 0)]
-    place = jnp.stack([core, row, lax.axis_index("z")]).astype(jnp.int32)
     shape = jax.ShapeDtypeStruct
 
     def swapped(value):
@@ -1070,11 +1018,11 @@
                 pairs.append((source * blocks + chip, home * blocks + target))
         return lax.ppermute(value, ("core", "row"), pairs)
 
-    sel_u, sel_rc, sel_q, starts, width = late_selections(parts)
+    starts, width = late_spans(parts)
     sel_1, sel_o, sel_2 = early_selections(parts)
 
     rows_weight = w_u.shape[0]
-    payload = shape((3 * packed_rows + GRID, LANES), BF16)
+    payload = shape((2 * packed_rows + GRID, LANES), BF16)
     shard = shape((rows_weight, 3 * LANES), BF16)
     sources = [value.reshape(images, rows_here * GRID, D) for value in (patches, cotangent)]
     if rows_weight % 16 == 0:
@@ -1082,12 +1030,11 @@
             depart_kernel,
             name="depart",
             out_shape=(shard,) + (payload,) * blocks,
-            in_specs=[SMEM] + [VMEM] * 10,
+            in_specs=[VMEM] * 10,
             out_specs=[VMEM] * (1 + blocks),
             compiler_params=compiler(LARGE),
         )(
-            place,
-            w_u.T,
+                w_u.T,
             decay_rate.T,
             out_coef.T,
             w_o.T,
@@ -1115,27 +1062,31 @@
             route_kernel,
             name="route",
             out_shape=(payload,) * blocks,
-            in_specs=[SMEM] + [VMEM] * 3,
+            in_specs=[VMEM] * 3,
             out_specs=[VMEM] * blocks,
             compiler_params=compiler(LARGE),
-        )(place, *sources, valid_mask)
-
-    weights = jnp.concatenate(exchanged([weights] * depth, "z"), axis=0)
+        )(*sources, valid_mask)
+
+    weights = jnp.stack(exchanged([weights] * depth, "z"))
     weights = exchanged([weights] * blocks, "row")
     weights = weights + [swapped(value) for value in weights]
     routed = [to_chips(value, j) for j, value in enumerate(routed)]
-    own, first, mask = pl.pallas_call(
-        norm_kernel,
+    own, first_own, mask, sel_u, sel_rc, sel_q = pl.pallas_call(
+        lambda *refs: norm_kernel(starts, parts, *refs),
         name="first_norm",
         out_shape=(
             shape((blocks, 2, rows_slots, D), BF16),
-            shape((SLOTS, D), BF16),
+            shape((OWN, D), BF16),
             shape((SLOTS, LANES), F32),
+            shape((parts * LANES, D), BF16),
+            shape((parts * LANES, LANES), BF16),
+            shape((3, width * LANES, TILE), BF16),
         ),
-        in_specs=[SMEM] + [VMEM] * (1 + blocks),
-        out_specs=[VMEM] * 3,
+        in_specs=[VMEM] * (1 + blocks),
+        out_specs=[VMEM] * 6,
         compiler_params=compiler(8 << 20),
-    )(place, norm_gains, *routed)
+    )(norm_gains, *routed)
+    first_other = swapped(first_own)
 
     head_own = shape((HEADS, OWN, LANES), BF16)
     head_all = shape((HEADS, SLOTS, LANES), BF16)
@@ -1154,13 +1105,13 @@
             shape((D, D), BF16),
             shape((3, D, TILE), BF16),
         ),
-        in_specs=[SMEM] + [VMEM] * (5 + 2 * blocks),
+        in_specs=[VMEM] * (6 + 2 * blocks),
         out_specs=[VMEM] * 9,
         scratch_shapes=[part_scratch]
         + [pltpu.VMEM((2, SLOTS, LANES), F32)] * 4
-        + [pltpu.VMEM((OWN, D), BF16)],
+        + [pltpu.VMEM((OWN, D), BF16), pltpu.VMEM((SLOTS, D), BF16)],
         compiler_params=compiler(),
-    )(place, first, mask, sel_u, sel_rc, sel_q, *weights)
+    )(first_own, first_other, mask, sel_u, sel_rc, sel_q, *weights)
 
     wire_early = shape((blocks, depth, rows_weight, 2 * LANES), BF16)
     soft, lifted, out_own, grad_middle, gain_two, early_keep, early_send = pl.pallas_call(
@@ -1175,7 +1126,7 @@
             wire_early,
             wire_early,
         ),
-        in_specs=[SMEM] + [VMEM] * (9 + 2 * blocks),
+        in_specs=[VMEM] * (9 + 2 * blocks),
         out_specs=[VMEM] * 7,
         scratch_shapes=[
             part_scratch,
@@ -1194,7 +1145,7 @@
             pltpu.VMEM((D, parts * LANES), F32),
         ],
         compiler_params=compiler(),
-    )(place, own, mask, norm_gains, sel_1, sel_o, sel_2, q, k, v, *weights)
+    )(own, mask, norm_gains, sel_1, sel_o, sel_2, q, k, v, *weights)
 
     early_recv = swapped(early_send)
 
@@ -1202,7 +1153,7 @@
         lambda *refs: attention_back_kernel(*refs, blocks=blocks),
         name="attention_backward",
         out_shape=(shape((SLOTS, D), BF16), shape((3, D, TILE), BF16)),
-        in_specs=[SMEM] + [VMEM] * 7,
+        in_specs=[VMEM] * 7,
         out_specs=[VMEM] * 2,
         scratch_shapes=[
             pltpu.VMEM((OWN, SLOTS), F32),
@@ -1213,7 +1164,7 @@
             pltpu.VMEM((SLOTS, D), F32),
         ],
         compiler_params=compiler(),
-    )(place, soft, lifted, q, k, v, scanned, wqkv)
+    )(soft, lifted, q, k, v, scanned, wqkv)
 
     part_got = swapped(part)
     early_keep, early_recv, part = lax.optimization_barrier((early_keep, early_recv, part))
@@ -1221,22 +1172,20 @@
         early_sum_kernel,
         name="early_sum",
         out_shape=(shape((depth, rows_weight, 2 * LANES), BF16),) * blocks,
-        in_specs=[SMEM] + [VMEM] * 2,
+        in_specs=[VMEM] * 2,
         out_specs=[VMEM] * blocks,
         compiler_params=compiler(8 << 20),
-    )(place, early_keep, early_recv)
+    )(early_keep, early_recv)
     early, part_got = lax.optimization_barrier((early, part_got))
     early = exchanged(early, "row")
-    wire_late = shape((blocks, depth, rows_weight, LANES), BF16)
-    payload = shape((2, packed_rows, LANES), BF16)
-    late_keep, late_send, gains, *routed = pl.pallas_call(
+    wire_late = shape((blocks * depth + 1, rows_weight, LANES), BF16)
+    late_keep, late_send, back = pl.pallas_call(
         lambda *refs: scan_back_kernel(starts, width, *refs),
         name="scan_backward",
-        out_shape=(wire_late, wire_late, shape((16, LANES), BF16)) + (payload,) * blocks,
-        in_specs=[SMEM] + [VMEM] * 17,
-        out_specs=[VMEM] * (3 + blocks),
+        out_shape=(wire_late, wire_late, shape((OWN, D), F32)),
+        in_specs=[VMEM] * 14,
+        out_specs=[VMEM] * 3,
         scratch_shapes=[
-            pltpu.VMEM((OWN, D), BF16),
             pltpu.VMEM((2, SLOTS, LANES), F32),
             pltpu.VMEM((2, OWN, LANES), F32),
             pltpu.VMEM((2, SLOTS, LANES), F32),
@@ -1247,48 +1196,52 @@
             pltpu.VMEM((2, 2, LAGS, 8, LANES), F32),
             pltpu.VMEM((2, LAGS, 2 * LANES), F32),
             pltpu.VMEM((OWN, D), BF16),
-            pltpu.VMEM((OWN, D), BF16),
             pltpu.VMEM((D, parts * LANES), F32),
         ],
         compiler_params=compiler(),
     )(
-        place,
         own,
         mask,
-        norm_gains,
         part,
         part_got,
         mixed,
-        first,
+        first_own,
         table,
         rates,
         wu,
-        grad_middle,
         grad_w,
         gain_two,
-        out_own,
         sel_u,
         sel_rc,
         sel_q,
     )
-
+    late_keep, late_send, early = lax.optimization_barrier((late_keep, late_send, early))
     late = pl.pallas_call(
         late_sum_kernel,
         name="late_sum",
         out_shape=(shape((depth, rows_weight + 16, LANES), BF16),) * blocks,
-        in_specs=[SMEM] + [VMEM] * 4,
+        in_specs=[VMEM] * 2,
         out_specs=[VMEM] * blocks,
         compiler_params=compiler(8 << 20),
-    )(place, late_keep, swapped(late_send), gains, swapped(gains))
+    )(late_keep, swapped(late_send))
+    payload = shape((2, packed_rows, LANES), BF16)
+    routed = pl.pallas_call(
+        last_norm_kernel,
+        name="last_norm",
+        out_shape=(payload,) * blocks,
+        in_specs=[VMEM] * 5,
+        out_specs=[VMEM] * blocks,
+        compiler_params=compiler(8 << 20),
+    )(own, norm_gains, back, grad_middle, out_own)
     late = exchanged(late, "row")
     summed = pl.pallas_call(
         lambda *refs: row_sum_kernel(blocks, *refs),
         name="row_sum",
         out_shape=(shape((rows_weight + 16, 3 * LANES), BF16),) * depth,
-        in_specs=[SMEM] + [VMEM] * (2 * blocks),
+        in_specs=[VMEM] * (2 * blocks),
         out_specs=[VMEM] * depth,
         compiler_params=compiler(8 << 20),
-    )(place, *early, *late)
+    )(*early, *late)
     summed = exchanged(summed, "z")
 
     routed = [to_homes(value, j) for j, value in enumerate(routed)]
@@ -1297,10 +1250,10 @@
         home_kernel,
         name="home",
         out_shape=(whole, whole),
-        in_specs=[SMEM] + [VMEM] * blocks,
+        in_specs=[VMEM] * blocks,
         out_specs=[VMEM] * 2,
         compiler_params=compiler(8 << 20),
-    )(place, *routed)
+    )(*routed)
 
     turned = (4 * STATE // parts, rows_weight)
     g1, g2, f_u, f_rate, f_coef, f_qkv, f_o, f_1, f_2 = pl.pallas_call(

time: 113 us -> 103 us (0.912)
  Pallas kernels: 54.6 us -> 49.5 us
  local copies, waits for them, and re-layouts: 4.81 us -> 0.7 us
  starting transfers between devices: 34.8 us -> 32.8 us
  waiting for transfers between devices: 16.6 us -> 17.9 us
    unnamed x25 -> x10, local copies, waits for them, and re-layouts: 4.8 us -> 0.7 us
    ppermute x4, starting transfers between devices: 7.55 us -> 4.99 us  [to_chips(): return lax.ppermute(value, ('core', 'row'), pairs)]
    ppermute x4, waiting for transfers between devices: 4.32 us -> 1.91 us  [to_chips(): return lax.ppermute(value, ('core', 'row'), pairs)]
    ppermute x8, waiting for transfers between devices: 2.07 us -> 4.12 us  [swapped(): return lax.ppermute(value, 'core', swap)]
    ppermute x15, waiting for transfers between devices: 10.2 us -> 11.9 us  [exchanged(): lax.ppermute(values[k], axis, [(i, i ^ k) for i in range(size)])]
    pallas_call x1 -> x2, Pallas kernels: 2.41 us -> 1.75 us  [the longest x1 1.09 us: per_device(): pl.pallas_call(lambda *refs: norm_kernel(starts, parts, *refs), name='fir...]
  transfers between devices with their start and end apart: 31 -> 31, of which waited for: 9 -> 11; matrix products, arithmetic and copies ran while one was open for 1% -> 1% of each run, Pallas kernels for 11% -> 19%
where the time goes in v3:
time: 103 us
  Pallas kernels  49.5 us (48%)
  starting transfers between devices  32.8 us (32%)
  waiting for transfers between devices  17.9 us (17%)
    ppermute x15, starting transfers between devices, exchanged(): lax.ppermute(values[k], axis, [(i, i ^ k) for i in range(size)])  24.3 us
    pallas_call x1, Pallas kernels, per_device(): pl.pallas_call(middle_kernel, name='attention_and_feed_forward', out_shap...  15.9 us
    ppermute x15, waiting for transfers between devices, exchanged(): lax.ppermute(values[k], axis, [(i, i ^ k) for i in range(size)])  11.9 us
    pallas_call x1, Pallas kernels, per_device(): pl.pallas_call(lambda *refs: scan_kernel(starts, width, *refs, blocks=blo...  10.8 us
    pallas_call x1, Pallas kernels, per_device(): pl.pallas_call(lambda *refs: scan_back_kernel(starts, width, *refs), name...  10.6 us
    pallas_call x1, Pallas kernels, per_device(): pl.pallas_call(lambda *refs: attention_back_kernel(*refs, blocks=blocks),...  6.47 us
    ppermute x4, starting transfers between devices, to_chips(): return lax.ppermute(value, ('core', 'row'), pairs)  4.99 us
    ppermute x8, waiting for transfers between devices, swapped(): return lax.ppermute(value, 'core', swap)  4.12 us
  transfers between devices with their start and end apart: 31, of which 11 were waited for; matrix products, arithmetic and copies ran while one was open for 1% of the time, Pallas kernels for 19%

profile of v3, /device:TPU:0, one launch (start us, length us, event | category | flops | bytes accessed | tf_op | source)
XLA Modules:
  0.0 102.5 jit_solution(469769929521156008)
XLA Ops:
  0.6 2.0 %depart.1 = (bf16[48,384]{1,0:T(8,128)(2,1)}, bf16[416,128]{1,0:T(8,128)(2,1)}, bf16[416,128]{1,0:T(8,128)(2,1)}, bf16[416,128]{1,0:T(8,128)(2,1)}, bf16[416,128]{1,0:T(8,128)(2,1)}) custom-call(bf16[24,48]{1,0:T(8,128)(2,1)} %bitcast.27, bf16[8,48]{1,0:T(8,128)(2,1)} %bitcast.29, bf16[8,48]{1,0:T(8,128)(2,1)} %bitcast.30, bf16[24,48]{1,0:T(8,128)(2,1)} %bitcast.28, ...), custom_call_target="tpu_custom_call" | custom-call | tf_op jit(solution)/shard_map/depart/pallas_call | solution.py:1029
  2.7 5.0 %collective-permute-start.7 = (bf16[48,384]{1,0:T(8,128)(2,1)}, bf16[48,384]{1,0:T(8,128)(2,1)S(1)}, u32[]{:S(2)}, u32[]{:S(2)}) collective-permute-start(bf16[48,384]{1,0:T(8,128)(2,1)} %get-tuple-element.94), channel_id=1, source_target_pairs={{0,24},{8,16},{16,8},{24,0},{1,25},{9,17},{17,9},{25,1},{2,26},{10... | collective-permute-start | bytes 110600 | tf_op jit(solution)/shard_map/ppermute | solution.py:1001
  8.3 1.5 %collective-permute-start = (bf16[416,128]{1,0:T(8,128)(2,1)}, bf16[416,128]{1,0:T(8,128)(2,1)S(1)}, u32[]{:S(2)}, u32[]{:S(2)}) collective-permute-start(bf16[416,128]{1,0:T(8,128)(2,1)} %get-tuple-element.84), channel_id=1, source_target_pairs={{0,0},{1,1},{2,4},{3,5},{4,2},{5,3},{6,6},{7,7},{8,8},{9,9},{10,12... | collective-permute-start | bytes 319496 | tf_op jit(solution)/shard_map/ppermute | solution.py:1010
  9.9 1.7 %collective-permute-start.1 = (bf16[416,128]{1,0:T(8,128)(2,1)}, bf16[416,128]{1,0:T(8,128)(2,1)S(1)}, u32[]{:S(2)}, u32[]{:S(2)}) collective-permute-start(bf16[416,128]{1,0:T(8,128)(2,1)} %get-tuple-element.85), channel_id=1, source_target_pairs={{0,1},{1,0},{2,5},{3,4},{4,3},{5,2},{6,7},{7,6},{8,9},{9,8},{10,13... | collective-permute-start | bytes 319496 | tf_op jit(solution)/shard_map/ppermute | solution.py:1010
  11.6 1.5 %collective-permute-start.2 = (bf16[416,128]{1,0:T(8,128)(2,1)}, bf16[416,128]{1,0:T(8,128)(2,1)S(1)}, u32[]{:S(2)}, u32[]{:S(2)}) collective-permute-start(bf16[416,128]{1,0:T(8,128)(2,1)} %get-tuple-element.86), channel_id=1, source_target_pairs={{0,4},{1,5},{2,0},{3,1},{4,6},{5,7},{6,2},{7,3},{8,12},{9,13},{10,... | collective-permute-start | bytes 319496 | tf_op jit(solution)/shard_map/ppermute | solution.py:1010
  13.3 0.8 pad_maximum_fusion.refs_6_.refs_0_
  14.1 2.7 %collective-permute-start.10 = (bf16[4,48,384]{2,1,0:T(8,128)(2,1)S(1)}, bf16[4,48,384]{2,1,0:T(8,128)(2,1)S(1)}, u32[]{:S(2)}, u32[]{:S(2)}) collective-permute-start(bf16[4,48,384]{2,1,0:T(8,128)(2,1)S(1)} %pad_maximum_fusion.refs_6_.refs_0_), channel_id=1, source_target_pairs={{0,3},{1,2},{2,1},{3,0},{4,7},{5,6},{6,5},{7,4},{8,11},{9,10},{10,... | collective-permute-start | bytes 442376 | tf_op jit(solution)/shard_map/ppermute | solution.py:1001
  17.1 1.1 %collective-permute-start.8 = (bf16[4,48,384]{2,1,0:T(8,128)(2,1)S(1)}, bf16[4,48,384]{2,1,0:T(8,128)(2,1)S(1)}, u32[]{:S(2)}, u32[]{:S(2)}) collective-permute-start(bf16[4,48,384]{2,1,0:T(8,128)(2,1)S(1)} %pad_maximum_fusion.refs_6_.refs_0_), channel_id=1, source_target_pairs={{0,1},{1,0},{2,3},{3,2},{4,5},{5,4},{6,7},{7,6},{8,9},{9,8},{10,11... | collective-permute-start | bytes 442376 | tf_op jit(solution)/shard_map/ppermute | solution.py:1001
  18.2 1.5 %collective-permute-done.2.refs_3_ = bf16[416,128]{1,0:T(8,128)(2,1)S(1)} collective-permute-done((bf16[416,128]{1,0:T(8,128)(2,1)}, bf16[416,128]{1,0:T(8,128)(2,1)S(1)}, u32[]{:S(2)}, u32[]{:S(2)}) %collective-permute-start.2) | collective-permute-done | bytes 106528 | tf_op jit(solution)/shard_map/ppermute | solution.py:1010
  20.1 0.7 copy-done.3
  20.7 1.1 %first_norm.1 = (bf16[4,2,128,192]{3,2,1,0:T(8,128)(2,1)S(1)}, bf16[512,192]{1,0:T(8,128)(2,1)S(1)}, f32[1024,128]{1,0:T(8,128)S(1)}, bf16[1024,192]{1,0:T(8,128...) custom-call(f32[2,192]{1,0:T(2,128)S(1)} %copy-done.3, ...), custom_call_target="tpu_custom_call" | custom-call | tf_op jit(solution)/shard_map/first_norm/pallas_call | solution.py:1074
  22.4 0.8 collective-permute-done.10.refs_9_.refs_3_
  23.2 3.0 %collective-permute-done.9.refs_8_.refs_2_ = bf16[4,48,384]{2,1,0:T(8,128)(2,1)S(1)} collective-permute-done((bf16[4,48,384]{2,1,0:T(8,128)(2,1)S(1)}, bf16[4,48,384]{2,1,0:T(8,128)(2,1)S(1)}, u32[]{:S(2)}, u32[]{:S(2)}) %collective-permute-start.9) | collective-permute-done | bytes 147488 | tf_op jit(solution)/shard_map/ppermute | solution.py:1001
  26.7 0.8 collective-permute-done.13.refs_12_.refs_6_
  27.7 10.8 %scan_forward.1 = (bf16[3,512,128]{2,1,0:T(8,128)(2,1)S(1)}, bf16[3,1024,128]{2,1,0:T(8,128)(2,1)S(1)}, bf16[3,1024,128]{2,1,0:T(8,128)(2,1)S(1)}, bf16[1024,192...) custom-call(bf16[512,192]{1,0:T(8,128)(2,1)S(1)} %get-tuple-element., ...), custom_call_target="tpu_custom_call" | custom-call | tf_op jit(solution)/shard_map/scan_forward/pallas_call | solution.py:1094
  38.6 15.9 %attention_and_feed_forward.1 = (bf16[3,512,1024]{2,1,0:T(8,128)(2,1)S(1)}, bf16[3,512,128]{2,1,0:T(8,128)(2,1)S(1)}, bf16[512,192]{1,0:T(8,128)(2,1)S(1)}, f32[...) custom-call(bf16[4,2,128,192]{3,2,1,0:T(8,128)(2,1)S(1)} %get-tuple-, ...), custom_call_target="tpu_custom_call" | custom-call | tf_op jit(solution)/shard_map/attention_and_feed_forward/pallas_call | solution.py:1117
  54.9 6.5 %attention_backward.1 = (bf16[1024,192]{1,0:T(8,128)(2,1)S(1)}, bf16[3,192,384]{2,1,0:T(8,128)(2,1)S(1)}) custom-call(bf16[3,512,1024]{2,1,0:T(8,128)(2,1)S(1)} %get-tuple-element.100.refs_0_, bf16[3,512,128]{2,1,0:T(8,128)(2,1)S(1)} %get-tuple-element.101.refs_1_, bf16[3,512,128]{2,1,0:T(8,128)(2,1)S(1)} %get-tuple-element.95.q_ref.refs_2_, ...), custom_call_target="tpu_custom_call" | custom-call | tf_op jit(solution)/shard_map/attention_backward/pallas_call | solution.py:1152
  61.7 1.6 %collective-permute-done.16.refs_3_ = bf16[1024,192]{1,0:T(8,128)(2,1)S(1)} collective-permute-done((bf16[1024,192]{1,0:T(8,128)(2,1)S(1)}, bf16[1024,192]{1,0:T(8,128)(2,1)S(1)}, u32[]{:S(2)}, u32[]{:S(2)}) %collective-permute-start.16) | collective-permute-done | bytes 393248 | tf_op jit(solution)/shard_map/ppermute | solution.py:996
  63.3 1.5 %collective-permute-start.21 = (bf16[4,48,256]{2,1,0:T(8,128)(2,1)S(1)}, bf16[4,48,256]{2,1,0:T(8,128)(2,1)S(1)}, u32[]{:S(2)}, u32[]{:S(2)}) collective-permute-start(bf16[4,48,256]{2,1,0:T(8,128)(2,1)S(1)} %get-tuple-element.131), channel_id=1, source_target_pairs={{0,1},{1,0},{2,3},{3,2},{4,5},{5,4},{6,7},{7,6},{8,9},{9,8},{10,11... | collective-permute-start | bytes 294920 | tf_op jit(solution)/shard_map/ppermute | solution.py:1001
  65.0 1.8 %collective-permute-start.23 = (bf16[4,48,256]{2,1,0:T(8,128)(2,1)S(1)}, bf16[4,48,256]{2,1,0:T(8,128)(2,1)S(1)}, u32[]{:S(2)}, u32[]{:S(2)}) collective-permute-start(bf16[4,48,256]{2,1,0:T(8,128)(2,1)S(1)} %get-tuple-element.133), channel_id=1, source_target_pairs={{0,3},{1,2},{2,1},{3,0},{4,7},{5,6},{6,5},{7,4},{8,11},{9,10},{10,... | collective-permute-start | bytes 294920 | tf_op jit(solution)/shard_map/ppermute | solution.py:1001
  66.8 10.6 %scan_backward.1 = (bf16[17,48,128]{2,1,0:T(8,128)(2,1)S(1)}, bf16[17,48,128]{2,1,0:T(8,128)(2,1)S(1)}, f32[512,192]{1,0:T(8,128)S(1)}) custom-call(bf16[4,2,128,192]{3,2,1,0:T(8,128)(2,1)S(1)} %get-tuple-element.88.own_ref.refs_0_, f32[1024,128]{1,0:T(8,128)S(1)} %get-tuple-element.89.refs_2_.mask_ref.refs_1_, ...), custom_call_target="tpu_custom_call" | custom-call | tf_op jit(solution)/shard_map/scan_backward/pallas_call | solution.py:1182
  77.6 1.4 %collective-permute-done.24.got_ref = bf16[17,48,128]{2,1,0:T(8,128)(2,1)S(1)} collective-permute-done((bf16[17,48,128]{2,1,0:T(8,128)(2,1)S(1)}, bf16[17,48,128]{2,1,0:T(8,128)(2,1)S(1)}, u32[]{:S(2)}, u32[]{:S(2)}) %collective-permute-start.24) | collective-permute-done | bytes 208928 | tf_op jit(solution)/shard_map/ppermute | solution.py:996
  79.1 1.5 %collective-permute-start.25 = (bf16[4,64,128]{2,1,0:T(8,128)(2,1)S(1)}, bf16[4,64,128]{2,1,0:T(8,128)(2,1)S(1)}, u32[]{:S(2)}, u32[]{:S(2)}) collective-permute-start(bf16[4,64,128]{2,1,0:T(8,128)(2,1)S(1)} %get-tuple-element.141), channel_id=1, source_target_pairs={{0,1},{1,0},{2,3},{3,2},{4,5},{5,4},{6,7},{7,6},{8,9},{9,8},{10,11... | collective-permute-start | bytes 196616 | tf_op jit(solution)/shard_map/ppermute | solution.py:1001
  82.2 0.8 collective-permute-start.18
  83.0 4.9 %collective-permute-start.27 = (bf16[4,64,128]{2,1,0:T(8,128)(2,1)S(1)}, bf16[4,64,128]{2,1,0:T(8,128)(2,1)S(1)}, u32[]{:S(2)}, u32[]{:S(2)}) collective-permute-start(bf16[4,64,128]{2,1,0:T(8,128)(2,1)S(1)} %get-tuple-element.143), channel_id=1, source_target_pairs={{0,3},{1,2},{2,1},{3,0},{4,7},{5,6},{6,5},{7,4},{8,11},{9,10},{10,... | collective-permute-start | bytes 196616 | tf_op jit(solution)/shard_map/ppermute | solution.py:1001
  88.1 3.4 %collective-permute-done.27.refs_7_ = bf16[4,64,128]{2,1,0:T(8,128)(2,1)S(1)} collective-permute-done((bf16[4,64,128]{2,1,0:T(8,128)(2,1)S(1)}, bf16[4,64,128]{2,1,0:T(8,128)(2,1)S(1)}, u32[]{:S(2)}, u32[]{:S(2)}) %collective-permute-start.27) | collective-permute-done | bytes 65568 | tf_op jit(solution)/shard_map/ppermute | solution.py:1001
  91.6 1.3 %collective-permute-start.28 = (bf16[64,384]{1,0:T(8,128)(2,1)S(1)}, bf16[64,384]{1,0:T(8,128)(2,1)S(1)}, u32[]{:S(2)}, u32[]{:S(2)}) collective-permute-start(bf16[64,384]{1,0:T(8,128)(2,1)S(1)} %get-tuple-element.145), channel_id=1, source_target_pairs={{0,8},{8,0},{16,24},{24,16},{1,9},{9,1},{17,25},{25,17},{2,10},{10... | collective-permute-start | bytes 147464 | tf_op jit(solution)/shard_map/ppermute | solution.py:1001
  92.9 2.9 %collective-permute-start.29 = (bf16[64,384]{1,0:T(8,128)(2,1)S(1)}, bf16[64,384]{1,0:T(8,128)(2,1)S(1)}, u32[]{:S(2)}, u32[]{:S(2)}) collective-permute-start(bf16[64,384]{1,0:T(8,128)(2,1)S(1)} %get-tuple-element.146), channel_id=1, source_target_pairs={{0,16},{8,24},{16,0},{24,8},{1,17},{9,25},{17,1},{25,9},{2,18},{10... | collective-permute-start | bytes 147464 | tf_op jit(solution)/shard_map/ppermute | solution.py:1001
  96.1 0.9 home.1
  97.0 2.0 %collective-permute-done.29.refs_2_ = bf16[64,384]{1,0:T(8,128)(2,1)S(1)} collective-permute-done((bf16[64,384]{1,0:T(8,128)(2,1)S(1)}, bf16[64,384]{1,0:T(8,128)(2,1)S(1)}, u32[]{:S(2)}, u32[]{:S(2)}) %collective-permute-start.29) | collective-permute-done | bytes 49184 | tf_op jit(solution)/shard_map/ppermute | solution.py:1001
  98.9 2.8 %collective-permute-done.30.refs_3_ = bf16[64,384]{1,0:T(8,128)(2,1)S(1)} collective-permute-done((bf16[64,384]{1,0:T(8,128)(2,1)S(1)}, bf16[64,384]{1,0:T(8,128)(2,1)S(1)}, u32[]{:S(2)}, u32[]{:S(2)}) %collective-permute-start.30) | collective-permute-done | bytes 49184 | tf_op jit(solution)/shard_map/ppermute | solution.py:1001
  101.7 0.8 final_sum.1
  (53 shorter events, 6.1 us)
Async XLA Ops:
  2.7 8.9 %collective-permute-start.7 = (bf16[48,384]{1,0:T(8,128)(2,1)}, bf16[48,384]{1,0:T(8,128)(2,1)S(1)}, u32[]{:S(2)}, u32[]{:S(2)}) collective-permute-start(bf16[48,384]{1,0:T(8,128)(2,1)} %get-tuple-element.94), channel_id=1, source_target_pairs={{0,24},{8,16},{16,8},{24,0},{1,25},{9,17},{17,9},{25,1},{2,26},{10... | collective-permute-start | bytes 110600 | tf_op jit(solution)/shard_map/ppermute | solution.py:1001
  7.7 5.3 %collective-permute-start.6 = (bf16[48,384]{1,0:T(8,128)(2,1)}, bf16[48,384]{1,0:T(8,128)(2,1)S(1)}, u32[]{:S(2)}, u32[]{:S(2)}) collective-permute-start(bf16[48,384]{1,0:T(8,128)(2,1)} %get-tuple-element.94), channel_id=1, source_target_pairs={{0,16},{8,24},{16,0},{24,8},{1,17},{9,25},{17,1},{25,9},{2,18},{10... | collective-permute-start | bytes 110600 | tf_op jit(solution)/shard_map/ppermute | solution.py:1001
  7.7 5.6 %collective-permute-start.5 = (bf16[48,384]{1,0:T(8,128)(2,1)}, bf16[48,384]{1,0:T(8,128)(2,1)S(1)}, u32[]{:S(2)}, u32[]{:S(2)}) collective-permute-start(bf16[48,384]{1,0:T(8,128)(2,1)} %get-tuple-element.94), channel_id=1, source_target_pairs={{0,8},{8,0},{16,24},{24,16},{1,9},{9,1},{17,25},{25,17},{2,10},{10... | collective-permute-start | bytes 110600 | tf_op jit(solution)/shard_map/ppermute | solution.py:1001
  8.3 8.5 %collective-permute-start = (bf16[416,128]{1,0:T(8,128)(2,1)}, bf16[416,128]{1,0:T(8,128)(2,1)S(1)}, u32[]{:S(2)}, u32[]{:S(2)}) collective-permute-start(bf16[416,128]{1,0:T(8,128)(2,1)} %get-tuple-element.84), channel_id=1, source_target_pairs={{0,0},{1,1},{2,4},{3,5},{4,2},{5,3},{6,6},{7,7},{8,8},{9,9},{10,12... | collective-permute-start | bytes 319496 | tf_op jit(solution)/shard_map/ppermute | solution.py:1010
  9.9 7.2 %collective-permute-start.1 = (bf16[416,128]{1,0:T(8,128)(2,1)}, bf16[416,128]{1,0:T(8,128)(2,1)S(1)}, u32[]{:S(2)}, u32[]{:S(2)}) collective-permute-start(bf16[416,128]{1,0:T(8,128)(2,1)} %get-tuple-element.85), channel_id=1, source_target_pairs={{0,1},{1,0},{2,5},{3,4},{4,3},{5,2},{6,7},{7,6},{8,9},{9,8},{10,13... | collective-permute-start | bytes 319496 | tf_op jit(solution)/shard_map/ppermute | solution.py:1010
  11.6 8.1 %collective-permute-start.2 = (bf16[416,128]{1,0:T(8,128)(2,1)}, bf16[416,128]{1,0:T(8,128)(2,1)S(1)}, u32[]{:S(2)}, u32[]{:S(2)}) collective-permute-start(bf16[416,128]{1,0:T(8,128)(2,1)} %get-tuple-element.86), channel_id=1, source_target_pairs={{0,4},{1,5},{2,0},{3,1},{4,6},{5,7},{6,2},{7,3},{8,12},{9,13},{10,... | collective-permute-start | bytes 319496 | tf_op jit(solution)/shard_map/ppermute | solution.py:1010
  13.1 7.0 %collective-permute-start.3 = (bf16[416,128]{1,0:T(8,128)(2,1)}, bf16[416,128]{1,0:T(8,128)(2,1)S(1)}, u32[]{:S(2)}, u32[]{:S(2)}) collective-permute-start(bf16[416,128]{1,0:T(8,128)(2,1)} %get-tuple-element.87), channel_id=1, source_target_pairs={{0,5},{1,4},{2,1},{3,0},{4,7},{5,6},{6,3},{7,2},{8,13},{9,12},{10,... | collective-permute-start | bytes 319496 | tf_op jit(solution)/shard_map/ppermute | solution.py:1010
  14.1 9.0 %collective-permute-start.10 = (bf16[4,48,384]{2,1,0:T(8,128)(2,1)S(1)}, bf16[4,48,384]{2,1,0:T(8,128)(2,1)S(1)}, u32[]{:S(2)}, u32[]{:S(2)}) collective-permute-start(bf16[4,48,384]{2,1,0:T(8,128)(2,1)S(1)} %pad_maximum_fusion.refs_6_.refs_0_), channel_id=1, source_target_pairs={{0,3},{1,2},{2,1},{3,0},{4,7},{5,6},{6,5},{7,4},{8,11},{9,10},{10,... | collective-permute-start | bytes 442376 | tf_op jit(solution)/shard_map/ppermute | solution.py:1001
  16.9 9.3 %collective-permute-start.9 = (bf16[4,48,384]{2,1,0:T(8,128)(2,1)S(1)}, bf16[4,48,384]{2,1,0:T(8,128)(2,1)S(1)}, u32[]{:S(2)}, u32[]{:S(2)}) collective-permute-start(bf16[4,48,384]{2,1,0:T(8,128)(2,1)S(1)} %pad_maximum_fusion.refs_6_.refs_0_), channel_id=1, source_target_pairs={{0,2},{1,3},{2,0},{3,1},{4,6},{5,7},{6,4},{7,5},{8,10},{9,11},{10,... | collective-permute-start | bytes 442376 | tf_op jit(solution)/shard_map/ppermute | solution.py:1001
  17.1 9.1 %collective-permute-start.8 = (bf16[4,48,384]{2,1,0:T(8,128)(2,1)S(1)}, bf16[4,48,384]{2,1,0:T(8,128)(2,1)S(1)}, u32[]{:S(2)}, u32[]{:S(2)}) collective-permute-start(bf16[4,48,384]{2,1,0:T(8,128)(2,1)S(1)} %pad_maximum_fusion.refs_6_.refs_0_), channel_id=1, source_target_pairs={{0,1},{1,0},{2,3},{3,2},{4,5},{5,4},{6,7},{7,6},{8,9},{9,8},{10,11... | collective-permute-start | bytes 442376 | tf_op jit(solution)/shard_map/ppermute | solution.py:1001
  21.8 4.8 %collective-permute-start.4 = (bf16[512,192]{1,0:T(8,128)(2,1)S(1)}, bf16[512,192]{1,0:T(8,128)(2,1)S(1)}, u32[]{:S(2)}, u32[]{:S(2)}) collective-permute-start(bf16[512,192]{1,0:T(8,128)(2,1)S(1)} %get-tuple-element.90.refs_0_.refs_5_), channel_id=1, source_target_pairs={{0,4},{4,0},{1,5},{5,1},{2,6},{6,2},{3,7},{7,3},{8,12},{12,8},{9,1... | collective-permute-start | bytes 589832 | tf_op jit(solution)/shard_map/ppermute | solution.py:996
  21.9 4.7 %collective-permute-start.11 = (bf16[4,48,384]{2,1,0:T(8,128)(2,1)S(1)}, bf16[4,48,384]{2,1,0:T(8,128)(2,1)S(1)}, u32[]{:S(2)}, u32[]{:S(2)}) collective-permute-start(bf16[4,48,384]{2,1,0:T(8,128)(2,1)S(1)} %pad_maximum_fusion.refs_6_.refs_0_), channel_id=1, source_target_pairs={{0,4},{4,0},{1,5},{5,1},{2,6},{6,2},{3,7},{7,3},{8,12},{12,8},{9,1... | collective-permute-start | bytes 442376 | tf_op jit(solution)/shard_map/ppermute | solution.py:996
  23.2 3.5 %collective-permute-start.14 = (bf16[4,48,384]{2,1,0:T(8,128)(2,1)S(1)}, bf16[4,48,384]{2,1,0:T(8,128)(2,1)S(1)}, u32[]{:S(2)}, u32[]{:S(2)}) collective-permute-start(bf16[4,48,384]{2,1,0:T(8,128)(2,1)S(1)} %collective-permute-done.10.refs_9_.refs_3_), channel_id=1, source_target_pairs={{0,4},{4,0},{1,5},{5,1},{2,6},{6,2},{3,7},{7,3},{8,12},{12,8},{9,1... | collective-permute-start | bytes 442376 | tf_op jit(solution)/shard_map/ppermute | solution.py:996
  26.1 1.4 %collective-permute-start.13 = (bf16[4,48,384]{2,1,0:T(8,128)(2,1)S(1)}, bf16[4,48,384]{2,1,0:T(8,128)(2,1)S(1)}, u32[]{:S(2)}, u32[]{:S(2)}) collective-permute-start(bf16[4,48,384]{2,1,0:T(8,128)(2,1)S(1)} %collective-permute-done.9.refs_8_.refs_2_), channel_id=1, source_target_pairs={{0,4},{4,0},{1,5},{5,1},{2,6},{6,2},{3,7},{7,3},{8,12},{12,8},{9,1... | collective-permute-start | bytes 442376 | tf_op jit(solution)/shard_map/ppermute | solution.py:996
  26.2 1.5 %collective-permute-start.12 = (bf16[4,48,384]{2,1,0:T(8,128)(2,1)S(1)}, bf16[4,48,384]{2,1,0:T(8,128)(2,1)S(1)}, u32[]{:S(2)}, u32[]{:S(2)}) collective-permute-start(bf16[4,48,384]{2,1,0:T(8,128)(2,1)S(1)} %collective-permute-done.8.refs_7_.refs_1_), channel_id=1, source_target_pairs={{0,4},{4,0},{1,5},{5,1},{2,6},{6,2},{3,7},{7,3},{8,12},{12,8},{9,1... | collective-permute-start | bytes 442376 | tf_op jit(solution)/shard_map/ppermute | solution.py:996
  27.7 10.8 %copy-start.4 = (f32[2,192]{1,0:T(2,128)S(1)}, f32[2,192]{1,0:T(2,128)}, u32[]{:S(2)}) copy-start(f32[2,192]{1,0:T(2,128)} %gains_ref.3) | copy-start | bytes 4612
  54.5 7.1 %collective-permute-start.15 = (bf16[4,4,48,256]{3,2,1,0:T(8,128)(2,1)S(1)}, bf16[4,4,48,256]{3,2,1,0:T(8,128)(2,1)S(1)}, u32[]{:S(2)}, u32[]{:S(2)}) collective-permute-start(bf16[4,4,48,256]{3,2,1,0:T(8,128)(2,1)S(1)} %get-tuple-element.99), channel_id=1, source_target_pairs={{0,4},{4,0},{1,5},{5,1},{2,6},{6,2},{3,7},{7,3},{8,12},{12,8},{9,1... | collective-permute-start | bytes 1179656 | tf_op jit(solution)/shard_map/ppermute | solution.py:996
  61.4 2.0 %collective-permute-start.16 = (bf16[1024,192]{1,0:T(8,128)(2,1)S(1)}, bf16[1024,192]{1,0:T(8,128)(2,1)S(1)}, u32[]{:S(2)}, u32[]{:S(2)}) collective-permute-start(bf16[1024,192]{1,0:T(8,128)(2,1)S(1)} %get-tuple-element.105.refs_2_), channel_id=1, source_target_pairs={{0,4},{4,0},{1,5},{5,1},{2,6},{6,2},{3,7},{7,3},{8,12},{12,8},{9,1... | collective-permute-start | bytes 1179656 | tf_op jit(solution)/shard_map/ppermute | solution.py:996
  63.3 14.1 %collective-permute-start.21 = (bf16[4,48,256]{2,1,0:T(8,128)(2,1)S(1)}, bf16[4,48,256]{2,1,0:T(8,128)(2,1)S(1)}, u32[]{:S(2)}, u32[]{:S(2)}) collective-permute-start(bf16[4,48,256]{2,1,0:T(8,128)(2,1)S(1)} %get-tuple-element.131), channel_id=1, source_target_pairs={{0,1},{1,0},{2,3},{3,2},{4,5},{5,4},{6,7},{7,6},{8,9},{9,8},{10,11... | collective-permute-start | bytes 294920 | tf_op jit(solution)/shard_map/ppermute | solution.py:1001
  64.8 12.7 %collective-permute-start.22 = (bf16[4,48,256]{2,1,0:T(8,128)(2,1)S(1)}, bf16[4,48,256]{2,1,0:T(8,128)(2,1)S(1)}, u32[]{:S(2)}, u32[]{:S(2)}) collective-permute-start(bf16[4,48,256]{2,1,0:T(8,128)(2,1)S(1)} %get-tuple-element.132), channel_id=1, source_target_pairs={{0,2},{1,3},{2,0},{3,1},{4,6},{5,7},{6,4},{7,5},{8,10},{9,11},{10,... | collective-permute-start | bytes 294920 | tf_op jit(solution)/shard_map/ppermute | solution.py:1001
  65.0 12.4 %collective-permute-start.23 = (bf16[4,48,256]{2,1,0:T(8,128)(2,1)S(1)}, bf16[4,48,256]{2,1,0:T(8,128)(2,1)S(1)}, u32[]{:S(2)}, u32[]{:S(2)}) collective-permute-start(bf16[4,48,256]{2,1,0:T(8,128)(2,1)S(1)} %get-tuple-element.133), channel_id=1, source_target_pairs={{0,3},{1,2},{2,1},{3,0},{4,7},{5,6},{6,5},{7,4},{8,11},{9,10},{10,... | collective-permute-start | bytes 294920 | tf_op jit(solution)/shard_map/ppermute | solution.py:1001
  77.5 1.5 %collective-permute-start.24 = (bf16[17,48,128]{2,1,0:T(8,128)(2,1)S(1)}, bf16[17,48,128]{2,1,0:T(8,128)(2,1)S(1)}, u32[]{:S(2)}, u32[]{:S(2)}) collective-permute-start(bf16[17,48,128]{2,1,0:T(8,128)(2,1)S(1)} %get-tuple-element.139), channel_id=1, source_target_pairs={{0,4},{4,0},{1,5},{5,1},{2,6},{6,2},{3,7},{7,3},{8,12},{12,8},{9,1... | collective-permute-start | bytes 626696 | tf_op jit(solution)/shard_map/ppermute | solution.py:996
  79.1 8.8 %collective-permute-start.25 = (bf16[4,64,128]{2,1,0:T(8,128)(2,1)S(1)}, bf16[4,64,128]{2,1,0:T(8,128)(2,1)S(1)}, u32[]{:S(2)}, u32[]{:S(2)}) collective-permute-start(bf16[4,64,128]{2,1,0:T(8,128)(2,1)S(1)} %get-tuple-element.141), channel_id=1, source_target_pairs={{0,1},{1,0},{2,3},{3,2},{4,5},{5,4},{6,7},{7,6},{8,9},{9,8},{10,11... | collective-permute-start | bytes 196616 | tf_op jit(solution)/shard_map/ppermute | solution.py:1001
  80.6 7.3 %collective-permute-start.26 = (bf16[4,64,128]{2,1,0:T(8,128)(2,1)S(1)}, bf16[4,64,128]{2,1,0:T(8,128)(2,1)S(1)}, u32[]{:S(2)}, u32[]{:S(2)}) collective-permute-start(bf16[4,64,128]{2,1,0:T(8,128)(2,1)S(1)} %get-tuple-element.142), channel_id=1, source_target_pairs={{0,2},{1,3},{2,0},{3,1},{4,6},{5,7},{6,4},{7,5},{8,10},{9,11},{10,... | collective-permute-start | bytes 196616 | tf_op jit(solution)/shard_map/ppermute | solution.py:1001
  81.5 11.4 %collective-permute-start.17 = (bf16[2,192,128]{2,1,0:T(8,128)(2,1)S(1)}, bf16[2,192,128]{2,1,0:T(8,128)(2,1)S(1)}, u32[]{:S(2)}, u32[]{:S(2)}) collective-permute-start(bf16[2,192,128]{2,1,0:T(8,128)(2,1)S(1)} %get-tuple-element.122), channel_id=1, source_target_pairs={{0,0},{1,1},{2,4},{3,5},{4,2},{5,3},{6,6},{7,7},{8,8},{9,9},{10,12... | collective-permute-start | bytes 294920 | tf_op jit(solution)/shard_map/ppermute | solution.py:1019
  82.2 13.7 %collective-permute-start.18 = (bf16[2,192,128]{2,1,0:T(8,128)(2,1)S(1)}, bf16[2,192,128]{2,1,0:T(8,128)(2,1)S(1)}, u32[]{:S(2)}, u32[]{:S(2)}) collective-permute-start(bf16[2,192,128]{2,1,0:T(8,128)(2,1)S(1)} %get-tuple-element.123), channel_id=1, source_target_pairs={{0,1},{1,0},{2,5},{3,4},{4,3},{5,2},{6,7},{7,6},{8,9},{9,8},{10,13... | collective-permute-start | bytes 294920 | tf_op jit(solution)/shard_map/ppermute | solution.py:1019
  83.0 8.5 %collective-permute-start.27 = (bf16[4,64,128]{2,1,0:T(8,128)(2,1)S(1)}, bf16[4,64,128]{2,1,0:T(8,128)(2,1)S(1)}, u32[]{:S(2)}, u32[]{:S(2)}) collective-permute-start(bf16[4,64,128]{2,1,0:T(8,128)(2,1)S(1)} %get-tuple-element.143), channel_id=1, source_target_pairs={{0,3},{1,2},{2,1},{3,0},{4,7},{5,6},{6,5},{7,4},{8,11},{9,10},{10,... | collective-permute-start | bytes 196616 | tf_op jit(solution)/shard_map/ppermute | solution.py:1001
  87.9 8.2 %collective-permute-start.19 = (bf16[2,192,128]{2,1,0:T(8,128)(2,1)S(1)}, bf16[2,192,128]{2,1,0:T(8,128)(2,1)S(1)}, u32[]{:S(2)}, u32[]{:S(2)}) collective-permute-start(bf16[2,192,128]{2,1,0:T(8,128)(2,1)S(1)} %get-tuple-element.124), channel_id=1, source_target_pairs={{0,2},{1,3},{2,6},{3,7},{4,0},{5,1},{6,4},{7,5},{8,10},{9,11},{10,... | collective-permute-start | bytes 294920 | tf_op jit(solution)/shard_map/ppermute | solution.py:1019
  87.9 8.2 %collective-permute-start.20 = (bf16[2,192,128]{2,1,0:T(8,128)(2,1)S(1)}, bf16[2,192,128]{2,1,0:T(8,128)(2,1)S(1)}, u32[]{:S(2)}, u32[]{:S(2)}) collective-permute-start(bf16[2,192,128]{2,1,0:T(8,128)(2,1)S(1)} %get-tuple-element.125), channel_id=1, source_target_pairs={{0,3},{1,2},{2,7},{3,6},{4,1},{5,0},{6,5},{7,4},{8,11},{9,10},{10,... | collective-permute-start | bytes 294920 | tf_op jit(solution)/shard_map/ppermute | solution.py:1019
  91.6 5.4 %collective-permute-start.28 = (bf16[64,384]{1,0:T(8,128)(2,1)S(1)}, bf16[64,384]{1,0:T(8,128)(2,1)S(1)}, u32[]{:S(2)}, u32[]{:S(2)}) collective-permute-start(bf16[64,384]{1,0:T(8,128)(2,1)S(1)} %get-tuple-element.145), channel_id=1, source_target_pairs={{0,8},{8,0},{16,24},{24,16},{1,9},{9,1},{17,25},{25,17},{2,10},{10... | collective-permute-start | bytes 147464 | tf_op jit(solution)/shard_map/ppermute | solution.py:1001
  92.9 6.1 %collective-permute-start.29 = (bf16[64,384]{1,0:T(8,128)(2,1)S(1)}, bf16[64,384]{1,0:T(8,128)(2,1)S(1)}, u32[]{:S(2)}, u32[]{:S(2)}) collective-permute-start(bf16[64,384]{1,0:T(8,128)(2,1)S(1)} %get-tuple-element.146), channel_id=1, source_target_pairs={{0,16},{8,24},{16,0},{24,8},{1,17},{9,25},{17,1},{25,9},{2,18},{10... | collective-permute-start | bytes 147464 | tf_op jit(solution)/shard_map/ppermute | solution.py:1001
  95.8 5.9 %collective-permute-start.30 = (bf16[64,384]{1,0:T(8,128)(2,1)S(1)}, bf16[64,384]{1,0:T(8,128)(2,1)S(1)}, u32[]{:S(2)}, u32[]{:S(2)}) collective-permute-start(bf16[64,384]{1,0:T(8,128)(2,1)S(1)} %get-tuple-element.147), channel_id=1, source_target_pairs={{0,24},{8,16},{16,8},{24,0},{1,25},{9,17},{17,9},{25,1},{2,26},{10... | collective-permute-start | bytes 147464 | tf_op jit(solution)/shard_map/ppermute | solution.py:1001
  (4 other events, 33.1 us)

commit v4 on v3

--- a/solution.py
+++ b/solution.py
@@ -127,25 +127,60 @@
         ref[r * depth + z] = value[r * rows : (r + 1) * rows]
 
 
-def put_lanes(ref, rows, values):
-    ref[0, rows, :] = values[:, :LANES]
-    ref[1, rows, : D - LANES] = values[:, LANES:]
-
-
-def block_sum(src, table, way, lane, first, count, step, offset, sublane, sign):
+def pair_lanes(first, second):
+    return jnp.concatenate([first, second], axis=1)
+
+
+def put_columns(wide, pairs, values):
+    wide[...] = values[:, :LANES]
+    tail = values[:, LANES:].reshape(values.shape[0] // GRID, 2, GRID // 2, D - LANES)
+    tail = pair_lanes(tail[:, 0].reshape(-1, D - LANES), tail[:, 1].reshape(-1, D - LANES))
+    pairs[...] = tail
+
+
+def put_rows(wide, pairs, from_wide, tail, together):
+    rows = from_wide.shape[0] // GRID
+    together[...] = pair_lanes(tail[: rows // 2 * GRID], tail[rows // 2 * GRID :])
+    for j in range(GRID):
+        wide[j * rows : (j + 1) * rows, :] = from_wide[pl.ds(j, rows, stride=GRID), :]
+        pairs[j * rows // 2 : (j + 1) * rows // 2, :] = together[pl.ds(j, rows // 2, stride=GRID), :]
+
+
+def units(index):
+    return [(0, (index * 2 + u) * 8) for u in range(2)] + [(1, index * 8)]
+
+
+def block_sum(src, table, way, kind, first, count, sublane, sign):
     total = [None] * count
+    step = src[kind].shape[0] // GRID
     for base in range(0, GRID, 8):
         low, high = -(base + 7), count - 1 - base
         coef = {
-            lag: table[way, lane, first * sign + (lag * sign + CENTER)]
+            lag: table[way, kind, first * sign + (lag * sign + CENTER)]
             for lag in range(low, high + 1)
         }
         for s in range(base, base + 8):
-            x = src[lane, pl.ds(pl.multiple_of(s * step + sublane, 8), 8), :]
+            x = src[kind][pl.ds(pl.multiple_of(s * step + sublane, 8), 8), :]
             for t in range(count):
                 term = coef[t - s] * x
                 total[t] = term if total[t] is None else total[t] + term
     return total
+
+
+def join_rows(i, count, rows, cols):
+    half = GRID // 2
+    narrow = D - LANES
+    across = rows[1][pl.ds(i, GRID, stride=count // 2), :]
+    found = []
+    for which in range(2):
+        row = i + which * (count // 2)
+        wide = cols[0][pl.ds(pl.multiple_of(row * GRID, GRID), GRID), :].astype(BF16).astype(F32)
+        wide = wide + rows[0][pl.ds(i + which * (count // 2), GRID, stride=count), :]
+        pairs = cols[1][pl.ds(pl.multiple_of(row * half, half), half), :].astype(BF16).astype(F32)
+        tail = jnp.concatenate([pairs[:, :narrow], pairs[:, narrow:]], axis=0)
+        tail = tail + across[:, which * narrow : (which + 1) * narrow]
+        found.append((row, jnp.concatenate([wide, tail], axis=1)))
+    return found
 
 
 def gather_parts(mine_refs, got_refs, block, out_ref):
@@ -257,17 +292,44 @@
     put_late_selections(starts, parts, *selections)
 
 
-def home_kernel(*refs):
-    row = lax.axis_index("row")
+def results_of(ref, rows):
+    start = ref.shape[0] - 2 * rows
+    return ref[start : start + rows], ref[start + rows :]
+
+
+def choose_kernel(*refs):
+    got_refs, out_ref = refs[:-1], refs[-1]
+    core, row = lax.axis_index("core"), lax.axis_index("row")
+    images, rows = out_ref.shape[0], out_ref.shape[1] // 2
+    for k, got in enumerate(got_refs):
+        image = row ^ k
+
+        @pl.when(image // images != core)
+        def _(got=got, image=image):
+            for which, value in enumerate(results_of(got, rows)):
+                out_ref[image % images, which * rows : (which + 1) * rows] = value
+
+
+def home_kernel(swapped_ref, *refs):
     got_refs, out_refs = refs[:-2], refs[-2:]
+    core, row = lax.axis_index("core"), lax.axis_index("row")
     images, slots, _ = out_refs[0].shape
     half = slots // 2
-    for j, got in enumerate(got_refs):
-        source = row ^ j
-        core, image = source // images, source % images
-        place = pl.ds(pl.multiple_of(core * half, half), half)
+    rows = half * 3 // 2
+    mine = pl.ds(pl.multiple_of(core * half, half), half)
+    theirs = pl.ds(pl.multiple_of((1 - core) * half, half), half)
+    for k, got in enumerate(got_refs):
+        image = row ^ k
+
+        @pl.when(image // images == core)
+        def _(got=got, image=image):
+            for out_ref, value in zip(out_refs, results_of(got, rows)):
+                out_ref[image % images, mine, :] = unpack(value)
+
+    for image in range(images):
         for which, out_ref in enumerate(out_refs):
-            out_ref[image, place, :] = unpack(got[which])
+            value = swapped_ref[image, which * rows : (which + 1) * rows]
+            out_ref[image, theirs, :] = unpack(value)
 
 
 def scan_kernel(
@@ -319,13 +381,19 @@
     wu_ref,
     wqkv_ref,
     late_ref,
-    xs,
-    xt,
-    cols,
-    rows,
+    xs_wide,
+    xs_pairs,
+    xt_wide,
+    xt_pairs,
+    cols_wide,
+    cols_pairs,
+    rows_wide,
+    rows_pairs,
     scanned_own,
     first_ref,
 ):
+    xs, xt = (xs_wide, xs_pairs), (xt_wide, xt_pairs)
+    cols, rows = (cols_wide, cols_pairs), (rows_wide, rows_pairs)
     core = lax.axis_index("core")
     blocks = len(mine_refs)
     rows_slots = OWN // blocks
@@ -348,10 +416,9 @@
 
     def store_lag(way, lag, row):
         row = row.astype(BF16).astype(F32)
-        for lane in range(2):
-            table_ref[way, lane, lag + CENTER] = jnp.broadcast_to(
-                row[:, lane * LANES : (lane + 1) * LANES], (8, LANES)
-            )
+        tail = row[:, LANES:D]
+        for kind, lanes in enumerate((row[:, :LANES], pair_lanes(tail, tail))):
+            table_ref[way, kind, lag + CENTER] = jnp.broadcast_to(lanes, (8, LANES))
 
     def lag_step(k, _):
         found = lag_row(k.astype(F32))
@@ -360,12 +427,11 @@
             store_lag(way, -k, found[2 * way + 1])
         return 0
 
-    lax.fori_loop(1, GRID, lag_step, 0)
+    lax.fori_loop(0, GRID, lag_step, 0, unroll=4)
     found = lag_row(0.0)
     for way in range(2):
         store_lag(way, 0, found[2 * way] + found[2 * way + 1])
 
-    xs[1, :, D - LANES :] = jnp.zeros((SLOTS, 2 * LANES - D), F32)
 
     for block in range(blocks):
         here = slice(block * rows_slots, (block + 1) * rows_slots)
@@ -376,36 +442,29 @@
     mixed = mixed.astype(BF16)
     mixed_ref[...] = mixed
     mixed = mixed.astype(F32)
-    put_lanes(xs, slice(None), mixed)
-    for lane in range(2):
-        for j in range(GRID):
-            xt[lane, j * GRID : (j + 1) * GRID, :] = xs[lane, pl.ds(j, GRID, stride=GRID), :]
+    put_columns(*xs, mixed)
+    put_rows(*xt, xs[0], mixed[:, LANES:], cols[1])
 
     def scan_step(index, _):
-        sublane = pl.multiple_of((index % 4) * 8, 8)
-        first = (index // 4) * 8
+        first = (index // 2) * 8
         for way, src, dst in ((0, xt, rows), (1, xs, cols)):
-            for lane in range(2):
-                total = block_sum(src, table_ref, way, lane, first, 8, GRID, 0, sublane, 1)
+            for kind, sublane in units(index % 2):
+                step = src[kind].shape[0] // GRID
+                total = block_sum(src, table_ref, way, kind, first, 8, sublane, 1)
                 for t in range(8):
-                    place = pl.multiple_of((first + t) * GRID + sublane, 8)
-                    dst[lane, pl.ds(place, 8), :] = total[t]
+                    place = pl.multiple_of((first + t) * step + sublane, 8)
+                    dst[kind][pl.ds(place, 8), :] = total[t]
         return 0
 
-    lax.fori_loop(0, 16, scan_step, 0)
+    lax.fori_loop(0, 8, scan_step, 0)
 
     def join_step(i, _):
-        place = pl.ds(pl.multiple_of(i * GRID, GRID), GRID)
-        mask = mask_ref[place, :]
-        both = []
-        for lane in range(2):
-            down = cols[lane, place, :].astype(BF16).astype(F32)
-            both.append((rows[lane, pl.ds(i, GRID, stride=GRID), :] + down) * mask)
-        both = jnp.concatenate([both[0], both[1][:, : D - LANES]], axis=1)
-        scanned_ref[place, :] = both.astype(BF16)
+        for row, value in join_rows(i, GRID, rows, cols):
+            place = pl.ds(pl.multiple_of(row * GRID, GRID), GRID)
+            scanned_ref[place, :] = (value * widen(mask_ref[place, :])).astype(BF16)
         return 0
 
-    lax.fori_loop(0, GRID, join_step, 0)
+    lax.fori_loop(0, GRID // 2, join_step, 0, unroll=2)
 
     for block in range(blocks):
         start = pl.multiple_of((block * 2 + core) * rows_slots, rows_slots)
@@ -486,9 +545,11 @@
     middle,
     second,
     pre,
+    grad_hidden,
     hidden,
     grad_pre,
     wire,
+    parted,
 ):
     core = lax.axis_index("core")
     blocks, _, rows_slots, _ = own_ref.shape
@@ -514,17 +575,22 @@
             w2[start : start + per_block] = part[r * per_block : (r + 1) * per_block].astype(BF16)
 
     for h in range(HEADS):
-        scores[...] = dot_nt(q_ref[h], k_ref[h])
-
-        def soft_step(i, _, h=h):
-            place = pl.ds(pl.multiple_of(i * 32, 32), 32)
-            values = scores[place, :]
-            top = jnp.max(values, -1, keepdims=True)
-            soft_ref[h, place, :] = jnp.exp(values - top).astype(BF16)
+        scores[...] = dot_nt(k_ref[h], q_ref[h])
+
+        def top_step(i, top):
+            values = scores[pl.ds(pl.multiple_of(i * 64, 64), 64), :]
+            return jnp.maximum(top, jnp.max(values.reshape(8, 8, OWN), 0))
+
+        top = lax.fori_loop(1, SLOTS // 64, top_step, jnp.max(scores[:64].reshape(8, 8, OWN), 0))
+        top = jnp.max(top, 0, keepdims=True)
+
+        def soft_step(i, _, h=h, top=top):
+            place = pl.ds(pl.multiple_of(i * 128, 128), 128)
+            soft_ref[h, place, :] = jnp.exp(scores[place, :] - top).astype(BF16)
             return 0
 
-        lax.fori_loop(0, OWN // 32, soft_step, 0)
-        raw = dot(soft_ref[h], v_ref[h])
+        lax.fori_loop(0, SLOTS // 128, soft_step, 0)
+        raw = dot_tn(soft_ref[h], v_ref[h])
         total = raw[:, HEAD_DIM : HEAD_DIM + 1]
         sums[h] = jnp.broadcast_to(1.0 / total, (OWN, LANES))
         result = raw * sums[h]
@@ -546,11 +612,11 @@
         second[place, :] = (unit * gain).astype(BF16)
         return 0
 
-    lax.fori_loop(0, blocks, norm_step, 0)
+    for block in range(blocks):
+        norm_step(block, 0)
 
     pre[...] = dot(second[...], w1[...])
     cot = jnp.concatenate([own_ref[b, 1] for b in range(blocks)], axis=0)
-    grad_hidden = scores.at[:, :FF]
     grad_hidden[...] = dot_nt(cot, w2[...])
 
     def gelu_step(i, _):
@@ -559,10 +625,10 @@
         phi = 0.5 * (1.0 + lax.erf(x * np.float32(0.5**0.5)))
         hidden[place, :] = (x * phi).astype(BF16)
         slope = phi + x * jnp.exp(x * x * -0.5) * np.float32((2 * np.pi) ** -0.5)
-        grad_pre[place, :] = (scores[place, :FF] * slope).astype(BF16)
+        grad_pre[place, :] = (grad_hidden[place, :] * slope).astype(BF16)
         return 0
 
-    lax.fori_loop(0, OWN // 16, gelu_step, 0)
+    lax.fori_loop(0, OWN // 16, gelu_step, 0, unroll=2)
 
     out_ref[...] = (middle[...] + dot(hidden[...], w2[...])).astype(BF16)
     grad_2 = dot_tn(hidden[...], cot).astype(BF16)
@@ -579,7 +645,10 @@
         second[place, :] = (grad * own_mask(block)).astype(BF16)
         return total
 
-    gain_ref[...] = lax.fori_loop(0, blocks, back_step, jnp.zeros((1, D), F32))
+    gain_two = jnp.zeros((1, D), F32)
+    for block in range(blocks):
+        gain_two = back_step(block, gain_two)
+    gain_ref[...] = gain_two
 
     grad_o = []
     lane_own = lax.broadcasted_iota(jnp.int32, (OWN, LANES), 1)
@@ -603,15 +672,10 @@
 
     def deliver(lanes):
         for m in range(parts):
-            value = wire[:, m * LANES : (m + 1) * LANES].astype(BF16)
-
-            @pl.when(core == m % 2)
-            def _(value=value, m=m):
-                put_blocks(keep_ref, m // 2, lanes, value)
-
-            @pl.when(core != m % 2)
-            def _(value=value, m=m):
-                put_blocks(send_ref, m // 2, lanes, value)
+            parted[m] = wire[:, m * LANES : (m + 1) * LANES].astype(BF16)
+        for z in range(parts // 2):
+            put_blocks(keep_ref, z, lanes, parted[2 * z + core])
+            put_blocks(send_ref, z, lanes, parted[2 * z + 1 - core])
 
     deliver(slice(0, LANES))
     total = None
@@ -649,21 +713,21 @@
     rows_slots = OWN // blocks
     for h in range(HEADS):
         tile = slice(h * LANES, (h + 1) * LANES)
-        scores[...] = dot_nt(lifted_ref[h], v_ref[h])
+        scores[...] = dot_nt(v_ref[h], lifted_ref[h])
 
         def back_step(i, _, h=h):
-            place = pl.ds(pl.multiple_of(i * 32, 32), 32)
+            place = pl.ds(pl.multiple_of(i * 64, 64), 64)
             grad_scores[place, :] = (soft_ref[h, place, :].astype(F32) * scores[place, :]).astype(
                 BF16
             )
             return 0
 
-        lax.fori_loop(0, OWN // 32, back_step, 0)
-        grad_q[:, tile] = (dot(grad_scores[...], k_ref[h]).astype(BF16) * HEAD_DIM ** (-0.5)).astype(
+        lax.fori_loop(0, SLOTS // 64, back_step, 0)
+        grad_q[:, tile] = (dot_tn(grad_scores[...], k_ref[h]).astype(BF16) * HEAD_DIM ** (-0.5)).astype(
             BF16
         )
-        triple[0, :, tile] = dot_tn(grad_scores[...], q_ref[h]).astype(BF16)
-        triple[1, :, tile] = dot_tn(soft_ref[h], lifted_ref[h]).astype(BF16)
+        triple[0, :, tile] = dot(grad_scores[...], q_ref[h]).astype(BF16)
+        triple[1, :, tile] = dot(soft_ref[h], lifted_ref[h]).astype(BF16)
 
     part[...] = dot_nt(triple[0], wqkv_ref[1]) + dot_nt(triple[1], wqkv_ref[2])
     from_q = dot_nt(grad_q[...], wqkv_ref[0])
@@ -698,107 +762,117 @@
     keep_ref,
     send_ref,
     back_ref,
-    gs,
-    gt,
-    xs,
-    xt,
+    gs_wide,
+    gs_pairs,
+    gt_wide,
+    gt_pairs,
+    xs_wide,
+    xs_pairs,
+    xt_wide,
+    xt_pairs,
+    rows_wide,
+    rows_pairs,
+    cols_wide,
+    cols_pairs,
+    grads_ref,
     own,
-    rows,
-    cols,
+    own_tail,
+    together,
     lag_sums,
     lag_rows,
     mixed_back,
     wire,
+    parted,
 ):
+    gs, gt = (gs_wide, gs_pairs), (gt_wide, gt_pairs)
+    xs, xt = (xs_wide, xs_pairs), (xt_wide, xt_pairs)
+    rows, cols = (rows_wide, rows_pairs), (cols_wide, cols_pairs)
     core = lax.axis_index("core")
     blocks, _, rows_slots, _ = own_ref.shape
     half_rows = rows_slots // GRID
     own_rows = GRID // 2
     parts = sel_rc_ref.shape[0] // LANES
-    pad = jnp.zeros((SLOTS, 2 * LANES - D), F32)
-
-    xs[1, :, D - LANES :] = pad
-    gs[1, :, D - LANES :] = pad
-    put_lanes(xs, slice(None), mixed_ref[...].astype(F32))
+    put_columns(*xs, mixed_ref[...].astype(F32))
     grads = (part_ref[...].astype(F32) + got_ref[...].astype(F32)) * widen(mask_ref[...])
-    put_lanes(gs, slice(None), grads.astype(BF16).astype(F32))
+    grads = grads.astype(BF16)
+    grads_ref[...] = grads
+    put_columns(*gs, grads.astype(F32))
 
     def place_of(block):
         return pl.ds(pl.multiple_of((block * 2 + core) * rows_slots, rows_slots), rows_slots)
 
-    for src, dst in ((gs, gt), (xs, xt)):
-        for lane in range(2):
-            for block in range(blocks):
-                here = slice(block * rows_slots, (block + 1) * rows_slots)
-                own[lane, here, :] = src[lane, place_of(block), :]
-            for j in range(GRID):
-                dst[lane, j * own_rows : (j + 1) * own_rows, :] = own[
-                    lane, pl.ds(j, own_rows, stride=GRID), :
-                ]
+    for source, dst in ((grads_ref, gt), (mixed_ref, xt)):
+        for block in range(blocks):
+            here = slice(block * rows_slots, (block + 1) * rows_slots)
+            value = source[place_of(block), :].astype(F32)
+            own[here, :] = value[:, :LANES]
+            own_tail[here, :] = value[:, LANES:]
+        put_rows(*dst, own, own_tail[...], together)
 
     def row_step(index, _):
-        sublane = pl.multiple_of((index % 2) * 8, 8)
-        first = (index // 2) * 8
-        for lane in range(2):
-            total = block_sum(gt, table_ref, 0, lane, first, 8, own_rows, 0, sublane, -1)
+        first = index * 8
+        for kind, sublane in units(0):
+            step = gt[kind].shape[0] // GRID
+            total = block_sum(gt, table_ref, 0, kind, first, 8, sublane, -1)
             for t in range(8):
-                rows[lane, pl.ds(pl.multiple_of((first + t) * own_rows + sublane, 8), 8), :] = total[
-                    t
-                ]
+                place = pl.multiple_of((first + t) * step + sublane, 8)
+                rows[kind][pl.ds(place, 8), :] = total[t]
         return 0
 
-    lax.fori_loop(0, 8, row_step, 0)
+    lax.fori_loop(0, 4, row_step, 0)
 
     def col_step(index, _):
-        sublane = pl.multiple_of((index % 4) * 8, 8)
-        block = index // 4
+        block = index // 2
         first = (block * 2 + core) * half_rows
-        for lane in range(2):
-            total = block_sum(gs, table_ref, 1, lane, first, half_rows, GRID, 0, sublane, -1)
+        for kind, sublane in units(index % 2):
+            step = gs[kind].shape[0] // GRID
+            total = block_sum(gs, table_ref, 1, kind, first, half_rows, sublane, -1)
             for t in range(half_rows):
-                at = pl.multiple_of((block * half_rows + t) * GRID + sublane, 8)
-                cols[lane, pl.ds(at, 8), :] = total[t]
+                place = pl.multiple_of((block * half_rows + t) * step + sublane, 8)
+                cols[kind][pl.ds(place, 8), :] = total[t]
         return 0
 
-    lax.fori_loop(0, blocks * 4, col_step, 0)
+    lax.fori_loop(0, blocks * 2, col_step, 0)
 
     lag_sums[...] = jnp.zeros_like(lag_sums)
 
-    def add_lags(way, lane, first, count, base, gref, xref, step, groups):
+    def add_lags(way, kind, first, count, base, gref, xref):
         total = {}
-        for u in range(groups):
+        step = gref[kind].shape[0] // GRID
+        for u in range(step // 8):
             g = [
-                gref[lane, pl.ds(pl.multiple_of((first + t) * step + u * 8, 8), 8), :]
+                gref[kind][pl.ds(pl.multiple_of((first + t) * step + u * 8, 8), 8), :]
                 for t in range(count)
             ]
             for s in range(8):
-                x = xref[lane, pl.ds(pl.multiple_of((base + s) * step + u * 8, 8), 8), :]
+                x = xref[kind][pl.ds(pl.multiple_of((base + s) * step + u * 8, 8), 8), :]
                 for t in range(count):
                     term = g[t] * x
                     total[t - s] = term if t - s not in total else total[t - s] + term
         for lag, value in total.items():
             at = first - base + (lag + CENTER)
-            lag_sums[way, lane, at] += value
+            lag_sums[way, kind, at] += value
 
     def lag_row_step(index, _):
-        first, base = (index // 4) * 8, (index % 4) * 8
-        for lane in range(2):
-            add_lags(0, lane, first, 8, base, gt, xt, own_rows, own_rows // 8)
+        for kind in range(2):
+            add_lags(0, kind, (index // 4) * 8, 8, (index % 4) * 8, gt, xt)
         return 0
 
     lax.fori_loop(0, 16, lag_row_step, 0)
 
     def lag_col_step(index, _):
-        first, base = ((index // 4) * 2 + core) * half_rows, (index % 4) * 8
-        for lane in range(2):
-            add_lags(1, lane, first, half_rows, base, gs, xs, GRID, GRID // 8)
+        first = ((index // 4) * 2 + core) * half_rows
+        for kind in range(2):
+            add_lags(1, kind, first, half_rows, (index % 4) * 8, gs, xs)
         return 0
 
     lax.fori_loop(0, blocks * 4, lag_col_step, 0)
 
     for way in range(2):
-        for lane in range(2):
-            lag_rows[way, :, lane * LANES : (lane + 1) * LANES] = jnp.sum(lag_sums[way, lane], 1)
+        lag_rows[way, :, :LANES] = jnp.sum(lag_sums[way, 0], 1)
+        tail = jnp.sum(lag_sums[way, 1], 1)
+        tail = tail[:, : D - LANES] + tail[:, D - LANES :]
+        lag_rows[way, :, LANES:] = pair_lanes(tail, jnp.zeros_like(tail))
 
     decay, coef = rates_ref[: 4 * STATE], rates_ref[4 * STATE :]
 
@@ -816,23 +890,18 @@
         return to_rate - lag * scaled, to_coef + scaled
 
     zero = jnp.zeros((4 * STATE, 2 * LANES), F32)
-    to_rate, to_coef = lax.fori_loop(0, GRID, table_step, (zero, zero))
+    to_rate, to_coef = lax.fori_loop(0, GRID, table_step, (zero, zero), unroll=4)
     grad_rc = jnp.concatenate([to_rate * coef, to_coef], axis=0).T[:D].astype(BF16)
 
     def join_step(i, _):
-        place = pl.ds(pl.multiple_of(i * GRID, GRID), GRID)
-        block = i // half_rows
-        at = ((block * 2 + core) * half_rows + i % half_rows) * GRID
-        mask = mask_ref[pl.ds(pl.multiple_of(at, GRID), GRID), :]
-        both = []
-        for lane in range(2):
-            down = cols[lane, place, :].astype(BF16).astype(F32)
-            both.append((rows[lane, pl.ds(i, GRID, stride=own_rows), :] + down) * mask)
-        both = jnp.concatenate([both[0], both[1][:, : D - LANES]], axis=1)
-        mixed_back[place, :] = both.astype(BF16)
+        for row, value in join_rows(i, own_rows, rows, cols):
+            at = ((row // half_rows * 2 + core) * half_rows + row % half_rows) * GRID
+            mask = mask_ref[pl.ds(pl.multiple_of(at, GRID), GRID), :]
+            place = pl.ds(pl.multiple_of(row * GRID, GRID), GRID)
+            mixed_back[place, :] = (value * widen(mask)).astype(BF16)
         return 0
 
-    lax.fori_loop(0, own_rows, join_step, 0)
+    lax.fori_loop(0, own_rows // 2, join_step, 0, unroll=2)
     grad_u = dot_tn(first_ref[...], mixed_back[...]).astype(BF16)
     grad_first = dot_nt(mixed_back[...], wu_ref[...])
     back_ref[...] = grad_first
@@ -847,15 +916,10 @@
         span = slice(starts[third] * LANES, (starts[third] + width) * LANES)
         wire[:, span] += dot_nt(grad_w_ref[third], sel_q_ref[third])
     for m in range(parts):
-        value = wire[:, m * LANES : (m + 1) * LANES].astype(BF16)
-
-        @pl.when(core == m % 2)
-        def _(value=value, m=m):
-            put_late(keep_ref, m // 2, value)
-
-        @pl.when(core != m % 2)
-        def _(value=value, m=m):
-            put_late(send_ref, m // 2, value)
+        parted[m] = wire[:, m * LANES : (m + 1) * LANES].astype(BF16)
+    for z in range(parts // 2):
+        put_late(keep_ref, z, parted[2 * z + core])
+        put_late(send_ref, z, parted[2 * z + 1 - core])
 
     lines = []
     for value in (gain_one, gain_two_ref[...]):
@@ -874,17 +938,20 @@
 def last_norm_kernel(
     own_ref, gains_ref, back_ref, grad_middle_ref, out_own_ref, *routed_refs
 ):
-    blocks, _, slots, _ = own_ref.shape
-    images = blocks // 2
-    mine = lax.axis_index("core") * images + lax.axis_index("row") % images
+    _, _, slots, _ = own_ref.shape
+    rows = slots * 3 // 2
     gain = gains_ref[0:1, :]
-    for j, routed in enumerate(routed_refs):
-        block = mine ^ j
+    for k, routed in enumerate(routed_refs):
+        block = lax.axis_index("row") ^ k
         place = pl.ds(pl.multiple_of(block * slots, slots), slots)
         unit, inverse = normalise(own_ref[block, 0].astype(F32))
         grad = grad_middle_ref[place, :] + norm_back(back_ref[place, :], gain, unit, inverse)
-        routed[0] = pack(out_own_ref[place, :])
-        routed[1] = pack(grad.astype(BF16))
+        routed[:rows] = pack(out_own_ref[place, :])
+        routed[rows:] = pack(grad.astype(BF16))
+
+
+def late_rows(rows):
+    return (rows + 31) // 16 * 16
 
 
 def split(value):
@@ -900,9 +967,11 @@
             out_ref[z] = total.astype(BF16)
 
 
-def late_sum_kernel(keep_ref, got_ref, *out_refs):
-    depth, rows, _ = out_refs[0].shape
-    rows -= 16
+def late_sum_kernel(depth, keep_ref, got_ref, *refs):
+    count = len(refs) // 2
+    routed_refs, out_refs = refs[:count], refs[count:]
+    rows = keep_ref.shape[1]
+    block_rows = late_rows(rows)
     last = keep_ref.shape[0] - 1
     gains = keep_ref[last, :8].astype(F32) + got_ref[last, :8].astype(F32)
     lines = []
@@ -911,29 +980,37 @@
             at = 4 * g + lane
             lines.append(gains[at : at + 1] + gains[at + 2 : at + 3])
     gains = split(jnp.concatenate(lines, axis=0))
-    gains = jnp.concatenate([gains, jnp.zeros((8, LANES), F32)], axis=0).astype(BF16)
+    gains = jnp.concatenate([gains, jnp.zeros((8, LANES), F32)], axis=0)
+    fill = jnp.zeros((block_rows - rows - 16, LANES), F32)
     for k, out_ref in enumerate(out_refs):
         block = lax.axis_index("row") ^ k
         for z in range(depth):
             at = block * depth + z
             total = keep_ref[at].astype(F32) + got_ref[at].astype(F32)
-            out_ref[z, :rows] = total.astype(BF16)
-            out_ref[z, rows:] = gains
+            pieces = [gains, total]
+            if block_rows > rows + 16:
+                pieces.append(fill)
+            out_ref[z * block_rows : (z + 1) * block_rows] = jnp.concatenate(pieces, axis=0).astype(
+                BF16
+            )
+        out_ref[depth * block_rows :] = routed_refs[k][...]
 
 
 def row_sum_kernel(blocks, *refs):
     early_refs, late_refs, out_refs = refs[:blocks], refs[blocks : 2 * blocks], refs[2 * blocks :]
     rows = early_refs[0].shape[1]
+    block_rows = late_rows(rows)
     for j, out_ref in enumerate(out_refs):
         z = lax.axis_index("z") ^ j
+        place = pl.ds(pl.multiple_of(z * block_rows, 16), block_rows)
         early = early_refs[0][z].astype(F32)
-        late = late_refs[0][z].astype(F32)
+        late = late_refs[0][place, :].astype(F32)
         for k in range(1, blocks):
             early = early + early_refs[k][z].astype(F32)
-            late = late + late_refs[k][z].astype(F32)
+            late = late + late_refs[k][place, :].astype(F32)
         out_ref[:rows, LANES:] = early.astype(BF16)
-        out_ref[:rows, :LANES] = late[:rows].astype(BF16)
-        gains = split(late[rows : rows + 4] + late[rows + 4 : rows + 8])
+        out_ref[:rows, :LANES] = late[16 : 16 + rows].astype(BF16)
+        gains = split(late[:4] + late[4:8])
         gains = jnp.concatenate([gains, jnp.zeros((8, LANES), F32)], axis=0).astype(BF16)
         out_ref[rows:, :LANES] = gains
         out_ref[rows:, LANES:] = jnp.zeros((16, 2 * LANES), BF16)
@@ -992,6 +1069,9 @@
     swap = [(0, 1), (1, 0)]
     shape = jax.ShapeDtypeStruct
 
+    def planes(slots):
+        return [pltpu.VMEM((slots, LANES), F32), pltpu.VMEM((slots // 2, LANES), F32)]
+
     def swapped(value):
         return lax.ppermute(value, "core", swap)
 
@@ -1007,15 +1087,6 @@
             for source in range(blocks):
                 target, image = divmod(source ^ j, images)
                 pairs.append((home * blocks + source, target * blocks + home * images + image))
-        return lax.ppermute(value, ("core", "row"), pairs)
-
-    def to_homes(value, j):
-        pairs = []
-        for source in range(2):
-            for chip in range(blocks):
-                home, image = divmod(chip, images)
-                target = (source * images + image) ^ j
-                pairs.append((source * blocks + chip, home * blocks + target))
         return lax.ppermute(value, ("core", "row"), pairs)
 
     starts, width = late_spans(parts)
@@ -1108,7 +1179,7 @@
         in_specs=[VMEM] * (6 + 2 * blocks),
         out_specs=[VMEM] * 9,
         scratch_shapes=[part_scratch]
-        + [pltpu.VMEM((2, SLOTS, LANES), F32)] * 4
+        + planes(SLOTS) * 4
         + [pltpu.VMEM((OWN, D), BF16), pltpu.VMEM((SLOTS, D), BF16)],
         compiler_params=compiler(),
     )(first_own, first_other, mask, sel_u, sel_rc, sel_q, *weights)
@@ -1118,7 +1189,7 @@
         middle_kernel,
         name="attention_and_feed_forward",
         out_shape=(
-            shape((HEADS, OWN, SLOTS), BF16),
+            shape((HEADS, SLOTS, OWN), BF16),
             head_own,
             shape((OWN, D), BF16),
             shape((OWN, D), F32),
@@ -1130,7 +1201,7 @@
         out_specs=[VMEM] * 7,
         scratch_shapes=[
             part_scratch,
-            pltpu.VMEM((OWN, SLOTS), F32),
+            pltpu.VMEM((SLOTS, OWN), F32),
             pltpu.VMEM((HEADS, LANES, D), BF16),
             pltpu.VMEM((D, FF), BF16),
             pltpu.VMEM((FF, D), BF16),
@@ -1140,9 +1211,11 @@
             pltpu.VMEM((OWN, D), F32),
             pltpu.VMEM((OWN, D), BF16),
             pltpu.VMEM((OWN, FF), F32),
+            pltpu.VMEM((OWN, FF), F32),
             pltpu.VMEM((OWN, FF), BF16),
             pltpu.VMEM((OWN, FF), BF16),
             pltpu.VMEM((D, parts * LANES), F32),
+            pltpu.VMEM((parts, D, LANES), BF16),
         ],
         compiler_params=compiler(),
     )(own, mask, norm_gains, sel_1, sel_o, sel_2, q, k, v, *weights)
@@ -1156,8 +1229,8 @@
         in_specs=[VMEM] * 7,
         out_specs=[VMEM] * 2,
         scratch_shapes=[
-            pltpu.VMEM((OWN, SLOTS), F32),
-            pltpu.VMEM((OWN, SLOTS), BF16),
+            pltpu.VMEM((SLOTS, OWN), F32),
+            pltpu.VMEM((SLOTS, OWN), BF16),
             pltpu.VMEM((2, SLOTS, TILE), BF16),
             pltpu.VMEM((OWN, TILE), BF16),
             pltpu.VMEM((OWN, D), BF16),
@@ -1166,7 +1239,6 @@
         compiler_params=compiler(),
     )(soft, lifted, q, k, v, scanned, wqkv)
 
-    part_got = swapped(part)
     early_keep, early_recv, part = lax.optimization_barrier((early_keep, early_recv, part))
     early = pl.pallas_call(
         early_sum_kernel,
@@ -1176,7 +1248,8 @@
         out_specs=[VMEM] * blocks,
         compiler_params=compiler(8 << 20),
     )(early_keep, early_recv)
-    early, part_got = lax.optimization_barrier((early, part_got))
+    early, part = lax.optimization_barrier((early, part))
+    part_got = swapped(part)
     early = exchanged(early, "row")
     wire_late = shape((blocks * depth + 1, rows_weight, LANES), BF16)
     late_keep, late_send, back = pl.pallas_call(
@@ -1185,18 +1258,17 @@
         out_shape=(wire_late, wire_late, shape((OWN, D), F32)),
         in_specs=[VMEM] * 14,
         out_specs=[VMEM] * 3,
-        scratch_shapes=[
-            pltpu.VMEM((2, SLOTS, LANES), F32),
-            pltpu.VMEM((2, OWN, LANES), F32),
-            pltpu.VMEM((2, SLOTS, LANES), F32),
-            pltpu.VMEM((2, OWN, LANES), F32),
-            pltpu.VMEM((2, OWN, LANES), F32),
-            pltpu.VMEM((2, OWN, LANES), F32),
-            pltpu.VMEM((2, OWN, LANES), F32),
+        scratch_shapes=planes(SLOTS) + planes(OWN) + planes(SLOTS) + planes(OWN) * 3
+        + [
+            pltpu.VMEM((SLOTS, D), BF16),
+            pltpu.VMEM((OWN, LANES), F32),
+            pltpu.VMEM((OWN, D - LANES), F32),
+            pltpu.VMEM((OWN // 2, LANES), F32),
             pltpu.VMEM((2, 2, LAGS, 8, LANES), F32),
             pltpu.VMEM((2, LAGS, 2 * LANES), F32),
             pltpu.VMEM((OWN, D), BF16),
             pltpu.VMEM((D, parts * LANES), F32),
+            pltpu.VMEM((parts, D, LANES), BF16),
         ],
         compiler_params=compiler(),
     )(
@@ -1216,15 +1288,7 @@
         sel_q,
     )
     late_keep, late_send, early = lax.optimization_barrier((late_keep, late_send, early))
-    late = pl.pallas_call(
-        late_sum_kernel,
-        name="late_sum",
-        out_shape=(shape((depth, rows_weight + 16, LANES), BF16),) * blocks,
-        in_specs=[VMEM] * 2,
-        out_specs=[VMEM] * blocks,
-        compiler_params=compiler(8 << 20),
-    )(late_keep, swapped(late_send))
-    payload = shape((2, packed_rows, LANES), BF16)
+    payload = shape((2 * packed_rows, LANES), BF16)
     routed = pl.pallas_call(
         last_norm_kernel,
         name="last_norm",
@@ -1233,6 +1297,15 @@
         out_specs=[VMEM] * blocks,
         compiler_params=compiler(8 << 20),
     )(own, norm_gains, back, grad_middle, out_own)
+    payload = shape((depth * late_rows(rows_weight) + 2 * packed_rows, LANES), BF16)
+    late = pl.pallas_call(
+        lambda *refs: late_sum_kernel(depth, *refs),
+        name="late_sum",
+        out_shape=(payload,) * blocks,
+        in_specs=[VMEM] * (2 + blocks),
+        out_specs=[VMEM] * blocks,
+        compiler_params=compiler(8 << 20),
+    )(late_keep, swapped(late_send), *routed)
     late = exchanged(late, "row")
     summed = pl.pallas_call(
         lambda *refs: row_sum_kernel(blocks, *refs),
@@ -1244,17 +1317,25 @@
     )(*early, *late)
     summed = exchanged(summed, "z")
 
-    routed = [to_homes(value, j) for j, value in enumerate(routed)]
+    chosen = pl.pallas_call(
+        choose_kernel,
+        name="choose",
+        out_shape=shape((images, 2 * packed_rows, LANES), BF16),
+        in_specs=[VMEM] * blocks,
+        out_specs=VMEM,
+        compiler_params=compiler(8 << 20),
+    )(*late)
     whole = shape((images, rows_here * GRID, D), BF16)
     block_out, grad_patches = pl.pallas_call(
         home_kernel,
         name="home",
         out_shape=(whole, whole),
-        in_specs=[VMEM] * blocks,
+        in_specs=[VMEM] * (1 + blocks),
         out_specs=[VMEM] * 2,
         compiler_params=compiler(8 << 20),
-    )(*routed)
-
+    )(swapped(chosen), *late)
+
+    summed, block_out, grad_patches = lax.optimization_barrier((summed, block_out, grad_patches))
     turned = (4 * STATE // parts, rows_weight)
     g1, g2, f_u, f_rate, f_coef, f_qkv, f_o, f_1, f_2 = pl.pallas_call(
         lambda *refs: final_kernel(parts, *refs),

time: 103 us -> 89.8 us (0.87)
  Pallas kernels: 49.5 us -> 39.7 us
  starting transfers between devices: 32.8 us -> 28 us
  waiting for transfers between devices: 17.9 us -> 19.5 us
    pallas_call x1, Pallas kernels: 15.9 us -> 10.3 us  [per_device(): pl.pallas_call(middle_kernel, name='attention_and_feed_forward', out_shap...]
    ppermute x15, waiting for transfers between devices: 11.9 us -> 15.8 us  [exchanged(): lax.ppermute(values[k], axis, [(i, i ^ k) for i in range(size)])]
    ppermute x15, starting transfers between devices: 24.3 us -> 21.2 us  [exchanged(): lax.ppermute(values[k], axis, [(i, i ^ k) for i in range(size)])]
    pallas_call x1, Pallas kernels: 10.6 us -> 8.01 us  [per_device(): pl.pallas_call(lambda *refs: scan_back_kernel(starts, width, *refs), name...]
    ppermute x8 -> x9, waiting for transfers between devices: 4.12 us -> 1.82 us  [swapped(): return lax.ppermute(value, 'core', swap)]
    pallas_call x1, Pallas kernels: 10.8 us -> 8.67 us  [per_device(): pl.pallas_call(lambda *refs: scan_kernel(starts, width, *refs, blocks=blo...]
    ppermute x4 -> x0, starting transfers between devices: 1.68 us -> none  [to_homes(): return lax.ppermute(value, ('core', 'row'), pairs)]
  transfers between devices with their start and end apart: 31 -> 28, of which waited for: 11 -> 11; matrix products, arithmetic and copies ran while one was open for 1% -> 1% of each run, Pallas kernels for 19% -> 20%
where the time goes in v4:
time: 89.8 us; the launch traced here: 89.5 us
  Pallas kernels  39.7 us (44%)
  starting transfers between devices  28 us (31%)
  waiting for transfers between devices  19.5 us (22%)
    ppermute x15, starting transfers between devices, exchanged(): lax.ppermute(values[k], axis, [(i, i ^ k) for i in range(size)])  21.2 us
    ppermute x15, waiting for transfers between devices, exchanged(): lax.ppermute(values[k], axis, [(i, i ^ k) for i in range(size)])  15.8 us
    pallas_call x1, Pallas kernels, per_device(): pl.pallas_call(middle_kernel, name='attention_and_feed_forward', out_shap...  10.3 us
    pallas_call x1, Pallas kernels, per_device(): pl.pallas_call(lambda *refs: scan_kernel(starts, width, *refs, blocks=blo...  8.67 us
    pallas_call x1, Pallas kernels, per_device(): pl.pallas_call(lambda *refs: scan_back_kernel(starts, width, *refs), name...  8.01 us
    pallas_call x1, Pallas kernels, per_device(): pl.pallas_call(lambda *refs: attention_back_kernel(*refs, blocks=blocks),...  6.76 us
    ppermute x4, starting transfers between devices, to_chips(): return lax.ppermute(value, ('core', 'row'), pairs)  4.98 us
    pallas_call x1, Pallas kernels, per_device(): pl.pallas_call(depart_kernel, name='depart', out_shape=(shard,) + (payloa...  2.03 us
  transfers between devices with their start and end apart: 28, of which 11 were waited for; matrix products, arithmetic and copies ran while one was open for 1% of the time, Pallas kernels for 20%

profile of v4, /device:TPU:0, one launch (start us, length us, event | category | flops | bytes accessed | tf_op | source)
XLA Modules:
  0.0 89.5 jit_solution(7989401704141178290)
XLA Ops:
  0.6 2.0 %depart.1 = (bf16[48,384]{1,0:T(8,128)(2,1)}, bf16[416,128]{1,0:T(8,128)(2,1)}, bf16[416,128]{1,0:T(8,128)(2,1)}, bf16[416,128]{1,0:T(8,128)(2,1)}, bf16[416,128]{1,0:T(8,128)(2,1)}) custom-call(bf16[24,48]{1,0:T(8,128)(2,1)} %bitcast.27, bf16[8,48]{1,0:T(8,128)(2,1)} %bitcast.29, bf16[8,48]{1,0:T(8,128)(2,1)} %bitcast.30, bf16[24,48]{1,0:T(8,128)(2,1)} %bitcast.28, ...), custom_call_target="tpu_custom_call" | custom-call | tf_op jit(solution)/shard_map/depart/pallas_call | solution.py:1100
  2.7 5.0 %collective-permute-start.7 = (bf16[48,384]{1,0:T(8,128)(2,1)}, bf16[48,384]{1,0:T(8,128)(2,1)S(1)}, u32[]{:S(2)}, u32[]{:S(2)}) collective-permute-start(bf16[48,384]{1,0:T(8,128)(2,1)} %get-tuple-element.100), channel_id=1, source_target_pairs={{0,24},{8,16},{16,8},{24,0},{1,25},{9,17},{17,9},{25,1},{2,26},{10... | collective-permute-start | bytes 110600 | tf_op jit(solution)/shard_map/ppermute | solution.py:1081
  8.3 1.5 %collective-permute-start = (bf16[416,128]{1,0:T(8,128)(2,1)}, bf16[416,128]{1,0:T(8,128)(2,1)S(1)}, u32[]{:S(2)}, u32[]{:S(2)}) collective-permute-start(bf16[416,128]{1,0:T(8,128)(2,1)} %get-tuple-element.90), channel_id=1, source_target_pairs={{0,0},{1,1},{2,4},{3,5},{4,2},{5,3},{6,6},{7,7},{8,8},{9,9},{10,12... | collective-permute-start | bytes 319496 | tf_op jit(solution)/shard_map/ppermute | solution.py:1090
  9.9 1.7 %collective-permute-start.1 = (bf16[416,128]{1,0:T(8,128)(2,1)}, bf16[416,128]{1,0:T(8,128)(2,1)S(1)}, u32[]{:S(2)}, u32[]{:S(2)}) collective-permute-start(bf16[416,128]{1,0:T(8,128)(2,1)} %get-tuple-element.91), channel_id=1, source_target_pairs={{0,1},{1,0},{2,5},{3,4},{4,3},{5,2},{6,7},{7,6},{8,9},{9,8},{10,13... | collective-permute-start | bytes 319496 | tf_op jit(solution)/shard_map/ppermute | solution.py:1090
  11.6 1.5 %collective-permute-start.2 = (bf16[416,128]{1,0:T(8,128)(2,1)}, bf16[416,128]{1,0:T(8,128)(2,1)S(1)}, u32[]{:S(2)}, u32[]{:S(2)}) collective-permute-start(bf16[416,128]{1,0:T(8,128)(2,1)} %get-tuple-element.92), channel_id=1, source_target_pairs={{0,4},{1,5},{2,0},{3,1},{4,6},{5,7},{6,2},{7,3},{8,12},{9,13},{10,... | collective-permute-start | bytes 319496 | tf_op jit(solution)/shard_map/ppermute | solution.py:1090
  13.3 0.8 pad_maximum_fusion.refs_6_.refs_0_
  14.1 2.7 %collective-permute-start.10 = (bf16[4,48,384]{2,1,0:T(8,128)(2,1)S(1)}, bf16[4,48,384]{2,1,0:T(8,128)(2,1)S(1)}, u32[]{:S(2)}, u32[]{:S(2)}) collective-permute-start(bf16[4,48,384]{2,1,0:T(8,128)(2,1)S(1)} %pad_maximum_fusion.refs_6_.refs_0_), channel_id=1, source_target_pairs={{0,3},{1,2},{2,1},{3,0},{4,7},{5,6},{6,5},{7,4},{8,11},{9,10},{10,... | collective-permute-start | bytes 442376 | tf_op jit(solution)/shard_map/ppermute | solution.py:1081
  17.1 1.1 %collective-permute-start.8 = (bf16[4,48,384]{2,1,0:T(8,128)(2,1)S(1)}, bf16[4,48,384]{2,1,0:T(8,128)(2,1)S(1)}, u32[]{:S(2)}, u32[]{:S(2)}) collective-permute-start(bf16[4,48,384]{2,1,0:T(8,128)(2,1)S(1)} %pad_maximum_fusion.refs_6_.refs_0_), channel_id=1, source_target_pairs={{0,1},{1,0},{2,3},{3,2},{4,5},{5,4},{6,7},{7,6},{8,9},{9,8},{10,11... | collective-permute-start | bytes 442376 | tf_op jit(solution)/shard_map/ppermute | solution.py:1081
  18.2 1.5 %collective-permute-done.2.refs_3_ = bf16[416,128]{1,0:T(8,128)(2,1)S(1)} collective-permute-done((bf16[416,128]{1,0:T(8,128)(2,1)}, bf16[416,128]{1,0:T(8,128)(2,1)S(1)}, u32[]{:S(2)}, u32[]{:S(2)}) %collective-permute-start.2) | collective-permute-done | bytes 106528 | tf_op jit(solution)/shard_map/ppermute | solution.py:1090
  20.1 0.7 copy-done.3
  20.7 1.1 %first_norm.1 = (bf16[4,2,128,192]{3,2,1,0:T(8,128)(2,1)S(1)}, bf16[512,192]{1,0:T(8,128)(2,1)S(1)}, f32[1024,128]{1,0:T(8,128)S(1)}, bf16[1024,192]{1,0:T(8,128...) custom-call(f32[2,192]{1,0:T(2,128)S(1)} %copy-done.3, ...), custom_call_target="tpu_custom_call" | custom-call | tf_op jit(solution)/shard_map/first_norm/pallas_call | solution.py:1145
  22.4 0.8 collective-permute-done.10.refs_9_.refs_3_
  23.2 3.0 %collective-permute-done.9.refs_8_.refs_2_ = bf16[4,48,384]{2,1,0:T(8,128)(2,1)S(1)} collective-permute-done((bf16[4,48,384]{2,1,0:T(8,128)(2,1)S(1)}, bf16[4,48,384]{2,1,0:T(8,128)(2,1)S(1)}, u32[]{:S(2)}, u32[]{:S(2)}) %collective-permute-start.9) | collective-permute-done | bytes 147488 | tf_op jit(solution)/shard_map/ppermute | solution.py:1081
  26.7 0.8 collective-permute-done.13.refs_12_.refs_6_
  27.7 8.7 %scan_forward.1 = (bf16[3,512,128]{2,1,0:T(8,128)(2,1)S(1)}, bf16[3,1024,128]{2,1,0:T(8,128)(2,1)S(1)}, bf16[3,1024,128]{2,1,0:T(8,128)(2,1)S(1)}, bf16[1024,192...) custom-call(bf16[512,192]{1,0:T(8,128)(2,1)S(1)} %get-tuple-element., ...), custom_call_target="tpu_custom_call" | custom-call | tf_op jit(solution)/shard_map/scan_forward/pallas_call | solution.py:1165
  36.5 10.3 %attention_and_feed_forward.1 = (bf16[3,1024,512]{2,1,0:T(8,128)(2,1)S(1)}, bf16[3,512,128]{2,1,0:T(8,128)(2,1)S(1)}, bf16[512,192]{1,0:T(8,128)(2,1)S(1)}, f32[...) custom-call(bf16[4,2,128,192]{3,2,1,0:T(8,128)(2,1)S(1)} %get-tuple-, ...), custom_call_target="tpu_custom_call" | custom-call | tf_op jit(solution)/shard_map/attention_and_feed_forward/pallas_call | solution.py:1188
  47.1 6.8 %attention_backward.1 = (bf16[1024,192]{1,0:T(8,128)(2,1)S(1)}, bf16[3,192,384]{2,1,0:T(8,128)(2,1)S(1)}) custom-call(bf16[3,1024,512]{2,1,0:T(8,128)(2,1)S(1)} %get-tuple-element.106.refs_0_, bf16[3,512,128]{2,1,0:T(8,128)(2,1)S(1)} %get-tuple-element.107.refs_1_, bf16[3,512,128]{2,1,0:T(8,128)(2,1)S(1)} %get-tuple-element.101.q_ref.refs_2_, ...), custom_call_target="tpu_custom_call" | custom-call | tf_op jit(solution)/shard_map/attention_backward/pallas_call | solution.py:1225
  54.3 1.4 %collective-permute-start.17 = (bf16[4,48,256]{2,1,0:T(8,128)(2,1)S(1)}, bf16[4,48,256]{2,1,0:T(8,128)(2,1)S(1)}, u32[]{:S(2)}, u32[]{:S(2)}) collective-permute-start(bf16[4,48,256]{2,1,0:T(8,128)(2,1)S(1)} %get-tuple-element.128), channel_id=1, source_target_pairs={{0,1},{1,0},{2,3},{3,2},{4,5},{5,4},{6,7},{7,6},{8,9},{9,8},{10,11... | collective-permute-start | bytes 294920 | tf_op jit(solution)/shard_map/ppermute | solution.py:1081
  56.1 1.6 %collective-permute-start.19 = (bf16[4,48,256]{2,1,0:T(8,128)(2,1)S(1)}, bf16[4,48,256]{2,1,0:T(8,128)(2,1)S(1)}, u32[]{:S(2)}, u32[]{:S(2)}) collective-permute-start(bf16[4,48,256]{2,1,0:T(8,128)(2,1)S(1)} %get-tuple-element.130), channel_id=1, source_target_pairs={{0,3},{1,2},{2,1},{3,0},{4,7},{5,6},{6,5},{7,4},{8,11},{9,10},{10,... | collective-permute-start | bytes 294920 | tf_op jit(solution)/shard_map/ppermute | solution.py:1081
  57.8 8.0 %scan_backward.1 = (bf16[17,48,128]{2,1,0:T(8,128)(2,1)S(1)}, bf16[17,48,128]{2,1,0:T(8,128)(2,1)S(1)}, f32[512,192]{1,0:T(8,128)S(1)}) custom-call(bf16[4,2,128,192]{3,2,1,0:T(8,128)(2,1)S(1)} %get-tuple-element.94.own_ref.refs_0_, f32[1024,128]{1,0:T(8,128)S(1)} %get-tuple-element.95.refs_2_.mask_ref.refs_1_, ...), custom_call_target="tpu_custom_call" | custom-call | tf_op jit(solution)/shard_map/scan_backward/pallas_call | solution.py:1255
  65.9 0.7 last_norm.1
  66.6 0.7 collective-permute-done.20.refs_1_
  67.4 1.5 %collective-permute-start.21 = (bf16[640,128]{1,0:T(8,128)(2,1)S(1)}, bf16[640,128]{1,0:T(8,128)(2,1)S(1)}, u32[]{:S(2)}, u32[]{:S(2)}) collective-permute-start(bf16[640,128]{1,0:T(8,128)(2,1)S(1)} %get-tuple-element.145), channel_id=1, source_target_pairs={{0,1},{1,0},{2,3},{3,2},{4,5},{5,4},{6,7},{7,6},{8,9},{9,8},{10,11... | collective-permute-start | bytes 491528 | tf_op jit(solution)/shard_map/ppermute | solution.py:1081
  69.3 1.6 %collective-permute-start.23 = (bf16[640,128]{1,0:T(8,128)(2,1)S(1)}, bf16[640,128]{1,0:T(8,128)(2,1)S(1)}, u32[]{:S(2)}, u32[]{:S(2)}) collective-permute-start(bf16[640,128]{1,0:T(8,128)(2,1)S(1)} %get-tuple-element.147), channel_id=1, source_target_pairs={{0,3},{1,2},{2,1},{3,0},{4,7},{5,6},{6,5},{7,4},{8,11},{9,10},{10,... | collective-permute-start | bytes 491528 | tf_op jit(solution)/shard_map/ppermute | solution.py:1081
  71.0 3.6 %collective-permute-done.21.refs_5_.refs_1_ = bf16[640,128]{1,0:T(8,128)(2,1)S(1)} collective-permute-done((bf16[640,128]{1,0:T(8,128)(2,1)S(1)}, bf16[640,128]{1,0:T(8,128)(2,1)S(1)}, u32[]{:S(2)}, u32[]{:S(2)}) %collective-permute-start.21) | collective-permute-done | bytes 163872 | tf_op jit(solution)/shard_map/ppermute | solution.py:1081
  74.5 3.9 %collective-permute-done.22.refs_6_.refs_2_ = bf16[640,128]{1,0:T(8,128)(2,1)S(1)} collective-permute-done((bf16[640,128]{1,0:T(8,128)(2,1)S(1)}, bf16[640,128]{1,0:T(8,128)(2,1)S(1)}, u32[]{:S(2)}, u32[]{:S(2)}) %collective-permute-start.22) | collective-permute-done | bytes 163872 | tf_op jit(solution)/shard_map/ppermute | solution.py:1081
  78.6 1.3 %collective-permute-start.24 = (bf16[64,384]{1,0:T(8,128)(2,1)S(1)}, bf16[64,384]{1,0:T(8,128)(2,1)S(1)}, u32[]{:S(2)}, u32[]{:S(2)}) collective-permute-start(bf16[64,384]{1,0:T(8,128)(2,1)S(1)} %get-tuple-element.149), channel_id=1, source_target_pairs={{0,8},{8,0},{16,24},{24,16},{1,9},{9,1},{17,25},{25,17},{2,10},{10... | collective-permute-start | bytes 147464 | tf_op jit(solution)/shard_map/ppermute | solution.py:1081
  79.9 2.9 %collective-permute-start.25 = (bf16[64,384]{1,0:T(8,128)(2,1)S(1)}, bf16[64,384]{1,0:T(8,128)(2,1)S(1)}, u32[]{:S(2)}, u32[]{:S(2)}) collective-permute-start(bf16[64,384]{1,0:T(8,128)(2,1)S(1)} %get-tuple-element.150), channel_id=1, source_target_pairs={{0,16},{8,24},{16,0},{24,8},{1,17},{9,25},{17,1},{25,9},{2,18},{10... | collective-permute-start | bytes 147464 | tf_op jit(solution)/shard_map/ppermute | solution.py:1081
  83.1 1.0 %home.1 = (bf16[2,256,192]{2,1,0:T(8,128)(2,1)}, bf16[2,256,192]{2,1,0:T(8,128)(2,1)}) custom-call(bf16[2,384,128]{2,1,0:T(8,128)(2,1)S(1)} %collective-permute-done.27.swapped_ref, bf16[640,128]{1,0:T(8,128)(2,1)S(1)} %get-tuple-element.144.refs_4_.refs_0_, bf16[640,128]{1,0:T(8,128)(2,1)S(1)} %collective-permute-done.21.refs_5_.refs_1_, ...), custom_call_target="tpu_custom_call" | custom-call | tf_op jit(solution)/shard_map/home/pallas_call | solution.py:1329
  84.1 2.0 %collective-permute-done.25.refs_2_ = bf16[64,384]{1,0:T(8,128)(2,1)S(1)} collective-permute-done((bf16[64,384]{1,0:T(8,128)(2,1)S(1)}, bf16[64,384]{1,0:T(8,128)(2,1)S(1)}, u32[]{:S(2)}, u32[]{:S(2)}) %collective-permute-start.25) | collective-permute-done | bytes 49184 | tf_op jit(solution)/shard_map/ppermute | solution.py:1081
  86.2 2.5 %collective-permute-done.26.refs_3_ = bf16[64,384]{1,0:T(8,128)(2,1)S(1)} collective-permute-done((bf16[64,384]{1,0:T(8,128)(2,1)S(1)}, bf16[64,384]{1,0:T(8,128)(2,1)S(1)}, u32[]{:S(2)}, u32[]{:S(2)}) %collective-permute-start.26) | collective-permute-done | bytes 49184 | tf_op jit(solution)/shard_map/ppermute | solution.py:1081
  88.7 0.8 final_sum.1
  (48 shorter events, 5.1 us)
Async XLA Ops:
  2.7 8.9 %collective-permute-start.7 = (bf16[48,384]{1,0:T(8,128)(2,1)}, bf16[48,384]{1,0:T(8,128)(2,1)S(1)}, u32[]{:S(2)}, u32[]{:S(2)}) collective-permute-start(bf16[48,384]{1,0:T(8,128)(2,1)} %get-tuple-element.100), channel_id=1, source_target_pairs={{0,24},{8,16},{16,8},{24,0},{1,25},{9,17},{17,9},{25,1},{2,26},{10... | collective-permute-start | bytes 110600 | tf_op jit(solution)/shard_map/ppermute | solution.py:1081
  7.7 5.3 %collective-permute-start.6 = (bf16[48,384]{1,0:T(8,128)(2,1)}, bf16[48,384]{1,0:T(8,128)(2,1)S(1)}, u32[]{:S(2)}, u32[]{:S(2)}) collective-permute-start(bf16[48,384]{1,0:T(8,128)(2,1)} %get-tuple-element.100), channel_id=1, source_target_pairs={{0,16},{8,24},{16,0},{24,8},{1,17},{9,25},{17,1},{25,9},{2,18},{10... | collective-permute-start | bytes 110600 | tf_op jit(solution)/shard_map/ppermute | solution.py:1081
  7.7 5.6 %collective-permute-start.5 = (bf16[48,384]{1,0:T(8,128)(2,1)}, bf16[48,384]{1,0:T(8,128)(2,1)S(1)}, u32[]{:S(2)}, u32[]{:S(2)}) collective-permute-start(bf16[48,384]{1,0:T(8,128)(2,1)} %get-tuple-element.100), channel_id=1, source_target_pairs={{0,8},{8,0},{16,24},{24,16},{1,9},{9,1},{17,25},{25,17},{2,10},{10... | collective-permute-start | bytes 110600 | tf_op jit(solution)/shard_map/ppermute | solution.py:1081
  8.3 8.5 %collective-permute-start = (bf16[416,128]{1,0:T(8,128)(2,1)}, bf16[416,128]{1,0:T(8,128)(2,1)S(1)}, u32[]{:S(2)}, u32[]{:S(2)}) collective-permute-start(bf16[416,128]{1,0:T(8,128)(2,1)} %get-tuple-element.90), channel_id=1, source_target_pairs={{0,0},{1,1},{2,4},{3,5},{4,2},{5,3},{6,6},{7,7},{8,8},{9,9},{10,12... | collective-permute-start | bytes 319496 | tf_op jit(solution)/shard_map/ppermute | solution.py:1090
  9.9 7.2 %collective-permute-start.1 = (bf16[416,128]{1,0:T(8,128)(2,1)}, bf16[416,128]{1,0:T(8,128)(2,1)S(1)}, u32[]{:S(2)}, u32[]{:S(2)}) collective-permute-start(bf16[416,128]{1,0:T(8,128)(2,1)} %get-tuple-element.91), channel_id=1, source_target_pairs={{0,1},{1,0},{2,5},{3,4},{4,3},{5,2},{6,7},{7,6},{8,9},{9,8},{10,13... | collective-permute-start | bytes 319496 | tf_op jit(solution)/shard_map/ppermute | solution.py:1090
  11.6 8.1 %collective-permute-start.2 = (bf16[416,128]{1,0:T(8,128)(2,1)}, bf16[416,128]{1,0:T(8,128)(2,1)S(1)}, u32[]{:S(2)}, u32[]{:S(2)}) collective-permute-start(bf16[416,128]{1,0:T(8,128)(2,1)} %get-tuple-element.92), channel_id=1, source_target_pairs={{0,4},{1,5},{2,0},{3,1},{4,6},{5,7},{6,2},{7,3},{8,12},{9,13},{10,... | collective-permute-start | bytes 319496 | tf_op jit(solution)/shard_map/ppermute | solution.py:1090
  13.1 7.0 %collective-permute-start.3 = (bf16[416,128]{1,0:T(8,128)(2,1)}, bf16[416,128]{1,0:T(8,128)(2,1)S(1)}, u32[]{:S(2)}, u32[]{:S(2)}) collective-permute-start(bf16[416,128]{1,0:T(8,128)(2,1)} %get-tuple-element.93), channel_id=1, source_target_pairs={{0,5},{1,4},{2,1},{3,0},{4,7},{5,6},{6,3},{7,2},{8,13},{9,12},{10,... | collective-permute-start | bytes 319496 | tf_op jit(solution)/shard_map/ppermute | solution.py:1090
  14.1 9.0 %collective-permute-start.10 = (bf16[4,48,384]{2,1,0:T(8,128)(2,1)S(1)}, bf16[4,48,384]{2,1,0:T(8,128)(2,1)S(1)}, u32[]{:S(2)}, u32[]{:S(2)}) collective-permute-start(bf16[4,48,384]{2,1,0:T(8,128)(2,1)S(1)} %pad_maximum_fusion.refs_6_.refs_0_), channel_id=1, source_target_pairs={{0,3},{1,2},{2,1},{3,0},{4,7},{5,6},{6,5},{7,4},{8,11},{9,10},{10,... | collective-permute-start | bytes 442376 | tf_op jit(solution)/shard_map/ppermute | solution.py:1081
  16.9 9.3 %collective-permute-start.9 = (bf16[4,48,384]{2,1,0:T(8,128)(2,1)S(1)}, bf16[4,48,384]{2,1,0:T(8,128)(2,1)S(1)}, u32[]{:S(2)}, u32[]{:S(2)}) collective-permute-start(bf16[4,48,384]{2,1,0:T(8,128)(2,1)S(1)} %pad_maximum_fusion.refs_6_.refs_0_), channel_id=1, source_target_pairs={{0,2},{1,3},{2,0},{3,1},{4,6},{5,7},{6,4},{7,5},{8,10},{9,11},{10,... | collective-permute-start | bytes 442376 | tf_op jit(solution)/shard_map/ppermute | solution.py:1081
  17.1 9.1 %collective-permute-start.8 = (bf16[4,48,384]{2,1,0:T(8,128)(2,1)S(1)}, bf16[4,48,384]{2,1,0:T(8,128)(2,1)S(1)}, u32[]{:S(2)}, u32[]{:S(2)}) collective-permute-start(bf16[4,48,384]{2,1,0:T(8,128)(2,1)S(1)} %pad_maximum_fusion.refs_6_.refs_0_), channel_id=1, source_target_pairs={{0,1},{1,0},{2,3},{3,2},{4,5},{5,4},{6,7},{7,6},{8,9},{9,8},{10,11... | collective-permute-start | bytes 442376 | tf_op jit(solution)/shard_map/ppermute | solution.py:1081
  21.8 4.8 %collective-permute-start.4 = (bf16[512,192]{1,0:T(8,128)(2,1)S(1)}, bf16[512,192]{1,0:T(8,128)(2,1)S(1)}, u32[]{:S(2)}, u32[]{:S(2)}) collective-permute-start(bf16[512,192]{1,0:T(8,128)(2,1)S(1)} %get-tuple-element.96.refs_0_.refs_5_), channel_id=1, source_target_pairs={{0,4},{4,0},{1,5},{5,1},{2,6},{6,2},{3,7},{7,3},{8,12},{12,8},{9,1... | collective-permute-start | bytes 589832 | tf_op jit(solution)/shard_map/ppermute | solution.py:1076
  21.9 4.7 %collective-permute-start.11 = (bf16[4,48,384]{2,1,0:T(8,128)(2,1)S(1)}, bf16[4,48,384]{2,1,0:T(8,128)(2,1)S(1)}, u32[]{:S(2)}, u32[]{:S(2)}) collective-permute-start(bf16[4,48,384]{2,1,0:T(8,128)(2,1)S(1)} %pad_maximum_fusion.refs_6_.refs_0_), channel_id=1, source_target_pairs={{0,4},{4,0},{1,5},{5,1},{2,6},{6,2},{3,7},{7,3},{8,12},{12,8},{9,1... | collective-permute-start | bytes 442376 | tf_op jit(solution)/shard_map/ppermute | solution.py:1076
  23.2 3.5 %collective-permute-start.14 = (bf16[4,48,384]{2,1,0:T(8,128)(2,1)S(1)}, bf16[4,48,384]{2,1,0:T(8,128)(2,1)S(1)}, u32[]{:S(2)}, u32[]{:S(2)}) collective-permute-start(bf16[4,48,384]{2,1,0:T(8,128)(2,1)S(1)} %collective-permute-done.10.refs_9_.refs_3_), channel_id=1, source_target_pairs={{0,4},{4,0},{1,5},{5,1},{2,6},{6,2},{3,7},{7,3},{8,12},{12,8},{9,1... | collective-permute-start | bytes 442376 | tf_op jit(solution)/shard_map/ppermute | solution.py:1076
  26.1 1.4 %collective-permute-start.13 = (bf16[4,48,384]{2,1,0:T(8,128)(2,1)S(1)}, bf16[4,48,384]{2,1,0:T(8,128)(2,1)S(1)}, u32[]{:S(2)}, u32[]{:S(2)}) collective-permute-start(bf16[4,48,384]{2,1,0:T(8,128)(2,1)S(1)} %collective-permute-done.9.refs_8_.refs_2_), channel_id=1, source_target_pairs={{0,4},{4,0},{1,5},{5,1},{2,6},{6,2},{3,7},{7,3},{8,12},{12,8},{9,1... | collective-permute-start | bytes 442376 | tf_op jit(solution)/shard_map/ppermute | solution.py:1076
  26.2 1.5 %collective-permute-start.12 = (bf16[4,48,384]{2,1,0:T(8,128)(2,1)S(1)}, bf16[4,48,384]{2,1,0:T(8,128)(2,1)S(1)}, u32[]{:S(2)}, u32[]{:S(2)}) collective-permute-start(bf16[4,48,384]{2,1,0:T(8,128)(2,1)S(1)} %collective-permute-done.8.refs_7_.refs_1_), channel_id=1, source_target_pairs={{0,4},{4,0},{1,5},{5,1},{2,6},{6,2},{3,7},{7,3},{8,12},{12,8},{9,1... | collective-permute-start | bytes 442376 | tf_op jit(solution)/shard_map/ppermute | solution.py:1076
  27.7 8.7 %copy-start = (bf16[4,1024,192]{2,1,0:T(8,128)(2,1)S(1)}, bf16[4,1024,192]{2,1,0:T(8,128)(2,1)}, u32[]{:S(2)}) copy-start(bf16[4,1024,192]{2,1,0:T(8,128)(2,1)} %constant.8.clone.sel_2_ref) | copy-start | bytes 4718596
  27.7 8.7 %copy-start.1 = (bf16[1024,192]{1,0:T(8,128)(2,1)S(1)}, bf16[1024,192]{1,0:T(8,128)(2,1)}, u32[]{:S(2)}) copy-start(bf16[1024,192]{1,0:T(8,128)(2,1)} %constant.7.clone.sel_o_ref) | copy-start | bytes 1179652
  27.7 8.7 %copy-start.2 = (bf16[512,384]{1,0:T(8,128)(2,1)S(1)}, bf16[512,384]{1,0:T(8,128)(2,1)}, u32[]{:S(2)}) copy-start(bf16[512,384]{1,0:T(8,128)(2,1)} %constant.6.clone.sel_1_ref) | copy-start | bytes 1179652
  27.7 8.7 %copy-start.4 = (f32[2,192]{1,0:T(2,128)S(1)}, f32[2,192]{1,0:T(2,128)}, u32[]{:S(2)}) copy-start(f32[2,192]{1,0:T(2,128)} %gains_ref.3) | copy-start | bytes 4612
  46.7 7.2 %collective-permute-start.15 = (bf16[4,4,48,256]{3,2,1,0:T(8,128)(2,1)S(1)}, bf16[4,4,48,256]{3,2,1,0:T(8,128)(2,1)S(1)}, u32[]{:S(2)}, u32[]{:S(2)}) collective-permute-start(bf16[4,4,48,256]{3,2,1,0:T(8,128)(2,1)S(1)} %get-tuple-element.105), channel_id=1, source_target_pairs={{0,4},{4,0},{1,5},{5,1},{2,6},{6,2},{3,7},{7,3},{8,12},{12,8},{9,1... | collective-permute-start | bytes 1179656 | tf_op jit(solution)/shard_map/ppermute | solution.py:1076
  54.0 3.7 %collective-permute-start.16 = (bf16[1024,192]{1,0:T(8,128)(2,1)S(1)}, bf16[1024,192]{1,0:T(8,128)(2,1)S(1)}, u32[]{:S(2)}, u32[]{:S(2)}) collective-permute-start(bf16[1024,192]{1,0:T(8,128)(2,1)S(1)} %get-tuple-element.118.refs_2_), channel_id=1, source_target_pairs={{0,4},{4,0},{1,5},{5,1},{2,6},{6,2},{3,7},{7,3},{8,12},{12,8},{9,1... | collective-permute-start | bytes 1179656 | tf_op jit(solution)/shard_map/ppermute | solution.py:1076
  54.3 11.5 %collective-permute-start.17 = (bf16[4,48,256]{2,1,0:T(8,128)(2,1)S(1)}, bf16[4,48,256]{2,1,0:T(8,128)(2,1)S(1)}, u32[]{:S(2)}, u32[]{:S(2)}) collective-permute-start(bf16[4,48,256]{2,1,0:T(8,128)(2,1)S(1)} %get-tuple-element.128), channel_id=1, source_target_pairs={{0,1},{1,0},{2,3},{3,2},{4,5},{5,4},{6,7},{7,6},{8,9},{9,8},{10,11... | collective-permute-start | bytes 294920 | tf_op jit(solution)/shard_map/ppermute | solution.py:1081
  55.7 10.1 %collective-permute-start.18 = (bf16[4,48,256]{2,1,0:T(8,128)(2,1)S(1)}, bf16[4,48,256]{2,1,0:T(8,128)(2,1)S(1)}, u32[]{:S(2)}, u32[]{:S(2)}) collective-permute-start(bf16[4,48,256]{2,1,0:T(8,128)(2,1)S(1)} %get-tuple-element.129), channel_id=1, source_target_pairs={{0,2},{1,3},{2,0},{3,1},{4,6},{5,7},{6,4},{7,5},{8,10},{9,11},{10,... | collective-permute-start | bytes 294920 | tf_op jit(solution)/shard_map/ppermute | solution.py:1081
  56.1 9.7 %collective-permute-start.19 = (bf16[4,48,256]{2,1,0:T(8,128)(2,1)S(1)}, bf16[4,48,256]{2,1,0:T(8,128)(2,1)S(1)}, u32[]{:S(2)}, u32[]{:S(2)}) collective-permute-start(bf16[4,48,256]{2,1,0:T(8,128)(2,1)S(1)} %get-tuple-element.130), channel_id=1, source_target_pairs={{0,3},{1,2},{2,1},{3,0},{4,7},{5,6},{6,5},{7,4},{8,11},{9,10},{10,... | collective-permute-start | bytes 294920 | tf_op jit(solution)/shard_map/ppermute | solution.py:1081
  65.8 1.5 %collective-permute-start.20 = (bf16[17,48,128]{2,1,0:T(8,128)(2,1)S(1)}, bf16[17,48,128]{2,1,0:T(8,128)(2,1)S(1)}, u32[]{:S(2)}, u32[]{:S(2)}) collective-permute-start(bf16[17,48,128]{2,1,0:T(8,128)(2,1)S(1)} %get-tuple-element.136), channel_id=1, source_target_pairs={{0,4},{4,0},{1,5},{5,1},{2,6},{6,2},{3,7},{7,3},{8,12},{12,8},{9,1... | collective-permute-start | bytes 626696 | tf_op jit(solution)/shard_map/ppermute | solution.py:1076
  67.4 7.1 %collective-permute-start.21 = (bf16[640,128]{1,0:T(8,128)(2,1)S(1)}, bf16[640,128]{1,0:T(8,128)(2,1)S(1)}, u32[]{:S(2)}, u32[]{:S(2)}) collective-permute-start(bf16[640,128]{1,0:T(8,128)(2,1)S(1)} %get-tuple-element.145), channel_id=1, source_target_pairs={{0,1},{1,0},{2,3},{3,2},{4,5},{5,4},{6,7},{7,6},{8,9},{9,8},{10,11... | collective-permute-start | bytes 491528 | tf_op jit(solution)/shard_map/ppermute | solution.py:1081
  68.9 9.5 %collective-permute-start.22 = (bf16[640,128]{1,0:T(8,128)(2,1)S(1)}, bf16[640,128]{1,0:T(8,128)(2,1)S(1)}, u32[]{:S(2)}, u32[]{:S(2)}) collective-permute-start(bf16[640,128]{1,0:T(8,128)(2,1)S(1)} %get-tuple-element.146), channel_id=1, source_target_pairs={{0,2},{1,3},{2,0},{3,1},{4,6},{5,7},{6,4},{7,5},{8,10},{9,11},{10,... | collective-permute-start | bytes 491528 | tf_op jit(solution)/shard_map/ppermute | solution.py:1081
  69.3 9.1 %collective-permute-start.23 = (bf16[640,128]{1,0:T(8,128)(2,1)S(1)}, bf16[640,128]{1,0:T(8,128)(2,1)S(1)}, u32[]{:S(2)}, u32[]{:S(2)}) collective-permute-start(bf16[640,128]{1,0:T(8,128)(2,1)S(1)} %get-tuple-element.147), channel_id=1, source_target_pairs={{0,3},{1,2},{2,1},{3,0},{4,7},{5,6},{6,5},{7,4},{8,11},{9,10},{10,... | collective-permute-start | bytes 491528 | tf_op jit(solution)/shard_map/ppermute | solution.py:1081
  78.4 4.6 %collective-permute-start.27 = (bf16[2,384,128]{2,1,0:T(8,128)(2,1)S(1)}, bf16[2,384,128]{2,1,0:T(8,128)(2,1)S(1)}, u32[]{:S(2)}, u32[]{:S(2)}) collective-permute-start(bf16[2,384,128]{2,1,0:T(8,128)(2,1)S(1)} %choose.1), channel_id=1, source_target_pairs={{0,4},{4,0},{1,5},{5,1},{2,6},{6,2},{3,7},{7,3},{8,12},{12,8},{9,1... | collective-permute-start | bytes 589832 | tf_op jit(solution)/shard_map/ppermute | solution.py:1076
  78.6 5.5 %collective-permute-start.24 = (bf16[64,384]{1,0:T(8,128)(2,1)S(1)}, bf16[64,384]{1,0:T(8,128)(2,1)S(1)}, u32[]{:S(2)}, u32[]{:S(2)}) collective-permute-start(bf16[64,384]{1,0:T(8,128)(2,1)S(1)} %get-tuple-element.149), channel_id=1, source_target_pairs={{0,8},{8,0},{16,24},{24,16},{1,9},{9,1},{17,25},{25,17},{2,10},{10... | collective-permute-start | bytes 147464 | tf_op jit(solution)/shard_map/ppermute | solution.py:1081
  79.9 6.3 %collective-permute-start.25 = (bf16[64,384]{1,0:T(8,128)(2,1)S(1)}, bf16[64,384]{1,0:T(8,128)(2,1)S(1)}, u32[]{:S(2)}, u32[]{:S(2)}) collective-permute-start(bf16[64,384]{1,0:T(8,128)(2,1)S(1)} %get-tuple-element.150), channel_id=1, source_target_pairs={{0,16},{8,24},{16,0},{24,8},{1,17},{9,25},{17,1},{25,9},{2,18},{10... | collective-permute-start | bytes 147464 | tf_op jit(solution)/shard_map/ppermute | solution.py:1081
  82.8 5.9 %collective-permute-start.26 = (bf16[64,384]{1,0:T(8,128)(2,1)S(1)}, bf16[64,384]{1,0:T(8,128)(2,1)S(1)}, u32[]{:S(2)}, u32[]{:S(2)}) collective-permute-start(bf16[64,384]{1,0:T(8,128)(2,1)S(1)} %get-tuple-element.151), channel_id=1, source_target_pairs={{0,24},{8,16},{16,8},{24,0},{1,25},{9,17},{17,9},{25,1},{2,26},{10... | collective-permute-start | bytes 147464 | tf_op jit(solution)/shard_map/ppermute | solution.py:1081
  (1 other events, 0.7 us)

commit v5 on v4

--- a/solution.py
+++ b/solution.py
@@ -292,21 +292,31 @@
     put_late_selections(starts, parts, *selections)
 
 
-def results_of(ref, rows):
-    start = ref.shape[0] - 2 * rows
-    return ref[start : start + rows], ref[start + rows :]
+def fold(packed):
+    half = packed.shape[0] // 2
+    return jnp.concatenate([packed[:half], packed[half:]], axis=1)
+
+
+def unfold(folded):
+    return jnp.concatenate([folded[:, :LANES], folded[:, LANES:]], axis=0)
+
+
+def results_of(early_ref, late_ref, rows):
+    early_start, late_start = early_ref.shape[0] - rows // 2, late_ref.shape[0] - rows
+    return unfold(early_ref[early_start:]), late_ref[late_start:]
 
 
 def choose_kernel(*refs):
     got_refs, out_ref = refs[:-1], refs[-1]
+    blocks = len(got_refs) // 2
     core, row = lax.axis_index("core"), lax.axis_index("row")
     images, rows = out_ref.shape[0], out_ref.shape[1] // 2
-    for k, got in enumerate(got_refs):
+    for k, got in enumerate(zip(got_refs[:blocks], got_refs[blocks:])):
         image = row ^ k
 
         @pl.when(image // images != core)
         def _(got=got, image=image):
-            for which, value in enumerate(results_of(got, rows)):
+            for which, value in enumerate(results_of(*got, rows)):
                 out_ref[image % images, which * rows : (which + 1) * rows] = value
 
 
@@ -316,14 +326,15 @@
     images, slots, _ = out_refs[0].shape
     half = slots // 2
     rows = half * 3 // 2
+    blocks = len(got_refs) // 2
     mine = pl.ds(pl.multiple_of(core * half, half), half)
     theirs = pl.ds(pl.multiple_of((1 - core) * half, half), half)
-    for k, got in enumerate(got_refs):
+    for k, got in enumerate(zip(got_refs[:blocks], got_refs[blocks:])):
         image = row ^ k
 
         @pl.when(image // images == core)
         def _(got=got, image=image):
-            for out_ref, value in zip(out_refs, results_of(got, rows)):
+            for out_ref, value in zip(out_refs, results_of(*got, rows)):
                 out_ref[image % images, mine, :] = unpack(value)
 
     for image in range(images):
@@ -427,7 +438,7 @@
             store_lag(way, -k, found[2 * way + 1])
         return 0
 
-    lax.fori_loop(0, GRID, lag_step, 0, unroll=4)
+    lax.fori_loop(0, GRID, lag_step, 0, unroll=True)
     found = lag_row(0.0)
     for way in range(2):
         store_lag(way, 0, found[2 * way] + found[2 * way + 1])
@@ -456,7 +467,7 @@
                     dst[kind][pl.ds(place, 8), :] = total[t]
         return 0
 
-    lax.fori_loop(0, 8, scan_step, 0)
+    lax.fori_loop(0, 8, scan_step, 0, unroll=2)
 
     def join_step(i, _):
         for row, value in join_rows(i, GRID, rows, cols):
@@ -464,7 +475,7 @@
             scanned_ref[place, :] = (value * widen(mask_ref[place, :])).astype(BF16)
         return 0
 
-    lax.fori_loop(0, GRID // 2, join_step, 0, unroll=2)
+    lax.fori_loop(0, GRID // 2, join_step, 0, unroll=True)
 
     for block in range(blocks):
         start = pl.multiple_of((block * 2 + core) * rows_slots, rows_slots)
@@ -581,7 +592,7 @@
             values = scores[pl.ds(pl.multiple_of(i * 64, 64), 64), :]
             return jnp.maximum(top, jnp.max(values.reshape(8, 8, OWN), 0))
 
-        top = lax.fori_loop(1, SLOTS // 64, top_step, jnp.max(scores[:64].reshape(8, 8, OWN), 0))
+        top = lax.fori_loop(1, SLOTS // 64, top_step, jnp.max(scores[:64].reshape(8, 8, OWN), 0), unroll=True)
         top = jnp.max(top, 0, keepdims=True)
 
         def soft_step(i, _, h=h, top=top):
@@ -589,7 +600,7 @@
             soft_ref[h, place, :] = jnp.exp(scores[place, :] - top).astype(BF16)
             return 0
 
-        lax.fori_loop(0, SLOTS // 128, soft_step, 0)
+        lax.fori_loop(0, SLOTS // 128, soft_step, 0, unroll=True)
         raw = dot_tn(soft_ref[h], v_ref[h])
         total = raw[:, HEAD_DIM : HEAD_DIM + 1]
         sums[h] = jnp.broadcast_to(1.0 / total, (OWN, LANES))
@@ -628,7 +639,7 @@
         grad_pre[place, :] = (grad_hidden[place, :] * slope).astype(BF16)
         return 0
 
-    lax.fori_loop(0, OWN // 16, gelu_step, 0, unroll=2)
+    lax.fori_loop(0, OWN // 16, gelu_step, 0, unroll=True)
 
     out_ref[...] = (middle[...] + dot(hidden[...], w2[...])).astype(BF16)
     grad_2 = dot_tn(hidden[...], cot).astype(BF16)
@@ -722,7 +733,7 @@
             )
             return 0
 
-        lax.fori_loop(0, SLOTS // 64, back_step, 0)
+        lax.fori_loop(0, SLOTS // 64, back_step, 0, unroll=True)
         grad_q[:, tile] = (dot_tn(grad_scores[...], k_ref[h]).astype(BF16) * HEAD_DIM ** (-0.5)).astype(
             BF16
         )
@@ -819,7 +830,7 @@
                 rows[kind][pl.ds(place, 8), :] = total[t]
         return 0
 
-    lax.fori_loop(0, 4, row_step, 0)
+    lax.fori_loop(0, 4, row_step, 0, unroll=True)
 
     def col_step(index, _):
         block = index // 2
@@ -901,7 +912,7 @@
             mixed_back[place, :] = (value * widen(mask)).astype(BF16)
         return 0
 
-    lax.fori_loop(0, own_rows // 2, join_step, 0, unroll=2)
+    lax.fori_loop(0, own_rows // 2, join_step, 0, unroll=True)
     grad_u = dot_tn(first_ref[...], mixed_back[...]).astype(BF16)
     grad_first = dot_nt(mixed_back[...], wu_ref[...])
     back_ref[...] = grad_first
@@ -935,23 +946,23 @@
         ref[ref.shape[0] - 1, 8:] = jnp.zeros((ref.shape[1] - 8, LANES), BF16)
 
 
-def last_norm_kernel(
-    own_ref, gains_ref, back_ref, grad_middle_ref, out_own_ref, *routed_refs
-):
+def last_norm_kernel(own_ref, gains_ref, back_ref, grad_middle_ref, *routed_refs):
     _, _, slots, _ = own_ref.shape
-    rows = slots * 3 // 2
     gain = gains_ref[0:1, :]
     for k, routed in enumerate(routed_refs):
         block = lax.axis_index("row") ^ k
         place = pl.ds(pl.multiple_of(block * slots, slots), slots)
         unit, inverse = normalise(own_ref[block, 0].astype(F32))
         grad = grad_middle_ref[place, :] + norm_back(back_ref[place, :], gain, unit, inverse)
-        routed[:rows] = pack(out_own_ref[place, :])
-        routed[rows:] = pack(grad.astype(BF16))
-
-
-def late_rows(rows):
-    return (rows + 31) // 16 * 16
+        routed[...] = pack(grad.astype(BF16))
+
+
+def aligned(rows):
+    return (rows + 15) // 16 * 16
+
+
+def spare_lanes(rows, parts):
+    return rows >= 32 and 4 * (D // parts) + 32 <= LANES
 
 
 def split(value):
@@ -959,19 +970,24 @@
     return jnp.concatenate([high, value - high], axis=0)
 
 
-def early_sum_kernel(keep_ref, got_ref, *out_refs):
+def early_sum_kernel(out_own_ref, keep_ref, got_ref, *out_refs):
+    _, depth, rows, _ = keep_ref.shape
+    slots = OWN // len(out_refs)
+    block_rows = aligned(rows)
     for k, out_ref in enumerate(out_refs):
         block = lax.axis_index("row") ^ k
-        for z in range(keep_ref.shape[1]):
+        for z in range(depth):
             total = keep_ref[block, z].astype(F32) + got_ref[block, z].astype(F32)
-            out_ref[z] = total.astype(BF16)
+            out_ref[z * block_rows : z * block_rows + rows] = total.astype(BF16)
+        place = pl.ds(pl.multiple_of(block * slots, slots), slots)
+        out_ref[depth * block_rows :] = fold(pack(out_own_ref[place, :]))
 
 
 def late_sum_kernel(depth, keep_ref, got_ref, *refs):
     count = len(refs) // 2
     routed_refs, out_refs = refs[:count], refs[count:]
     rows = keep_ref.shape[1]
-    block_rows = late_rows(rows)
+    block_rows = aligned(rows)
     last = keep_ref.shape[0] - 1
     gains = keep_ref[last, :8].astype(F32) + got_ref[last, :8].astype(F32)
     lines = []
@@ -980,40 +996,43 @@
             at = 4 * g + lane
             lines.append(gains[at : at + 1] + gains[at + 2 : at + 3])
     gains = split(jnp.concatenate(lines, axis=0))
-    gains = jnp.concatenate([gains, jnp.zeros((8, LANES), F32)], axis=0)
-    fill = jnp.zeros((block_rows - rows - 16, LANES), F32)
+    gains = jnp.concatenate([gains, jnp.zeros((8, LANES), F32)], axis=0).astype(BF16)
     for k, out_ref in enumerate(out_refs):
         block = lax.axis_index("row") ^ k
         for z in range(depth):
             at = block * depth + z
             total = keep_ref[at].astype(F32) + got_ref[at].astype(F32)
-            pieces = [gains, total]
-            if block_rows > rows + 16:
-                pieces.append(fill)
-            out_ref[z * block_rows : (z + 1) * block_rows] = jnp.concatenate(pieces, axis=0).astype(
-                BF16
-            )
-        out_ref[depth * block_rows :] = routed_refs[k][...]
-
-
-def row_sum_kernel(blocks, *refs):
+            out_ref[z * block_rows : z * block_rows + rows] = total.astype(BF16)
+        out_ref[depth * block_rows : depth * block_rows + 16] = gains
+        out_ref[depth * block_rows + 16 :] = routed_refs[k][...]
+
+
+def row_sum_kernel(blocks, depth, rows, *refs):
     early_refs, late_refs, out_refs = refs[:blocks], refs[blocks : 2 * blocks], refs[2 * blocks :]
-    rows = early_refs[0].shape[1]
-    block_rows = late_rows(rows)
+    block_rows = aligned(rows)
+    gains = late_refs[0][depth * block_rows : depth * block_rows + 16].astype(F32)
+    for k in range(1, blocks):
+        gains = gains + late_refs[k][depth * block_rows : depth * block_rows + 16].astype(F32)
+    gains = split(gains[:4] + gains[4:8])
     for j, out_ref in enumerate(out_refs):
         z = lax.axis_index("z") ^ j
         place = pl.ds(pl.multiple_of(z * block_rows, 16), block_rows)
-        early = early_refs[0][z].astype(F32)
+        early = early_refs[0][place, :].astype(F32)
         late = late_refs[0][place, :].astype(F32)
         for k in range(1, blocks):
-            early = early + early_refs[k][z].astype(F32)
+            early = early + early_refs[k][place, :].astype(F32)
             late = late + late_refs[k][place, :].astype(F32)
-        out_ref[:rows, LANES:] = early.astype(BF16)
-        out_ref[:rows, :LANES] = late[16 : 16 + rows].astype(BF16)
-        gains = split(late[:4] + late[4:8])
-        gains = jnp.concatenate([gains, jnp.zeros((8, LANES), F32)], axis=0).astype(BF16)
-        out_ref[rows:, :LANES] = gains
-        out_ref[rows:, LANES:] = jnp.zeros((16, 2 * LANES), BF16)
+        if spare_lanes(rows, 2 * depth):
+            chunks = [gains[:, q * 32 : (q + 1) * 32] for q in range(4)]
+            chunks.append(jnp.zeros((rows - 32, 32), F32))
+            early = jnp.concatenate([early[:, :-32], jnp.concatenate(chunks, axis=0)], axis=1)
+        else:
+            out_ref[rows:, :LANES] = jnp.concatenate(
+                [gains, jnp.zeros((8, LANES), F32)], axis=0
+            ).astype(BF16)
+            out_ref[rows:, LANES:] = jnp.zeros((16, 2 * LANES), BF16)
+        out_ref[:rows, LANES:] = early[:rows].astype(BF16)
+        out_ref[:rows, :LANES] = late[:rows].astype(BF16)
 
 
 def final_kernel(parts, *refs):
@@ -1040,7 +1059,13 @@
     early = total[: fc1_ref.shape[0], LANES:]
     total = total[:, :LANES]
     rows = fc1_ref.shape[0]
-    weights, gains = total[:rows], total[rows:]
+    weights = total[:rows]
+    if spare_lanes(rows, parts):
+        gains = jnp.concatenate(
+            [early[q * 8 : (q + 1) * 8, 2 * LANES - 32 :] for q in range(4)], axis=1
+        )
+    else:
+        gains = total[rows:]
     turned = weights.T
     wu_ref[...] = turned[o_u : o_u + a_u]
     rate_ref[...] = turned[o_r : o_r + a_r]
@@ -1240,14 +1265,15 @@
     )(soft, lifted, q, k, v, scanned, wqkv)
 
     early_keep, early_recv, part = lax.optimization_barrier((early_keep, early_recv, part))
+    payload = shape((depth * aligned(rows_weight) + packed_rows // 2, 2 * LANES), BF16)
     early = pl.pallas_call(
         early_sum_kernel,
         name="early_sum",
-        out_shape=(shape((depth, rows_weight, 2 * LANES), BF16),) * blocks,
-        in_specs=[VMEM] * 2,
+        out_shape=(payload,) * blocks,
+        in_specs=[VMEM] * 3,
         out_specs=[VMEM] * blocks,
         compiler_params=compiler(8 << 20),
-    )(early_keep, early_recv)
+    )(out_own, early_keep, early_recv)
     early, part = lax.optimization_barrier((early, part))
     part_got = swapped(part)
     early = exchanged(early, "row")
@@ -1288,16 +1314,16 @@
         sel_q,
     )
     late_keep, late_send, early = lax.optimization_barrier((late_keep, late_send, early))
-    payload = shape((2 * packed_rows, LANES), BF16)
+    payload = shape((packed_rows, LANES), BF16)
     routed = pl.pallas_call(
         last_norm_kernel,
         name="last_norm",
         out_shape=(payload,) * blocks,
-        in_specs=[VMEM] * 5,
+        in_specs=[VMEM] * 4,
         out_specs=[VMEM] * blocks,
         compiler_params=compiler(8 << 20),
-    )(own, norm_gains, back, grad_middle, out_own)
-    payload = shape((depth * late_rows(rows_weight) + 2 * packed_rows, LANES), BF16)
+    )(own, norm_gains, back, grad_middle)
+    payload = shape((depth * aligned(rows_weight) + 16 + packed_rows, LANES), BF16)
     late = pl.pallas_call(
         lambda *refs: late_sum_kernel(depth, *refs),
         name="late_sum",
@@ -1307,10 +1333,11 @@
         compiler_params=compiler(8 << 20),
     )(late_keep, swapped(late_send), *routed)
     late = exchanged(late, "row")
+    final_rows = rows_weight if spare_lanes(rows_weight, parts) else rows_weight + 16
     summed = pl.pallas_call(
-        lambda *refs: row_sum_kernel(blocks, *refs),
+        lambda *refs: row_sum_kernel(blocks, depth, rows_weight, *refs),
         name="row_sum",
-        out_shape=(shape((rows_weight + 16, 3 * LANES), BF16),) * depth,
+        out_shape=(shape((final_rows, 3 * LANES), BF16),) * depth,
         in_specs=[VMEM] * (2 * blocks),
         out_specs=[VMEM] * depth,
         compiler_params=compiler(8 << 20),
@@ -1321,19 +1348,19 @@
         choose_kernel,
         name="choose",
         out_shape=shape((images, 2 * packed_rows, LANES), BF16),
-        in_specs=[VMEM] * blocks,
+        in_specs=[VMEM] * (2 * blocks),
         out_specs=VMEM,
         compiler_params=compiler(8 << 20),
-    )(*late)
+    )(*early, *late)
     whole = shape((images, rows_here * GRID, D), BF16)
     block_out, grad_patches = pl.pallas_call(
         home_kernel,
         name="home",
         out_shape=(whole, whole),
-        in_specs=[VMEM] * (1 + blocks),
+        in_specs=[VMEM] * (1 + 2 * blocks),
         out_specs=[VMEM] * 2,
         compiler_params=compiler(8 << 20),
-    )(swapped(chosen), *late)
+    )(swapped(chosen), *early, *late)
 
     summed, block_out, grad_patches = lax.optimization_barrier((summed, block_out, grad_patches))
     turned = (4 * STATE // parts, rows_weight)

time: 89.8 us -> 81.8 us (0.911)
  Pallas kernels: 39.7 us -> 34.4 us
  waiting for transfers between devices: 19.5 us -> 16.9 us
    ppermute x15, waiting for transfers between devices: 15.8 us -> 13 us  [exchanged(): lax.ppermute(values[k], axis, [(i, i ^ k) for i in range(size)])]
    pallas_call x1, Pallas kernels: 10.3 us -> 8.11 us  [per_device(): pl.pallas_call(middle_kernel, name='attention_and_feed_forward', out_shap...]
    pallas_call x1, Pallas kernels: 6.76 us -> 5.37 us  [per_device(): pl.pallas_call(lambda *refs: attention_back_kernel(*refs, blocks=blocks),...]
    pallas_call x1, Pallas kernels: 8.67 us -> 7.63 us  [per_device(): pl.pallas_call(lambda *refs: scan_kernel(starts, width, *refs, blocks=blo...]
  transfers between devices with their start and end apart: 28 -> 28, of which waited for: 11 -> 11; matrix products, arithmetic and copies ran while one was open for 1% -> 1% of each run, Pallas kernels for 20% -> 19%
where the time goes in v5:
time: 81.8 us; the launch traced here: 81.6 us
  Pallas kernels  34.4 us (42%)
  starting transfers between devices  28 us (34%)
  waiting for transfers between devices  16.9 us (21%)
    ppermute x15, starting transfers between devices, exchanged(): lax.ppermute(values[k], axis, [(i, i ^ k) for i in range(size)])  21.2 us
    ppermute x15, waiting for transfers between devices, exchanged(): lax.ppermute(values[k], axis, [(i, i ^ k) for i in range(size)])  13 us
    pallas_call x1, Pallas kernels, per_device(): pl.pallas_call(middle_kernel, name='attention_and_feed_forward', out_shap...  8.11 us
    pallas_call x1, Pallas kernels, per_device(): pl.pallas_call(lambda *refs: scan_kernel(starts, width, *refs, blocks=blo...  7.63 us
    pallas_call x1, Pallas kernels, per_device(): pl.pallas_call(lambda *refs: scan_back_kernel(starts, width, *refs), name...  7.35 us
    pallas_call x1, Pallas kernels, per_device(): pl.pallas_call(lambda *refs: attention_back_kernel(*refs, blocks=blocks),...  5.37 us
    ppermute x4, starting transfers between devices, to_chips(): return lax.ppermute(value, ('core', 'row'), pairs)  4.98 us
    pallas_call x1, Pallas kernels, per_device(): pl.pallas_call(depart_kernel, name='depart', out_shape=(shard,) + (payloa...  2.03 us
  transfers between devices with their start and end apart: 28, of which 11 were waited for; matrix products, arithmetic and copies ran while one was open for 1% of the time, Pallas kernels for 19%

profile of v5, /device:TPU:0, one launch (start us, length us, event | category | flops | bytes accessed | tf_op | source)
XLA Modules:
  0.0 81.6 jit_solution(4224356018745860426)
XLA Ops:
  0.6 2.0 %depart.1 = (bf16[48,384]{1,0:T(8,128)(2,1)}, bf16[416,128]{1,0:T(8,128)(2,1)}, bf16[416,128]{1,0:T(8,128)(2,1)}, bf16[416,128]{1,0:T(8,128)(2,1)}, bf16[416,128]{1,0:T(8,128)(2,1)}) custom-call(bf16[24,48]{1,0:T(8,128)(2,1)} %bitcast.27, bf16[8,48]{1,0:T(8,128)(2,1)} %bitcast.29, bf16[8,48]{1,0:T(8,128)(2,1)} %bitcast.30, bf16[24,48]{1,0:T(8,128)(2,1)} %bitcast.28, ...), custom_call_target="tpu_custom_call" | custom-call | tf_op jit(solution)/shard_map/depart/pallas_call | solution.py:1125
  2.7 5.0 %collective-permute-start.7 = (bf16[48,384]{1,0:T(8,128)(2,1)}, bf16[48,384]{1,0:T(8,128)(2,1)S(1)}, u32[]{:S(2)}, u32[]{:S(2)}) collective-permute-start(bf16[48,384]{1,0:T(8,128)(2,1)} %get-tuple-element.100), channel_id=1, source_target_pairs={{0,24},{8,16},{16,8},{24,0},{1,25},{9,17},{17,9},{25,1},{2,26},{10... | collective-permute-start | bytes 110600 | tf_op jit(solution)/shard_map/ppermute | solution.py:1106
  7.7 0.6 collective-permute-start.5
  8.3 1.5 %collective-permute-start = (bf16[416,128]{1,0:T(8,128)(2,1)}, bf16[416,128]{1,0:T(8,128)(2,1)S(1)}, u32[]{:S(2)}, u32[]{:S(2)}) collective-permute-start(bf16[416,128]{1,0:T(8,128)(2,1)} %get-tuple-element.90), channel_id=1, source_target_pairs={{0,0},{1,1},{2,4},{3,5},{4,2},{5,3},{6,6},{7,7},{8,8},{9,9},{10,12... | collective-permute-start | bytes 319496 | tf_op jit(solution)/shard_map/ppermute | solution.py:1115
  9.9 1.7 %collective-permute-start.1 = (bf16[416,128]{1,0:T(8,128)(2,1)}, bf16[416,128]{1,0:T(8,128)(2,1)S(1)}, u32[]{:S(2)}, u32[]{:S(2)}) collective-permute-start(bf16[416,128]{1,0:T(8,128)(2,1)} %get-tuple-element.91), channel_id=1, source_target_pairs={{0,1},{1,0},{2,5},{3,4},{4,3},{5,2},{6,7},{7,6},{8,9},{9,8},{10,13... | collective-permute-start | bytes 319496 | tf_op jit(solution)/shard_map/ppermute | solution.py:1115
  11.6 1.5 %collective-permute-start.2 = (bf16[416,128]{1,0:T(8,128)(2,1)}, bf16[416,128]{1,0:T(8,128)(2,1)S(1)}, u32[]{:S(2)}, u32[]{:S(2)}) collective-permute-start(bf16[416,128]{1,0:T(8,128)(2,1)} %get-tuple-element.92), channel_id=1, source_target_pairs={{0,4},{1,5},{2,0},{3,1},{4,6},{5,7},{6,2},{7,3},{8,12},{9,13},{10,... | collective-permute-start | bytes 319496 | tf_op jit(solution)/shard_map/ppermute | solution.py:1115
  13.3 0.8 pad_maximum_fusion.refs_6_.refs_0_
  14.1 2.7 %collective-permute-start.10 = (bf16[4,48,384]{2,1,0:T(8,128)(2,1)S(1)}, bf16[4,48,384]{2,1,0:T(8,128)(2,1)S(1)}, u32[]{:S(2)}, u32[]{:S(2)}) collective-permute-start(bf16[4,48,384]{2,1,0:T(8,128)(2,1)S(1)} %pad_maximum_fusion.refs_6_.refs_0_), channel_id=1, source_target_pairs={{0,3},{1,2},{2,1},{3,0},{4,7},{5,6},{6,5},{7,4},{8,11},{9,10},{10,... | collective-permute-start | bytes 442376 | tf_op jit(solution)/shard_map/ppermute | solution.py:1106
  17.1 1.1 %collective-permute-start.8 = (bf16[4,48,384]{2,1,0:T(8,128)(2,1)S(1)}, bf16[4,48,384]{2,1,0:T(8,128)(2,1)S(1)}, u32[]{:S(2)}, u32[]{:S(2)}) collective-permute-start(bf16[4,48,384]{2,1,0:T(8,128)(2,1)S(1)} %pad_maximum_fusion.refs_6_.refs_0_), channel_id=1, source_target_pairs={{0,1},{1,0},{2,3},{3,2},{4,5},{5,4},{6,7},{7,6},{8,9},{9,8},{10,11... | collective-permute-start | bytes 442376 | tf_op jit(solution)/shard_map/ppermute | solution.py:1106
  18.2 1.5 %collective-permute-done.2.refs_3_ = bf16[416,128]{1,0:T(8,128)(2,1)S(1)} collective-permute-done((bf16[416,128]{1,0:T(8,128)(2,1)}, bf16[416,128]{1,0:T(8,128)(2,1)S(1)}, u32[]{:S(2)}, u32[]{:S(2)}) %collective-permute-start.2) | collective-permute-done | bytes 106528 | tf_op jit(solution)/shard_map/ppermute | solution.py:1115
  20.1 0.7 copy-done.3
  20.7 1.1 %first_norm.1 = (bf16[4,2,128,192]{3,2,1,0:T(8,128)(2,1)S(1)}, bf16[512,192]{1,0:T(8,128)(2,1)S(1)}, f32[1024,128]{1,0:T(8,128)S(1)}, bf16[1024,192]{1,0:T(8,128...) custom-call(f32[2,192]{1,0:T(2,128)S(1)} %copy-done.3, ...), custom_call_target="tpu_custom_call" | custom-call | tf_op jit(solution)/shard_map/first_norm/pallas_call | solution.py:1170
  22.4 0.8 collective-permute-done.10.refs_9_.refs_3_
  23.2 3.0 %collective-permute-done.9.refs_8_.refs_2_ = bf16[4,48,384]{2,1,0:T(8,128)(2,1)S(1)} collective-permute-done((bf16[4,48,384]{2,1,0:T(8,128)(2,1)S(1)}, bf16[4,48,384]{2,1,0:T(8,128)(2,1)S(1)}, u32[]{:S(2)}, u32[]{:S(2)}) %collective-permute-start.9) | collective-permute-done | bytes 147488 | tf_op jit(solution)/shard_map/ppermute | solution.py:1106
  26.7 0.8 %collective-permute-done.13.refs_12_.refs_6_ = bf16[4,48,384]{2,1,0:T(8,128)(2,1)S(1)} collective-permute-done((bf16[4,48,384]{2,1,0:T(8,128)(2,1)S(1)}, bf16[4,48,384]{2,1,0:T(8,128)(2,1)S(1)}, u32[]{:S(2)}, u32[]{:S(2)}) %collective-permute-start.13) | collective-permute-done | bytes 147488 | tf_op jit(solution)/shard_map/ppermute | solution.py:1101
  27.7 7.6 %scan_forward.1 = (bf16[3,512,128]{2,1,0:T(8,128)(2,1)S(1)}, bf16[3,1024,128]{2,1,0:T(8,128)(2,1)S(1)}, bf16[3,1024,128]{2,1,0:T(8,128)(2,1)S(1)}, bf16[1024,192...) custom-call(bf16[512,192]{1,0:T(8,128)(2,1)S(1)} %get-tuple-element., ...), custom_call_target="tpu_custom_call" | custom-call | tf_op jit(solution)/shard_map/scan_forward/pallas_call | solution.py:1190
  35.4 8.1 %attention_and_feed_forward.1 = (bf16[3,1024,512]{2,1,0:T(8,128)(2,1)S(1)}, bf16[3,512,128]{2,1,0:T(8,128)(2,1)S(1)}, bf16[512,192]{1,0:T(8,128)(2,1)S(1)}, f32[...) custom-call(bf16[4,2,128,192]{3,2,1,0:T(8,128)(2,1)S(1)} %get-tuple-, ...), custom_call_target="tpu_custom_call" | custom-call | tf_op jit(solution)/shard_map/attention_and_feed_forward/pallas_call | solution.py:1213
  43.9 5.4 %attention_backward.1 = (bf16[1024,192]{1,0:T(8,128)(2,1)S(1)}, bf16[3,192,384]{2,1,0:T(8,128)(2,1)S(1)}) custom-call(bf16[3,1024,512]{2,1,0:T(8,128)(2,1)S(1)} %get-tuple-element.107.refs_0_, bf16[3,512,128]{2,1,0:T(8,128)(2,1)S(1)} %get-tuple-element.108.refs_1_, bf16[3,512,128]{2,1,0:T(8,128)(2,1)S(1)} %get-tuple-element.101.q_ref.refs_2_, ...), custom_call_target="tpu_custom_call" | custom-call | tf_op jit(solution)/shard_map/attention_backward/pallas_call | solution.py:1250
  49.7 1.5 %collective-permute-start.17 = (bf16[288,256]{1,0:T(8,128)(2,1)S(1)}, bf16[288,256]{1,0:T(8,128)(2,1)S(1)}, u32[]{:S(2)}, u32[]{:S(2)}) collective-permute-start(bf16[288,256]{1,0:T(8,128)(2,1)S(1)} %get-tuple-element.129), channel_id=1, source_target_pairs={{0,1},{1,0},{2,3},{3,2},{4,5},{5,4},{6,7},{7,6},{8,9},{9,8},{10,11... | collective-permute-start | bytes 442376 | tf_op jit(solution)/shard_map/ppermute | solution.py:1106
  51.6 1.6 %collective-permute-start.19 = (bf16[288,256]{1,0:T(8,128)(2,1)S(1)}, bf16[288,256]{1,0:T(8,128)(2,1)S(1)}, u32[]{:S(2)}, u32[]{:S(2)}) collective-permute-start(bf16[288,256]{1,0:T(8,128)(2,1)S(1)} %get-tuple-element.131), channel_id=1, source_target_pairs={{0,3},{1,2},{2,1},{3,0},{4,7},{5,6},{6,5},{7,4},{8,11},{9,10},{10,... | collective-permute-start | bytes 442376 | tf_op jit(solution)/shard_map/ppermute | solution.py:1106
  53.2 7.3 %scan_backward.1 = (bf16[17,48,128]{2,1,0:T(8,128)(2,1)S(1)}, bf16[17,48,128]{2,1,0:T(8,128)(2,1)S(1)}, f32[512,192]{1,0:T(8,128)S(1)}) custom-call(bf16[4,2,128,192]{3,2,1,0:T(8,128)(2,1)S(1)} %get-tuple-element.94.own_ref.refs_0_, f32[1024,128]{1,0:T(8,128)S(1)} %get-tuple-element.95.refs_2_.mask_ref.refs_1_, ...), custom_call_target="tpu_custom_call" | custom-call | tf_op jit(solution)/shard_map/scan_backward/pallas_call | solution.py:1281
  61.2 0.9 %collective-permute-done.20.refs_1_ = bf16[17,48,128]{2,1,0:T(8,128)(2,1)S(1)} collective-permute-done((bf16[17,48,128]{2,1,0:T(8,128)(2,1)S(1)}, bf16[17,48,128]{2,1,0:T(8,128)(2,1)S(1)}, u32[]{:S(2)}, u32[]{:S(2)}) %collective-permute-start.20) | collective-permute-done | bytes 208928 | tf_op jit(solution)/shard_map/ppermute | solution.py:1101
  62.2 1.5 %collective-permute-start.21 = (bf16[400,128]{1,0:T(8,128)(2,1)S(1)}, bf16[400,128]{1,0:T(8,128)(2,1)S(1)}, u32[]{:S(2)}, u32[]{:S(2)}) collective-permute-start(bf16[400,128]{1,0:T(8,128)(2,1)S(1)} %get-tuple-element.145), channel_id=1, source_target_pairs={{0,1},{1,0},{2,3},{3,2},{4,5},{5,4},{6,7},{7,6},{8,9},{9,8},{10,11... | collective-permute-start | bytes 307208 | tf_op jit(solution)/shard_map/ppermute | solution.py:1106
  64.1 1.6 %collective-permute-start.23 = (bf16[400,128]{1,0:T(8,128)(2,1)S(1)}, bf16[400,128]{1,0:T(8,128)(2,1)S(1)}, u32[]{:S(2)}, u32[]{:S(2)}) collective-permute-start(bf16[400,128]{1,0:T(8,128)(2,1)S(1)} %get-tuple-element.147), channel_id=1, source_target_pairs={{0,3},{1,2},{2,1},{3,0},{4,7},{5,6},{6,5},{7,4},{8,11},{9,10},{10,... | collective-permute-start | bytes 307208 | tf_op jit(solution)/shard_map/ppermute | solution.py:1106
  65.7 1.4 %collective-permute-done.21.refs_5_ = bf16[400,128]{1,0:T(8,128)(2,1)S(1)} collective-permute-done((bf16[400,128]{1,0:T(8,128)(2,1)S(1)}, bf16[400,128]{1,0:T(8,128)(2,1)S(1)}, u32[]{:S(2)}, u32[]{:S(2)}) %collective-permute-start.21) | collective-permute-done | bytes 102432 | tf_op jit(solution)/shard_map/ppermute | solution.py:1106
  67.2 3.4 %collective-permute-done.22.refs_6_ = bf16[400,128]{1,0:T(8,128)(2,1)S(1)} collective-permute-done((bf16[400,128]{1,0:T(8,128)(2,1)S(1)}, bf16[400,128]{1,0:T(8,128)(2,1)S(1)}, u32[]{:S(2)}, u32[]{:S(2)}) %collective-permute-start.22) | collective-permute-done | bytes 102432 | tf_op jit(solution)/shard_map/ppermute | solution.py:1106
  70.8 1.3 %collective-permute-start.24 = (bf16[48,384]{1,0:T(8,128)(2,1)S(1)}, bf16[48,384]{1,0:T(8,128)(2,1)S(1)}, u32[]{:S(2)}, u32[]{:S(2)}) collective-permute-start(bf16[48,384]{1,0:T(8,128)(2,1)S(1)} %get-tuple-element.149), channel_id=1, source_target_pairs={{0,8},{8,0},{16,24},{24,16},{1,9},{9,1},{17,25},{25,17},{2,10},{10... | collective-permute-start | bytes 110600 | tf_op jit(solution)/shard_map/ppermute | solution.py:1106
  72.1 2.9 %collective-permute-start.25 = (bf16[48,384]{1,0:T(8,128)(2,1)S(1)}, bf16[48,384]{1,0:T(8,128)(2,1)S(1)}, u32[]{:S(2)}, u32[]{:S(2)}) collective-permute-start(bf16[48,384]{1,0:T(8,128)(2,1)S(1)} %get-tuple-element.150), channel_id=1, source_target_pairs={{0,16},{8,24},{16,0},{24,8},{1,17},{9,25},{17,1},{25,9},{2,18},{10... | collective-permute-start | bytes 110600 | tf_op jit(solution)/shard_map/ppermute | solution.py:1106
  75.3 1.0 %home.1 = (bf16[2,256,192]{2,1,0:T(8,128)(2,1)}, bf16[2,256,192]{2,1,0:T(8,128)(2,1)}) custom-call(bf16[2,384,128]{2,1,0:T(8,128)(2,1)S(1)} %collective-permute-done.27.swapped_ref, bf16[288,256]{1,0:T(8,128)(2,1)S(1)} %get-tuple-element.132.refs_0_, bf16[288,256]{1,0:T(8,128)(2,1)S(1)} %collective-permute-done.17.refs_1_, ...), custom_call_target="tpu_custom_call" | custom-call | tf_op jit(solution)/shard_map/home/pallas_call | solution.py:1356
  76.3 1.5 %collective-permute-done.25.refs_2_ = bf16[48,384]{1,0:T(8,128)(2,1)S(1)} collective-permute-done((bf16[48,384]{1,0:T(8,128)(2,1)S(1)}, bf16[48,384]{1,0:T(8,128)(2,1)S(1)}, u32[]{:S(2)}, u32[]{:S(2)}) %collective-permute-start.25) | collective-permute-done | bytes 36896 | tf_op jit(solution)/shard_map/ppermute | solution.py:1106
  77.8 2.9 %collective-permute-done.26.refs_3_ = bf16[48,384]{1,0:T(8,128)(2,1)S(1)} collective-permute-done((bf16[48,384]{1,0:T(8,128)(2,1)S(1)}, bf16[48,384]{1,0:T(8,128)(2,1)S(1)}, u32[]{:S(2)}, u32[]{:S(2)}) %collective-permute-start.26) | collective-permute-done | bytes 36896 | tf_op jit(solution)/shard_map/ppermute | solution.py:1106
  80.8 0.8 final_sum.1
  (48 shorter events, 5.1 us)
Async XLA Ops:
  2.7 8.9 %collective-permute-start.7 = (bf16[48,384]{1,0:T(8,128)(2,1)}, bf16[48,384]{1,0:T(8,128)(2,1)S(1)}, u32[]{:S(2)}, u32[]{:S(2)}) collective-permute-start(bf16[48,384]{1,0:T(8,128)(2,1)} %get-tuple-element.100), channel_id=1, source_target_pairs={{0,24},{8,16},{16,8},{24,0},{1,25},{9,17},{17,9},{25,1},{2,26},{10... | collective-permute-start | bytes 110600 | tf_op jit(solution)/shard_map/ppermute | solution.py:1106
  7.7 5.3 %collective-permute-start.6 = (bf16[48,384]{1,0:T(8,128)(2,1)}, bf16[48,384]{1,0:T(8,128)(2,1)S(1)}, u32[]{:S(2)}, u32[]{:S(2)}) collective-permute-start(bf16[48,384]{1,0:T(8,128)(2,1)} %get-tuple-element.100), channel_id=1, source_target_pairs={{0,16},{8,24},{16,0},{24,8},{1,17},{9,25},{17,1},{25,9},{2,18},{10... | collective-permute-start | bytes 110600 | tf_op jit(solution)/shard_map/ppermute | solution.py:1106
  7.7 5.6 %collective-permute-start.5 = (bf16[48,384]{1,0:T(8,128)(2,1)}, bf16[48,384]{1,0:T(8,128)(2,1)S(1)}, u32[]{:S(2)}, u32[]{:S(2)}) collective-permute-start(bf16[48,384]{1,0:T(8,128)(2,1)} %get-tuple-element.100), channel_id=1, source_target_pairs={{0,8},{8,0},{16,24},{24,16},{1,9},{9,1},{17,25},{25,17},{2,10},{10... | collective-permute-start | bytes 110600 | tf_op jit(solution)/shard_map/ppermute | solution.py:1106
  8.3 8.5 %collective-permute-start = (bf16[416,128]{1,0:T(8,128)(2,1)}, bf16[416,128]{1,0:T(8,128)(2,1)S(1)}, u32[]{:S(2)}, u32[]{:S(2)}) collective-permute-start(bf16[416,128]{1,0:T(8,128)(2,1)} %get-tuple-element.90), channel_id=1, source_target_pairs={{0,0},{1,1},{2,4},{3,5},{4,2},{5,3},{6,6},{7,7},{8,8},{9,9},{10,12... | collective-permute-start | bytes 319496 | tf_op jit(solution)/shard_map/ppermute | solution.py:1115
  9.9 7.2 %collective-permute-start.1 = (bf16[416,128]{1,0:T(8,128)(2,1)}, bf16[416,128]{1,0:T(8,128)(2,1)S(1)}, u32[]{:S(2)}, u32[]{:S(2)}) collective-permute-start(bf16[416,128]{1,0:T(8,128)(2,1)} %get-tuple-element.91), channel_id=1, source_target_pairs={{0,1},{1,0},{2,5},{3,4},{4,3},{5,2},{6,7},{7,6},{8,9},{9,8},{10,13... | collective-permute-start | bytes 319496 | tf_op jit(solution)/shard_map/ppermute | solution.py:1115
  11.6 8.1 %collective-permute-start.2 = (bf16[416,128]{1,0:T(8,128)(2,1)}, bf16[416,128]{1,0:T(8,128)(2,1)S(1)}, u32[]{:S(2)}, u32[]{:S(2)}) collective-permute-start(bf16[416,128]{1,0:T(8,128)(2,1)} %get-tuple-element.92), channel_id=1, source_target_pairs={{0,4},{1,5},{2,0},{3,1},{4,6},{5,7},{6,2},{7,3},{8,12},{9,13},{10,... | collective-permute-start | bytes 319496 | tf_op jit(solution)/shard_map/ppermute | solution.py:1115
  13.1 7.0 %collective-permute-start.3 = (bf16[416,128]{1,0:T(8,128)(2,1)}, bf16[416,128]{1,0:T(8,128)(2,1)S(1)}, u32[]{:S(2)}, u32[]{:S(2)}) collective-permute-start(bf16[416,128]{1,0:T(8,128)(2,1)} %get-tuple-element.93), channel_id=1, source_target_pairs={{0,5},{1,4},{2,1},{3,0},{4,7},{5,6},{6,3},{7,2},{8,13},{9,12},{10,... | collective-permute-start | bytes 319496 | tf_op jit(solution)/shard_map/ppermute | solution.py:1115
  14.1 9.0 %collective-permute-start.10 = (bf16[4,48,384]{2,1,0:T(8,128)(2,1)S(1)}, bf16[4,48,384]{2,1,0:T(8,128)(2,1)S(1)}, u32[]{:S(2)}, u32[]{:S(2)}) collective-permute-start(bf16[4,48,384]{2,1,0:T(8,128)(2,1)S(1)} %pad_maximum_fusion.refs_6_.refs_0_), channel_id=1, source_target_pairs={{0,3},{1,2},{2,1},{3,0},{4,7},{5,6},{6,5},{7,4},{8,11},{9,10},{10,... | collective-permute-start | bytes 442376 | tf_op jit(solution)/shard_map/ppermute | solution.py:1106
  16.9 9.3 %collective-permute-start.9 = (bf16[4,48,384]{2,1,0:T(8,128)(2,1)S(1)}, bf16[4,48,384]{2,1,0:T(8,128)(2,1)S(1)}, u32[]{:S(2)}, u32[]{:S(2)}) collective-permute-start(bf16[4,48,384]{2,1,0:T(8,128)(2,1)S(1)} %pad_maximum_fusion.refs_6_.refs_0_), channel_id=1, source_target_pairs={{0,2},{1,3},{2,0},{3,1},{4,6},{5,7},{6,4},{7,5},{8,10},{9,11},{10,... | collective-permute-start | bytes 442376 | tf_op jit(solution)/shard_map/ppermute | solution.py:1106
  17.1 9.1 %collective-permute-start.8 = (bf16[4,48,384]{2,1,0:T(8,128)(2,1)S(1)}, bf16[4,48,384]{2,1,0:T(8,128)(2,1)S(1)}, u32[]{:S(2)}, u32[]{:S(2)}) collective-permute-start(bf16[4,48,384]{2,1,0:T(8,128)(2,1)S(1)} %pad_maximum_fusion.refs_6_.refs_0_), channel_id=1, source_target_pairs={{0,1},{1,0},{2,3},{3,2},{4,5},{5,4},{6,7},{7,6},{8,9},{9,8},{10,11... | collective-permute-start | bytes 442376 | tf_op jit(solution)/shard_map/ppermute | solution.py:1106
  21.8 4.8 %collective-permute-start.4 = (bf16[512,192]{1,0:T(8,128)(2,1)S(1)}, bf16[512,192]{1,0:T(8,128)(2,1)S(1)}, u32[]{:S(2)}, u32[]{:S(2)}) collective-permute-start(bf16[512,192]{1,0:T(8,128)(2,1)S(1)} %get-tuple-element.96.refs_0_.refs_5_), channel_id=1, source_target_pairs={{0,4},{4,0},{1,5},{5,1},{2,6},{6,2},{3,7},{7,3},{8,12},{12,8},{9,1... | collective-permute-start | bytes 589832 | tf_op jit(solution)/shard_map/ppermute | solution.py:1101
  21.9 4.7 %collective-permute-start.11 = (bf16[4,48,384]{2,1,0:T(8,128)(2,1)S(1)}, bf16[4,48,384]{2,1,0:T(8,128)(2,1)S(1)}, u32[]{:S(2)}, u32[]{:S(2)}) collective-permute-start(bf16[4,48,384]{2,1,0:T(8,128)(2,1)S(1)} %pad_maximum_fusion.refs_6_.refs_0_), channel_id=1, source_target_pairs={{0,4},{4,0},{1,5},{5,1},{2,6},{6,2},{3,7},{7,3},{8,12},{12,8},{9,1... | collective-permute-start | bytes 442376 | tf_op jit(solution)/shard_map/ppermute | solution.py:1101
  23.2 3.5 %collective-permute-start.14 = (bf16[4,48,384]{2,1,0:T(8,128)(2,1)S(1)}, bf16[4,48,384]{2,1,0:T(8,128)(2,1)S(1)}, u32[]{:S(2)}, u32[]{:S(2)}) collective-permute-start(bf16[4,48,384]{2,1,0:T(8,128)(2,1)S(1)} %collective-permute-done.10.refs_9_.refs_3_), channel_id=1, source_target_pairs={{0,4},{4,0},{1,5},{5,1},{2,6},{6,2},{3,7},{7,3},{8,12},{12,8},{9,1... | collective-permute-start | bytes 442376 | tf_op jit(solution)/shard_map/ppermute | solution.py:1101
  26.1 1.4 %collective-permute-start.13 = (bf16[4,48,384]{2,1,0:T(8,128)(2,1)S(1)}, bf16[4,48,384]{2,1,0:T(8,128)(2,1)S(1)}, u32[]{:S(2)}, u32[]{:S(2)}) collective-permute-start(bf16[4,48,384]{2,1,0:T(8,128)(2,1)S(1)} %collective-permute-done.9.refs_8_.refs_2_), channel_id=1, source_target_pairs={{0,4},{4,0},{1,5},{5,1},{2,6},{6,2},{3,7},{7,3},{8,12},{12,8},{9,1... | collective-permute-start | bytes 442376 | tf_op jit(solution)/shard_map/ppermute | solution.py:1101
  26.2 1.5 %collective-permute-start.12 = (bf16[4,48,384]{2,1,0:T(8,128)(2,1)S(1)}, bf16[4,48,384]{2,1,0:T(8,128)(2,1)S(1)}, u32[]{:S(2)}, u32[]{:S(2)}) collective-permute-start(bf16[4,48,384]{2,1,0:T(8,128)(2,1)S(1)} %collective-permute-done.8.refs_7_.refs_1_), channel_id=1, source_target_pairs={{0,4},{4,0},{1,5},{5,1},{2,6},{6,2},{3,7},{7,3},{8,12},{12,8},{9,1... | collective-permute-start | bytes 442376 | tf_op jit(solution)/shard_map/ppermute | solution.py:1101
  27.7 7.6 %copy-start = (bf16[4,1024,192]{2,1,0:T(8,128)(2,1)S(1)}, bf16[4,1024,192]{2,1,0:T(8,128)(2,1)}, u32[]{:S(2)}) copy-start(bf16[4,1024,192]{2,1,0:T(8,128)(2,1)} %constant.8.clone.sel_2_ref) | copy-start | bytes 4718596
  27.7 7.7 %copy-start.1 = (bf16[1024,192]{1,0:T(8,128)(2,1)S(1)}, bf16[1024,192]{1,0:T(8,128)(2,1)}, u32[]{:S(2)}) copy-start(bf16[1024,192]{1,0:T(8,128)(2,1)} %constant.7.clone.sel_o_ref) | copy-start | bytes 1179652
  27.7 7.7 %copy-start.2 = (bf16[512,384]{1,0:T(8,128)(2,1)S(1)}, bf16[512,384]{1,0:T(8,128)(2,1)}, u32[]{:S(2)}) copy-start(bf16[512,384]{1,0:T(8,128)(2,1)} %constant.6.clone.sel_1_ref) | copy-start | bytes 1179652
  27.7 7.7 %copy-start.4 = (f32[2,192]{1,0:T(2,128)S(1)}, f32[2,192]{1,0:T(2,128)}, u32[]{:S(2)}) copy-start(f32[2,192]{1,0:T(2,128)} %gains_ref.3) | copy-start | bytes 4612
  43.5 5.8 %collective-permute-start.15 = (bf16[4,4,48,256]{3,2,1,0:T(8,128)(2,1)S(1)}, bf16[4,4,48,256]{3,2,1,0:T(8,128)(2,1)S(1)}, u32[]{:S(2)}, u32[]{:S(2)}) collective-permute-start(bf16[4,4,48,256]{3,2,1,0:T(8,128)(2,1)S(1)} %get-tuple-element.106), channel_id=1, source_target_pairs={{0,4},{4,0},{1,5},{5,1},{2,6},{6,2},{3,7},{7,3},{8,12},{12,8},{9,1... | collective-permute-start | bytes 1179656 | tf_op jit(solution)/shard_map/ppermute | solution.py:1101
  49.5 3.7 %collective-permute-start.16 = (bf16[1024,192]{1,0:T(8,128)(2,1)S(1)}, bf16[1024,192]{1,0:T(8,128)(2,1)S(1)}, u32[]{:S(2)}, u32[]{:S(2)}) collective-permute-start(bf16[1024,192]{1,0:T(8,128)(2,1)S(1)} %get-tuple-element.119.refs_2_), channel_id=1, source_target_pairs={{0,4},{4,0},{1,5},{5,1},{2,6},{6,2},{3,7},{7,3},{8,12},{12,8},{9,1... | collective-permute-start | bytes 1179656 | tf_op jit(solution)/shard_map/ppermute | solution.py:1101
  49.7 10.9 %collective-permute-start.17 = (bf16[288,256]{1,0:T(8,128)(2,1)S(1)}, bf16[288,256]{1,0:T(8,128)(2,1)S(1)}, u32[]{:S(2)}, u32[]{:S(2)}) collective-permute-start(bf16[288,256]{1,0:T(8,128)(2,1)S(1)} %get-tuple-element.129), channel_id=1, source_target_pairs={{0,1},{1,0},{2,3},{3,2},{4,5},{5,4},{6,7},{7,6},{8,9},{9,8},{10,11... | collective-permute-start | bytes 442376 | tf_op jit(solution)/shard_map/ppermute | solution.py:1106
  51.2 9.4 %collective-permute-start.18 = (bf16[288,256]{1,0:T(8,128)(2,1)S(1)}, bf16[288,256]{1,0:T(8,128)(2,1)S(1)}, u32[]{:S(2)}, u32[]{:S(2)}) collective-permute-start(bf16[288,256]{1,0:T(8,128)(2,1)S(1)} %get-tuple-element.130), channel_id=1, source_target_pairs={{0,2},{1,3},{2,0},{3,1},{4,6},{5,7},{6,4},{7,5},{8,10},{9,11},{10,... | collective-permute-start | bytes 442376 | tf_op jit(solution)/shard_map/ppermute | solution.py:1106
  51.6 9.0 %collective-permute-start.19 = (bf16[288,256]{1,0:T(8,128)(2,1)S(1)}, bf16[288,256]{1,0:T(8,128)(2,1)S(1)}, u32[]{:S(2)}, u32[]{:S(2)}) collective-permute-start(bf16[288,256]{1,0:T(8,128)(2,1)S(1)} %get-tuple-element.131), channel_id=1, source_target_pairs={{0,3},{1,2},{2,1},{3,0},{4,7},{5,6},{6,5},{7,4},{8,11},{9,10},{10,... | collective-permute-start | bytes 442376 | tf_op jit(solution)/shard_map/ppermute | solution.py:1106
  60.6 1.5 %collective-permute-start.20 = (bf16[17,48,128]{2,1,0:T(8,128)(2,1)S(1)}, bf16[17,48,128]{2,1,0:T(8,128)(2,1)S(1)}, u32[]{:S(2)}, u32[]{:S(2)}) collective-permute-start(bf16[17,48,128]{2,1,0:T(8,128)(2,1)S(1)} %get-tuple-element.137), channel_id=1, source_target_pairs={{0,4},{4,0},{1,5},{5,1},{2,6},{6,2},{3,7},{7,3},{8,12},{12,8},{9,1... | collective-permute-start | bytes 626696 | tf_op jit(solution)/shard_map/ppermute | solution.py:1101
  62.2 5.0 %collective-permute-start.21 = (bf16[400,128]{1,0:T(8,128)(2,1)S(1)}, bf16[400,128]{1,0:T(8,128)(2,1)S(1)}, u32[]{:S(2)}, u32[]{:S(2)}) collective-permute-start(bf16[400,128]{1,0:T(8,128)(2,1)S(1)} %get-tuple-element.145), channel_id=1, source_target_pairs={{0,1},{1,0},{2,3},{3,2},{4,5},{5,4},{6,7},{7,6},{8,9},{9,8},{10,11... | collective-permute-start | bytes 307208 | tf_op jit(solution)/shard_map/ppermute | solution.py:1106
  63.7 6.8 %collective-permute-start.22 = (bf16[400,128]{1,0:T(8,128)(2,1)S(1)}, bf16[400,128]{1,0:T(8,128)(2,1)S(1)}, u32[]{:S(2)}, u32[]{:S(2)}) collective-permute-start(bf16[400,128]{1,0:T(8,128)(2,1)S(1)} %get-tuple-element.146), channel_id=1, source_target_pairs={{0,2},{1,3},{2,0},{3,1},{4,6},{5,7},{6,4},{7,5},{8,10},{9,11},{10,... | collective-permute-start | bytes 307208 | tf_op jit(solution)/shard_map/ppermute | solution.py:1106
  64.1 6.5 %collective-permute-start.23 = (bf16[400,128]{1,0:T(8,128)(2,1)S(1)}, bf16[400,128]{1,0:T(8,128)(2,1)S(1)}, u32[]{:S(2)}, u32[]{:S(2)}) collective-permute-start(bf16[400,128]{1,0:T(8,128)(2,1)S(1)} %get-tuple-element.147), channel_id=1, source_target_pairs={{0,3},{1,2},{2,1},{3,0},{4,7},{5,6},{6,5},{7,4},{8,11},{9,10},{10,... | collective-permute-start | bytes 307208 | tf_op jit(solution)/shard_map/ppermute | solution.py:1106
  70.6 4.7 %collective-permute-start.27 = (bf16[2,384,128]{2,1,0:T(8,128)(2,1)S(1)}, bf16[2,384,128]{2,1,0:T(8,128)(2,1)S(1)}, u32[]{:S(2)}, u32[]{:S(2)}) collective-permute-start(bf16[2,384,128]{2,1,0:T(8,128)(2,1)S(1)} %choose.1), channel_id=1, source_target_pairs={{0,4},{4,0},{1,5},{5,1},{2,6},{6,2},{3,7},{7,3},{8,12},{12,8},{9,1... | collective-permute-start | bytes 589832 | tf_op jit(solution)/shard_map/ppermute | solution.py:1101
  70.8 5.5 %collective-permute-start.24 = (bf16[48,384]{1,0:T(8,128)(2,1)S(1)}, bf16[48,384]{1,0:T(8,128)(2,1)S(1)}, u32[]{:S(2)}, u32[]{:S(2)}) collective-permute-start(bf16[48,384]{1,0:T(8,128)(2,1)S(1)} %get-tuple-element.149), channel_id=1, source_target_pairs={{0,8},{8,0},{16,24},{24,16},{1,9},{9,1},{17,25},{25,17},{2,10},{10... | collective-permute-start | bytes 110600 | tf_op jit(solution)/shard_map/ppermute | solution.py:1106
  72.1 5.7 %collective-permute-start.25 = (bf16[48,384]{1,0:T(8,128)(2,1)S(1)}, bf16[48,384]{1,0:T(8,128)(2,1)S(1)}, u32[]{:S(2)}, u32[]{:S(2)}) collective-permute-start(bf16[48,384]{1,0:T(8,128)(2,1)S(1)} %get-tuple-element.150), channel_id=1, source_target_pairs={{0,16},{8,24},{16,0},{24,8},{1,17},{9,25},{17,1},{25,9},{2,18},{10... | collective-permute-start | bytes 110600 | tf_op jit(solution)/shard_map/ppermute | solution.py:1106
  75.0 5.8 %collective-permute-start.26 = (bf16[48,384]{1,0:T(8,128)(2,1)S(1)}, bf16[48,384]{1,0:T(8,128)(2,1)S(1)}, u32[]{:S(2)}, u32[]{:S(2)}) collective-permute-start(bf16[48,384]{1,0:T(8,128)(2,1)S(1)} %get-tuple-element.151), channel_id=1, source_target_pairs={{0,24},{8,16},{16,8},{24,0},{1,25},{9,17},{17,9},{25,1},{2,26},{10... | collective-permute-start | bytes 110600 | tf_op jit(solution)/shard_map/ppermute | solution.py:1106
  (1 other events, 0.7 us)

commit v6 on v5

--- a/solution.py
+++ b/solution.py
@@ -150,21 +150,106 @@
     return [(0, (index * 2 + u) * 8) for u in range(2)] + [(1, index * 8)]
 
 
-def block_sum(src, table, way, kind, first, count, sublane, sign):
-    total = [None] * count
+def lag_tables(lags):
+    lines = []
+    near = lags[16:47]
+    for table in (near, lags[0:31] - near, lags[32:63] - near):
+        center = table[8:23]
+        for part in (center, table[0:15] - center, table[16:31] - center):
+            lines += [part, jnp.zeros((1, LANES), F32)]
+    return jnp.concatenate(lines, axis=0)
+
+
+def plus(left, right):
+    return [a + b for a, b in zip(left, right)]
+
+
+def own_places(own_rows):
+    if own_rows is None:
+        return list(range(8)), 0
+    places = [i // own_rows * 2 * own_rows + i % own_rows for i in range(4)]
+    return places, lax.axis_index("core") * own_rows
+
+
+def three(left, right, work):
+    a, b = len(left) // 2, len(right) // 2
+    work(0, plus(left[:a], left[a:]), plus(right[:b], right[b:]))
+    work(1, left[:a], right[b:])
+    work(2, left[a:], right[:b])
+
+
+def add_lags(sums, way, kind, sublane, grads, values, own_rows=None):
+    step = values[kind].shape[0] // GRID
+    places, shift = own_places(own_rows)
+
+    def line(ref, at):
+        return ref[kind][pl.ds(pl.multiple_of(at * step + sublane, 8), 8), :]
+
+    g = [line(grads, base + place + shift) for base in range(0, GRID, 8) for place in places]
+    x = [line(values, s) for s in range(GRID)]
+
+    def leaf(first, second, g, x):
+        total = {}
+        for i, t in enumerate(places):
+            for s in range(8):
+                term = g[i] * x[s]
+                total[t - s] = term if t - s not in total else total[t - s] + term
+        start = (first * 3 + second) * 16 + 7
+        for lag, value in total.items():
+            sums[way, kind, start + lag + shift] += value
+
+    three(g, x, lambda p, g, x: three(g, x, lambda q, g, x: leaf(p, q, g, x)))
+
+
+def gather_lags(sums, way, kind):
+    def join(parts, reach):
+        found = [None] * (2 * (2 * reach + 1) + 1)
+        width = 2 * reach - 1
+        middle = [a - b - c for a, b, c in zip(*parts)]
+        for start, part in ((reach, middle), (0, parts[1]), (2 * reach, parts[2])):
+            for i in range(width):
+                at = start + i
+                found[at] = part[i] if found[at] is None else found[at] + part[i]
+        return found[: 4 * reach - 1]
+
+    thirds = []
+    for first in range(3):
+        tables = [
+            [sums[way, kind, (first * 3 + second) * 16 + i] for i in range(15)]
+            for second in range(3)
+        ]
+        thirds.append(join(tables, 8))
+    return join(thirds, 16)
+
+
+def toeplitz(src, table, way, kind, sublane, sign, own_rows=None):
     step = src[kind].shape[0] // GRID
-    for base in range(0, GRID, 8):
-        low, high = -(base + 7), count - 1 - base
-        coef = {
-            lag: table[way, kind, first * sign + (lag * sign + CENTER)]
-            for lag in range(low, high + 1)
-        }
-        for s in range(base, base + 8):
-            x = src[kind][pl.ds(pl.multiple_of(s * step + sublane, 8), 8), :]
-            for t in range(count):
-                term = coef[t - s] * x
-                total[t] = term if total[t] is None else total[t] + term
-    return total
+    places, shift = own_places(own_rows)
+    shift = shift * sign
+
+    def leaf(x, first, second):
+        if sign < 0:
+            first, second = (0, 2, 1)[first], (0, 2, 1)[second]
+        start = (first * 3 + second) * 16 + 7
+        coef = {}
+        total = [None] * len(places)
+        for s in range(8):
+            for i, t in enumerate(places):
+                lag = t - s
+                if lag not in coef:
+                    line = table[way, kind, pl.ds(start + lag * sign + shift, 1), :]
+                    coef[lag] = jnp.broadcast_to(line, (8, LANES))
+                term = coef[lag] * x[s]
+                total[i] = term if total[i] is None else total[i] + term
+        return total
+
+    def quarter(x, first):
+        middle = leaf(plus(x[:8], x[8:]), first, 0)
+        return plus(middle, leaf(x[8:], first, 1)) + plus(middle, leaf(x[:8], first, 2))
+
+    x = [src[kind][pl.ds(pl.multiple_of(s * step + sublane, 8), 8), :] for s in range(GRID)]
+    middle = quarter(plus(x[:16], x[16:]), 0)
+    return plus(middle, quarter(x[16:], 1)) + plus(middle, quarter(x[:16], 2))
 
 
 def join_rows(i, count, rows, cols):
@@ -402,6 +487,7 @@
     rows_pairs,
     scanned_own,
     first_ref,
+    lags,
 ):
     xs, xt = (xs_wide, xs_pairs), (xt_wide, xt_pairs)
     cols, rows = (cols_wide, cols_pairs), (rows_wide, rows_pairs)
@@ -429,7 +515,7 @@
         row = row.astype(BF16).astype(F32)
         tail = row[:, LANES:D]
         for kind, lanes in enumerate((row[:, :LANES], pair_lanes(tail, tail))):
-            table_ref[way, kind, lag + CENTER] = jnp.broadcast_to(lanes, (8, LANES))
+            lags[way, kind, pl.ds(lag + CENTER, 1), :] = lanes
 
     def lag_step(k, _):
         found = lag_row(k.astype(F32))
@@ -442,6 +528,8 @@
     found = lag_row(0.0)
     for way in range(2):
         store_lag(way, 0, found[2 * way] + found[2 * way + 1])
+        for kind in range(2):
+            table_ref[way, kind] = lag_tables(lags[way, kind])
 
 
     for block in range(blocks):
@@ -457,17 +545,14 @@
     put_rows(*xt, xs[0], mixed[:, LANES:], cols[1])
 
     def scan_step(index, _):
-        first = (index // 2) * 8
         for way, src, dst in ((0, xt, rows), (1, xs, cols)):
-            for kind, sublane in units(index % 2):
+            for kind, sublane in units(index):
                 step = src[kind].shape[0] // GRID
-                total = block_sum(src, table_ref, way, kind, first, 8, sublane, 1)
-                for t in range(8):
-                    place = pl.multiple_of((first + t) * step + sublane, 8)
-                    dst[kind][pl.ds(place, 8), :] = total[t]
+                for t, value in enumerate(toeplitz(src, table_ref, way, kind, sublane, 1)):
+                    dst[kind][pl.ds(pl.multiple_of(t * step + sublane, 8), 8), :] = value
         return 0
 
-    lax.fori_loop(0, 8, scan_step, 0, unroll=2)
+    lax.fori_loop(0, 2, scan_step, 0, unroll=True)
 
     def join_step(i, _):
         for row, value in join_rows(i, GRID, rows, cols):
@@ -790,6 +875,7 @@
     own_tail,
     together,
     lag_sums,
+    lag_lines,
     lag_rows,
     mixed_back,
     wire,
@@ -820,68 +906,41 @@
             own_tail[here, :] = value[:, LANES:]
         put_rows(*dst, own, own_tail[...], together)
 
-    def row_step(index, _):
-        first = index * 8
-        for kind, sublane in units(0):
-            step = gt[kind].shape[0] // GRID
-            total = block_sum(gt, table_ref, 0, kind, first, 8, sublane, -1)
-            for t in range(8):
-                place = pl.multiple_of((first + t) * step + sublane, 8)
-                rows[kind][pl.ds(place, 8), :] = total[t]
+    for kind, sublane in units(0):
+        step = gt[kind].shape[0] // GRID
+        for t, value in enumerate(toeplitz(gt, table_ref, 0, kind, sublane, -1)):
+            rows[kind][t * step + sublane : t * step + sublane + 8, :] = value
+
+    def col_step(index, _):
+        for kind, sublane in units(index):
+            step = gs[kind].shape[0] // GRID
+            found = toeplitz(gs, table_ref, 1, kind, sublane, -1, half_rows)
+            for t, value in enumerate(found):
+                cols[kind][pl.ds(pl.multiple_of(t * step + sublane, 8), 8), :] = value
         return 0
 
-    lax.fori_loop(0, 4, row_step, 0, unroll=True)
-
-    def col_step(index, _):
-        block = index // 2
-        first = (block * 2 + core) * half_rows
-        for kind, sublane in units(index % 2):
-            step = gs[kind].shape[0] // GRID
-            total = block_sum(gs, table_ref, 1, kind, first, half_rows, sublane, -1)
-            for t in range(half_rows):
-                place = pl.multiple_of((block * half_rows + t) * step + sublane, 8)
-                cols[kind][pl.ds(place, 8), :] = total[t]
+    lax.fori_loop(0, 2, col_step, 0)
+
+    lag_sums[...] = jnp.zeros_like(lag_sums)
+
+    for kind, sublane in units(0):
+        add_lags(lag_sums, 0, kind, sublane, gt, xt)
+
+    def lag_step(index, _):
+        for kind, sublane in units(index):
+            add_lags(lag_sums, 1, kind, sublane, gs, xs, half_rows)
         return 0
 
-    lax.fori_loop(0, blocks * 2, col_step, 0)
-
-    lag_sums[...] = jnp.zeros_like(lag_sums)
-
-    def add_lags(way, kind, first, count, base, gref, xref):
-        total = {}
-        step = gref[kind].shape[0] // GRID
-        for u in range(step // 8):
-            g = [
-                gref[kind][pl.ds(pl.multiple_of((first + t) * step + u * 8, 8), 8), :]
-                for t in range(count)
-            ]
-            for s in range(8):
-                x = xref[kind][pl.ds(pl.multiple_of((base + s) * step + u * 8, 8), 8), :]
-                for t in range(count):
-                    term = g[t] * x
-                    total[t - s] = term if t - s not in total else total[t - s] + term
-        for lag, value in total.items():
-            at = first - base + (lag + CENTER)
-            lag_sums[way, kind, at] += value
-
-    def lag_row_step(index, _):
+    lax.fori_loop(0, 2, lag_step, 0)
+    for way in range(2):
         for kind in range(2):
-            add_lags(0, kind, (index // 4) * 8, 8, (index % 4) * 8, gt, xt)
-        return 0
-
-    lax.fori_loop(0, 16, lag_row_step, 0)
-
-    def lag_col_step(index, _):
-        first = ((index // 4) * 2 + core) * half_rows
-        for kind in range(2):
-            add_lags(1, kind, first, half_rows, (index % 4) * 8, gs, xs)
-        return 0
-
-    lax.fori_loop(0, blocks * 4, lag_col_step, 0)
+            for lag, value in enumerate(gather_lags(lag_sums, way, kind)):
+                lag_lines[way, kind, lag] = value
+            lag_lines[way, kind, LAGS - 1] = jnp.zeros((8, LANES), F32)
 
     for way in range(2):
-        lag_rows[way, :, :LANES] = jnp.sum(lag_sums[way, 0], 1)
-        tail = jnp.sum(lag_sums[way, 1], 1)
+        lag_rows[way, :, :LANES] = jnp.sum(lag_lines[way, 0], 1)
+        tail = jnp.sum(lag_lines[way, 1], 1)
         tail = tail[:, : D - LANES] + tail[:, D - LANES :]
         lag_rows[way, :, LANES:] = pair_lanes(tail, jnp.zeros_like(tail))
 
@@ -1196,7 +1255,7 @@
             head_all,
             shape((SLOTS, D), BF16),
             shape((SLOTS, D), BF16),
-            shape((2, 2, LAGS, 8, LANES), F32),
+            shape((2, 2, 9 * 16, LANES), F32),
             shape((LANES, 2 * LANES), F32),
             shape((D, D), BF16),
             shape((3, D, TILE), BF16),
@@ -1205,7 +1264,8 @@
         out_specs=[VMEM] * 9,
         scratch_shapes=[part_scratch]
         + planes(SLOTS) * 4
-        + [pltpu.VMEM((OWN, D), BF16), pltpu.VMEM((SLOTS, D), BF16)],
+        + [pltpu.VMEM((OWN, D), BF16), pltpu.VMEM((SLOTS, D), BF16)]
+        + [pltpu.VMEM((2, 2, LAGS, LANES), F32)],
         compiler_params=compiler(),
     )(first_own, first_other, mask, sel_u, sel_rc, sel_q, *weights)
 
@@ -1290,6 +1350,7 @@
             pltpu.VMEM((OWN, LANES), F32),
             pltpu.VMEM((OWN, D - LANES), F32),
             pltpu.VMEM((OWN // 2, LANES), F32),
+            pltpu.VMEM((2, 2, 9 * 16, 8, LANES), F32),
             pltpu.VMEM((2, 2, LAGS, 8, LANES), F32),
             pltpu.VMEM((2, LAGS, 2 * LANES), F32),
             pltpu.VMEM((OWN, D), BF16),

time: 81.8 us -> 78.6 us (0.961)
  Pallas kernels: 34.4 us -> 30.9 us
    pallas_call x1, Pallas kernels: 7.63 us -> 5.75 us  [per_device(): pl.pallas_call(lambda *refs: scan_kernel(starts, width, *refs, blocks=blo...]
    pallas_call x1, Pallas kernels: 7.35 us -> 5.79 us  [per_device(): pl.pallas_call(lambda *refs: scan_back_kernel(starts, width, *refs), name...]
  transfers between devices with their start and end apart: 28 -> 28, of which waited for: 11 -> 12; matrix products, arithmetic and copies ran while one was open for 1% -> 1% of each run, Pallas kernels for 19% -> 18%
where the time goes in v6:
time: 78.6 us; the launch traced here: 78.3 us
  Pallas kernels  30.9 us (39%)
  starting transfers between devices  27.9 us (35%)
  waiting for transfers between devices  17.2 us (22%)
  other arithmetic  0.79 us (1%)
  between operations  0.79 us (1%)
    ppermute x15, starting transfers between devices, exchanged(): lax.ppermute(values[k], axis, [(i, i ^ k) for i in range(size)])  21.2 us
    ppermute x15, waiting for transfers between devices, exchanged(): lax.ppermute(values[k], axis, [(i, i ^ k) for i in range(size)])  13.3 us
    pallas_call x1, Pallas kernels, per_device(): pl.pallas_call(middle_kernel, name='attention_and_feed_forward', out_shap...  8.3 us
    pallas_call x1, Pallas kernels, per_device(): pl.pallas_call(lambda *refs: scan_back_kernel(starts, width, *refs), name...  5.79 us
    pallas_call x1, Pallas kernels, per_device(): pl.pallas_call(lambda *refs: scan_kernel(starts, width, *refs, blocks=blo...  5.75 us
    pallas_call x1, Pallas kernels, per_device(): pl.pallas_call(lambda *refs: attention_back_kernel(*refs, blocks=blocks),...  5.12 us
    ppermute x4, starting transfers between devices, to_chips(): return lax.ppermute(value, ('core', 'row'), pairs)  4.98 us
    pallas_call x1, Pallas kernels, per_device(): pl.pallas_call(depart_kernel, name='depart', out_shape=(shard,) + (payloa...  2.03 us
  transfers between devices with their start and end apart: 28, of which 12 were waited for; matrix products, arithmetic and copies ran while one was open for 1% of the time, Pallas kernels for 18%

profile of v6, /device:TPU:0, one launch (start us, length us, event | category | flops | bytes accessed | tf_op | source)
XLA Modules:
  0.0 78.3 jit_solution(5942833398741133899)
XLA Ops:
  0.6 2.0 %depart.1 = (bf16[48,384]{1,0:T(8,128)(2,1)}, bf16[416,128]{1,0:T(8,128)(2,1)}, bf16[416,128]{1,0:T(8,128)(2,1)}, bf16[416,128]{1,0:T(8,128)(2,1)}, bf16[416,128]{1,0:T(8,128)(2,1)}) custom-call(bf16[24,48]{1,0:T(8,128)(2,1)} %bitcast.27, bf16[8,48]{1,0:T(8,128)(2,1)} %bitcast.29, bf16[8,48]{1,0:T(8,128)(2,1)} %bitcast.30, bf16[24,48]{1,0:T(8,128)(2,1)} %bitcast.28, ...), custom_call_target="tpu_custom_call" | custom-call | tf_op jit(solution)/shard_map/depart/pallas_call | solution.py:1184
  2.7 5.0 %collective-permute-start.7 = (bf16[48,384]{1,0:T(8,128)(2,1)}, bf16[48,384]{1,0:T(8,128)(2,1)S(1)}, u32[]{:S(2)}, u32[]{:S(2)}) collective-permute-start(bf16[48,384]{1,0:T(8,128)(2,1)} %get-tuple-element.100), channel_id=1, source_target_pairs={{0,24},{8,16},{16,8},{24,0},{1,25},{9,17},{17,9},{25,1},{2,26},{10... | collective-permute-start | bytes 110600 | tf_op jit(solution)/shard_map/ppermute | solution.py:1165
  8.3 1.5 %collective-permute-start = (bf16[416,128]{1,0:T(8,128)(2,1)}, bf16[416,128]{1,0:T(8,128)(2,1)S(1)}, u32[]{:S(2)}, u32[]{:S(2)}) collective-permute-start(bf16[416,128]{1,0:T(8,128)(2,1)} %get-tuple-element.90), channel_id=1, source_target_pairs={{0,0},{1,1},{2,4},{3,5},{4,2},{5,3},{6,6},{7,7},{8,8},{9,9},{10,12... | collective-permute-start | bytes 319496 | tf_op jit(solution)/shard_map/ppermute | solution.py:1174
  9.9 1.7 %collective-permute-start.1 = (bf16[416,128]{1,0:T(8,128)(2,1)}, bf16[416,128]{1,0:T(8,128)(2,1)S(1)}, u32[]{:S(2)}, u32[]{:S(2)}) collective-permute-start(bf16[416,128]{1,0:T(8,128)(2,1)} %get-tuple-element.91), channel_id=1, source_target_pairs={{0,1},{1,0},{2,5},{3,4},{4,3},{5,2},{6,7},{7,6},{8,9},{9,8},{10,13... | collective-permute-start | bytes 319496 | tf_op jit(solution)/shard_map/ppermute | solution.py:1174
  11.6 1.5 %collective-permute-start.2 = (bf16[416,128]{1,0:T(8,128)(2,1)}, bf16[416,128]{1,0:T(8,128)(2,1)S(1)}, u32[]{:S(2)}, u32[]{:S(2)}) collective-permute-start(bf16[416,128]{1,0:T(8,128)(2,1)} %get-tuple-element.92), channel_id=1, source_target_pairs={{0,4},{1,5},{2,0},{3,1},{4,6},{5,7},{6,2},{7,3},{8,12},{9,13},{10,... | collective-permute-start | bytes 319496 | tf_op jit(solution)/shard_map/ppermute | solution.py:1174
  13.3 0.8 %pad_maximum_fusion.refs_6_.refs_0_ = bf16[4,48,384]{2,1,0:T(8,128)(2,1)S(1)} fusion(bf16[1,48,384]{2,1,0:T(8,128)(2,1)S(1)} %bitcast.23, bf16[1,48,384]{2,1,0:T(8,128)(2,1)S(1)} %bitcast.24, bf16[1,48,384]{2,1,0:T(8,128)(2,1)S(1)} %bitcast.25, bf16[1,48,384]{2,1,0:T(8,128)(2,1)} %bitcast.22), kind=kLoop, calls=%fused_computation | loop fusion | flops 221184 | bytes 294912 | tf_op jit(solution)/shard_map/stack | solution.py:1225
  14.1 2.7 %collective-permute-start.10 = (bf16[4,48,384]{2,1,0:T(8,128)(2,1)S(1)}, bf16[4,48,384]{2,1,0:T(8,128)(2,1)S(1)}, u32[]{:S(2)}, u32[]{:S(2)}) collective-permute-start(bf16[4,48,384]{2,1,0:T(8,128)(2,1)S(1)} %pad_maximum_fusion.refs_6_.refs_0_), channel_id=1, source_target_pairs={{0,3},{1,2},{2,1},{3,0},{4,7},{5,6},{6,5},{7,4},{8,11},{9,10},{10,... | collective-permute-start | bytes 442376 | tf_op jit(solution)/shard_map/ppermute | solution.py:1165
  17.1 1.1 %collective-permute-start.8 = (bf16[4,48,384]{2,1,0:T(8,128)(2,1)S(1)}, bf16[4,48,384]{2,1,0:T(8,128)(2,1)S(1)}, u32[]{:S(2)}, u32[]{:S(2)}) collective-permute-start(bf16[4,48,384]{2,1,0:T(8,128)(2,1)S(1)} %pad_maximum_fusion.refs_6_.refs_0_), channel_id=1, source_target_pairs={{0,1},{1,0},{2,3},{3,2},{4,5},{5,4},{6,7},{7,6},{8,9},{9,8},{10,11... | collective-permute-start | bytes 442376 | tf_op jit(solution)/shard_map/ppermute | solution.py:1165
  18.2 1.5 %collective-permute-done.2.refs_3_ = bf16[416,128]{1,0:T(8,128)(2,1)S(1)} collective-permute-done((bf16[416,128]{1,0:T(8,128)(2,1)}, bf16[416,128]{1,0:T(8,128)(2,1)S(1)}, u32[]{:S(2)}, u32[]{:S(2)}) %collective-permute-start.2) | collective-permute-done | bytes 106528 | tf_op jit(solution)/shard_map/ppermute | solution.py:1174
  20.1 0.7 copy-done.3
  20.7 1.1 %first_norm.1 = (bf16[4,2,128,192]{3,2,1,0:T(8,128)(2,1)S(1)}, bf16[512,192]{1,0:T(8,128)(2,1)S(1)}, f32[1024,128]{1,0:T(8,128)S(1)}, bf16[1024,192]{1,0:T(8,128...) custom-call(f32[2,192]{1,0:T(2,128)S(1)} %copy-done.3, ...), custom_call_target="tpu_custom_call" | custom-call | tf_op jit(solution)/shard_map/first_norm/pallas_call | solution.py:1229
  22.4 0.8 collective-permute-done.10.refs_9_.refs_3_
  23.2 3.0 %collective-permute-done.9.refs_8_.refs_2_ = bf16[4,48,384]{2,1,0:T(8,128)(2,1)S(1)} collective-permute-done((bf16[4,48,384]{2,1,0:T(8,128)(2,1)S(1)}, bf16[4,48,384]{2,1,0:T(8,128)(2,1)S(1)}, u32[]{:S(2)}, u32[]{:S(2)}) %collective-permute-start.9) | collective-permute-done | bytes 147488 | tf_op jit(solution)/shard_map/ppermute | solution.py:1165
  26.7 0.8 %collective-permute-done.13.refs_12_.refs_6_ = bf16[4,48,384]{2,1,0:T(8,128)(2,1)S(1)} collective-permute-done((bf16[4,48,384]{2,1,0:T(8,128)(2,1)S(1)}, bf16[4,48,384]{2,1,0:T(8,128)(2,1)S(1)}, u32[]{:S(2)}, u32[]{:S(2)}) %collective-permute-start.13) | collective-permute-done | bytes 147488 | tf_op jit(solution)/shard_map/ppermute | solution.py:1160
  27.7 5.8 %scan_forward.1 = (bf16[3,512,128]{2,1,0:T(8,128)(2,1)S(1)}, bf16[3,1024,128]{2,1,0:T(8,128)(2,1)S(1)}, bf16[3,1024,128]{2,1,0:T(8,128)(2,1)S(1)}, bf16[1024,192...) custom-call(bf16[512,192]{1,0:T(8,128)(2,1)S(1)} %get-tuple-element., ...), custom_call_target="tpu_custom_call" | custom-call | tf_op jit(solution)/shard_map/scan_forward/pallas_call | solution.py:1249
  33.5 8.3 %attention_and_feed_forward.1 = (bf16[3,1024,512]{2,1,0:T(8,128)(2,1)S(1)}, bf16[3,512,128]{2,1,0:T(8,128)(2,1)S(1)}, bf16[512,192]{1,0:T(8,128)(2,1)S(1)}, f32[...) custom-call(bf16[4,2,128,192]{3,2,1,0:T(8,128)(2,1)S(1)} %get-tuple-, ...), custom_call_target="tpu_custom_call" | custom-call | tf_op jit(solution)/shard_map/attention_and_feed_forward/pallas_call | solution.py:1273
  42.2 5.1 %attention_backward.1 = (bf16[1024,192]{1,0:T(8,128)(2,1)S(1)}, bf16[3,192,384]{2,1,0:T(8,128)(2,1)S(1)}) custom-call(bf16[3,1024,512]{2,1,0:T(8,128)(2,1)S(1)} %get-tuple-element.107.refs_0_, bf16[3,512,128]{2,1,0:T(8,128)(2,1)S(1)} %get-tuple-element.108.refs_1_, bf16[3,512,128]{2,1,0:T(8,128)(2,1)S(1)} %get-tuple-element.101.q_ref.refs_2_, ...), custom_call_target="tpu_custom_call" | custom-call | tf_op jit(solution)/shard_map/attention_backward/pallas_call | solution.py:1310
  47.8 1.5 %collective-permute-start.17 = (bf16[288,256]{1,0:T(8,128)(2,1)S(1)}, bf16[288,256]{1,0:T(8,128)(2,1)S(1)}, u32[]{:S(2)}, u32[]{:S(2)}) collective-permute-start(bf16[288,256]{1,0:T(8,128)(2,1)S(1)} %get-tuple-element.129), channel_id=1, source_target_pairs={{0,1},{1,0},{2,3},{3,2},{4,5},{5,4},{6,7},{7,6},{8,9},{9,8},{10,11... | collective-permute-start | bytes 442376 | tf_op jit(solution)/shard_map/ppermute | solution.py:1165
  49.6 1.7 %collective-permute-start.19 = (bf16[288,256]{1,0:T(8,128)(2,1)S(1)}, bf16[288,256]{1,0:T(8,128)(2,1)S(1)}, u32[]{:S(2)}, u32[]{:S(2)}) collective-permute-start(bf16[288,256]{1,0:T(8,128)(2,1)S(1)} %get-tuple-element.131), channel_id=1, source_target_pairs={{0,3},{1,2},{2,1},{3,0},{4,7},{5,6},{6,5},{7,4},{8,11},{9,10},{10,... | collective-permute-start | bytes 442376 | tf_op jit(solution)/shard_map/ppermute | solution.py:1165
  51.3 5.8 %scan_backward.1 = (bf16[17,48,128]{2,1,0:T(8,128)(2,1)S(1)}, bf16[17,48,128]{2,1,0:T(8,128)(2,1)S(1)}, f32[512,192]{1,0:T(8,128)S(1)}) custom-call(bf16[4,2,128,192]{3,2,1,0:T(8,128)(2,1)S(1)} %get-tuple-element.94.own_ref.refs_0_, f32[1024,128]{1,0:T(8,128)S(1)} %get-tuple-element.95.refs_2_.mask_ref.refs_1_, ...), custom_call_target="tpu_custom_call" | custom-call | tf_op jit(solution)/shard_map/scan_backward/pallas_call | solution.py:1341
  57.1 1.1 %collective-permute-done.18.refs_2_ = bf16[288,256]{1,0:T(8,128)(2,1)S(1)} collective-permute-done((bf16[288,256]{1,0:T(8,128)(2,1)S(1)}, bf16[288,256]{1,0:T(8,128)(2,1)S(1)}, u32[]{:S(2)}, u32[]{:S(2)}) %collective-permute-start.18) | collective-permute-done | bytes 147488 | tf_op jit(solution)/shard_map/ppermute | solution.py:1165
  58.8 0.9 %collective-permute-done.20.refs_1_ = bf16[17,48,128]{2,1,0:T(8,128)(2,1)S(1)} collective-permute-done((bf16[17,48,128]{2,1,0:T(8,128)(2,1)S(1)}, bf16[17,48,128]{2,1,0:T(8,128)(2,1)S(1)}, u32[]{:S(2)}, u32[]{:S(2)}) %collective-permute-start.20) | collective-permute-done | bytes 208928 | tf_op jit(solution)/shard_map/ppermute | solution.py:1160
  60.4 1.2 %collective-permute-start.22 = (bf16[400,128]{1,0:T(8,128)(2,1)S(1)}, bf16[400,128]{1,0:T(8,128)(2,1)S(1)}, u32[]{:S(2)}, u32[]{:S(2)}) collective-permute-start(bf16[400,128]{1,0:T(8,128)(2,1)S(1)} %get-tuple-element.146), channel_id=1, source_target_pairs={{0,2},{1,3},{2,0},{3,1},{4,6},{5,7},{6,4},{7,5},{8,10},{9,11},{10,... | collective-permute-start | bytes 307208 | tf_op jit(solution)/shard_map/ppermute | solution.py:1165
  61.5 1.8 %collective-permute-start.23 = (bf16[400,128]{1,0:T(8,128)(2,1)S(1)}, bf16[400,128]{1,0:T(8,128)(2,1)S(1)}, u32[]{:S(2)}, u32[]{:S(2)}) collective-permute-start(bf16[400,128]{1,0:T(8,128)(2,1)S(1)} %get-tuple-element.147), channel_id=1, source_target_pairs={{0,3},{1,2},{2,1},{3,0},{4,7},{5,6},{6,5},{7,4},{8,11},{9,10},{10,... | collective-permute-start | bytes 307208 | tf_op jit(solution)/shard_map/ppermute | solution.py:1165
  63.3 2.2 %collective-permute-done.21.refs_5_ = bf16[400,128]{1,0:T(8,128)(2,1)S(1)} collective-permute-done((bf16[400,128]{1,0:T(8,128)(2,1)S(1)}, bf16[400,128]{1,0:T(8,128)(2,1)S(1)}, u32[]{:S(2)}, u32[]{:S(2)}) %collective-permute-start.21) | collective-permute-done | bytes 102432 | tf_op jit(solution)/shard_map/ppermute | solution.py:1165
  65.5 1.7 %collective-permute-done.22.refs_6_ = bf16[400,128]{1,0:T(8,128)(2,1)S(1)} collective-permute-done((bf16[400,128]{1,0:T(8,128)(2,1)S(1)}, bf16[400,128]{1,0:T(8,128)(2,1)S(1)}, u32[]{:S(2)}, u32[]{:S(2)}) %collective-permute-start.22) | collective-permute-done | bytes 102432 | tf_op jit(solution)/shard_map/ppermute | solution.py:1165
  67.5 1.3 %collective-permute-start.24 = (bf16[48,384]{1,0:T(8,128)(2,1)S(1)}, bf16[48,384]{1,0:T(8,128)(2,1)S(1)}, u32[]{:S(2)}, u32[]{:S(2)}) collective-permute-start(bf16[48,384]{1,0:T(8,128)(2,1)S(1)} %get-tuple-element.149), channel_id=1, source_target_pairs={{0,8},{8,0},{16,24},{24,16},{1,9},{9,1},{17,25},{25,17},{2,10},{10... | collective-permute-start | bytes 110600 | tf_op jit(solution)/shard_map/ppermute | solution.py:1165
  68.8 2.9 %collective-permute-start.25 = (bf16[48,384]{1,0:T(8,128)(2,1)S(1)}, bf16[48,384]{1,0:T(8,128)(2,1)S(1)}, u32[]{:S(2)}, u32[]{:S(2)}) collective-permute-start(bf16[48,384]{1,0:T(8,128)(2,1)S(1)} %get-tuple-element.150), channel_id=1, source_target_pairs={{0,16},{8,24},{16,0},{24,8},{1,17},{9,25},{17,1},{25,9},{2,18},{10... | collective-permute-start | bytes 110600 | tf_op jit(solution)/shard_map/ppermute | solution.py:1165
  72.0 1.0 %home.1 = (bf16[2,256,192]{2,1,0:T(8,128)(2,1)}, bf16[2,256,192]{2,1,0:T(8,128)(2,1)}) custom-call(bf16[2,384,128]{2,1,0:T(8,128)(2,1)S(1)} %collective-permute-done.27.swapped_ref, bf16[288,256]{1,0:T(8,128)(2,1)S(1)} %get-tuple-element.132.refs_0_, bf16[288,256]{1,0:T(8,128)(2,1)S(1)} %collective-permute-done.17.refs_1_, ...), custom_call_target="tpu_custom_call" | custom-call | tf_op jit(solution)/shard_map/home/pallas_call | solution.py:1417
  73.0 1.6 %collective-permute-done.25.refs_2_ = bf16[48,384]{1,0:T(8,128)(2,1)S(1)} collective-permute-done((bf16[48,384]{1,0:T(8,128)(2,1)S(1)}, bf16[48,384]{1,0:T(8,128)(2,1)S(1)}, u32[]{:S(2)}, u32[]{:S(2)}) %collective-permute-start.25) | collective-permute-done | bytes 36896 | tf_op jit(solution)/shard_map/ppermute | solution.py:1165
  74.6 2.9 %collective-permute-done.26.refs_3_ = bf16[48,384]{1,0:T(8,128)(2,1)S(1)} collective-permute-done((bf16[48,384]{1,0:T(8,128)(2,1)S(1)}, bf16[48,384]{1,0:T(8,128)(2,1)S(1)}, u32[]{:S(2)}, u32[]{:S(2)}) %collective-permute-start.26) | collective-permute-done | bytes 36896 | tf_op jit(solution)/shard_map/ppermute | solution.py:1165
  77.5 0.8 %final_sum.1 = (f32[1,192]{1,0:T(1,128)}, f32[1,192]{1,0:T(1,128)}, f32[24,48]{1,0:T(8,128)}, f32[8,48]{1,0:T(8,128)}, f32[8,48]{1,0:T(8,128)}, /*index=5*/f32[4...) custom-call(bf16[48,384]{1,0:T(8,128)(2,1)S(1)} %get-tuple-element.156.refs_0_, ...), custom_call_target="tpu_custom_call" | custom-call | tf_op jit(solution)/shard_map/final_sum/pallas_call | solution.py:1428
  (48 shorter events, 5.8 us)
Async XLA Ops:
  2.7 8.9 %collective-permute-start.7 = (bf16[48,384]{1,0:T(8,128)(2,1)}, bf16[48,384]{1,0:T(8,128)(2,1)S(1)}, u32[]{:S(2)}, u32[]{:S(2)}) collective-permute-start(bf16[48,384]{1,0:T(8,128)(2,1)} %get-tuple-element.100), channel_id=1, source_target_pairs={{0,24},{8,16},{16,8},{24,0},{1,25},{9,17},{17,9},{25,1},{2,26},{10... | collective-permute-start | bytes 110600 | tf_op jit(solution)/shard_map/ppermute | solution.py:1165
  7.7 5.3 %collective-permute-start.6 = (bf16[48,384]{1,0:T(8,128)(2,1)}, bf16[48,384]{1,0:T(8,128)(2,1)S(1)}, u32[]{:S(2)}, u32[]{:S(2)}) collective-permute-start(bf16[48,384]{1,0:T(8,128)(2,1)} %get-tuple-element.100), channel_id=1, source_target_pairs={{0,16},{8,24},{16,0},{24,8},{1,17},{9,25},{17,1},{25,9},{2,18},{10... | collective-permute-start | bytes 110600 | tf_op jit(solution)/shard_map/ppermute | solution.py:1165
  7.7 5.6 %collective-permute-start.5 = (bf16[48,384]{1,0:T(8,128)(2,1)}, bf16[48,384]{1,0:T(8,128)(2,1)S(1)}, u32[]{:S(2)}, u32[]{:S(2)}) collective-permute-start(bf16[48,384]{1,0:T(8,128)(2,1)} %get-tuple-element.100), channel_id=1, source_target_pairs={{0,8},{8,0},{16,24},{24,16},{1,9},{9,1},{17,25},{25,17},{2,10},{10... | collective-permute-start | bytes 110600 | tf_op jit(solution)/shard_map/ppermute | solution.py:1165
  8.3 8.5 %collective-permute-start = (bf16[416,128]{1,0:T(8,128)(2,1)}, bf16[416,128]{1,0:T(8,128)(2,1)S(1)}, u32[]{:S(2)}, u32[]{:S(2)}) collective-permute-start(bf16[416,128]{1,0:T(8,128)(2,1)} %get-tuple-element.90), channel_id=1, source_target_pairs={{0,0},{1,1},{2,4},{3,5},{4,2},{5,3},{6,6},{7,7},{8,8},{9,9},{10,12... | collective-permute-start | bytes 319496 | tf_op jit(solution)/shard_map/ppermute | solution.py:1174
  9.9 7.2 %collective-permute-start.1 = (bf16[416,128]{1,0:T(8,128)(2,1)}, bf16[416,128]{1,0:T(8,128)(2,1)S(1)}, u32[]{:S(2)}, u32[]{:S(2)}) collective-permute-start(bf16[416,128]{1,0:T(8,128)(2,1)} %get-tuple-element.91), channel_id=1, source_target_pairs={{0,1},{1,0},{2,5},{3,4},{4,3},{5,2},{6,7},{7,6},{8,9},{9,8},{10,13... | collective-permute-start | bytes 319496 | tf_op jit(solution)/shard_map/ppermute | solution.py:1174
  11.6 8.1 %collective-permute-start.2 = (bf16[416,128]{1,0:T(8,128)(2,1)}, bf16[416,128]{1,0:T(8,128)(2,1)S(1)}, u32[]{:S(2)}, u32[]{:S(2)}) collective-permute-start(bf16[416,128]{1,0:T(8,128)(2,1)} %get-tuple-element.92), channel_id=1, source_target_pairs={{0,4},{1,5},{2,0},{3,1},{4,6},{5,7},{6,2},{7,3},{8,12},{9,13},{10,... | collective-permute-start | bytes 319496 | tf_op jit(solution)/shard_map/ppermute | solution.py:1174
  13.1 7.0 %collective-permute-start.3 = (bf16[416,128]{1,0:T(8,128)(2,1)}, bf16[416,128]{1,0:T(8,128)(2,1)S(1)}, u32[]{:S(2)}, u32[]{:S(2)}) collective-permute-start(bf16[416,128]{1,0:T(8,128)(2,1)} %get-tuple-element.93), channel_id=1, source_target_pairs={{0,5},{1,4},{2,1},{3,0},{4,7},{5,6},{6,3},{7,2},{8,13},{9,12},{10,... | collective-permute-start | bytes 319496 | tf_op jit(solution)/shard_map/ppermute | solution.py:1174
  14.1 9.0 %collective-permute-start.10 = (bf16[4,48,384]{2,1,0:T(8,128)(2,1)S(1)}, bf16[4,48,384]{2,1,0:T(8,128)(2,1)S(1)}, u32[]{:S(2)}, u32[]{:S(2)}) collective-permute-start(bf16[4,48,384]{2,1,0:T(8,128)(2,1)S(1)} %pad_maximum_fusion.refs_6_.refs_0_), channel_id=1, source_target_pairs={{0,3},{1,2},{2,1},{3,0},{4,7},{5,6},{6,5},{7,4},{8,11},{9,10},{10,... | collective-permute-start | bytes 442376 | tf_op jit(solution)/shard_map/ppermute | solution.py:1165
  16.9 9.3 %collective-permute-start.9 = (bf16[4,48,384]{2,1,0:T(8,128)(2,1)S(1)}, bf16[4,48,384]{2,1,0:T(8,128)(2,1)S(1)}, u32[]{:S(2)}, u32[]{:S(2)}) collective-permute-start(bf16[4,48,384]{2,1,0:T(8,128)(2,1)S(1)} %pad_maximum_fusion.refs_6_.refs_0_), channel_id=1, source_target_pairs={{0,2},{1,3},{2,0},{3,1},{4,6},{5,7},{6,4},{7,5},{8,10},{9,11},{10,... | collective-permute-start | bytes 442376 | tf_op jit(solution)/shard_map/ppermute | solution.py:1165
  17.1 9.1 %collective-permute-start.8 = (bf16[4,48,384]{2,1,0:T(8,128)(2,1)S(1)}, bf16[4,48,384]{2,1,0:T(8,128)(2,1)S(1)}, u32[]{:S(2)}, u32[]{:S(2)}) collective-permute-start(bf16[4,48,384]{2,1,0:T(8,128)(2,1)S(1)} %pad_maximum_fusion.refs_6_.refs_0_), channel_id=1, source_target_pairs={{0,1},{1,0},{2,3},{3,2},{4,5},{5,4},{6,7},{7,6},{8,9},{9,8},{10,11... | collective-permute-start | bytes 442376 | tf_op jit(solution)/shard_map/ppermute | solution.py:1165
  21.8 4.8 %collective-permute-start.4 = (bf16[512,192]{1,0:T(8,128)(2,1)S(1)}, bf16[512,192]{1,0:T(8,128)(2,1)S(1)}, u32[]{:S(2)}, u32[]{:S(2)}) collective-permute-start(bf16[512,192]{1,0:T(8,128)(2,1)S(1)} %get-tuple-element.96.refs_0_.refs_5_), channel_id=1, source_target_pairs={{0,4},{4,0},{1,5},{5,1},{2,6},{6,2},{3,7},{7,3},{8,12},{12,8},{9,1... | collective-permute-start | bytes 589832 | tf_op jit(solution)/shard_map/ppermute | solution.py:1160
  21.9 4.7 %collective-permute-start.11 = (bf16[4,48,384]{2,1,0:T(8,128)(2,1)S(1)}, bf16[4,48,384]{2,1,0:T(8,128)(2,1)S(1)}, u32[]{:S(2)}, u32[]{:S(2)}) collective-permute-start(bf16[4,48,384]{2,1,0:T(8,128)(2,1)S(1)} %pad_maximum_fusion.refs_6_.refs_0_), channel_id=1, source_target_pairs={{0,4},{4,0},{1,5},{5,1},{2,6},{6,2},{3,7},{7,3},{8,12},{12,8},{9,1... | collective-permute-start | bytes 442376 | tf_op jit(solution)/shard_map/ppermute | solution.py:1160
  23.2 3.5 %collective-permute-start.14 = (bf16[4,48,384]{2,1,0:T(8,128)(2,1)S(1)}, bf16[4,48,384]{2,1,0:T(8,128)(2,1)S(1)}, u32[]{:S(2)}, u32[]{:S(2)}) collective-permute-start(bf16[4,48,384]{2,1,0:T(8,128)(2,1)S(1)} %collective-permute-done.10.refs_9_.refs_3_), channel_id=1, source_target_pairs={{0,4},{4,0},{1,5},{5,1},{2,6},{6,2},{3,7},{7,3},{8,12},{12,8},{9,1... | collective-permute-start | bytes 442376 | tf_op jit(solution)/shard_map/ppermute | solution.py:1160
  26.1 1.4 %collective-permute-start.13 = (bf16[4,48,384]{2,1,0:T(8,128)(2,1)S(1)}, bf16[4,48,384]{2,1,0:T(8,128)(2,1)S(1)}, u32[]{:S(2)}, u32[]{:S(2)}) collective-permute-start(bf16[4,48,384]{2,1,0:T(8,128)(2,1)S(1)} %collective-permute-done.9.refs_8_.refs_2_), channel_id=1, source_target_pairs={{0,4},{4,0},{1,5},{5,1},{2,6},{6,2},{3,7},{7,3},{8,12},{12,8},{9,1... | collective-permute-start | bytes 442376 | tf_op jit(solution)/shard_map/ppermute | solution.py:1160
  26.2 1.5 %collective-permute-start.12 = (bf16[4,48,384]{2,1,0:T(8,128)(2,1)S(1)}, bf16[4,48,384]{2,1,0:T(8,128)(2,1)S(1)}, u32[]{:S(2)}, u32[]{:S(2)}) collective-permute-start(bf16[4,48,384]{2,1,0:T(8,128)(2,1)S(1)} %collective-permute-done.8.refs_7_.refs_1_), channel_id=1, source_target_pairs={{0,4},{4,0},{1,5},{5,1},{2,6},{6,2},{3,7},{7,3},{8,12},{12,8},{9,1... | collective-permute-start | bytes 442376 | tf_op jit(solution)/shard_map/ppermute | solution.py:1160
  27.7 5.8 %copy-start = (bf16[4,1024,192]{2,1,0:T(8,128)(2,1)S(1)}, bf16[4,1024,192]{2,1,0:T(8,128)(2,1)}, u32[]{:S(2)}) copy-start(bf16[4,1024,192]{2,1,0:T(8,128)(2,1)} %constant.8.clone.sel_2_ref) | copy-start | bytes 4718596
  27.7 5.8 %copy-start.1 = (bf16[1024,192]{1,0:T(8,128)(2,1)S(1)}, bf16[1024,192]{1,0:T(8,128)(2,1)}, u32[]{:S(2)}) copy-start(bf16[1024,192]{1,0:T(8,128)(2,1)} %constant.7.clone.sel_o_ref) | copy-start | bytes 1179652
  27.7 5.8 %copy-start.2 = (bf16[512,384]{1,0:T(8,128)(2,1)S(1)}, bf16[512,384]{1,0:T(8,128)(2,1)}, u32[]{:S(2)}) copy-start(bf16[512,384]{1,0:T(8,128)(2,1)} %constant.6.clone.sel_1_ref) | copy-start | bytes 1179652
  27.7 5.8 %copy-start.4 = (f32[2,192]{1,0:T(2,128)S(1)}, f32[2,192]{1,0:T(2,128)}, u32[]{:S(2)}) copy-start(f32[2,192]{1,0:T(2,128)} %gains_ref.3) | copy-start | bytes 4612
  41.8 5.5 %collective-permute-start.15 = (bf16[4,4,48,256]{3,2,1,0:T(8,128)(2,1)S(1)}, bf16[4,4,48,256]{3,2,1,0:T(8,128)(2,1)S(1)}, u32[]{:S(2)}, u32[]{:S(2)}) collective-permute-start(bf16[4,4,48,256]{3,2,1,0:T(8,128)(2,1)S(1)} %get-tuple-element.106), channel_id=1, source_target_pairs={{0,4},{4,0},{1,5},{5,1},{2,6},{6,2},{3,7},{7,3},{8,12},{12,8},{9,1... | collective-permute-start | bytes 1179656 | tf_op jit(solution)/shard_map/ppermute | solution.py:1160
  47.6 3.7 %collective-permute-start.16 = (bf16[1024,192]{1,0:T(8,128)(2,1)S(1)}, bf16[1024,192]{1,0:T(8,128)(2,1)S(1)}, u32[]{:S(2)}, u32[]{:S(2)}) collective-permute-start(bf16[1024,192]{1,0:T(8,128)(2,1)S(1)} %get-tuple-element.119.refs_2_), channel_id=1, source_target_pairs={{0,4},{4,0},{1,5},{5,1},{2,6},{6,2},{3,7},{7,3},{8,12},{12,8},{9,1... | collective-permute-start | bytes 1179656 | tf_op jit(solution)/shard_map/ppermute | solution.py:1160
  47.8 9.3 %collective-permute-start.17 = (bf16[288,256]{1,0:T(8,128)(2,1)S(1)}, bf16[288,256]{1,0:T(8,128)(2,1)S(1)}, u32[]{:S(2)}, u32[]{:S(2)}) collective-permute-start(bf16[288,256]{1,0:T(8,128)(2,1)S(1)} %get-tuple-element.129), channel_id=1, source_target_pairs={{0,1},{1,0},{2,3},{3,2},{4,5},{5,4},{6,7},{7,6},{8,9},{9,8},{10,11... | collective-permute-start | bytes 442376 | tf_op jit(solution)/shard_map/ppermute | solution.py:1165
  49.2 9.0 %collective-permute-start.18 = (bf16[288,256]{1,0:T(8,128)(2,1)S(1)}, bf16[288,256]{1,0:T(8,128)(2,1)S(1)}, u32[]{:S(2)}, u32[]{:S(2)}) collective-permute-start(bf16[288,256]{1,0:T(8,128)(2,1)S(1)} %get-tuple-element.130), channel_id=1, source_target_pairs={{0,2},{1,3},{2,0},{3,1},{4,6},{5,7},{6,4},{7,5},{8,10},{9,11},{10,... | collective-permute-start | bytes 442376 | tf_op jit(solution)/shard_map/ppermute | solution.py:1165
  49.6 8.6 %collective-permute-start.19 = (bf16[288,256]{1,0:T(8,128)(2,1)S(1)}, bf16[288,256]{1,0:T(8,128)(2,1)S(1)}, u32[]{:S(2)}, u32[]{:S(2)}) collective-permute-start(bf16[288,256]{1,0:T(8,128)(2,1)S(1)} %get-tuple-element.131), channel_id=1, source_target_pairs={{0,3},{1,2},{2,1},{3,0},{4,7},{5,6},{6,5},{7,4},{8,11},{9,10},{10,... | collective-permute-start | bytes 442376 | tf_op jit(solution)/shard_map/ppermute | solution.py:1165
  58.2 1.5 %collective-permute-start.20 = (bf16[17,48,128]{2,1,0:T(8,128)(2,1)S(1)}, bf16[17,48,128]{2,1,0:T(8,128)(2,1)S(1)}, u32[]{:S(2)}, u32[]{:S(2)}) collective-permute-start(bf16[17,48,128]{2,1,0:T(8,128)(2,1)S(1)} %get-tuple-element.137), channel_id=1, source_target_pairs={{0,4},{4,0},{1,5},{5,1},{2,6},{6,2},{3,7},{7,3},{8,12},{12,8},{9,1... | collective-permute-start | bytes 626696 | tf_op jit(solution)/shard_map/ppermute | solution.py:1160
  59.7 5.8 %collective-permute-start.21 = (bf16[400,128]{1,0:T(8,128)(2,1)S(1)}, bf16[400,128]{1,0:T(8,128)(2,1)S(1)}, u32[]{:S(2)}, u32[]{:S(2)}) collective-permute-start(bf16[400,128]{1,0:T(8,128)(2,1)S(1)} %get-tuple-element.145), channel_id=1, source_target_pairs={{0,1},{1,0},{2,3},{3,2},{4,5},{5,4},{6,7},{7,6},{8,9},{9,8},{10,11... | collective-permute-start | bytes 307208 | tf_op jit(solution)/shard_map/ppermute | solution.py:1165
  60.4 6.9 %collective-permute-start.22 = (bf16[400,128]{1,0:T(8,128)(2,1)S(1)}, bf16[400,128]{1,0:T(8,128)(2,1)S(1)}, u32[]{:S(2)}, u32[]{:S(2)}) collective-permute-start(bf16[400,128]{1,0:T(8,128)(2,1)S(1)} %get-tuple-element.146), channel_id=1, source_target_pairs={{0,2},{1,3},{2,0},{3,1},{4,6},{5,7},{6,4},{7,5},{8,10},{9,11},{10,... | collective-permute-start | bytes 307208 | tf_op jit(solution)/shard_map/ppermute | solution.py:1165
  61.5 5.7 %collective-permute-start.23 = (bf16[400,128]{1,0:T(8,128)(2,1)S(1)}, bf16[400,128]{1,0:T(8,128)(2,1)S(1)}, u32[]{:S(2)}, u32[]{:S(2)}) collective-permute-start(bf16[400,128]{1,0:T(8,128)(2,1)S(1)} %get-tuple-element.147), channel_id=1, source_target_pairs={{0,3},{1,2},{2,1},{3,0},{4,7},{5,6},{6,5},{7,4},{8,11},{9,10},{10,... | collective-permute-start | bytes 307208 | tf_op jit(solution)/shard_map/ppermute | solution.py:1165
  67.3 4.7 %collective-permute-start.27 = (bf16[2,384,128]{2,1,0:T(8,128)(2,1)S(1)}, bf16[2,384,128]{2,1,0:T(8,128)(2,1)S(1)}, u32[]{:S(2)}, u32[]{:S(2)}) collective-permute-start(bf16[2,384,128]{2,1,0:T(8,128)(2,1)S(1)} %choose.1), channel_id=1, source_target_pairs={{0,4},{4,0},{1,5},{5,1},{2,6},{6,2},{3,7},{7,3},{8,12},{12,8},{9,1... | collective-permute-start | bytes 589832 | tf_op jit(solution)/shard_map/ppermute | solution.py:1160
  67.5 5.5 %collective-permute-start.24 = (bf16[48,384]{1,0:T(8,128)(2,1)S(1)}, bf16[48,384]{1,0:T(8,128)(2,1)S(1)}, u32[]{:S(2)}, u32[]{:S(2)}) collective-permute-start(bf16[48,384]{1,0:T(8,128)(2,1)S(1)} %get-tuple-element.149), channel_id=1, source_target_pairs={{0,8},{8,0},{16,24},{24,16},{1,9},{9,1},{17,25},{25,17},{2,10},{10... | collective-permute-start | bytes 110600 | tf_op jit(solution)/shard_map/ppermute | solution.py:1165
  68.8 5.7 %collective-permute-start.25 = (bf16[48,384]{1,0:T(8,128)(2,1)S(1)}, bf16[48,384]{1,0:T(8,128)(2,1)S(1)}, u32[]{:S(2)}, u32[]{:S(2)}) collective-permute-start(bf16[48,384]{1,0:T(8,128)(2,1)S(1)} %get-tuple-element.150), channel_id=1, source_target_pairs={{0,16},{8,24},{16,0},{24,8},{1,17},{9,25},{17,1},{25,9},{2,18},{10... | collective-permute-start | bytes 110600 | tf_op jit(solution)/shard_map/ppermute | solution.py:1165
  71.8 5.8 %collective-permute-start.26 = (bf16[48,384]{1,0:T(8,128)(2,1)S(1)}, bf16[48,384]{1,0:T(8,128)(2,1)S(1)}, u32[]{:S(2)}, u32[]{:S(2)}) collective-permute-start(bf16[48,384]{1,0:T(8,128)(2,1)S(1)} %get-tuple-element.151), channel_id=1, source_target_pairs={{0,24},{8,16},{16,8},{24,0},{1,25},{9,17},{17,9},{25,1},{2,26},{10... | collective-permute-start | bytes 110600 | tf_op jit(solution)/shard_map/ppermute | solution.py:1165
  (1 other events, 0.7 us)

commit v7 on v6

--- a/solution.py
+++ b/solution.py
@@ -573,13 +573,16 @@
     bias = jnp.where(lane_all == HEAD_DIM, (mask_ref[...] - 1.0) * 1e30, 0.0)
     ones = jnp.where((lane_all == HEAD_DIM) | (lane_all == HEAD_DIM + 1), 1.0, 0.0)
     one_own = jnp.where(lane_own == HEAD_DIM, 1.0, 0.0)
+    found = dot(scanned_own[...], wqkv_ref[0]) * HEAD_DIM ** (-0.5)
     for h in range(HEADS):
-        tile = slice(h * LANES, (h + 1) * LANES)
-        q_ref[h] = (
-            dot(scanned_own[...], wqkv_ref[0, :, tile]) * HEAD_DIM ** (-0.5) + one_own
-        ).astype(BF16)
-        k_ref[h] = (dot(scanned_ref[...], wqkv_ref[1, :, tile]) + bias).astype(BF16)
-        v_ref[h] = (dot(scanned_ref[...], wqkv_ref[2, :, tile]) + ones).astype(BF16)
+        q_ref[h] = (found[:, h * LANES : (h + 1) * LANES] + one_own).astype(BF16)
+    targets = [(k_ref, h, 1, bias) for h in range(HEADS)] + [(v_ref, h, 2, ones) for h in range(HEADS)]
+    for pair in range(HEADS):
+        two = targets[2 * pair : 2 * pair + 2]
+        weight = [wqkv_ref[third, :, h * LANES : (h + 1) * LANES] for _, h, third, _ in two]
+        found = dot(scanned_ref[...], jnp.concatenate(weight, axis=1))
+        for i, (ref, h, _, extra) in enumerate(two):
+            ref[h] = (found[:, i * LANES : (i + 1) * LANES] + extra).astype(BF16)
 
 
 def middle_kernel(
@@ -686,7 +689,7 @@
             return 0
 
         lax.fori_loop(0, SLOTS // 128, soft_step, 0, unroll=True)
-        raw = dot_tn(soft_ref[h], v_ref[h])
+        raw = dot_tn(v_ref[h], soft_ref[h]).T
         total = raw[:, HEAD_DIM : HEAD_DIM + 1]
         sums[h] = jnp.broadcast_to(1.0 / total, (OWN, LANES))
         result = raw * sums[h]
@@ -819,7 +822,7 @@
             return 0
 
         lax.fori_loop(0, SLOTS // 64, back_step, 0, unroll=True)
-        grad_q[:, tile] = (dot_tn(grad_scores[...], k_ref[h]).astype(BF16) * HEAD_DIM ** (-0.5)).astype(
+        grad_q[:, tile] = (dot_tn(k_ref[h], grad_scores[...]).T.astype(BF16) * HEAD_DIM ** (-0.5)).astype(
             BF16
         )
         triple[0, :, tile] = dot(grad_scores[...], q_ref[h]).astype(BF16)
@@ -946,21 +949,21 @@
 
     decay, coef = rates_ref[: 4 * STATE], rates_ref[4 * STATE :]
 
-    def table_step(k, carry):
-        to_rate, to_coef = carry
-        lag = k.astype(F32)
-        powers = jnp.exp(-decay * lag)
-        grads = []
-        for way in range(2):
-            for at in (CENTER + k, CENTER - k):
-                grads.append(
-                    jnp.broadcast_to(lag_rows[way, pl.ds(at, 1), :], (STATE, 2 * LANES))
-                )
-        scaled = jnp.concatenate(grads, axis=0) * powers
-        return to_rate - lag * scaled, to_coef + scaled
-
-    zero = jnp.zeros((4 * STATE, 2 * LANES), F32)
-    to_rate, to_coef = lax.fori_loop(0, GRID, table_step, (zero, zero), unroll=4)
+    to_rate, to_coef = [], []
+    for d in range(4):
+        way, side = divmod(d, 2)
+        rate = decay[d * STATE : (d + 1) * STATE]
+        rate_sum = jnp.zeros((STATE, 2 * LANES), F32)
+        coef_sum = jnp.broadcast_to(lag_rows[way, CENTER : CENTER + 1, :], (STATE, 2 * LANES))
+        for k in range(1, GRID):
+            at = CENTER - k if side else CENTER + k
+            line = jnp.broadcast_to(lag_rows[way, at : at + 1, :], (STATE, 2 * LANES))
+            scaled = line * jnp.exp(rate * float(-k))
+            coef_sum = coef_sum + scaled
+            rate_sum = rate_sum - scaled * float(k)
+        to_rate.append(rate_sum)
+        to_coef.append(coef_sum)
+    to_rate, to_coef = jnp.concatenate(to_rate, axis=0), jnp.concatenate(to_coef, axis=0)
     grad_rc = jnp.concatenate([to_rate * coef, to_coef], axis=0).T[:D].astype(BF16)
 
     def join_step(i, _):

time: 78.6 us -> 77.1 us (0.981)
  Pallas kernels: 30.9 us -> 29 us
  transfers between devices with their start and end apart: 28 -> 28, of which waited for: 12 -> 12; matrix products, arithmetic and copies ran while one was open for 1% -> 1% of each run, Pallas kernels for 18% -> 17%
where the time goes in v7:
time: 77.1 us; the launch traced here: 76.8 us
  Pallas kernels  29 us (38%)
  starting transfers between devices  27.9 us (36%)
  waiting for transfers between devices  17.6 us (23%)
  other arithmetic  0.79 us (1%)
  between operations  0.79 us (1%)
    ppermute x15, starting transfers between devices, exchanged(): lax.ppermute(values[k], axis, [(i, i ^ k) for i in range(size)])  21.2 us
    ppermute x15, waiting for transfers between devices, exchanged(): lax.ppermute(values[k], axis, [(i, i ^ k) for i in range(size)])  13.7 us
    pallas_call x1, Pallas kernels, per_device(): pl.pallas_call(middle_kernel, name='attention_and_feed_forward', out_shap...  7.92 us
    pallas_call x1, Pallas kernels, per_device(): pl.pallas_call(lambda *refs: scan_back_kernel(starts, width, *refs), name...  5.38 us
    pallas_call x1, Pallas kernels, per_device(): pl.pallas_call(lambda *refs: scan_kernel(starts, width, *refs, blocks=blo...  5.25 us
    ppermute x4, starting transfers between devices, to_chips(): return lax.ppermute(value, ('core', 'row'), pairs)  4.98 us
    pallas_call x1, Pallas kernels, per_device(): pl.pallas_call(lambda *refs: attention_back_kernel(*refs, blocks=blocks),...  4.49 us
    pallas_call x1, Pallas kernels, per_device(): pl.pallas_call(depart_kernel, name='depart', out_shape=(shard,) + (payloa...  2.03 us
  transfers between devices with their start and end apart: 28, of which 12 were waited for; matrix products, arithmetic and copies ran while one was open for 1% of the time, Pallas kernels for 17%

profile of v7, /device:TPU:0, one launch (start us, length us, event | category | flops | bytes accessed | tf_op | source)
XLA Modules:
  0.0 76.8 jit_solution(10860200386093744459)
XLA Ops:
  0.6 2.0 %depart.1 = (bf16[48,384]{1,0:T(8,128)(2,1)}, bf16[416,128]{1,0:T(8,128)(2,1)}, bf16[416,128]{1,0:T(8,128)(2,1)}, bf16[416,128]{1,0:T(8,128)(2,1)}, bf16[416,128]{1,0:T(8,128)(2,1)}) custom-call(bf16[24,48]{1,0:T(8,128)(2,1)} %bitcast.27, bf16[8,48]{1,0:T(8,128)(2,1)} %bitcast.29, bf16[8,48]{1,0:T(8,128)(2,1)} %bitcast.30, bf16[24,48]{1,0:T(8,128)(2,1)} %bitcast.28, ...), custom_call_target="tpu_custom_call" | custom-call | tf_op jit(solution)/shard_map/depart/pallas_call | solution.py:1187
  2.7 5.0 %collective-permute-start.7 = (bf16[48,384]{1,0:T(8,128)(2,1)}, bf16[48,384]{1,0:T(8,128)(2,1)S(1)}, u32[]{:S(2)}, u32[]{:S(2)}) collective-permute-start(bf16[48,384]{1,0:T(8,128)(2,1)} %get-tuple-element.100), channel_id=1, source_target_pairs={{0,24},{8,16},{16,8},{24,0},{1,25},{9,17},{17,9},{25,1},{2,26},{10... | collective-permute-start | bytes 110600 | tf_op jit(solution)/shard_map/ppermute | solution.py:1168
  8.3 1.5 %collective-permute-start = (bf16[416,128]{1,0:T(8,128)(2,1)}, bf16[416,128]{1,0:T(8,128)(2,1)S(1)}, u32[]{:S(2)}, u32[]{:S(2)}) collective-permute-start(bf16[416,128]{1,0:T(8,128)(2,1)} %get-tuple-element.90), channel_id=1, source_target_pairs={{0,0},{1,1},{2,4},{3,5},{4,2},{5,3},{6,6},{7,7},{8,8},{9,9},{10,12... | collective-permute-start | bytes 319496 | tf_op jit(solution)/shard_map/ppermute | solution.py:1177
  9.9 1.7 %collective-permute-start.1 = (bf16[416,128]{1,0:T(8,128)(2,1)}, bf16[416,128]{1,0:T(8,128)(2,1)S(1)}, u32[]{:S(2)}, u32[]{:S(2)}) collective-permute-start(bf16[416,128]{1,0:T(8,128)(2,1)} %get-tuple-element.91), channel_id=1, source_target_pairs={{0,1},{1,0},{2,5},{3,4},{4,3},{5,2},{6,7},{7,6},{8,9},{9,8},{10,13... | collective-permute-start | bytes 319496 | tf_op jit(solution)/shard_map/ppermute | solution.py:1177
  11.6 1.5 %collective-permute-start.2 = (bf16[416,128]{1,0:T(8,128)(2,1)}, bf16[416,128]{1,0:T(8,128)(2,1)S(1)}, u32[]{:S(2)}, u32[]{:S(2)}) collective-permute-start(bf16[416,128]{1,0:T(8,128)(2,1)} %get-tuple-element.92), channel_id=1, source_target_pairs={{0,4},{1,5},{2,0},{3,1},{4,6},{5,7},{6,2},{7,3},{8,12},{9,13},{10,... | collective-permute-start | bytes 319496 | tf_op jit(solution)/shard_map/ppermute | solution.py:1177
  13.3 0.8 %pad_maximum_fusion.refs_6_.refs_0_ = bf16[4,48,384]{2,1,0:T(8,128)(2,1)S(1)} fusion(bf16[1,48,384]{2,1,0:T(8,128)(2,1)S(1)} %bitcast.23, bf16[1,48,384]{2,1,0:T(8,128)(2,1)S(1)} %bitcast.24, bf16[1,48,384]{2,1,0:T(8,128)(2,1)S(1)} %bitcast.25, bf16[1,48,384]{2,1,0:T(8,128)(2,1)} %bitcast.22), kind=kLoop, calls=%fused_computation | loop fusion | flops 221184 | bytes 294912 | tf_op jit(solution)/shard_map/stack | solution.py:1228
  14.1 2.7 %collective-permute-start.10 = (bf16[4,48,384]{2,1,0:T(8,128)(2,1)S(1)}, bf16[4,48,384]{2,1,0:T(8,128)(2,1)S(1)}, u32[]{:S(2)}, u32[]{:S(2)}) collective-permute-start(bf16[4,48,384]{2,1,0:T(8,128)(2,1)S(1)} %pad_maximum_fusion.refs_6_.refs_0_), channel_id=1, source_target_pairs={{0,3},{1,2},{2,1},{3,0},{4,7},{5,6},{6,5},{7,4},{8,11},{9,10},{10,... | collective-permute-start | bytes 442376 | tf_op jit(solution)/shard_map/ppermute | solution.py:1168
  17.1 1.1 %collective-permute-start.8 = (bf16[4,48,384]{2,1,0:T(8,128)(2,1)S(1)}, bf16[4,48,384]{2,1,0:T(8,128)(2,1)S(1)}, u32[]{:S(2)}, u32[]{:S(2)}) collective-permute-start(bf16[4,48,384]{2,1,0:T(8,128)(2,1)S(1)} %pad_maximum_fusion.refs_6_.refs_0_), channel_id=1, source_target_pairs={{0,1},{1,0},{2,3},{3,2},{4,5},{5,4},{6,7},{7,6},{8,9},{9,8},{10,11... | collective-permute-start | bytes 442376 | tf_op jit(solution)/shard_map/ppermute | solution.py:1168
  18.2 1.5 %collective-permute-done.2.refs_3_ = bf16[416,128]{1,0:T(8,128)(2,1)S(1)} collective-permute-done((bf16[416,128]{1,0:T(8,128)(2,1)}, bf16[416,128]{1,0:T(8,128)(2,1)S(1)}, u32[]{:S(2)}, u32[]{:S(2)}) %collective-permute-start.2) | collective-permute-done | bytes 106528 | tf_op jit(solution)/shard_map/ppermute | solution.py:1177
  20.1 0.7 copy-done.3
  20.7 1.1 %first_norm.1 = (bf16[4,2,128,192]{3,2,1,0:T(8,128)(2,1)S(1)}, bf16[512,192]{1,0:T(8,128)(2,1)S(1)}, f32[1024,128]{1,0:T(8,128)S(1)}, bf16[1024,192]{1,0:T(8,128...) custom-call(f32[2,192]{1,0:T(2,128)S(1)} %copy-done.3, ...), custom_call_target="tpu_custom_call" | custom-call | tf_op jit(solution)/shard_map/first_norm/pallas_call | solution.py:1232
  22.4 0.8 collective-permute-done.10.refs_9_.refs_3_
  23.2 3.0 %collective-permute-done.9.refs_8_.refs_2_ = bf16[4,48,384]{2,1,0:T(8,128)(2,1)S(1)} collective-permute-done((bf16[4,48,384]{2,1,0:T(8,128)(2,1)S(1)}, bf16[4,48,384]{2,1,0:T(8,128)(2,1)S(1)}, u32[]{:S(2)}, u32[]{:S(2)}) %collective-permute-start.9) | collective-permute-done | bytes 147488 | tf_op jit(solution)/shard_map/ppermute | solution.py:1168
  26.7 0.8 %collective-permute-done.13.refs_12_.refs_6_ = bf16[4,48,384]{2,1,0:T(8,128)(2,1)S(1)} collective-permute-done((bf16[4,48,384]{2,1,0:T(8,128)(2,1)S(1)}, bf16[4,48,384]{2,1,0:T(8,128)(2,1)S(1)}, u32[]{:S(2)}, u32[]{:S(2)}) %collective-permute-start.13) | collective-permute-done | bytes 147488 | tf_op jit(solution)/shard_map/ppermute | solution.py:1163
  27.7 5.2 %scan_forward.1 = (bf16[3,512,128]{2,1,0:T(8,128)(2,1)S(1)}, bf16[3,1024,128]{2,1,0:T(8,128)(2,1)S(1)}, bf16[3,1024,128]{2,1,0:T(8,128)(2,1)S(1)}, bf16[1024,192...) custom-call(bf16[512,192]{1,0:T(8,128)(2,1)S(1)} %get-tuple-element., ...), custom_call_target="tpu_custom_call" | custom-call | tf_op jit(solution)/shard_map/scan_forward/pallas_call | solution.py:1252
  33.0 7.9 %attention_and_feed_forward.1 = (bf16[3,1024,512]{2,1,0:T(8,128)(2,1)S(1)}, bf16[3,512,128]{2,1,0:T(8,128)(2,1)S(1)}, bf16[512,192]{1,0:T(8,128)(2,1)S(1)}, f32[...) custom-call(bf16[4,2,128,192]{3,2,1,0:T(8,128)(2,1)S(1)} %get-tuple-, ...), custom_call_target="tpu_custom_call" | custom-call | tf_op jit(solution)/shard_map/attention_and_feed_forward/pallas_call | solution.py:1276
  41.4 4.5 %attention_backward.1 = (bf16[1024,192]{1,0:T(8,128)(2,1)S(1)}, bf16[3,192,384]{2,1,0:T(8,128)(2,1)S(1)}) custom-call(bf16[3,1024,512]{2,1,0:T(8,128)(2,1)S(1)} %get-tuple-element.107.refs_0_, bf16[3,512,128]{2,1,0:T(8,128)(2,1)S(1)} %get-tuple-element.108.refs_1_, bf16[3,512,128]{2,1,0:T(8,128)(2,1)S(1)} %get-tuple-element.101.q_ref.refs_2_, ...), custom_call_target="tpu_custom_call" | custom-call | tf_op jit(solution)/shard_map/attention_backward/pallas_call | solution.py:1313
  46.3 1.5 %collective-permute-start.17 = (bf16[288,256]{1,0:T(8,128)(2,1)S(1)}, bf16[288,256]{1,0:T(8,128)(2,1)S(1)}, u32[]{:S(2)}, u32[]{:S(2)}) collective-permute-start(bf16[288,256]{1,0:T(8,128)(2,1)S(1)} %get-tuple-element.129), channel_id=1, source_target_pairs={{0,1},{1,0},{2,3},{3,2},{4,5},{5,4},{6,7},{7,6},{8,9},{9,8},{10,11... | collective-permute-start | bytes 442376 | tf_op jit(solution)/shard_map/ppermute | solution.py:1168
  48.1 1.7 %collective-permute-start.19 = (bf16[288,256]{1,0:T(8,128)(2,1)S(1)}, bf16[288,256]{1,0:T(8,128)(2,1)S(1)}, u32[]{:S(2)}, u32[]{:S(2)}) collective-permute-start(bf16[288,256]{1,0:T(8,128)(2,1)S(1)} %get-tuple-element.131), channel_id=1, source_target_pairs={{0,3},{1,2},{2,1},{3,0},{4,7},{5,6},{6,5},{7,4},{8,11},{9,10},{10,... | collective-permute-start | bytes 442376 | tf_op jit(solution)/shard_map/ppermute | solution.py:1168
  49.8 5.4 %scan_backward.1 = (bf16[17,48,128]{2,1,0:T(8,128)(2,1)S(1)}, bf16[17,48,128]{2,1,0:T(8,128)(2,1)S(1)}, f32[512,192]{1,0:T(8,128)S(1)}) custom-call(bf16[4,2,128,192]{3,2,1,0:T(8,128)(2,1)S(1)} %get-tuple-element.94.own_ref.refs_0_, f32[1024,128]{1,0:T(8,128)S(1)} %get-tuple-element.95.refs_2_.mask_ref.refs_1_, ...), custom_call_target="tpu_custom_call" | custom-call | tf_op jit(solution)/shard_map/scan_backward/pallas_call | solution.py:1344
  55.1 1.5 %collective-permute-done.18.refs_2_ = bf16[288,256]{1,0:T(8,128)(2,1)S(1)} collective-permute-done((bf16[288,256]{1,0:T(8,128)(2,1)S(1)}, bf16[288,256]{1,0:T(8,128)(2,1)S(1)}, u32[]{:S(2)}, u32[]{:S(2)}) %collective-permute-start.18) | collective-permute-done | bytes 147488 | tf_op jit(solution)/shard_map/ppermute | solution.py:1168
  57.3 0.9 %collective-permute-done.20.refs_1_ = bf16[17,48,128]{2,1,0:T(8,128)(2,1)S(1)} collective-permute-done((bf16[17,48,128]{2,1,0:T(8,128)(2,1)S(1)}, bf16[17,48,128]{2,1,0:T(8,128)(2,1)S(1)}, u32[]{:S(2)}, u32[]{:S(2)}) %collective-permute-start.20) | collective-permute-done | bytes 208928 | tf_op jit(solution)/shard_map/ppermute | solution.py:1163
  58.9 1.2 %collective-permute-start.22 = (bf16[400,128]{1,0:T(8,128)(2,1)S(1)}, bf16[400,128]{1,0:T(8,128)(2,1)S(1)}, u32[]{:S(2)}, u32[]{:S(2)}) collective-permute-start(bf16[400,128]{1,0:T(8,128)(2,1)S(1)} %get-tuple-element.146), channel_id=1, source_target_pairs={{0,2},{1,3},{2,0},{3,1},{4,6},{5,7},{6,4},{7,5},{8,10},{9,11},{10,... | collective-permute-start | bytes 307208 | tf_op jit(solution)/shard_map/ppermute | solution.py:1168
  60.0 1.8 %collective-permute-start.23 = (bf16[400,128]{1,0:T(8,128)(2,1)S(1)}, bf16[400,128]{1,0:T(8,128)(2,1)S(1)}, u32[]{:S(2)}, u32[]{:S(2)}) collective-permute-start(bf16[400,128]{1,0:T(8,128)(2,1)S(1)} %get-tuple-element.147), channel_id=1, source_target_pairs={{0,3},{1,2},{2,1},{3,0},{4,7},{5,6},{6,5},{7,4},{8,11},{9,10},{10,... | collective-permute-start | bytes 307208 | tf_op jit(solution)/shard_map/ppermute | solution.py:1168
  61.8 2.2 %collective-permute-done.21.refs_5_ = bf16[400,128]{1,0:T(8,128)(2,1)S(1)} collective-permute-done((bf16[400,128]{1,0:T(8,128)(2,1)S(1)}, bf16[400,128]{1,0:T(8,128)(2,1)S(1)}, u32[]{:S(2)}, u32[]{:S(2)}) %collective-permute-start.21) | collective-permute-done | bytes 102432 | tf_op jit(solution)/shard_map/ppermute | solution.py:1168
  64.0 1.8 %collective-permute-done.22.refs_6_ = bf16[400,128]{1,0:T(8,128)(2,1)S(1)} collective-permute-done((bf16[400,128]{1,0:T(8,128)(2,1)S(1)}, bf16[400,128]{1,0:T(8,128)(2,1)S(1)}, u32[]{:S(2)}, u32[]{:S(2)}) %collective-permute-start.22) | collective-permute-done | bytes 102432 | tf_op jit(solution)/shard_map/ppermute | solution.py:1168
  66.0 1.3 %collective-permute-start.24 = (bf16[48,384]{1,0:T(8,128)(2,1)S(1)}, bf16[48,384]{1,0:T(8,128)(2,1)S(1)}, u32[]{:S(2)}, u32[]{:S(2)}) collective-permute-start(bf16[48,384]{1,0:T(8,128)(2,1)S(1)} %get-tuple-element.149), channel_id=1, source_target_pairs={{0,8},{8,0},{16,24},{24,16},{1,9},{9,1},{17,25},{25,17},{2,10},{10... | collective-permute-start | bytes 110600 | tf_op jit(solution)/shard_map/ppermute | solution.py:1168
  67.3 2.9 %collective-permute-start.25 = (bf16[48,384]{1,0:T(8,128)(2,1)S(1)}, bf16[48,384]{1,0:T(8,128)(2,1)S(1)}, u32[]{:S(2)}, u32[]{:S(2)}) collective-permute-start(bf16[48,384]{1,0:T(8,128)(2,1)S(1)} %get-tuple-element.150), channel_id=1, source_target_pairs={{0,16},{8,24},{16,0},{24,8},{1,17},{9,25},{17,1},{25,9},{2,18},{10... | collective-permute-start | bytes 110600 | tf_op jit(solution)/shard_map/ppermute | solution.py:1168
  70.5 1.0 %home.1 = (bf16[2,256,192]{2,1,0:T(8,128)(2,1)}, bf16[2,256,192]{2,1,0:T(8,128)(2,1)}) custom-call(bf16[2,384,128]{2,1,0:T(8,128)(2,1)S(1)} %collective-permute-done.27.swapped_ref, bf16[288,256]{1,0:T(8,128)(2,1)S(1)} %get-tuple-element.132.refs_0_, bf16[288,256]{1,0:T(8,128)(2,1)S(1)} %collective-permute-done.17.refs_1_, ...), custom_call_target="tpu_custom_call" | custom-call | tf_op jit(solution)/shard_map/home/pallas_call | solution.py:1420
  71.5 1.6 %collective-permute-done.25.refs_2_ = bf16[48,384]{1,0:T(8,128)(2,1)S(1)} collective-permute-done((bf16[48,384]{1,0:T(8,128)(2,1)S(1)}, bf16[48,384]{1,0:T(8,128)(2,1)S(1)}, u32[]{:S(2)}, u32[]{:S(2)}) %collective-permute-start.25) | collective-permute-done | bytes 36896 | tf_op jit(solution)/shard_map/ppermute | solution.py:1168
  73.1 2.9 %collective-permute-done.26.refs_3_ = bf16[48,384]{1,0:T(8,128)(2,1)S(1)} collective-permute-done((bf16[48,384]{1,0:T(8,128)(2,1)S(1)}, bf16[48,384]{1,0:T(8,128)(2,1)S(1)}, u32[]{:S(2)}, u32[]{:S(2)}) %collective-permute-start.26) | collective-permute-done | bytes 36896 | tf_op jit(solution)/shard_map/ppermute | solution.py:1168
  76.0 0.8 %final_sum.1 = (f32[1,192]{1,0:T(1,128)}, f32[1,192]{1,0:T(1,128)}, f32[24,48]{1,0:T(8,128)}, f32[8,48]{1,0:T(8,128)}, f32[8,48]{1,0:T(8,128)}, /*index=5*/f32[4...) custom-call(bf16[48,384]{1,0:T(8,128)(2,1)S(1)} %get-tuple-element.156.refs_0_, ...), custom_call_target="tpu_custom_call" | custom-call | tf_op jit(solution)/shard_map/final_sum/pallas_call | solution.py:1431
  (48 shorter events, 5.8 us)
Async XLA Ops:
  2.7 8.9 %collective-permute-start.7 = (bf16[48,384]{1,0:T(8,128)(2,1)}, bf16[48,384]{1,0:T(8,128)(2,1)S(1)}, u32[]{:S(2)}, u32[]{:S(2)}) collective-permute-start(bf16[48,384]{1,0:T(8,128)(2,1)} %get-tuple-element.100), channel_id=1, source_target_pairs={{0,24},{8,16},{16,8},{24,0},{1,25},{9,17},{17,9},{25,1},{2,26},{10... | collective-permute-start | bytes 110600 | tf_op jit(solution)/shard_map/ppermute | solution.py:1168
  7.7 5.3 %collective-permute-start.6 = (bf16[48,384]{1,0:T(8,128)(2,1)}, bf16[48,384]{1,0:T(8,128)(2,1)S(1)}, u32[]{:S(2)}, u32[]{:S(2)}) collective-permute-start(bf16[48,384]{1,0:T(8,128)(2,1)} %get-tuple-element.100), channel_id=1, source_target_pairs={{0,16},{8,24},{16,0},{24,8},{1,17},{9,25},{17,1},{25,9},{2,18},{10... | collective-permute-start | bytes 110600 | tf_op jit(solution)/shard_map/ppermute | solution.py:1168
  7.7 5.6 %collective-permute-start.5 = (bf16[48,384]{1,0:T(8,128)(2,1)}, bf16[48,384]{1,0:T(8,128)(2,1)S(1)}, u32[]{:S(2)}, u32[]{:S(2)}) collective-permute-start(bf16[48,384]{1,0:T(8,128)(2,1)} %get-tuple-element.100), channel_id=1, source_target_pairs={{0,8},{8,0},{16,24},{24,16},{1,9},{9,1},{17,25},{25,17},{2,10},{10... | collective-permute-start | bytes 110600 | tf_op jit(solution)/shard_map/ppermute | solution.py:1168
  8.3 8.5 %collective-permute-start = (bf16[416,128]{1,0:T(8,128)(2,1)}, bf16[416,128]{1,0:T(8,128)(2,1)S(1)}, u32[]{:S(2)}, u32[]{:S(2)}) collective-permute-start(bf16[416,128]{1,0:T(8,128)(2,1)} %get-tuple-element.90), channel_id=1, source_target_pairs={{0,0},{1,1},{2,4},{3,5},{4,2},{5,3},{6,6},{7,7},{8,8},{9,9},{10,12... | collective-permute-start | bytes 319496 | tf_op jit(solution)/shard_map/ppermute | solution.py:1177
  9.9 7.2 %collective-permute-start.1 = (bf16[416,128]{1,0:T(8,128)(2,1)}, bf16[416,128]{1,0:T(8,128)(2,1)S(1)}, u32[]{:S(2)}, u32[]{:S(2)}) collective-permute-start(bf16[416,128]{1,0:T(8,128)(2,1)} %get-tuple-element.91), channel_id=1, source_target_pairs={{0,1},{1,0},{2,5},{3,4},{4,3},{5,2},{6,7},{7,6},{8,9},{9,8},{10,13... | collective-permute-start | bytes 319496 | tf_op jit(solution)/shard_map/ppermute | solution.py:1177
  11.6 8.1 %collective-permute-start.2 = (bf16[416,128]{1,0:T(8,128)(2,1)}, bf16[416,128]{1,0:T(8,128)(2,1)S(1)}, u32[]{:S(2)}, u32[]{:S(2)}) collective-permute-start(bf16[416,128]{1,0:T(8,128)(2,1)} %get-tuple-element.92), channel_id=1, source_target_pairs={{0,4},{1,5},{2,0},{3,1},{4,6},{5,7},{6,2},{7,3},{8,12},{9,13},{10,... | collective-permute-start | bytes 319496 | tf_op jit(solution)/shard_map/ppermute | solution.py:1177
  13.1 7.0 %collective-permute-start.3 = (bf16[416,128]{1,0:T(8,128)(2,1)}, bf16[416,128]{1,0:T(8,128)(2,1)S(1)}, u32[]{:S(2)}, u32[]{:S(2)}) collective-permute-start(bf16[416,128]{1,0:T(8,128)(2,1)} %get-tuple-element.93), channel_id=1, source_target_pairs={{0,5},{1,4},{2,1},{3,0},{4,7},{5,6},{6,3},{7,2},{8,13},{9,12},{10,... | collective-permute-start | bytes 319496 | tf_op jit(solution)/shard_map/ppermute | solution.py:1177
  14.1 9.0 %collective-permute-start.10 = (bf16[4,48,384]{2,1,0:T(8,128)(2,1)S(1)}, bf16[4,48,384]{2,1,0:T(8,128)(2,1)S(1)}, u32[]{:S(2)}, u32[]{:S(2)}) collective-permute-start(bf16[4,48,384]{2,1,0:T(8,128)(2,1)S(1)} %pad_maximum_fusion.refs_6_.refs_0_), channel_id=1, source_target_pairs={{0,3},{1,2},{2,1},{3,0},{4,7},{5,6},{6,5},{7,4},{8,11},{9,10},{10,... | collective-permute-start | bytes 442376 | tf_op jit(solution)/shard_map/ppermute | solution.py:1168
  16.9 9.3 %collective-permute-start.9 = (bf16[4,48,384]{2,1,0:T(8,128)(2,1)S(1)}, bf16[4,48,384]{2,1,0:T(8,128)(2,1)S(1)}, u32[]{:S(2)}, u32[]{:S(2)}) collective-permute-start(bf16[4,48,384]{2,1,0:T(8,128)(2,1)S(1)} %pad_maximum_fusion.refs_6_.refs_0_), channel_id=1, source_target_pairs={{0,2},{1,3},{2,0},{3,1},{4,6},{5,7},{6,4},{7,5},{8,10},{9,11},{10,... | collective-permute-start | bytes 442376 | tf_op jit(solution)/shard_map/ppermute | solution.py:1168
  17.1 9.1 %collective-permute-start.8 = (bf16[4,48,384]{2,1,0:T(8,128)(2,1)S(1)}, bf16[4,48,384]{2,1,0:T(8,128)(2,1)S(1)}, u32[]{:S(2)}, u32[]{:S(2)}) collective-permute-start(bf16[4,48,384]{2,1,0:T(8,128)(2,1)S(1)} %pad_maximum_fusion.refs_6_.refs_0_), channel_id=1, source_target_pairs={{0,1},{1,0},{2,3},{3,2},{4,5},{5,4},{6,7},{7,6},{8,9},{9,8},{10,11... | collective-permute-start | bytes 442376 | tf_op jit(solution)/shard_map/ppermute | solution.py:1168
  21.8 4.8 %collective-permute-start.4 = (bf16[512,192]{1,0:T(8,128)(2,1)S(1)}, bf16[512,192]{1,0:T(8,128)(2,1)S(1)}, u32[]{:S(2)}, u32[]{:S(2)}) collective-permute-start(bf16[512,192]{1,0:T(8,128)(2,1)S(1)} %get-tuple-element.96.refs_0_.refs_5_), channel_id=1, source_target_pairs={{0,4},{4,0},{1,5},{5,1},{2,6},{6,2},{3,7},{7,3},{8,12},{12,8},{9,1... | collective-permute-start | bytes 589832 | tf_op jit(solution)/shard_map/ppermute | solution.py:1163
  21.9 4.7 %collective-permute-start.11 = (bf16[4,48,384]{2,1,0:T(8,128)(2,1)S(1)}, bf16[4,48,384]{2,1,0:T(8,128)(2,1)S(1)}, u32[]{:S(2)}, u32[]{:S(2)}) collective-permute-start(bf16[4,48,384]{2,1,0:T(8,128)(2,1)S(1)} %pad_maximum_fusion.refs_6_.refs_0_), channel_id=1, source_target_pairs={{0,4},{4,0},{1,5},{5,1},{2,6},{6,2},{3,7},{7,3},{8,12},{12,8},{9,1... | collective-permute-start | bytes 442376 | tf_op jit(solution)/shard_map/ppermute | solution.py:1163
  23.2 3.5 %collective-permute-start.14 = (bf16[4,48,384]{2,1,0:T(8,128)(2,1)S(1)}, bf16[4,48,384]{2,1,0:T(8,128)(2,1)S(1)}, u32[]{:S(2)}, u32[]{:S(2)}) collective-permute-start(bf16[4,48,384]{2,1,0:T(8,128)(2,1)S(1)} %collective-permute-done.10.refs_9_.refs_3_), channel_id=1, source_target_pairs={{0,4},{4,0},{1,5},{5,1},{2,6},{6,2},{3,7},{7,3},{8,12},{12,8},{9,1... | collective-permute-start | bytes 442376 | tf_op jit(solution)/shard_map/ppermute | solution.py:1163
  26.1 1.4 %collective-permute-start.13 = (bf16[4,48,384]{2,1,0:T(8,128)(2,1)S(1)}, bf16[4,48,384]{2,1,0:T(8,128)(2,1)S(1)}, u32[]{:S(2)}, u32[]{:S(2)}) collective-permute-start(bf16[4,48,384]{2,1,0:T(8,128)(2,1)S(1)} %collective-permute-done.9.refs_8_.refs_2_), channel_id=1, source_target_pairs={{0,4},{4,0},{1,5},{5,1},{2,6},{6,2},{3,7},{7,3},{8,12},{12,8},{9,1... | collective-permute-start | bytes 442376 | tf_op jit(solution)/shard_map/ppermute | solution.py:1163
  26.2 1.5 %collective-permute-start.12 = (bf16[4,48,384]{2,1,0:T(8,128)(2,1)S(1)}, bf16[4,48,384]{2,1,0:T(8,128)(2,1)S(1)}, u32[]{:S(2)}, u32[]{:S(2)}) collective-permute-start(bf16[4,48,384]{2,1,0:T(8,128)(2,1)S(1)} %collective-permute-done.8.refs_7_.refs_1_), channel_id=1, source_target_pairs={{0,4},{4,0},{1,5},{5,1},{2,6},{6,2},{3,7},{7,3},{8,12},{12,8},{9,1... | collective-permute-start | bytes 442376 | tf_op jit(solution)/shard_map/ppermute | solution.py:1163
  27.7 5.3 %copy-start = (bf16[4,1024,192]{2,1,0:T(8,128)(2,1)S(1)}, bf16[4,1024,192]{2,1,0:T(8,128)(2,1)}, u32[]{:S(2)}) copy-start(bf16[4,1024,192]{2,1,0:T(8,128)(2,1)} %constant.8.clone.sel_2_ref) | copy-start | bytes 4718596
  27.7 5.3 %copy-start.1 = (bf16[1024,192]{1,0:T(8,128)(2,1)S(1)}, bf16[1024,192]{1,0:T(8,128)(2,1)}, u32[]{:S(2)}) copy-start(bf16[1024,192]{1,0:T(8,128)(2,1)} %constant.7.clone.sel_o_ref) | copy-start | bytes 1179652
  27.7 5.3 %copy-start.2 = (bf16[512,384]{1,0:T(8,128)(2,1)S(1)}, bf16[512,384]{1,0:T(8,128)(2,1)}, u32[]{:S(2)}) copy-start(bf16[512,384]{1,0:T(8,128)(2,1)} %constant.6.clone.sel_1_ref) | copy-start | bytes 1179652
  27.7 5.3 %copy-start.4 = (f32[2,192]{1,0:T(2,128)S(1)}, f32[2,192]{1,0:T(2,128)}, u32[]{:S(2)}) copy-start(f32[2,192]{1,0:T(2,128)} %gains_ref.3) | copy-start | bytes 4612
  41.0 4.9 %collective-permute-start.15 = (bf16[4,4,48,256]{3,2,1,0:T(8,128)(2,1)S(1)}, bf16[4,4,48,256]{3,2,1,0:T(8,128)(2,1)S(1)}, u32[]{:S(2)}, u32[]{:S(2)}) collective-permute-start(bf16[4,4,48,256]{3,2,1,0:T(8,128)(2,1)S(1)} %get-tuple-element.106), channel_id=1, source_target_pairs={{0,4},{4,0},{1,5},{5,1},{2,6},{6,2},{3,7},{7,3},{8,12},{12,8},{9,1... | collective-permute-start | bytes 1179656 | tf_op jit(solution)/shard_map/ppermute | solution.py:1163
  46.0 3.7 %collective-permute-start.16 = (bf16[1024,192]{1,0:T(8,128)(2,1)S(1)}, bf16[1024,192]{1,0:T(8,128)(2,1)S(1)}, u32[]{:S(2)}, u32[]{:S(2)}) collective-permute-start(bf16[1024,192]{1,0:T(8,128)(2,1)S(1)} %get-tuple-element.119.refs_2_), channel_id=1, source_target_pairs={{0,4},{4,0},{1,5},{5,1},{2,6},{6,2},{3,7},{7,3},{8,12},{12,8},{9,1... | collective-permute-start | bytes 1179656 | tf_op jit(solution)/shard_map/ppermute | solution.py:1163
  46.3 8.9 %collective-permute-start.17 = (bf16[288,256]{1,0:T(8,128)(2,1)S(1)}, bf16[288,256]{1,0:T(8,128)(2,1)S(1)}, u32[]{:S(2)}, u32[]{:S(2)}) collective-permute-start(bf16[288,256]{1,0:T(8,128)(2,1)S(1)} %get-tuple-element.129), channel_id=1, source_target_pairs={{0,1},{1,0},{2,3},{3,2},{4,5},{5,4},{6,7},{7,6},{8,9},{9,8},{10,11... | collective-permute-start | bytes 442376 | tf_op jit(solution)/shard_map/ppermute | solution.py:1168
  47.7 9.0 %collective-permute-start.18 = (bf16[288,256]{1,0:T(8,128)(2,1)S(1)}, bf16[288,256]{1,0:T(8,128)(2,1)S(1)}, u32[]{:S(2)}, u32[]{:S(2)}) collective-permute-start(bf16[288,256]{1,0:T(8,128)(2,1)S(1)} %get-tuple-element.130), channel_id=1, source_target_pairs={{0,2},{1,3},{2,0},{3,1},{4,6},{5,7},{6,4},{7,5},{8,10},{9,11},{10,... | collective-permute-start | bytes 442376 | tf_op jit(solution)/shard_map/ppermute | solution.py:1168
  48.1 8.6 %collective-permute-start.19 = (bf16[288,256]{1,0:T(8,128)(2,1)S(1)}, bf16[288,256]{1,0:T(8,128)(2,1)S(1)}, u32[]{:S(2)}, u32[]{:S(2)}) collective-permute-start(bf16[288,256]{1,0:T(8,128)(2,1)S(1)} %get-tuple-element.131), channel_id=1, source_target_pairs={{0,3},{1,2},{2,1},{3,0},{4,7},{5,6},{6,5},{7,4},{8,11},{9,10},{10,... | collective-permute-start | bytes 442376 | tf_op jit(solution)/shard_map/ppermute | solution.py:1168
  56.7 1.5 %collective-permute-start.20 = (bf16[17,48,128]{2,1,0:T(8,128)(2,1)S(1)}, bf16[17,48,128]{2,1,0:T(8,128)(2,1)S(1)}, u32[]{:S(2)}, u32[]{:S(2)}) collective-permute-start(bf16[17,48,128]{2,1,0:T(8,128)(2,1)S(1)} %get-tuple-element.137), channel_id=1, source_target_pairs={{0,4},{4,0},{1,5},{5,1},{2,6},{6,2},{3,7},{7,3},{8,12},{12,8},{9,1... | collective-permute-start | bytes 626696 | tf_op jit(solution)/shard_map/ppermute | solution.py:1163
  58.2 5.7 %collective-permute-start.21 = (bf16[400,128]{1,0:T(8,128)(2,1)S(1)}, bf16[400,128]{1,0:T(8,128)(2,1)S(1)}, u32[]{:S(2)}, u32[]{:S(2)}) collective-permute-start(bf16[400,128]{1,0:T(8,128)(2,1)S(1)} %get-tuple-element.145), channel_id=1, source_target_pairs={{0,1},{1,0},{2,3},{3,2},{4,5},{5,4},{6,7},{7,6},{8,9},{9,8},{10,11... | collective-permute-start | bytes 307208 | tf_op jit(solution)/shard_map/ppermute | solution.py:1168
  58.9 6.9 %collective-permute-start.22 = (bf16[400,128]{1,0:T(8,128)(2,1)S(1)}, bf16[400,128]{1,0:T(8,128)(2,1)S(1)}, u32[]{:S(2)}, u32[]{:S(2)}) collective-permute-start(bf16[400,128]{1,0:T(8,128)(2,1)S(1)} %get-tuple-element.146), channel_id=1, source_target_pairs={{0,2},{1,3},{2,0},{3,1},{4,6},{5,7},{6,4},{7,5},{8,10},{9,11},{10,... | collective-permute-start | bytes 307208 | tf_op jit(solution)/shard_map/ppermute | solution.py:1168
  60.0 5.7 %collective-permute-start.23 = (bf16[400,128]{1,0:T(8,128)(2,1)S(1)}, bf16[400,128]{1,0:T(8,128)(2,1)S(1)}, u32[]{:S(2)}, u32[]{:S(2)}) collective-permute-start(bf16[400,128]{1,0:T(8,128)(2,1)S(1)} %get-tuple-element.147), channel_id=1, source_target_pairs={{0,3},{1,2},{2,1},{3,0},{4,7},{5,6},{6,5},{7,4},{8,11},{9,10},{10,... | collective-permute-start | bytes 307208 | tf_op jit(solution)/shard_map/ppermute | solution.py:1168
  65.8 4.7 %collective-permute-start.27 = (bf16[2,384,128]{2,1,0:T(8,128)(2,1)S(1)}, bf16[2,384,128]{2,1,0:T(8,128)(2,1)S(1)}, u32[]{:S(2)}, u32[]{:S(2)}) collective-permute-start(bf16[2,384,128]{2,1,0:T(8,128)(2,1)S(1)} %choose.1), channel_id=1, source_target_pairs={{0,4},{4,0},{1,5},{5,1},{2,6},{6,2},{3,7},{7,3},{8,12},{12,8},{9,1... | collective-permute-start | bytes 589832 | tf_op jit(solution)/shard_map/ppermute | solution.py:1163
  66.0 5.5 %collective-permute-start.24 = (bf16[48,384]{1,0:T(8,128)(2,1)S(1)}, bf16[48,384]{1,0:T(8,128)(2,1)S(1)}, u32[]{:S(2)}, u32[]{:S(2)}) collective-permute-start(bf16[48,384]{1,0:T(8,128)(2,1)S(1)} %get-tuple-element.149), channel_id=1, source_target_pairs={{0,8},{8,0},{16,24},{24,16},{1,9},{9,1},{17,25},{25,17},{2,10},{10... | collective-permute-start | bytes 110600 | tf_op jit(solution)/shard_map/ppermute | solution.py:1168
  67.3 5.7 %collective-permute-start.25 = (bf16[48,384]{1,0:T(8,128)(2,1)S(1)}, bf16[48,384]{1,0:T(8,128)(2,1)S(1)}, u32[]{:S(2)}, u32[]{:S(2)}) collective-permute-start(bf16[48,384]{1,0:T(8,128)(2,1)S(1)} %get-tuple-element.150), channel_id=1, source_target_pairs={{0,16},{8,24},{16,0},{24,8},{1,17},{9,25},{17,1},{25,9},{2,18},{10... | collective-permute-start | bytes 110600 | tf_op jit(solution)/shard_map/ppermute | solution.py:1168
  70.2 5.8 %collective-permute-start.26 = (bf16[48,384]{1,0:T(8,128)(2,1)S(1)}, bf16[48,384]{1,0:T(8,128)(2,1)S(1)}, u32[]{:S(2)}, u32[]{:S(2)}) collective-permute-start(bf16[48,384]{1,0:T(8,128)(2,1)S(1)} %get-tuple-element.151), channel_id=1, source_target_pairs={{0,24},{8,16},{16,8},{24,0},{1,25},{9,17},{17,9},{25,1},{2,26},{10... | collective-permute-start | bytes 110600 | tf_op jit(solution)/shard_map/ppermute | solution.py:1168
  (1 other events, 0.7 us)

commit v8 on v7

--- a/solution.py
+++ b/solution.py
@@ -795,15 +795,12 @@
     q_ref,
     k_ref,
     v_ref,
-    scanned_ref,
     wqkv_ref,
     part_ref,
-    grad_w_ref,
+    triple,
+    grad_q,
     scores,
     grad_scores,
-    triple,
-    grad_q,
-    scanned_own,
     part,
     *,
     blocks,
@@ -834,11 +831,7 @@
         here = slice(block * rows_slots, (block + 1) * rows_slots)
         place = pl.ds(pl.multiple_of((block * 2 + core) * rows_slots, rows_slots), rows_slots)
         part[place, :] += from_q[here]
-        scanned_own[here, :] = scanned_ref[place, :]
     part_ref[...] = part[...].astype(BF16)
-    grad_w_ref[0] = dot_tn(scanned_own[...], grad_q[...]).astype(BF16)
-    grad_w_ref[1] = dot_tn(scanned_ref[...], triple[0]).astype(BF16)
-    grad_w_ref[2] = dot_tn(scanned_ref[...], triple[1]).astype(BF16)
 
 
 def scan_back_kernel(
@@ -853,7 +846,9 @@
     table_ref,
     rates_ref,
     wu_ref,
-    grad_w_ref,
+    triple_ref,
+    grad_q_ref,
+    scanned_ref,
     gain_two_ref,
     sel_u_ref,
     sel_rc_ref,
@@ -883,6 +878,7 @@
     mixed_back,
     wire,
     parted,
+    grad_w_ref,
 ):
     gs, gt = (gs_wide, gs_pairs), (gt_wide, gt_pairs)
     xs, xt = (xs_wide, xs_pairs), (xt_wide, xt_pairs)
@@ -908,6 +904,14 @@
             own[here, :] = value[:, :LANES]
             own_tail[here, :] = value[:, LANES:]
         put_rows(*dst, own, own_tail[...], together)
+
+    grad_w = [None, dot_tn(scanned_ref[...], triple_ref[0]), dot_tn(scanned_ref[...], triple_ref[1])]
+    for block in range(blocks):
+        here = slice(block * rows_slots, (block + 1) * rows_slots)
+        term = dot_tn(scanned_ref[place_of(block), :], grad_q_ref[here, :])
+        grad_w[0] = term if block == 0 else grad_w[0] + term
+    for third in range(3):
+        grad_w_ref[third] = grad_w[third].astype(BF16)
 
     for kind, sublane in units(0):
         step = gt[kind].shape[0] // GRID
@@ -1310,22 +1314,23 @@
 
     early_recv = swapped(early_send)
 
-    part, grad_w = pl.pallas_call(
+    part, triple, grad_q = pl.pallas_call(
         lambda *refs: attention_back_kernel(*refs, blocks=blocks),
         name="attention_backward",
-        out_shape=(shape((SLOTS, D), BF16), shape((3, D, TILE), BF16)),
-        in_specs=[VMEM] * 7,
-        out_specs=[VMEM] * 2,
+        out_shape=(
+            shape((SLOTS, D), BF16),
+            shape((2, SLOTS, TILE), BF16),
+            shape((OWN, TILE), BF16),
+        ),
+        in_specs=[VMEM] * 6,
+        out_specs=[VMEM] * 3,
         scratch_shapes=[
             pltpu.VMEM((SLOTS, OWN), F32),
             pltpu.VMEM((SLOTS, OWN), BF16),
-            pltpu.VMEM((2, SLOTS, TILE), BF16),
-            pltpu.VMEM((OWN, TILE), BF16),
-            pltpu.VMEM((OWN, D), BF16),
             pltpu.VMEM((SLOTS, D), F32),
         ],
         compiler_params=compiler(),
-    )(soft, lifted, q, k, v, scanned, wqkv)
+    )(soft, lifted, q, k, v, wqkv)
 
     early_keep, early_recv, part = lax.optimization_barrier((early_keep, early_recv, part))
     payload = shape((depth * aligned(rows_weight) + packed_rows // 2, 2 * LANES), BF16)
@@ -1345,7 +1350,7 @@
         lambda *refs: scan_back_kernel(starts, width, *refs),
         name="scan_backward",
         out_shape=(wire_late, wire_late, shape((OWN, D), F32)),
-        in_specs=[VMEM] * 14,
+        in_specs=[VMEM] * 16,
         out_specs=[VMEM] * 3,
         scratch_shapes=planes(SLOTS) + planes(OWN) + planes(SLOTS) + planes(OWN) * 3
         + [
@@ -1359,6 +1364,7 @@
             pltpu.VMEM((OWN, D), BF16),
             pltpu.VMEM((D, parts * LANES), F32),
             pltpu.VMEM((parts, D, LANES), BF16),
+            pltpu.VMEM((3, D, TILE), BF16),
         ],
         compiler_params=compiler(),
     )(
@@ -1371,7 +1377,9 @@
         table,
         rates,
         wu,
-        grad_w,
+        triple,
+        grad_q,
+        scanned,
         gain_two,
         sel_u,
         sel_rc,

time: 77.1 us -> 77.1 us (level)
  no operation moved by 1% of the time
where the time goes in v8:
time: 77.1 us; the launch traced here: 76.8 us
  Pallas kernels  29.6 us (38%)
  starting transfers between devices  27.9 us (36%)
  waiting for transfers between devices  17 us (22%)
  other arithmetic  0.79 us (1%)
  between operations  0.78 us (1%)
    ppermute x15, starting transfers between devices, exchanged(): lax.ppermute(values[k], axis, [(i, i ^ k) for i in range(size)])  21.2 us
    ppermute x15, waiting for transfers between devices, exchanged(): lax.ppermute(values[k], axis, [(i, i ^ k) for i in range(size)])  13.1 us
    pallas_call x1, Pallas kernels, per_device(): pl.pallas_call(middle_kernel, name='attention_and_feed_forward', out_shap...  7.92 us
    pallas_call x1, Pallas kernels, per_device(): pl.pallas_call(lambda *refs: scan_back_kernel(starts, width, *refs), name...  6.06 us
    pallas_call x1, Pallas kernels, per_device(): pl.pallas_call(lambda *refs: scan_kernel(starts, width, *refs, blocks=blo...  5.22 us
    ppermute x4, starting transfers between devices, to_chips(): return lax.ppermute(value, ('core', 'row'), pairs)  4.98 us
    pallas_call x1, Pallas kernels, per_device(): pl.pallas_call(lambda *refs: attention_back_kernel(*refs, blocks=blocks),...  4.47 us
    pallas_call x1, Pallas kernels, per_device(): pl.pallas_call(depart_kernel, name='depart', out_shape=(shard,) + (payloa...  2.03 us
  transfers between devices with their start and end apart: 28, of which 12 were waited for; matrix products, arithmetic and copies ran while one was open for 1% of the time, Pallas kernels for 17%

profile of v8, /device:TPU:0, one launch (start us, length us, event | category | flops | bytes accessed | tf_op | source)
XLA Modules:
  0.0 76.8 jit_solution(17848471513219120418)
XLA Ops:
  0.6 2.0 %depart.1 = (bf16[48,384]{1,0:T(8,128)(2,1)}, bf16[416,128]{1,0:T(8,128)(2,1)}, bf16[416,128]{1,0:T(8,128)(2,1)}, bf16[416,128]{1,0:T(8,128)(2,1)}, bf16[416,128]{1,0:T(8,128)(2,1)}) custom-call(bf16[24,48]{1,0:T(8,128)(2,1)} %bitcast.27, bf16[8,48]{1,0:T(8,128)(2,1)} %bitcast.29, bf16[8,48]{1,0:T(8,128)(2,1)} %bitcast.30, bf16[24,48]{1,0:T(8,128)(2,1)} %bitcast.28, ...), custom_call_target="tpu_custom_call" | custom-call | tf_op jit(solution)/shard_map/depart/pallas_call | solution.py:1191
  2.7 5.0 %collective-permute-start.7 = (bf16[48,384]{1,0:T(8,128)(2,1)}, bf16[48,384]{1,0:T(8,128)(2,1)S(1)}, u32[]{:S(2)}, u32[]{:S(2)}) collective-permute-start(bf16[48,384]{1,0:T(8,128)(2,1)} %get-tuple-element.101), channel_id=1, source_target_pairs={{0,24},{8,16},{16,8},{24,0},{1,25},{9,17},{17,9},{25,1},{2,26},{10... | collective-permute-start | bytes 110600 | tf_op jit(solution)/shard_map/ppermute | solution.py:1172
  8.3 1.5 %collective-permute-start = (bf16[416,128]{1,0:T(8,128)(2,1)}, bf16[416,128]{1,0:T(8,128)(2,1)S(1)}, u32[]{:S(2)}, u32[]{:S(2)}) collective-permute-start(bf16[416,128]{1,0:T(8,128)(2,1)} %get-tuple-element.91), channel_id=1, source_target_pairs={{0,0},{1,1},{2,4},{3,5},{4,2},{5,3},{6,6},{7,7},{8,8},{9,9},{10,12... | collective-permute-start | bytes 319496 | tf_op jit(solution)/shard_map/ppermute | solution.py:1181
  9.9 1.7 %collective-permute-start.1 = (bf16[416,128]{1,0:T(8,128)(2,1)}, bf16[416,128]{1,0:T(8,128)(2,1)S(1)}, u32[]{:S(2)}, u32[]{:S(2)}) collective-permute-start(bf16[416,128]{1,0:T(8,128)(2,1)} %get-tuple-element.92), channel_id=1, source_target_pairs={{0,1},{1,0},{2,5},{3,4},{4,3},{5,2},{6,7},{7,6},{8,9},{9,8},{10,13... | collective-permute-start | bytes 319496 | tf_op jit(solution)/shard_map/ppermute | solution.py:1181
  11.6 1.5 %collective-permute-start.2 = (bf16[416,128]{1,0:T(8,128)(2,1)}, bf16[416,128]{1,0:T(8,128)(2,1)S(1)}, u32[]{:S(2)}, u32[]{:S(2)}) collective-permute-start(bf16[416,128]{1,0:T(8,128)(2,1)} %get-tuple-element.93), channel_id=1, source_target_pairs={{0,4},{1,5},{2,0},{3,1},{4,6},{5,7},{6,2},{7,3},{8,12},{9,13},{10,... | collective-permute-start | bytes 319496 | tf_op jit(solution)/shard_map/ppermute | solution.py:1181
  13.3 0.8 %pad_maximum_fusion.refs_6_.refs_0_ = bf16[4,48,384]{2,1,0:T(8,128)(2,1)S(1)} fusion(bf16[1,48,384]{2,1,0:T(8,128)(2,1)S(1)} %bitcast.23, bf16[1,48,384]{2,1,0:T(8,128)(2,1)S(1)} %bitcast.24, bf16[1,48,384]{2,1,0:T(8,128)(2,1)S(1)} %bitcast.25, bf16[1,48,384]{2,1,0:T(8,128)(2,1)} %bitcast.22), kind=kLoop, calls=%fused_computation | loop fusion | flops 221184 | bytes 294912 | tf_op jit(solution)/shard_map/stack | solution.py:1232
  14.1 2.7 %collective-permute-start.10 = (bf16[4,48,384]{2,1,0:T(8,128)(2,1)S(1)}, bf16[4,48,384]{2,1,0:T(8,128)(2,1)S(1)}, u32[]{:S(2)}, u32[]{:S(2)}) collective-permute-start(bf16[4,48,384]{2,1,0:T(8,128)(2,1)S(1)} %pad_maximum_fusion.refs_6_.refs_0_), channel_id=1, source_target_pairs={{0,3},{1,2},{2,1},{3,0},{4,7},{5,6},{6,5},{7,4},{8,11},{9,10},{10,... | collective-permute-start | bytes 442376 | tf_op jit(solution)/shard_map/ppermute | solution.py:1172
  17.1 1.1 %collective-permute-start.8 = (bf16[4,48,384]{2,1,0:T(8,128)(2,1)S(1)}, bf16[4,48,384]{2,1,0:T(8,128)(2,1)S(1)}, u32[]{:S(2)}, u32[]{:S(2)}) collective-permute-start(bf16[4,48,384]{2,1,0:T(8,128)(2,1)S(1)} %pad_maximum_fusion.refs_6_.refs_0_), channel_id=1, source_target_pairs={{0,1},{1,0},{2,3},{3,2},{4,5},{5,4},{6,7},{7,6},{8,9},{9,8},{10,11... | collective-permute-start | bytes 442376 | tf_op jit(solution)/shard_map/ppermute | solution.py:1172
  18.2 1.5 %collective-permute-done.2.refs_3_ = bf16[416,128]{1,0:T(8,128)(2,1)S(1)} collective-permute-done((bf16[416,128]{1,0:T(8,128)(2,1)}, bf16[416,128]{1,0:T(8,128)(2,1)S(1)}, u32[]{:S(2)}, u32[]{:S(2)}) %collective-permute-start.2) | collective-permute-done | bytes 106528 | tf_op jit(solution)/shard_map/ppermute | solution.py:1181
  20.7 1.1 %first_norm.1 = (bf16[4,2,128,192]{3,2,1,0:T(8,128)(2,1)S(1)}, bf16[512,192]{1,0:T(8,128)(2,1)S(1)}, f32[1024,128]{1,0:T(8,128)S(1)}, bf16[1024,192]{1,0:T(8,128...) custom-call(f32[2,192]{1,0:T(2,128)S(1)} %copy-done.3, ...), custom_call_target="tpu_custom_call" | custom-call | tf_op jit(solution)/shard_map/first_norm/pallas_call | solution.py:1236
  22.4 0.8 collective-permute-done.10.refs_9_.refs_3_
  23.2 3.0 %collective-permute-done.9.refs_8_.refs_2_ = bf16[4,48,384]{2,1,0:T(8,128)(2,1)S(1)} collective-permute-done((bf16[4,48,384]{2,1,0:T(8,128)(2,1)S(1)}, bf16[4,48,384]{2,1,0:T(8,128)(2,1)S(1)}, u32[]{:S(2)}, u32[]{:S(2)}) %collective-permute-start.9) | collective-permute-done | bytes 147488 | tf_op jit(solution)/shard_map/ppermute | solution.py:1172
  26.7 0.8 %collective-permute-done.13.refs_12_.refs_6_ = bf16[4,48,384]{2,1,0:T(8,128)(2,1)S(1)} collective-permute-done((bf16[4,48,384]{2,1,0:T(8,128)(2,1)S(1)}, bf16[4,48,384]{2,1,0:T(8,128)(2,1)S(1)}, u32[]{:S(2)}, u32[]{:S(2)}) %collective-permute-start.13) | collective-permute-done | bytes 147488 | tf_op jit(solution)/shard_map/ppermute | solution.py:1167
  27.7 5.2 %scan_forward.1 = (bf16[3,512,128]{2,1,0:T(8,128)(2,1)S(1)}, bf16[3,1024,128]{2,1,0:T(8,128)(2,1)S(1)}, bf16[3,1024,128]{2,1,0:T(8,128)(2,1)S(1)}, bf16[1024,192...) custom-call(bf16[512,192]{1,0:T(8,128)(2,1)S(1)} %get-tuple-element., ...), custom_call_target="tpu_custom_call" | custom-call | tf_op jit(solution)/shard_map/scan_forward/pallas_call | solution.py:1256
  33.0 7.9 %attention_and_feed_forward.1 = (bf16[3,1024,512]{2,1,0:T(8,128)(2,1)S(1)}, bf16[3,512,128]{2,1,0:T(8,128)(2,1)S(1)}, bf16[512,192]{1,0:T(8,128)(2,1)S(1)}, f32[...) custom-call(bf16[4,2,128,192]{3,2,1,0:T(8,128)(2,1)S(1)} %get-tuple-, ...), custom_call_target="tpu_custom_call" | custom-call | tf_op jit(solution)/shard_map/attention_and_feed_forward/pallas_call | solution.py:1280
  41.4 4.5 %attention_backward.1 = (bf16[1024,192]{1,0:T(8,128)(2,1)S(1)}, bf16[2,1024,384]{2,1,0:T(8,128)(2,1)S(1)}, bf16[512,384]{1,0:T(8,128)(2,1)S(1)}) custom-call(bf16[3,1024,512]{2,1,0:T(8,128)(2,1)S(1)} %get-tuple-element.108.refs_0_, bf16[3,512,128]{2,1,0:T(8,128)(2,1)S(1)} %get-tuple-element.109.refs_1_, ...), custom_call_target="tpu_custom_call" | custom-call | tf_op jit(solution)/shard_map/attention_backward/pallas_call | solution.py:1317
  46.2 1.5 %collective-permute-start.17 = (bf16[288,256]{1,0:T(8,128)(2,1)S(1)}, bf16[288,256]{1,0:T(8,128)(2,1)S(1)}, u32[]{:S(2)}, u32[]{:S(2)}) collective-permute-start(bf16[288,256]{1,0:T(8,128)(2,1)S(1)} %get-tuple-element.131), channel_id=1, source_target_pairs={{0,1},{1,0},{2,3},{3,2},{4,5},{5,4},{6,7},{7,6},{8,9},{9,8},{10,11... | collective-permute-start | bytes 442376 | tf_op jit(solution)/shard_map/ppermute | solution.py:1172
  48.0 1.7 %collective-permute-start.19 = (bf16[288,256]{1,0:T(8,128)(2,1)S(1)}, bf16[288,256]{1,0:T(8,128)(2,1)S(1)}, u32[]{:S(2)}, u32[]{:S(2)}) collective-permute-start(bf16[288,256]{1,0:T(8,128)(2,1)S(1)} %get-tuple-element.133), channel_id=1, source_target_pairs={{0,3},{1,2},{2,1},{3,0},{4,7},{5,6},{6,5},{7,4},{8,11},{9,10},{10,... | collective-permute-start | bytes 442376 | tf_op jit(solution)/shard_map/ppermute | solution.py:1172
  49.7 6.1 %scan_backward.1 = (bf16[17,48,128]{2,1,0:T(8,128)(2,1)S(1)}, bf16[17,48,128]{2,1,0:T(8,128)(2,1)S(1)}, f32[512,192]{1,0:T(8,128)S(1)}) custom-call(bf16[4,2,128,192]{3,2,1,0:T(8,128)(2,1)S(1)} %get-tuple-element.95.own_ref.refs_0_, f32[1024,128]{1,0:T(8,128)S(1)} %get-tuple-element.96.refs_2_.mask_ref.refs_1_, ...), custom_call_target="tpu_custom_call" | custom-call | tf_op jit(solution)/shard_map/scan_backward/pallas_call | solution.py:1349
  55.8 0.9 %collective-permute-done.18.refs_2_ = bf16[288,256]{1,0:T(8,128)(2,1)S(1)} collective-permute-done((bf16[288,256]{1,0:T(8,128)(2,1)S(1)}, bf16[288,256]{1,0:T(8,128)(2,1)S(1)}, u32[]{:S(2)}, u32[]{:S(2)}) %collective-permute-start.18) | collective-permute-done | bytes 147488 | tf_op jit(solution)/shard_map/ppermute | solution.py:1172
  57.2 0.9 %collective-permute-done.20.refs_1_ = bf16[17,48,128]{2,1,0:T(8,128)(2,1)S(1)} collective-permute-done((bf16[17,48,128]{2,1,0:T(8,128)(2,1)S(1)}, bf16[17,48,128]{2,1,0:T(8,128)(2,1)S(1)}, u32[]{:S(2)}, u32[]{:S(2)}) %collective-permute-start.20) | collective-permute-done | bytes 208928 | tf_op jit(solution)/shard_map/ppermute | solution.py:1167
  58.2 0.7 collective-permute-start.21
  58.9 1.1 %collective-permute-start.22 = (bf16[400,128]{1,0:T(8,128)(2,1)S(1)}, bf16[400,128]{1,0:T(8,128)(2,1)S(1)}, u32[]{:S(2)}, u32[]{:S(2)}) collective-permute-start(bf16[400,128]{1,0:T(8,128)(2,1)S(1)} %get-tuple-element.148), channel_id=1, source_target_pairs={{0,2},{1,3},{2,0},{3,1},{4,6},{5,7},{6,4},{7,5},{8,10},{9,11},{10,... | collective-permute-start | bytes 307208 | tf_op jit(solution)/shard_map/ppermute | solution.py:1172
  60.0 1.8 %collective-permute-start.23 = (bf16[400,128]{1,0:T(8,128)(2,1)S(1)}, bf16[400,128]{1,0:T(8,128)(2,1)S(1)}, u32[]{:S(2)}, u32[]{:S(2)}) collective-permute-start(bf16[400,128]{1,0:T(8,128)(2,1)S(1)} %get-tuple-element.149), channel_id=1, source_target_pairs={{0,3},{1,2},{2,1},{3,0},{4,7},{5,6},{6,5},{7,4},{8,11},{9,10},{10,... | collective-permute-start | bytes 307208 | tf_op jit(solution)/shard_map/ppermute | solution.py:1172
  61.7 2.1 %collective-permute-done.21.refs_5_ = bf16[400,128]{1,0:T(8,128)(2,1)S(1)} collective-permute-done((bf16[400,128]{1,0:T(8,128)(2,1)S(1)}, bf16[400,128]{1,0:T(8,128)(2,1)S(1)}, u32[]{:S(2)}, u32[]{:S(2)}) %collective-permute-start.21) | collective-permute-done | bytes 102432 | tf_op jit(solution)/shard_map/ppermute | solution.py:1172
  63.9 1.9 %collective-permute-done.22.refs_6_ = bf16[400,128]{1,0:T(8,128)(2,1)S(1)} collective-permute-done((bf16[400,128]{1,0:T(8,128)(2,1)S(1)}, bf16[400,128]{1,0:T(8,128)(2,1)S(1)}, u32[]{:S(2)}, u32[]{:S(2)}) %collective-permute-start.22) | collective-permute-done | bytes 102432 | tf_op jit(solution)/shard_map/ppermute | solution.py:1172
  66.1 1.3 %collective-permute-start.24 = (bf16[48,384]{1,0:T(8,128)(2,1)S(1)}, bf16[48,384]{1,0:T(8,128)(2,1)S(1)}, u32[]{:S(2)}, u32[]{:S(2)}) collective-permute-start(bf16[48,384]{1,0:T(8,128)(2,1)S(1)} %get-tuple-element.151), channel_id=1, source_target_pairs={{0,8},{8,0},{16,24},{24,16},{1,9},{9,1},{17,25},{25,17},{2,10},{10... | collective-permute-start | bytes 110600 | tf_op jit(solution)/shard_map/ppermute | solution.py:1172
  67.3 2.9 %collective-permute-start.25 = (bf16[48,384]{1,0:T(8,128)(2,1)S(1)}, bf16[48,384]{1,0:T(8,128)(2,1)S(1)}, u32[]{:S(2)}, u32[]{:S(2)}) collective-permute-start(bf16[48,384]{1,0:T(8,128)(2,1)S(1)} %get-tuple-element.152), channel_id=1, source_target_pairs={{0,16},{8,24},{16,0},{24,8},{1,17},{9,25},{17,1},{25,9},{2,18},{10... | collective-permute-start | bytes 110600 | tf_op jit(solution)/shard_map/ppermute | solution.py:1172
  70.5 1.0 %home.1 = (bf16[2,256,192]{2,1,0:T(8,128)(2,1)}, bf16[2,256,192]{2,1,0:T(8,128)(2,1)}) custom-call(bf16[2,384,128]{2,1,0:T(8,128)(2,1)S(1)} %collective-permute-done.27.swapped_ref, bf16[288,256]{1,0:T(8,128)(2,1)S(1)} %get-tuple-element.134.refs_0_, bf16[288,256]{1,0:T(8,128)(2,1)S(1)} %collective-permute-done.17.refs_1_, ...), custom_call_target="tpu_custom_call" | custom-call | tf_op jit(solution)/shard_map/home/pallas_call | solution.py:1428
  71.5 1.5 %collective-permute-done.25.refs_2_ = bf16[48,384]{1,0:T(8,128)(2,1)S(1)} collective-permute-done((bf16[48,384]{1,0:T(8,128)(2,1)S(1)}, bf16[48,384]{1,0:T(8,128)(2,1)S(1)}, u32[]{:S(2)}, u32[]{:S(2)}) %collective-permute-start.25) | collective-permute-done | bytes 36896 | tf_op jit(solution)/shard_map/ppermute | solution.py:1172
  73.1 2.9 %collective-permute-done.26.refs_3_ = bf16[48,384]{1,0:T(8,128)(2,1)S(1)} collective-permute-done((bf16[48,384]{1,0:T(8,128)(2,1)S(1)}, bf16[48,384]{1,0:T(8,128)(2,1)S(1)}, u32[]{:S(2)}, u32[]{:S(2)}) %collective-permute-start.26) | collective-permute-done | bytes 36896 | tf_op jit(solution)/shard_map/ppermute | solution.py:1172
  76.0 0.8 %final_sum.1 = (f32[1,192]{1,0:T(1,128)}, f32[1,192]{1,0:T(1,128)}, f32[24,48]{1,0:T(8,128)}, f32[8,48]{1,0:T(8,128)}, f32[8,48]{1,0:T(8,128)}, /*index=5*/f32[4...) custom-call(bf16[48,384]{1,0:T(8,128)(2,1)S(1)} %get-tuple-element.158.refs_0_, ...), custom_call_target="tpu_custom_call" | custom-call | tf_op jit(solution)/shard_map/final_sum/pallas_call | solution.py:1439
  (48 shorter events, 5.9 us)
Async XLA Ops:
  2.7 8.9 %collective-permute-start.7 = (bf16[48,384]{1,0:T(8,128)(2,1)}, bf16[48,384]{1,0:T(8,128)(2,1)S(1)}, u32[]{:S(2)}, u32[]{:S(2)}) collective-permute-start(bf16[48,384]{1,0:T(8,128)(2,1)} %get-tuple-element.101), channel_id=1, source_target_pairs={{0,24},{8,16},{16,8},{24,0},{1,25},{9,17},{17,9},{25,1},{2,26},{10... | collective-permute-start | bytes 110600 | tf_op jit(solution)/shard_map/ppermute | solution.py:1172
  7.7 5.3 %collective-permute-start.6 = (bf16[48,384]{1,0:T(8,128)(2,1)}, bf16[48,384]{1,0:T(8,128)(2,1)S(1)}, u32[]{:S(2)}, u32[]{:S(2)}) collective-permute-start(bf16[48,384]{1,0:T(8,128)(2,1)} %get-tuple-element.101), channel_id=1, source_target_pairs={{0,16},{8,24},{16,0},{24,8},{1,17},{9,25},{17,1},{25,9},{2,18},{10... | collective-permute-start | bytes 110600 | tf_op jit(solution)/shard_map/ppermute | solution.py:1172
  7.7 5.6 %collective-permute-start.5 = (bf16[48,384]{1,0:T(8,128)(2,1)}, bf16[48,384]{1,0:T(8,128)(2,1)S(1)}, u32[]{:S(2)}, u32[]{:S(2)}) collective-permute-start(bf16[48,384]{1,0:T(8,128)(2,1)} %get-tuple-element.101), channel_id=1, source_target_pairs={{0,8},{8,0},{16,24},{24,16},{1,9},{9,1},{17,25},{25,17},{2,10},{10... | collective-permute-start | bytes 110600 | tf_op jit(solution)/shard_map/ppermute | solution.py:1172
  8.3 8.5 %collective-permute-start = (bf16[416,128]{1,0:T(8,128)(2,1)}, bf16[416,128]{1,0:T(8,128)(2,1)S(1)}, u32[]{:S(2)}, u32[]{:S(2)}) collective-permute-start(bf16[416,128]{1,0:T(8,128)(2,1)} %get-tuple-element.91), channel_id=1, source_target_pairs={{0,0},{1,1},{2,4},{3,5},{4,2},{5,3},{6,6},{7,7},{8,8},{9,9},{10,12... | collective-permute-start | bytes 319496 | tf_op jit(solution)/shard_map/ppermute | solution.py:1181
  9.9 7.2 %collective-permute-start.1 = (bf16[416,128]{1,0:T(8,128)(2,1)}, bf16[416,128]{1,0:T(8,128)(2,1)S(1)}, u32[]{:S(2)}, u32[]{:S(2)}) collective-permute-start(bf16[416,128]{1,0:T(8,128)(2,1)} %get-tuple-element.92), channel_id=1, source_target_pairs={{0,1},{1,0},{2,5},{3,4},{4,3},{5,2},{6,7},{7,6},{8,9},{9,8},{10,13... | collective-permute-start | bytes 319496 | tf_op jit(solution)/shard_map/ppermute | solution.py:1181
  11.6 8.1 %collective-permute-start.2 = (bf16[416,128]{1,0:T(8,128)(2,1)}, bf16[416,128]{1,0:T(8,128)(2,1)S(1)}, u32[]{:S(2)}, u32[]{:S(2)}) collective-permute-start(bf16[416,128]{1,0:T(8,128)(2,1)} %get-tuple-element.93), channel_id=1, source_target_pairs={{0,4},{1,5},{2,0},{3,1},{4,6},{5,7},{6,2},{7,3},{8,12},{9,13},{10,... | collective-permute-start | bytes 319496 | tf_op jit(solution)/shard_map/ppermute | solution.py:1181
  13.1 7.0 %collective-permute-start.3 = (bf16[416,128]{1,0:T(8,128)(2,1)}, bf16[416,128]{1,0:T(8,128)(2,1)S(1)}, u32[]{:S(2)}, u32[]{:S(2)}) collective-permute-start(bf16[416,128]{1,0:T(8,128)(2,1)} %get-tuple-element.94), channel_id=1, source_target_pairs={{0,5},{1,4},{2,1},{3,0},{4,7},{5,6},{6,3},{7,2},{8,13},{9,12},{10,... | collective-permute-start | bytes 319496 | tf_op jit(solution)/shard_map/ppermute | solution.py:1181
  14.1 9.0 %collective-permute-start.10 = (bf16[4,48,384]{2,1,0:T(8,128)(2,1)S(1)}, bf16[4,48,384]{2,1,0:T(8,128)(2,1)S(1)}, u32[]{:S(2)}, u32[]{:S(2)}) collective-permute-start(bf16[4,48,384]{2,1,0:T(8,128)(2,1)S(1)} %pad_maximum_fusion.refs_6_.refs_0_), channel_id=1, source_target_pairs={{0,3},{1,2},{2,1},{3,0},{4,7},{5,6},{6,5},{7,4},{8,11},{9,10},{10,... | collective-permute-start | bytes 442376 | tf_op jit(solution)/shard_map/ppermute | solution.py:1172
  16.9 9.3 %collective-permute-start.9 = (bf16[4,48,384]{2,1,0:T(8,128)(2,1)S(1)}, bf16[4,48,384]{2,1,0:T(8,128)(2,1)S(1)}, u32[]{:S(2)}, u32[]{:S(2)}) collective-permute-start(bf16[4,48,384]{2,1,0:T(8,128)(2,1)S(1)} %pad_maximum_fusion.refs_6_.refs_0_), channel_id=1, source_target_pairs={{0,2},{1,3},{2,0},{3,1},{4,6},{5,7},{6,4},{7,5},{8,10},{9,11},{10,... | collective-permute-start | bytes 442376 | tf_op jit(solution)/shard_map/ppermute | solution.py:1172
  17.1 9.1 %collective-permute-start.8 = (bf16[4,48,384]{2,1,0:T(8,128)(2,1)S(1)}, bf16[4,48,384]{2,1,0:T(8,128)(2,1)S(1)}, u32[]{:S(2)}, u32[]{:S(2)}) collective-permute-start(bf16[4,48,384]{2,1,0:T(8,128)(2,1)S(1)} %pad_maximum_fusion.refs_6_.refs_0_), channel_id=1, source_target_pairs={{0,1},{1,0},{2,3},{3,2},{4,5},{5,4},{6,7},{7,6},{8,9},{9,8},{10,11... | collective-permute-start | bytes 442376 | tf_op jit(solution)/shard_map/ppermute | solution.py:1172
  21.8 4.8 %collective-permute-start.4 = (bf16[512,192]{1,0:T(8,128)(2,1)S(1)}, bf16[512,192]{1,0:T(8,128)(2,1)S(1)}, u32[]{:S(2)}, u32[]{:S(2)}) collective-permute-start(bf16[512,192]{1,0:T(8,128)(2,1)S(1)} %get-tuple-element.97.refs_0_.refs_5_), channel_id=1, source_target_pairs={{0,4},{4,0},{1,5},{5,1},{2,6},{6,2},{3,7},{7,3},{8,12},{12,8},{9,1... | collective-permute-start | bytes 589832 | tf_op jit(solution)/shard_map/ppermute | solution.py:1167
  21.9 4.7 %collective-permute-start.11 = (bf16[4,48,384]{2,1,0:T(8,128)(2,1)S(1)}, bf16[4,48,384]{2,1,0:T(8,128)(2,1)S(1)}, u32[]{:S(2)}, u32[]{:S(2)}) collective-permute-start(bf16[4,48,384]{2,1,0:T(8,128)(2,1)S(1)} %pad_maximum_fusion.refs_6_.refs_0_), channel_id=1, source_target_pairs={{0,4},{4,0},{1,5},{5,1},{2,6},{6,2},{3,7},{7,3},{8,12},{12,8},{9,1... | collective-permute-start | bytes 442376 | tf_op jit(solution)/shard_map/ppermute | solution.py:1167
  23.2 3.5 %collective-permute-start.14 = (bf16[4,48,384]{2,1,0:T(8,128)(2,1)S(1)}, bf16[4,48,384]{2,1,0:T(8,128)(2,1)S(1)}, u32[]{:S(2)}, u32[]{:S(2)}) collective-permute-start(bf16[4,48,384]{2,1,0:T(8,128)(2,1)S(1)} %collective-permute-done.10.refs_9_.refs_3_), channel_id=1, source_target_pairs={{0,4},{4,0},{1,5},{5,1},{2,6},{6,2},{3,7},{7,3},{8,12},{12,8},{9,1... | collective-permute-start | bytes 442376 | tf_op jit(solution)/shard_map/ppermute | solution.py:1167
  26.1 1.4 %collective-permute-start.13 = (bf16[4,48,384]{2,1,0:T(8,128)(2,1)S(1)}, bf16[4,48,384]{2,1,0:T(8,128)(2,1)S(1)}, u32[]{:S(2)}, u32[]{:S(2)}) collective-permute-start(bf16[4,48,384]{2,1,0:T(8,128)(2,1)S(1)} %collective-permute-done.9.refs_8_.refs_2_), channel_id=1, source_target_pairs={{0,4},{4,0},{1,5},{5,1},{2,6},{6,2},{3,7},{7,3},{8,12},{12,8},{9,1... | collective-permute-start | bytes 442376 | tf_op jit(solution)/shard_map/ppermute | solution.py:1167
  26.2 1.5 %collective-permute-start.12 = (bf16[4,48,384]{2,1,0:T(8,128)(2,1)S(1)}, bf16[4,48,384]{2,1,0:T(8,128)(2,1)S(1)}, u32[]{:S(2)}, u32[]{:S(2)}) collective-permute-start(bf16[4,48,384]{2,1,0:T(8,128)(2,1)S(1)} %collective-permute-done.8.refs_7_.refs_1_), channel_id=1, source_target_pairs={{0,4},{4,0},{1,5},{5,1},{2,6},{6,2},{3,7},{7,3},{8,12},{12,8},{9,1... | collective-permute-start | bytes 442376 | tf_op jit(solution)/shard_map/ppermute | solution.py:1167
  27.7 5.2 %copy-start = (bf16[4,1024,192]{2,1,0:T(8,128)(2,1)S(1)}, bf16[4,1024,192]{2,1,0:T(8,128)(2,1)}, u32[]{:S(2)}) copy-start(bf16[4,1024,192]{2,1,0:T(8,128)(2,1)} %constant.8.clone.sel_2_ref) | copy-start | bytes 4718596
  27.7 5.2 %copy-start.1 = (bf16[1024,192]{1,0:T(8,128)(2,1)S(1)}, bf16[1024,192]{1,0:T(8,128)(2,1)}, u32[]{:S(2)}) copy-start(bf16[1024,192]{1,0:T(8,128)(2,1)} %constant.7.clone.sel_o_ref) | copy-start | bytes 1179652
  27.7 5.3 %copy-start.2 = (bf16[512,384]{1,0:T(8,128)(2,1)S(1)}, bf16[512,384]{1,0:T(8,128)(2,1)}, u32[]{:S(2)}) copy-start(bf16[512,384]{1,0:T(8,128)(2,1)} %constant.6.clone.sel_1_ref) | copy-start | bytes 1179652
  40.9 4.9 %collective-permute-start.15 = (bf16[4,4,48,256]{3,2,1,0:T(8,128)(2,1)S(1)}, bf16[4,4,48,256]{3,2,1,0:T(8,128)(2,1)S(1)}, u32[]{:S(2)}, u32[]{:S(2)}) collective-permute-start(bf16[4,4,48,256]{3,2,1,0:T(8,128)(2,1)S(1)} %get-tuple-element.107), channel_id=1, source_target_pairs={{0,4},{4,0},{1,5},{5,1},{2,6},{6,2},{3,7},{7,3},{8,12},{12,8},{9,1... | collective-permute-start | bytes 1179656 | tf_op jit(solution)/shard_map/ppermute | solution.py:1167
  46.0 3.7 %collective-permute-start.16 = (bf16[1024,192]{1,0:T(8,128)(2,1)S(1)}, bf16[1024,192]{1,0:T(8,128)(2,1)S(1)}, u32[]{:S(2)}, u32[]{:S(2)}) collective-permute-start(bf16[1024,192]{1,0:T(8,128)(2,1)S(1)} %get-tuple-element.119.refs_2_), channel_id=1, source_target_pairs={{0,4},{4,0},{1,5},{5,1},{2,6},{6,2},{3,7},{7,3},{8,12},{12,8},{9,1... | collective-permute-start | bytes 1179656 | tf_op jit(solution)/shard_map/ppermute | solution.py:1167
  46.2 9.6 %collective-permute-start.17 = (bf16[288,256]{1,0:T(8,128)(2,1)S(1)}, bf16[288,256]{1,0:T(8,128)(2,1)S(1)}, u32[]{:S(2)}, u32[]{:S(2)}) collective-permute-start(bf16[288,256]{1,0:T(8,128)(2,1)S(1)} %get-tuple-element.131), channel_id=1, source_target_pairs={{0,1},{1,0},{2,3},{3,2},{4,5},{5,4},{6,7},{7,6},{8,9},{9,8},{10,11... | collective-permute-start | bytes 442376 | tf_op jit(solution)/shard_map/ppermute | solution.py:1172
  47.7 9.0 %collective-permute-start.18 = (bf16[288,256]{1,0:T(8,128)(2,1)S(1)}, bf16[288,256]{1,0:T(8,128)(2,1)S(1)}, u32[]{:S(2)}, u32[]{:S(2)}) collective-permute-start(bf16[288,256]{1,0:T(8,128)(2,1)S(1)} %get-tuple-element.132), channel_id=1, source_target_pairs={{0,2},{1,3},{2,0},{3,1},{4,6},{5,7},{6,4},{7,5},{8,10},{9,11},{10,... | collective-permute-start | bytes 442376 | tf_op jit(solution)/shard_map/ppermute | solution.py:1172
  48.0 8.6 %collective-permute-start.19 = (bf16[288,256]{1,0:T(8,128)(2,1)S(1)}, bf16[288,256]{1,0:T(8,128)(2,1)S(1)}, u32[]{:S(2)}, u32[]{:S(2)}) collective-permute-start(bf16[288,256]{1,0:T(8,128)(2,1)S(1)} %get-tuple-element.133), channel_id=1, source_target_pairs={{0,3},{1,2},{2,1},{3,0},{4,7},{5,6},{6,5},{7,4},{8,11},{9,10},{10,... | collective-permute-start | bytes 442376 | tf_op jit(solution)/shard_map/ppermute | solution.py:1172
  49.7 7.0 %copy-start.4 = (f32[2,192]{1,0:T(2,128)S(1)}, f32[2,192]{1,0:T(2,128)}, u32[]{:S(2)}) copy-start(f32[2,192]{1,0:T(2,128)} %gains_ref.3) | copy-start | bytes 4612
  56.7 1.5 %collective-permute-start.20 = (bf16[17,48,128]{2,1,0:T(8,128)(2,1)S(1)}, bf16[17,48,128]{2,1,0:T(8,128)(2,1)S(1)}, u32[]{:S(2)}, u32[]{:S(2)}) collective-permute-start(bf16[17,48,128]{2,1,0:T(8,128)(2,1)S(1)} %get-tuple-element.139), channel_id=1, source_target_pairs={{0,4},{4,0},{1,5},{5,1},{2,6},{6,2},{3,7},{7,3},{8,12},{12,8},{9,1... | collective-permute-start | bytes 626696 | tf_op jit(solution)/shard_map/ppermute | solution.py:1167
  58.2 5.7 %collective-permute-start.21 = (bf16[400,128]{1,0:T(8,128)(2,1)S(1)}, bf16[400,128]{1,0:T(8,128)(2,1)S(1)}, u32[]{:S(2)}, u32[]{:S(2)}) collective-permute-start(bf16[400,128]{1,0:T(8,128)(2,1)S(1)} %get-tuple-element.147), channel_id=1, source_target_pairs={{0,1},{1,0},{2,3},{3,2},{4,5},{5,4},{6,7},{7,6},{8,9},{9,8},{10,11... | collective-permute-start | bytes 307208 | tf_op jit(solution)/shard_map/ppermute | solution.py:1172
  58.9 6.9 %collective-permute-start.22 = (bf16[400,128]{1,0:T(8,128)(2,1)S(1)}, bf16[400,128]{1,0:T(8,128)(2,1)S(1)}, u32[]{:S(2)}, u32[]{:S(2)}) collective-permute-start(bf16[400,128]{1,0:T(8,128)(2,1)S(1)} %get-tuple-element.148), channel_id=1, source_target_pairs={{0,2},{1,3},{2,0},{3,1},{4,6},{5,7},{6,4},{7,5},{8,10},{9,11},{10,... | collective-permute-start | bytes 307208 | tf_op jit(solution)/shard_map/ppermute | solution.py:1172
  60.0 5.8 %collective-permute-start.23 = (bf16[400,128]{1,0:T(8,128)(2,1)S(1)}, bf16[400,128]{1,0:T(8,128)(2,1)S(1)}, u32[]{:S(2)}, u32[]{:S(2)}) collective-permute-start(bf16[400,128]{1,0:T(8,128)(2,1)S(1)} %get-tuple-element.149), channel_id=1, source_target_pairs={{0,3},{1,2},{2,1},{3,0},{4,7},{5,6},{6,5},{7,4},{8,11},{9,10},{10,... | collective-permute-start | bytes 307208 | tf_op jit(solution)/shard_map/ppermute | solution.py:1172
  65.8 4.7 %collective-permute-start.27 = (bf16[2,384,128]{2,1,0:T(8,128)(2,1)S(1)}, bf16[2,384,128]{2,1,0:T(8,128)(2,1)S(1)}, u32[]{:S(2)}, u32[]{:S(2)}) collective-permute-start(bf16[2,384,128]{2,1,0:T(8,128)(2,1)S(1)} %choose.1), channel_id=1, source_target_pairs={{0,4},{4,0},{1,5},{5,1},{2,6},{6,2},{3,7},{7,3},{8,12},{12,8},{9,1... | collective-permute-start | bytes 589832 | tf_op jit(solution)/shard_map/ppermute | solution.py:1167
  66.1 5.5 %collective-permute-start.24 = (bf16[48,384]{1,0:T(8,128)(2,1)S(1)}, bf16[48,384]{1,0:T(8,128)(2,1)S(1)}, u32[]{:S(2)}, u32[]{:S(2)}) collective-permute-start(bf16[48,384]{1,0:T(8,128)(2,1)S(1)} %get-tuple-element.151), channel_id=1, source_target_pairs={{0,8},{8,0},{16,24},{24,16},{1,9},{9,1},{17,25},{25,17},{2,10},{10... | collective-permute-start | bytes 110600 | tf_op jit(solution)/shard_map/ppermute | solution.py:1172
  67.3 5.8 %collective-permute-start.25 = (bf16[48,384]{1,0:T(8,128)(2,1)S(1)}, bf16[48,384]{1,0:T(8,128)(2,1)S(1)}, u32[]{:S(2)}, u32[]{:S(2)}) collective-permute-start(bf16[48,384]{1,0:T(8,128)(2,1)S(1)} %get-tuple-element.152), channel_id=1, source_target_pairs={{0,16},{8,24},{16,0},{24,8},{1,17},{9,25},{17,1},{25,9},{2,18},{10... | collective-permute-start | bytes 110600 | tf_op jit(solution)/shard_map/ppermute | solution.py:1172
  70.2 5.8 %collective-permute-start.26 = (bf16[48,384]{1,0:T(8,128)(2,1)S(1)}, bf16[48,384]{1,0:T(8,128)(2,1)S(1)}, u32[]{:S(2)}, u32[]{:S(2)}) collective-permute-start(bf16[48,384]{1,0:T(8,128)(2,1)S(1)} %get-tuple-element.153), channel_id=1, source_target_pairs={{0,24},{8,16},{16,8},{24,0},{1,25},{9,17},{17,9},{25,1},{2,26},{10... | collective-permute-start | bytes 110600 | tf_op jit(solution)/shard_map/ppermute | solution.py:1172
  (1 other events, 0.7 us)

commit v9 on v8

--- a/solution.py
+++ b/solution.py
@@ -340,9 +340,10 @@
         place = pl.ds(pl.multiple_of(core * half, half), half)
         out_ref[:packed] = pack(patch_ref[image, place, :])
         out_ref[packed : 2 * packed] = pack(cot_ref[image, place, :])
-        valid = valid_ref[image].astype(F32).astype(BF16)
-        out_ref[2 * packed :] = jnp.concatenate(
-            [valid, jnp.zeros((GRID, LANES - GRID), BF16)], axis=1
+        valid = valid_ref[image].astype(F32)
+        valid = jnp.concatenate([valid[8 * q : 8 * q + 8] for q in range(4)], axis=1)
+        out_ref[2 * packed :] = jnp.concatenate([valid, jnp.zeros((8, LANES), F32)], axis=0).astype(
+            BF16
         )
 
 
@@ -369,7 +370,9 @@
         first_ref[pl.ds(pl.multiple_of(block * slots, slots), slots), :] = (unit * gain).astype(
             BF16
         )
-    valid = got_refs[0][2 * packed :].astype(F32).T
+    valid = got_refs[0][2 * packed :].astype(F32)
+    valid = jnp.concatenate([valid[:8, q * GRID : (q + 1) * GRID] for q in range(4)], axis=0)
+    valid = jnp.concatenate([valid, jnp.zeros((GRID, LANES - GRID), F32)], axis=1).T
     for i in range(GRID):
         mask_ref[i * GRID : (i + 1) * GRID, :] = jnp.broadcast_to(
             valid[:GRID, i : i + 1], (GRID, LANES)
@@ -1184,7 +1187,7 @@
     sel_1, sel_o, sel_2 = early_selections(parts)
 
     rows_weight = w_u.shape[0]
-    payload = shape((2 * packed_rows + GRID, LANES), BF16)
+    payload = shape((2 * packed_rows + 16, LANES), BF16)
     shard = shape((rows_weight, 3 * LANES), BF16)
     sources = [value.reshape(images, rows_here * GRID, D) for value in (patches, cotangent)]
     if rows_weight % 16 == 0:

time: 77.1 us -> 77 us (level)
  transfers between devices with their start and end apart: 28 -> 28, of which waited for: 12 -> 12; matrix products, arithmetic and copies ran while one was open for 1% -> 1% of each run, Pallas kernels for 17% -> 18%
where the time goes in v9:
time: 77 us; the launch traced here: 76.7 us
  Pallas kernels  29.8 us (39%)
  starting transfers between devices  27.9 us (36%)
  waiting for transfers between devices  16.8 us (22%)
  other arithmetic  0.79 us (1%)
  between operations  0.78 us (1%)
    ppermute x15, starting transfers between devices, exchanged(): lax.ppermute(values[k], axis, [(i, i ^ k) for i in range(size)])  21.2 us
    ppermute x15, waiting for transfers between devices, exchanged(): lax.ppermute(values[k], axis, [(i, i ^ k) for i in range(size)])  13 us
    pallas_call x1, Pallas kernels, per_device(): pl.pallas_call(middle_kernel, name='attention_and_feed_forward', out_shap...  7.92 us
    pallas_call x1, Pallas kernels, per_device(): pl.pallas_call(lambda *refs: scan_back_kernel(starts, width, *refs), name...  6.06 us
    pallas_call x1, Pallas kernels, per_device(): pl.pallas_call(lambda *refs: scan_kernel(starts, width, *refs, blocks=blo...  5.22 us
    ppermute x4, starting transfers between devices, to_chips(): return lax.ppermute(value, ('core', 'row'), pairs)  4.98 us
    pallas_call x1, Pallas kernels, per_device(): pl.pallas_call(lambda *refs: attention_back_kernel(*refs, blocks=blocks),...  4.47 us
    pallas_call x1, Pallas kernels, per_device(): pl.pallas_call(depart_kernel, name='depart', out_shape=(shard,) + (payloa...  2.03 us
  transfers between devices with their start and end apart: 28, of which 12 were waited for; matrix products, arithmetic and copies ran while one was open for 1% of the time, Pallas kernels for 18%

profile of v9, /device:TPU:0, one launch (start us, length us, event | category | flops | bytes accessed | tf_op | source)
XLA Modules:
  0.0 76.7 jit_solution(18244880056997356273)
XLA Ops:
  0.6 2.0 %depart.1 = (bf16[48,384]{1,0:T(8,128)(2,1)}, bf16[400,128]{1,0:T(8,128)(2,1)}, bf16[400,128]{1,0:T(8,128)(2,1)}, bf16[400,128]{1,0:T(8,128)(2,1)}, bf16[400,128]{1,0:T(8,128)(2,1)}) custom-call(bf16[24,48]{1,0:T(8,128)(2,1)} %bitcast.27, bf16[8,48]{1,0:T(8,128)(2,1)} %bitcast.29, bf16[8,48]{1,0:T(8,128)(2,1)} %bitcast.30, bf16[24,48]{1,0:T(8,128)(2,1)} %bitcast.28, ...), custom_call_target="tpu_custom_call" | custom-call | tf_op jit(solution)/shard_map/depart/pallas_call | solution.py:1194
  2.7 5.0 %collective-permute-start.7 = (bf16[48,384]{1,0:T(8,128)(2,1)}, bf16[48,384]{1,0:T(8,128)(2,1)S(1)}, u32[]{:S(2)}, u32[]{:S(2)}) collective-permute-start(bf16[48,384]{1,0:T(8,128)(2,1)} %get-tuple-element.101), channel_id=1, source_target_pairs={{0,24},{8,16},{16,8},{24,0},{1,25},{9,17},{17,9},{25,1},{2,26},{10... | collective-permute-start | bytes 110600 | tf_op jit(solution)/shard_map/ppermute | solution.py:1175
  8.3 1.5 %collective-permute-start = (bf16[400,128]{1,0:T(8,128)(2,1)}, bf16[400,128]{1,0:T(8,128)(2,1)S(1)}, u32[]{:S(2)}, u32[]{:S(2)}) collective-permute-start(bf16[400,128]{1,0:T(8,128)(2,1)} %get-tuple-element.91), channel_id=1, source_target_pairs={{0,0},{1,1},{2,4},{3,5},{4,2},{5,3},{6,6},{7,7},{8,8},{9,9},{10,12... | collective-permute-start | bytes 307208 | tf_op jit(solution)/shard_map/ppermute | solution.py:1184
  9.9 1.7 %collective-permute-start.1 = (bf16[400,128]{1,0:T(8,128)(2,1)}, bf16[400,128]{1,0:T(8,128)(2,1)S(1)}, u32[]{:S(2)}, u32[]{:S(2)}) collective-permute-start(bf16[400,128]{1,0:T(8,128)(2,1)} %get-tuple-element.92), channel_id=1, source_target_pairs={{0,1},{1,0},{2,5},{3,4},{4,3},{5,2},{6,7},{7,6},{8,9},{9,8},{10,13... | collective-permute-start | bytes 307208 | tf_op jit(solution)/shard_map/ppermute | solution.py:1184
  11.5 1.5 %collective-permute-start.2 = (bf16[400,128]{1,0:T(8,128)(2,1)}, bf16[400,128]{1,0:T(8,128)(2,1)S(1)}, u32[]{:S(2)}, u32[]{:S(2)}) collective-permute-start(bf16[400,128]{1,0:T(8,128)(2,1)} %get-tuple-element.93), channel_id=1, source_target_pairs={{0,4},{1,5},{2,0},{3,1},{4,6},{5,7},{6,2},{7,3},{8,12},{9,13},{10,... | collective-permute-start | bytes 307208 | tf_op jit(solution)/shard_map/ppermute | solution.py:1184
  13.3 0.8 %pad_maximum_fusion.refs_6_.refs_0_ = bf16[4,48,384]{2,1,0:T(8,128)(2,1)S(1)} fusion(bf16[1,48,384]{2,1,0:T(8,128)(2,1)S(1)} %bitcast.23, bf16[1,48,384]{2,1,0:T(8,128)(2,1)S(1)} %bitcast.24, bf16[1,48,384]{2,1,0:T(8,128)(2,1)S(1)} %bitcast.25, bf16[1,48,384]{2,1,0:T(8,128)(2,1)} %bitcast.22), kind=kLoop, calls=%fused_computation | loop fusion | flops 221184 | bytes 294912 | tf_op jit(solution)/shard_map/stack | solution.py:1235
  14.1 2.7 %collective-permute-start.10 = (bf16[4,48,384]{2,1,0:T(8,128)(2,1)S(1)}, bf16[4,48,384]{2,1,0:T(8,128)(2,1)S(1)}, u32[]{:S(2)}, u32[]{:S(2)}) collective-permute-start(bf16[4,48,384]{2,1,0:T(8,128)(2,1)S(1)} %pad_maximum_fusion.refs_6_.refs_0_), channel_id=1, source_target_pairs={{0,3},{1,2},{2,1},{3,0},{4,7},{5,6},{6,5},{7,4},{8,11},{9,10},{10,... | collective-permute-start | bytes 442376 | tf_op jit(solution)/shard_map/ppermute | solution.py:1175
  17.1 1.1 %collective-permute-start.8 = (bf16[4,48,384]{2,1,0:T(8,128)(2,1)S(1)}, bf16[4,48,384]{2,1,0:T(8,128)(2,1)S(1)}, u32[]{:S(2)}, u32[]{:S(2)}) collective-permute-start(bf16[4,48,384]{2,1,0:T(8,128)(2,1)S(1)} %pad_maximum_fusion.refs_6_.refs_0_), channel_id=1, source_target_pairs={{0,1},{1,0},{2,3},{3,2},{4,5},{5,4},{6,7},{7,6},{8,9},{9,8},{10,11... | collective-permute-start | bytes 442376 | tf_op jit(solution)/shard_map/ppermute | solution.py:1175
  18.2 1.3 %collective-permute-done.2.refs_3_ = bf16[400,128]{1,0:T(8,128)(2,1)S(1)} collective-permute-done((bf16[400,128]{1,0:T(8,128)(2,1)}, bf16[400,128]{1,0:T(8,128)(2,1)S(1)}, u32[]{:S(2)}, u32[]{:S(2)}) %collective-permute-start.2) | collective-permute-done | bytes 102432 | tf_op jit(solution)/shard_map/ppermute | solution.py:1184
  20.0 0.7 copy-done.3
  20.7 1.2 %first_norm.1 = (bf16[4,2,128,192]{3,2,1,0:T(8,128)(2,1)S(1)}, bf16[512,192]{1,0:T(8,128)(2,1)S(1)}, f32[1024,128]{1,0:T(8,128)S(1)}, bf16[1024,192]{1,0:T(8,128...) custom-call(f32[2,192]{1,0:T(2,128)S(1)} %copy-done.3, ...), custom_call_target="tpu_custom_call" | custom-call | tf_op jit(solution)/shard_map/first_norm/pallas_call | solution.py:1239
  23.1 2.9 %collective-permute-done.9.refs_8_.refs_2_ = bf16[4,48,384]{2,1,0:T(8,128)(2,1)S(1)} collective-permute-done((bf16[4,48,384]{2,1,0:T(8,128)(2,1)S(1)}, bf16[4,48,384]{2,1,0:T(8,128)(2,1)S(1)}, u32[]{:S(2)}, u32[]{:S(2)}) %collective-permute-start.9) | collective-permute-done | bytes 147488 | tf_op jit(solution)/shard_map/ppermute | solution.py:1175
  26.5 0.8 %collective-permute-done.13.refs_12_.refs_6_ = bf16[4,48,384]{2,1,0:T(8,128)(2,1)S(1)} collective-permute-done((bf16[4,48,384]{2,1,0:T(8,128)(2,1)S(1)}, bf16[4,48,384]{2,1,0:T(8,128)(2,1)S(1)}, u32[]{:S(2)}, u32[]{:S(2)}) %collective-permute-start.13) | collective-permute-done | bytes 147488 | tf_op jit(solution)/shard_map/ppermute | solution.py:1170
  27.6 5.2 %scan_forward.1 = (bf16[3,512,128]{2,1,0:T(8,128)(2,1)S(1)}, bf16[3,1024,128]{2,1,0:T(8,128)(2,1)S(1)}, bf16[3,1024,128]{2,1,0:T(8,128)(2,1)S(1)}, bf16[1024,192...) custom-call(bf16[512,192]{1,0:T(8,128)(2,1)S(1)} %get-tuple-element., ...), custom_call_target="tpu_custom_call" | custom-call | tf_op jit(solution)/shard_map/scan_forward/pallas_call | solution.py:1259
  32.9 7.9 %attention_and_feed_forward.1 = (bf16[3,1024,512]{2,1,0:T(8,128)(2,1)S(1)}, bf16[3,512,128]{2,1,0:T(8,128)(2,1)S(1)}, bf16[512,192]{1,0:T(8,128)(2,1)S(1)}, f32[...) custom-call(bf16[4,2,128,192]{3,2,1,0:T(8,128)(2,1)S(1)} %get-tuple-, ...), custom_call_target="tpu_custom_call" | custom-call | tf_op jit(solution)/shard_map/attention_and_feed_forward/pallas_call | solution.py:1283
  41.2 4.5 %attention_backward.1 = (bf16[1024,192]{1,0:T(8,128)(2,1)S(1)}, bf16[2,1024,384]{2,1,0:T(8,128)(2,1)S(1)}, bf16[512,384]{1,0:T(8,128)(2,1)S(1)}) custom-call(bf16[3,1024,512]{2,1,0:T(8,128)(2,1)S(1)} %get-tuple-element.108.refs_0_, bf16[3,512,128]{2,1,0:T(8,128)(2,1)S(1)} %get-tuple-element.109.refs_1_, ...), custom_call_target="tpu_custom_call" | custom-call | tf_op jit(solution)/shard_map/attention_backward/pallas_call | solution.py:1320
  46.1 1.5 %collective-permute-start.17 = (bf16[288,256]{1,0:T(8,128)(2,1)S(1)}, bf16[288,256]{1,0:T(8,128)(2,1)S(1)}, u32[]{:S(2)}, u32[]{:S(2)}) collective-permute-start(bf16[288,256]{1,0:T(8,128)(2,1)S(1)} %get-tuple-element.131), channel_id=1, source_target_pairs={{0,1},{1,0},{2,3},{3,2},{4,5},{5,4},{6,7},{7,6},{8,9},{9,8},{10,11... | collective-permute-start | bytes 442376 | tf_op jit(solution)/shard_map/ppermute | solution.py:1175
  47.9 1.7 %collective-permute-start.19 = (bf16[288,256]{1,0:T(8,128)(2,1)S(1)}, bf16[288,256]{1,0:T(8,128)(2,1)S(1)}, u32[]{:S(2)}, u32[]{:S(2)}) collective-permute-start(bf16[288,256]{1,0:T(8,128)(2,1)S(1)} %get-tuple-element.133), channel_id=1, source_target_pairs={{0,3},{1,2},{2,1},{3,0},{4,7},{5,6},{6,5},{7,4},{8,11},{9,10},{10,... | collective-permute-start | bytes 442376 | tf_op jit(solution)/shard_map/ppermute | solution.py:1175
  49.6 6.1 %scan_backward.1 = (bf16[17,48,128]{2,1,0:T(8,128)(2,1)S(1)}, bf16[17,48,128]{2,1,0:T(8,128)(2,1)S(1)}, f32[512,192]{1,0:T(8,128)S(1)}) custom-call(bf16[4,2,128,192]{3,2,1,0:T(8,128)(2,1)S(1)} %get-tuple-element.95.own_ref.refs_0_, f32[1024,128]{1,0:T(8,128)S(1)} %get-tuple-element.96.refs_2_.mask_ref.refs_1_, ...), custom_call_target="tpu_custom_call" | custom-call | tf_op jit(solution)/shard_map/scan_backward/pallas_call | solution.py:1352
  55.6 0.9 %collective-permute-done.18.refs_2_ = bf16[288,256]{1,0:T(8,128)(2,1)S(1)} collective-permute-done((bf16[288,256]{1,0:T(8,128)(2,1)S(1)}, bf16[288,256]{1,0:T(8,128)(2,1)S(1)}, u32[]{:S(2)}, u32[]{:S(2)}) %collective-permute-start.18) | collective-permute-done | bytes 147488 | tf_op jit(solution)/shard_map/ppermute | solution.py:1175
  57.1 0.9 %collective-permute-done.20.refs_1_ = bf16[17,48,128]{2,1,0:T(8,128)(2,1)S(1)} collective-permute-done((bf16[17,48,128]{2,1,0:T(8,128)(2,1)S(1)}, bf16[17,48,128]{2,1,0:T(8,128)(2,1)S(1)}, u32[]{:S(2)}, u32[]{:S(2)}) %collective-permute-start.20) | collective-permute-done | bytes 208928 | tf_op jit(solution)/shard_map/ppermute | solution.py:1170
  58.1 0.7 collective-permute-start.21
  58.8 1.1 %collective-permute-start.22 = (bf16[400,128]{1,0:T(8,128)(2,1)S(1)}, bf16[400,128]{1,0:T(8,128)(2,1)S(1)}, u32[]{:S(2)}, u32[]{:S(2)}) collective-permute-start(bf16[400,128]{1,0:T(8,128)(2,1)S(1)} %get-tuple-element.148), channel_id=1, source_target_pairs={{0,2},{1,3},{2,0},{3,1},{4,6},{5,7},{6,4},{7,5},{8,10},{9,11},{10,... | collective-permute-start | bytes 307208 | tf_op jit(solution)/shard_map/ppermute | solution.py:1175
  59.9 1.8 %collective-permute-start.23 = (bf16[400,128]{1,0:T(8,128)(2,1)S(1)}, bf16[400,128]{1,0:T(8,128)(2,1)S(1)}, u32[]{:S(2)}, u32[]{:S(2)}) collective-permute-start(bf16[400,128]{1,0:T(8,128)(2,1)S(1)} %get-tuple-element.149), channel_id=1, source_target_pairs={{0,3},{1,2},{2,1},{3,0},{4,7},{5,6},{6,5},{7,4},{8,11},{9,10},{10,... | collective-permute-start | bytes 307208 | tf_op jit(solution)/shard_map/ppermute | solution.py:1175
  61.6 2.1 %collective-permute-done.21.refs_5_ = bf16[400,128]{1,0:T(8,128)(2,1)S(1)} collective-permute-done((bf16[400,128]{1,0:T(8,128)(2,1)S(1)}, bf16[400,128]{1,0:T(8,128)(2,1)S(1)}, u32[]{:S(2)}, u32[]{:S(2)}) %collective-permute-start.21) | collective-permute-done | bytes 102432 | tf_op jit(solution)/shard_map/ppermute | solution.py:1175
  63.8 1.9 %collective-permute-done.22.refs_6_ = bf16[400,128]{1,0:T(8,128)(2,1)S(1)} collective-permute-done((bf16[400,128]{1,0:T(8,128)(2,1)S(1)}, bf16[400,128]{1,0:T(8,128)(2,1)S(1)}, u32[]{:S(2)}, u32[]{:S(2)}) %collective-permute-start.22) | collective-permute-done | bytes 102432 | tf_op jit(solution)/shard_map/ppermute | solution.py:1175
  66.0 1.3 %collective-permute-start.24 = (bf16[48,384]{1,0:T(8,128)(2,1)S(1)}, bf16[48,384]{1,0:T(8,128)(2,1)S(1)}, u32[]{:S(2)}, u32[]{:S(2)}) collective-permute-start(bf16[48,384]{1,0:T(8,128)(2,1)S(1)} %get-tuple-element.151), channel_id=1, source_target_pairs={{0,8},{8,0},{16,24},{24,16},{1,9},{9,1},{17,25},{25,17},{2,10},{10... | collective-permute-start | bytes 110600 | tf_op jit(solution)/shard_map/ppermute | solution.py:1175
  67.2 2.9 %collective-permute-start.25 = (bf16[48,384]{1,0:T(8,128)(2,1)S(1)}, bf16[48,384]{1,0:T(8,128)(2,1)S(1)}, u32[]{:S(2)}, u32[]{:S(2)}) collective-permute-start(bf16[48,384]{1,0:T(8,128)(2,1)S(1)} %get-tuple-element.152), channel_id=1, source_target_pairs={{0,16},{8,24},{16,0},{24,8},{1,17},{9,25},{17,1},{25,9},{2,18},{10... | collective-permute-start | bytes 110600 | tf_op jit(solution)/shard_map/ppermute | solution.py:1175
  70.4 1.0 %home.1 = (bf16[2,256,192]{2,1,0:T(8,128)(2,1)}, bf16[2,256,192]{2,1,0:T(8,128)(2,1)}) custom-call(bf16[2,384,128]{2,1,0:T(8,128)(2,1)S(1)} %collective-permute-done.27.swapped_ref, bf16[288,256]{1,0:T(8,128)(2,1)S(1)} %get-tuple-element.134.refs_0_, bf16[288,256]{1,0:T(8,128)(2,1)S(1)} %collective-permute-done.17.refs_1_, ...), custom_call_target="tpu_custom_call" | custom-call | tf_op jit(solution)/shard_map/home/pallas_call | solution.py:1431
  71.4 1.5 %collective-permute-done.25.refs_2_ = bf16[48,384]{1,0:T(8,128)(2,1)S(1)} collective-permute-done((bf16[48,384]{1,0:T(8,128)(2,1)S(1)}, bf16[48,384]{1,0:T(8,128)(2,1)S(1)}, u32[]{:S(2)}, u32[]{:S(2)}) %collective-permute-start.25) | collective-permute-done | bytes 36896 | tf_op jit(solution)/shard_map/ppermute | solution.py:1175
  73.0 2.9 %collective-permute-done.26.refs_3_ = bf16[48,384]{1,0:T(8,128)(2,1)S(1)} collective-permute-done((bf16[48,384]{1,0:T(8,128)(2,1)S(1)}, bf16[48,384]{1,0:T(8,128)(2,1)S(1)}, u32[]{:S(2)}, u32[]{:S(2)}) %collective-permute-start.26) | collective-permute-done | bytes 36896 | tf_op jit(solution)/shard_map/ppermute | solution.py:1175
  75.9 0.8 %final_sum.1 = (f32[1,192]{1,0:T(1,128)}, f32[1,192]{1,0:T(1,128)}, f32[24,48]{1,0:T(8,128)}, f32[8,48]{1,0:T(8,128)}, f32[8,48]{1,0:T(8,128)}, /*index=5*/f32[4...) custom-call(bf16[48,384]{1,0:T(8,128)(2,1)S(1)} %get-tuple-element.158.refs_0_, ...), custom_call_target="tpu_custom_call" | custom-call | tf_op jit(solution)/shard_map/final_sum/pallas_call | solution.py:1442
  (48 shorter events, 5.9 us)
Async XLA Ops:
  2.7 8.9 %collective-permute-start.7 = (bf16[48,384]{1,0:T(8,128)(2,1)}, bf16[48,384]{1,0:T(8,128)(2,1)S(1)}, u32[]{:S(2)}, u32[]{:S(2)}) collective-permute-start(bf16[48,384]{1,0:T(8,128)(2,1)} %get-tuple-element.101), channel_id=1, source_target_pairs={{0,24},{8,16},{16,8},{24,0},{1,25},{9,17},{17,9},{25,1},{2,26},{10... | collective-permute-start | bytes 110600 | tf_op jit(solution)/shard_map/ppermute | solution.py:1175
  7.7 5.3 %collective-permute-start.6 = (bf16[48,384]{1,0:T(8,128)(2,1)}, bf16[48,384]{1,0:T(8,128)(2,1)S(1)}, u32[]{:S(2)}, u32[]{:S(2)}) collective-permute-start(bf16[48,384]{1,0:T(8,128)(2,1)} %get-tuple-element.101), channel_id=1, source_target_pairs={{0,16},{8,24},{16,0},{24,8},{1,17},{9,25},{17,1},{25,9},{2,18},{10... | collective-permute-start | bytes 110600 | tf_op jit(solution)/shard_map/ppermute | solution.py:1175
  7.7 5.6 %collective-permute-start.5 = (bf16[48,384]{1,0:T(8,128)(2,1)}, bf16[48,384]{1,0:T(8,128)(2,1)S(1)}, u32[]{:S(2)}, u32[]{:S(2)}) collective-permute-start(bf16[48,384]{1,0:T(8,128)(2,1)} %get-tuple-element.101), channel_id=1, source_target_pairs={{0,8},{8,0},{16,24},{24,16},{1,9},{9,1},{17,25},{25,17},{2,10},{10... | collective-permute-start | bytes 110600 | tf_op jit(solution)/shard_map/ppermute | solution.py:1175
  8.3 8.5 %collective-permute-start = (bf16[400,128]{1,0:T(8,128)(2,1)}, bf16[400,128]{1,0:T(8,128)(2,1)S(1)}, u32[]{:S(2)}, u32[]{:S(2)}) collective-permute-start(bf16[400,128]{1,0:T(8,128)(2,1)} %get-tuple-element.91), channel_id=1, source_target_pairs={{0,0},{1,1},{2,4},{3,5},{4,2},{5,3},{6,6},{7,7},{8,8},{9,9},{10,12... | collective-permute-start | bytes 307208 | tf_op jit(solution)/shard_map/ppermute | solution.py:1184
  9.9 7.2 %collective-permute-start.1 = (bf16[400,128]{1,0:T(8,128)(2,1)}, bf16[400,128]{1,0:T(8,128)(2,1)S(1)}, u32[]{:S(2)}, u32[]{:S(2)}) collective-permute-start(bf16[400,128]{1,0:T(8,128)(2,1)} %get-tuple-element.92), channel_id=1, source_target_pairs={{0,1},{1,0},{2,5},{3,4},{4,3},{5,2},{6,7},{7,6},{8,9},{9,8},{10,13... | collective-permute-start | bytes 307208 | tf_op jit(solution)/shard_map/ppermute | solution.py:1184
  11.5 7.9 %collective-permute-start.2 = (bf16[400,128]{1,0:T(8,128)(2,1)}, bf16[400,128]{1,0:T(8,128)(2,1)S(1)}, u32[]{:S(2)}, u32[]{:S(2)}) collective-permute-start(bf16[400,128]{1,0:T(8,128)(2,1)} %get-tuple-element.93), channel_id=1, source_target_pairs={{0,4},{1,5},{2,0},{3,1},{4,6},{5,7},{6,2},{7,3},{8,12},{9,13},{10,... | collective-permute-start | bytes 307208 | tf_op jit(solution)/shard_map/ppermute | solution.py:1184
  13.1 6.9 %collective-permute-start.3 = (bf16[400,128]{1,0:T(8,128)(2,1)}, bf16[400,128]{1,0:T(8,128)(2,1)S(1)}, u32[]{:S(2)}, u32[]{:S(2)}) collective-permute-start(bf16[400,128]{1,0:T(8,128)(2,1)} %get-tuple-element.94), channel_id=1, source_target_pairs={{0,5},{1,4},{2,1},{3,0},{4,7},{5,6},{6,3},{7,2},{8,13},{9,12},{10,... | collective-permute-start | bytes 307208 | tf_op jit(solution)/shard_map/ppermute | solution.py:1184
  14.1 8.9 %collective-permute-start.10 = (bf16[4,48,384]{2,1,0:T(8,128)(2,1)S(1)}, bf16[4,48,384]{2,1,0:T(8,128)(2,1)S(1)}, u32[]{:S(2)}, u32[]{:S(2)}) collective-permute-start(bf16[4,48,384]{2,1,0:T(8,128)(2,1)S(1)} %pad_maximum_fusion.refs_6_.refs_0_), channel_id=1, source_target_pairs={{0,3},{1,2},{2,1},{3,0},{4,7},{5,6},{6,5},{7,4},{8,11},{9,10},{10,... | collective-permute-start | bytes 442376 | tf_op jit(solution)/shard_map/ppermute | solution.py:1175
  16.9 9.1 %collective-permute-start.9 = (bf16[4,48,384]{2,1,0:T(8,128)(2,1)S(1)}, bf16[4,48,384]{2,1,0:T(8,128)(2,1)S(1)}, u32[]{:S(2)}, u32[]{:S(2)}) collective-permute-start(bf16[4,48,384]{2,1,0:T(8,128)(2,1)S(1)} %pad_maximum_fusion.refs_6_.refs_0_), channel_id=1, source_target_pairs={{0,2},{1,3},{2,0},{3,1},{4,6},{5,7},{6,4},{7,5},{8,10},{9,11},{10,... | collective-permute-start | bytes 442376 | tf_op jit(solution)/shard_map/ppermute | solution.py:1175
  17.1 9.0 %collective-permute-start.8 = (bf16[4,48,384]{2,1,0:T(8,128)(2,1)S(1)}, bf16[4,48,384]{2,1,0:T(8,128)(2,1)S(1)}, u32[]{:S(2)}, u32[]{:S(2)}) collective-permute-start(bf16[4,48,384]{2,1,0:T(8,128)(2,1)S(1)} %pad_maximum_fusion.refs_6_.refs_0_), channel_id=1, source_target_pairs={{0,1},{1,0},{2,3},{3,2},{4,5},{5,4},{6,7},{7,6},{8,9},{9,8},{10,11... | collective-permute-start | bytes 442376 | tf_op jit(solution)/shard_map/ppermute | solution.py:1175
  21.9 4.7 %collective-permute-start.4 = (bf16[512,192]{1,0:T(8,128)(2,1)S(1)}, bf16[512,192]{1,0:T(8,128)(2,1)S(1)}, u32[]{:S(2)}, u32[]{:S(2)}) collective-permute-start(bf16[512,192]{1,0:T(8,128)(2,1)S(1)} %get-tuple-element.97.refs_0_.refs_5_), channel_id=1, source_target_pairs={{0,4},{4,0},{1,5},{5,1},{2,6},{6,2},{3,7},{7,3},{8,12},{12,8},{9,1... | collective-permute-start | bytes 589832 | tf_op jit(solution)/shard_map/ppermute | solution.py:1170
  21.9 4.6 %collective-permute-start.11 = (bf16[4,48,384]{2,1,0:T(8,128)(2,1)S(1)}, bf16[4,48,384]{2,1,0:T(8,128)(2,1)S(1)}, u32[]{:S(2)}, u32[]{:S(2)}) collective-permute-start(bf16[4,48,384]{2,1,0:T(8,128)(2,1)S(1)} %pad_maximum_fusion.refs_6_.refs_0_), channel_id=1, source_target_pairs={{0,4},{4,0},{1,5},{5,1},{2,6},{6,2},{3,7},{7,3},{8,12},{12,8},{9,1... | collective-permute-start | bytes 442376 | tf_op jit(solution)/shard_map/ppermute | solution.py:1170
  23.1 3.4 %collective-permute-start.14 = (bf16[4,48,384]{2,1,0:T(8,128)(2,1)S(1)}, bf16[4,48,384]{2,1,0:T(8,128)(2,1)S(1)}, u32[]{:S(2)}, u32[]{:S(2)}) collective-permute-start(bf16[4,48,384]{2,1,0:T(8,128)(2,1)S(1)} %collective-permute-done.10.refs_9_.refs_3_), channel_id=1, source_target_pairs={{0,4},{4,0},{1,5},{5,1},{2,6},{6,2},{3,7},{7,3},{8,12},{12,8},{9,1... | collective-permute-start | bytes 442376 | tf_op jit(solution)/shard_map/ppermute | solution.py:1170
  26.0 1.4 %collective-permute-start.13 = (bf16[4,48,384]{2,1,0:T(8,128)(2,1)S(1)}, bf16[4,48,384]{2,1,0:T(8,128)(2,1)S(1)}, u32[]{:S(2)}, u32[]{:S(2)}) collective-permute-start(bf16[4,48,384]{2,1,0:T(8,128)(2,1)S(1)} %collective-permute-done.9.refs_8_.refs_2_), channel_id=1, source_target_pairs={{0,4},{4,0},{1,5},{5,1},{2,6},{6,2},{3,7},{7,3},{8,12},{12,8},{9,1... | collective-permute-start | bytes 442376 | tf_op jit(solution)/shard_map/ppermute | solution.py:1170
  26.1 1.5 %collective-permute-start.12 = (bf16[4,48,384]{2,1,0:T(8,128)(2,1)S(1)}, bf16[4,48,384]{2,1,0:T(8,128)(2,1)S(1)}, u32[]{:S(2)}, u32[]{:S(2)}) collective-permute-start(bf16[4,48,384]{2,1,0:T(8,128)(2,1)S(1)} %collective-permute-done.8.refs_7_.refs_1_), channel_id=1, source_target_pairs={{0,4},{4,0},{1,5},{5,1},{2,6},{6,2},{3,7},{7,3},{8,12},{12,8},{9,1... | collective-permute-start | bytes 442376 | tf_op jit(solution)/shard_map/ppermute | solution.py:1170
  27.6 5.2 %copy-start = (bf16[4,1024,192]{2,1,0:T(8,128)(2,1)S(1)}, bf16[4,1024,192]{2,1,0:T(8,128)(2,1)}, u32[]{:S(2)}) copy-start(bf16[4,1024,192]{2,1,0:T(8,128)(2,1)} %constant.8.clone.sel_2_ref) | copy-start | bytes 4718596
  27.6 5.2 %copy-start.1 = (bf16[1024,192]{1,0:T(8,128)(2,1)S(1)}, bf16[1024,192]{1,0:T(8,128)(2,1)}, u32[]{:S(2)}) copy-start(bf16[1024,192]{1,0:T(8,128)(2,1)} %constant.7.clone.sel_o_ref) | copy-start | bytes 1179652
  27.6 5.3 %copy-start.2 = (bf16[512,384]{1,0:T(8,128)(2,1)S(1)}, bf16[512,384]{1,0:T(8,128)(2,1)}, u32[]{:S(2)}) copy-start(bf16[512,384]{1,0:T(8,128)(2,1)} %constant.6.clone.sel_1_ref) | copy-start | bytes 1179652
  40.8 4.9 %collective-permute-start.15 = (bf16[4,4,48,256]{3,2,1,0:T(8,128)(2,1)S(1)}, bf16[4,4,48,256]{3,2,1,0:T(8,128)(2,1)S(1)}, u32[]{:S(2)}, u32[]{:S(2)}) collective-permute-start(bf16[4,4,48,256]{3,2,1,0:T(8,128)(2,1)S(1)} %get-tuple-element.107), channel_id=1, source_target_pairs={{0,4},{4,0},{1,5},{5,1},{2,6},{6,2},{3,7},{7,3},{8,12},{12,8},{9,1... | collective-permute-start | bytes 1179656 | tf_op jit(solution)/shard_map/ppermute | solution.py:1170
  45.9 3.7 %collective-permute-start.16 = (bf16[1024,192]{1,0:T(8,128)(2,1)S(1)}, bf16[1024,192]{1,0:T(8,128)(2,1)S(1)}, u32[]{:S(2)}, u32[]{:S(2)}) collective-permute-start(bf16[1024,192]{1,0:T(8,128)(2,1)S(1)} %get-tuple-element.119.refs_2_), channel_id=1, source_target_pairs={{0,4},{4,0},{1,5},{5,1},{2,6},{6,2},{3,7},{7,3},{8,12},{12,8},{9,1... | collective-permute-start | bytes 1179656 | tf_op jit(solution)/shard_map/ppermute | solution.py:1170
  46.1 9.6 %collective-permute-start.17 = (bf16[288,256]{1,0:T(8,128)(2,1)S(1)}, bf16[288,256]{1,0:T(8,128)(2,1)S(1)}, u32[]{:S(2)}, u32[]{:S(2)}) collective-permute-start(bf16[288,256]{1,0:T(8,128)(2,1)S(1)} %get-tuple-element.131), channel_id=1, source_target_pairs={{0,1},{1,0},{2,3},{3,2},{4,5},{5,4},{6,7},{7,6},{8,9},{9,8},{10,11... | collective-permute-start | bytes 442376 | tf_op jit(solution)/shard_map/ppermute | solution.py:1175
  47.6 9.0 %collective-permute-start.18 = (bf16[288,256]{1,0:T(8,128)(2,1)S(1)}, bf16[288,256]{1,0:T(8,128)(2,1)S(1)}, u32[]{:S(2)}, u32[]{:S(2)}) collective-permute-start(bf16[288,256]{1,0:T(8,128)(2,1)S(1)} %get-tuple-element.132), channel_id=1, source_target_pairs={{0,2},{1,3},{2,0},{3,1},{4,6},{5,7},{6,4},{7,5},{8,10},{9,11},{10,... | collective-permute-start | bytes 442376 | tf_op jit(solution)/shard_map/ppermute | solution.py:1175
  47.9 8.7 %collective-permute-start.19 = (bf16[288,256]{1,0:T(8,128)(2,1)S(1)}, bf16[288,256]{1,0:T(8,128)(2,1)S(1)}, u32[]{:S(2)}, u32[]{:S(2)}) collective-permute-start(bf16[288,256]{1,0:T(8,128)(2,1)S(1)} %get-tuple-element.133), channel_id=1, source_target_pairs={{0,3},{1,2},{2,1},{3,0},{4,7},{5,6},{6,5},{7,4},{8,11},{9,10},{10,... | collective-permute-start | bytes 442376 | tf_op jit(solution)/shard_map/ppermute | solution.py:1175
  49.6 7.0 %copy-start.4 = (f32[2,192]{1,0:T(2,128)S(1)}, f32[2,192]{1,0:T(2,128)}, u32[]{:S(2)}) copy-start(f32[2,192]{1,0:T(2,128)} %gains_ref.3) | copy-start | bytes 4612
  56.6 1.5 %collective-permute-start.20 = (bf16[17,48,128]{2,1,0:T(8,128)(2,1)S(1)}, bf16[17,48,128]{2,1,0:T(8,128)(2,1)S(1)}, u32[]{:S(2)}, u32[]{:S(2)}) collective-permute-start(bf16[17,48,128]{2,1,0:T(8,128)(2,1)S(1)} %get-tuple-element.139), channel_id=1, source_target_pairs={{0,4},{4,0},{1,5},{5,1},{2,6},{6,2},{3,7},{7,3},{8,12},{12,8},{9,1... | collective-permute-start | bytes 626696 | tf_op jit(solution)/shard_map/ppermute | solution.py:1170
  58.1 5.7 %collective-permute-start.21 = (bf16[400,128]{1,0:T(8,128)(2,1)S(1)}, bf16[400,128]{1,0:T(8,128)(2,1)S(1)}, u32[]{:S(2)}, u32[]{:S(2)}) collective-permute-start(bf16[400,128]{1,0:T(8,128)(2,1)S(1)} %get-tuple-element.147), channel_id=1, source_target_pairs={{0,1},{1,0},{2,3},{3,2},{4,5},{5,4},{6,7},{7,6},{8,9},{9,8},{10,11... | collective-permute-start | bytes 307208 | tf_op jit(solution)/shard_map/ppermute | solution.py:1175
  58.8 6.9 %collective-permute-start.22 = (bf16[400,128]{1,0:T(8,128)(2,1)S(1)}, bf16[400,128]{1,0:T(8,128)(2,1)S(1)}, u32[]{:S(2)}, u32[]{:S(2)}) collective-permute-start(bf16[400,128]{1,0:T(8,128)(2,1)S(1)} %get-tuple-element.148), channel_id=1, source_target_pairs={{0,2},{1,3},{2,0},{3,1},{4,6},{5,7},{6,4},{7,5},{8,10},{9,11},{10,... | collective-permute-start | bytes 307208 | tf_op jit(solution)/shard_map/ppermute | solution.py:1175
  59.9 5.8 %collective-permute-start.23 = (bf16[400,128]{1,0:T(8,128)(2,1)S(1)}, bf16[400,128]{1,0:T(8,128)(2,1)S(1)}, u32[]{:S(2)}, u32[]{:S(2)}) collective-permute-start(bf16[400,128]{1,0:T(8,128)(2,1)S(1)} %get-tuple-element.149), channel_id=1, source_target_pairs={{0,3},{1,2},{2,1},{3,0},{4,7},{5,6},{6,5},{7,4},{8,11},{9,10},{10,... | collective-permute-start | bytes 307208 | tf_op jit(solution)/shard_map/ppermute | solution.py:1175
  65.7 4.7 %collective-permute-start.27 = (bf16[2,384,128]{2,1,0:T(8,128)(2,1)S(1)}, bf16[2,384,128]{2,1,0:T(8,128)(2,1)S(1)}, u32[]{:S(2)}, u32[]{:S(2)}) collective-permute-start(bf16[2,384,128]{2,1,0:T(8,128)(2,1)S(1)} %choose.1), channel_id=1, source_target_pairs={{0,4},{4,0},{1,5},{5,1},{2,6},{6,2},{3,7},{7,3},{8,12},{12,8},{9,1... | collective-permute-start | bytes 589832 | tf_op jit(solution)/shard_map/ppermute | solution.py:1170
  66.0 5.5 %collective-permute-start.24 = (bf16[48,384]{1,0:T(8,128)(2,1)S(1)}, bf16[48,384]{1,0:T(8,128)(2,1)S(1)}, u32[]{:S(2)}, u32[]{:S(2)}) collective-permute-start(bf16[48,384]{1,0:T(8,128)(2,1)S(1)} %get-tuple-element.151), channel_id=1, source_target_pairs={{0,8},{8,0},{16,24},{24,16},{1,9},{9,1},{17,25},{25,17},{2,10},{10... | collective-permute-start | bytes 110600 | tf_op jit(solution)/shard_map/ppermute | solution.py:1175
  67.2 5.8 %collective-permute-start.25 = (bf16[48,384]{1,0:T(8,128)(2,1)S(1)}, bf16[48,384]{1,0:T(8,128)(2,1)S(1)}, u32[]{:S(2)}, u32[]{:S(2)}) collective-permute-start(bf16[48,384]{1,0:T(8,128)(2,1)S(1)} %get-tuple-element.152), channel_id=1, source_target_pairs={{0,16},{8,24},{16,0},{24,8},{1,17},{9,25},{17,1},{25,9},{2,18},{10... | collective-permute-start | bytes 110600 | tf_op jit(solution)/shard_map/ppermute | solution.py:1175
  70.2 5.8 %collective-permute-start.26 = (bf16[48,384]{1,0:T(8,128)(2,1)S(1)}, bf16[48,384]{1,0:T(8,128)(2,1)S(1)}, u32[]{:S(2)}, u32[]{:S(2)}) collective-permute-start(bf16[48,384]{1,0:T(8,128)(2,1)S(1)} %get-tuple-element.153), channel_id=1, source_target_pairs={{0,24},{8,16},{16,8},{24,0},{1,25},{9,17},{17,9},{25,1},{2,26},{10... | collective-permute-start | bytes 110600 | tf_op jit(solution)/shard_map/ppermute | solution.py:1175
  (1 other events, 0.7 us)
